TPU v7x, 32 devices: a whole 2x2x4 slice. The times are simulated.
32 devices in a mesh: gx: 4 (over z), gy: 2 (over x), gz: 4 (over y, core).
Axes of the slice: x: 2, y: 2, z: 4, core: 2. Of those that a mesh axis runs over, the one named last changes fastest.
Arguments:
- features: bfloat16 [32, 16, 16, 256], P('gx', 'gy', 'gz'), may hold values from -64 to 64
- occupancy: int32 [4, 2, 16], P(None, 'gy', 'gz'), may hold values from 0 to 1, as said below
- norm_gain: float32 [2, 32], replicated, may hold values from 0.1 to 1.9
- norm_shift: float32 [2, 32], replicated, may hold values from -3 to 3
- conv_weight: bfloat16 [2, 32, 864], replicated, may hold values from -0.21875 to 0.21875
- conv_bias: float32 [2, 32], replicated, may hold values from -3 to 3
- qkv_weight: bfloat16 [3, 1024, 1024], P(None, 'gx'), may hold values from -1 to 1
Outputs:
- fine_out: bfloat16 [32, 16, 16, 256], P('gx', 'gy', 'gz')
- attention: bfloat16 [8, 256, 1024], P(('gy', 'gz'), 'gx')
Inputs may be any that keep to these rules, and one draw needn't show every extreme that they name: `occupancy`: each aligned block of 4 bricks along the third dimension holds at least one occupied brick.
All inputs are finite; a program needn't handle non-finite values.
Results may differ from a plain program's by a relative error of at most 0.015.
The roundings to bfloat16 on the way count: a program that leaves them out, or rounds other values in their place, can miss the bound.
Values may be sent and summed in bfloat16 or wider, within the bound.
No kernel may reach another device: no remote copies, remote signals or barrier semaphores. Data moves between devices by JAX's collectives and lax.ppermute only.
A program may use at most 64 MiB of HBM per device.

v0:
```python
import jax
import jax.numpy as jnp
from jax import lax
from jax.sharding import PartitionSpec as P

C = 32
GROUPS_NORM = 8
D = 1024
HD = 64


EPS = 1e-05


def with_halo(x, sides, width):
    for axis, dim in sides:
        peers, length = (lax.axis_size(axis), x.shape[dim])
        up = [(i, (i + 1) % peers) for i in range(peers - 1)]
        down = [(j, i) for i, j in up]
        last = lax.slice_in_dim(x, length - width, length, axis=dim)
        first = lax.slice_in_dim(x, 0, width, axis=dim)
        before = lax.ppermute(last, axis, up)
        after = lax.ppermute(first, axis, down)
        x = jnp.concatenate([before, x, after], axis=dim)
    return x


def convolve(padded, weight):
    channels = padded.shape[0]
    extent = (padded.shape[1] - 2, padded.shape[2] - 2, padded.shape[3] - 2)
    volume = extent[0] * extent[1] * extent[2]
    accumulated = jnp.zeros((weight.shape[0], volume), jnp.float32)
    for shift_x in range(3):
        pieces = []
        for shift_y in range(3):
            for shift_z in range(3):
                pieces.append(
                    padded[
                        :,
                        shift_x : shift_x + extent[0],
                        shift_y : shift_y + extent[1],
                        shift_z : shift_z + extent[2],
                    ].reshape(channels, volume)
                )
        stacked = jnp.concatenate(pieces, axis=0)
        columns = weight[:, shift_x * 9 * channels : (shift_x + 1) * 9 * channels]
        accumulated = accumulated + jnp.dot(columns, stacked, preferred_element_type=jnp.float32)
    return accumulated.reshape((weight.shape[0],) + extent)


def moments(values, voxel_mask):
    group_width = C // GROUPS_NORM
    shaped = values.reshape(GROUPS_NORM, group_width, -1)
    flat_mask = voxel_mask.reshape(1, 1, -1)
    occupied = jnp.sum(voxel_mask) * group_width
    masked = shaped * flat_mask
    group_sums, squares, counted = lax.psum(
        (jnp.sum(masked, axis=(1, 2)), jnp.sum(masked * shaped, axis=(1, 2)), occupied),
        ("gx", "gy", "gz"),
    )
    centre = group_sums / counted
    spread = squares / counted - centre * centre
    return (centre, spread)


def normalize(values, voxel_mask, centre, spread, gain_row, shift_row):
    group_width = values.shape[0] // GROUPS_NORM
    shaped = values.reshape((GROUPS_NORM, group_width) + values.shape[1:])
    normed = (shaped - centre[:, None, None, None, None]) * lax.rsqrt(spread + EPS)[
        :, None, None, None, None
    ]
    normed = (
        normed.reshape(values.shape) * gain_row[:, None, None, None]
        + shift_row[:, None, None, None]
    )
    return jax.nn.silu(normed) * voxel_mask


def with_faces(field):
    return with_halo(field, (("gx", 1), ("gy", 2), ("gz", 3)), 1)


def body(features, occupancy, norm_gain, norm_shift, conv_weight, conv_bias, qkv_weight):
    member = lax.axis_index("gx")
    size_x, size_y, brick_count = (features.shape[0], features.shape[1], features.shape[2])
    extent = (size_x, size_y, brick_count * 8)
    field = (
        features.reshape(size_x, size_y, brick_count, C, 8)
        .transpose(3, 0, 1, 2, 4)
        .reshape((C,) + extent)
    )
    group_bricks = occupancy[:, 0, :].astype(jnp.float32)
    own_bricks = lax.dynamic_index_in_dim(group_bricks, member, 0, keepdims=False)
    voxel_mask = jnp.broadcast_to(jnp.repeat(own_bricks, 8), (1,) + extent)
    inputs = field * voxel_mask.astype(jnp.bfloat16)
    centre, spread = moments(inputs.astype(jnp.float32), voxel_mask)
    first_act = normalize(
        inputs.astype(jnp.float32), voxel_mask, centre, spread, norm_gain[0], norm_shift[0]
    ).astype(jnp.bfloat16)
    first_bias = conv_bias[0][:, None, None, None]
    middle = (convolve(with_faces(first_act), conv_weight[0]) + first_bias) * voxel_mask
    centre, spread = moments(middle, voxel_mask)
    second_act = normalize(middle, voxel_mask, centre, spread, norm_gain[1], norm_shift[1]).astype(
        jnp.bfloat16
    )
    padded = with_faces(second_act)
    second_term = convolve(padded, conv_weight[1]) + conv_bias[1][:, None, None, None]
    out_field = ((inputs.astype(jnp.float32) + second_term) * voxel_mask).astype(jnp.bfloat16)
    fine_out = (
        out_field.reshape(C, size_x, size_y, brick_count, 8)
        .transpose(1, 2, 3, 0, 4)
        .reshape(size_x, size_y, brick_count, C * 8)
    )
    depth_z = extent[2]
    tokens = (
        out_field.reshape(C, 4, 2, 2, 4, depth_z // 4, 4)
        .transpose(1, 3, 5, 0, 2, 4, 6)
        .reshape(-1, D)
    )
    brick_keep = jnp.repeat(group_bricks, 2, axis=1)
    member_count = brick_keep.shape[0]
    key_keep = jnp.broadcast_to(
        brick_keep[:, None, None, :], (member_count, 4, 2, depth_z // 4)
    ).reshape(-1)
    own_keep = jnp.broadcast_to(
        jnp.repeat(own_bricks, 2)[None, None, :], (4, 2, depth_z // 4)
    ).reshape(-1)
    local_cols = qkv_weight.shape[1]
    contract = (((1,), (1,)), ((), ()))
    portion = lax.all_gather(tokens, "gx", axis=0, tiled=True)
    flat_weight = qkv_weight.reshape(3 * local_cols, D)
    product = lax.dot_general(
        portion, flat_weight, contract, preferred_element_type=jnp.float32
    ).astype(jnp.bfloat16)
    projected = product.reshape(portion.shape[0], 3, local_cols)
    seq_len = projected.shape[0]
    head_count = local_cols // HD
    queries = projected[:, 0].reshape(seq_len, head_count, HD)
    keys_all = projected[:, 1].reshape(seq_len, head_count, HD)
    values_all = projected[:, 2].reshape(seq_len, head_count, HD)
    block_rows = min(512, seq_len)
    blocks = queries.reshape(seq_len // block_rows, block_rows, head_count, HD)
    score_scale = float(HD) ** (-0.5)

    def attend_rows(query_block):
        scores = (
            jnp.einsum("qhd,khd->hqk", query_block, keys_all, preferred_element_type=jnp.float32)
            * score_scale
        )
        scores = jnp.where(key_keep[None, None, :] > 0, scores, -jnp.inf)
        row_max = jnp.max(scores, axis=2, keepdims=True)
        weights = jnp.exp(scores - row_max)
        totals = jnp.sum(weights, axis=2)
        mixed_rows = jnp.einsum(
            "hqk,khd->qhd",
            weights.astype(jnp.bfloat16),
            values_all,
            preferred_element_type=jnp.float32,
        )
        return (
            (mixed_rows / totals.T[:, :, None])
            .astype(jnp.bfloat16)
            .reshape(block_rows, head_count * HD)
        )

    outputs = lax.map(attend_rows, blocks).reshape(seq_len, local_cols)
    arrived = lax.all_to_all(outputs, "gx", split_axis=0, concat_axis=1, tiled=True)
    attention = arrived * own_keep[:, None].astype(jnp.bfloat16)
    return (fine_out, attention[None])


def solution(mesh):
    placed = (
        P("gx", "gy", "gz", None),
        P(None, "gy", "gz"),
        P(),
        P(),
        P(),
        P(),
        P(None, "gx", None),
    )
    return jax.shard_map(
        body,
        mesh=mesh,
        in_specs=placed,
        out_specs=(P("gx", "gy", "gz", None), P(("gy", "gz"), "gx", None)),
        check_vma=False,
    )
```

profile of v0, /device:TPU:0, one launch (start us, length us, event | category | flops | bytes accessed | tf_op | source)
XLA Modules:
  0.0 264.6 jit_solution(11229883575295770750)
XLA Ops:
  2.2 4.3 %reshape.405 = bf16[8,8,4,32,8]{4,3,2,1,0:T(8,128)(2,1)} reshape(bf16[8,8,4,256]{3,2,1,0:T(4,128)(2,1)} %param.7) | data formatting | bytes 262144 | tf_op jit(solution)/shard_map/reshape | solution.py:88
  6.5 2.0 copy.142
  10.0 42.0 %all-reduce.1 = (f32[8]{0:T(128)S(1)}, f32[]{:T(128)}, f32[8]{0:T(128)S(1)}) all-reduce(f32[8]{0:T(128)S(1)} %reduce_sum.89, f32[]{:T(128)S(6)} %mul.202, f32[8]{0:T(128)S(1)} %reduce_sum.93), channel_id=1, replica_groups=mesh['gx'=4,'gy'=2,'gz'=4] {'gx','gy','gz'}, use_global_device_ids=true, to_apply=%region_2.3 | all-reduce | flops 17 | bytes 136 | tf_op jit(solution)/shard_map/psum | solution.py:57
  54.1 3.4 %collective-permute-start = (bf16[32,1,8,32]{0,3,2,1:T(8,128)(2,1)S(1)}, bf16[32,1,8,32]{0,3,2,1:T(8,128)(2,1)S(1)}, u32[]{:S(2)}, u32[]{:S(2)}) collective-permute-start(bf16[32,1,8,32]{0,3,2,1:T(8,128)(2,1)S(1)} %get-tuple-element.115), channel_id=1, source_target_pairs={{0,8},{8,16},{16,24},{1,9},{9,17},{17,25},{2,10},{10,18},{18,26},{... | collective-permute-start | bytes 49160 | tf_op jit(solution)/shard_map/ppermute | solution.py:22
  57.5 1.3 collective-permute-start.1
  60.3 0.8 copy.147
  61.1 2.5 collective-permute-done.1
  63.7 4.2 %collective-permute-start.2 = (bf16[32,10,1,32]{0,3,2,1:T(8,128)(2,1)S(1)}, bf16[32,10,1,32]{0,3,2,1:T(8,128)(2,1)S(1)}, u32[]{:S(2)}, u32[]{:S(2)}) collective-permute-start(bf16[32,10,1,32]{0,3,2,1:T(8,128)(2,1)S(1)} %get-tuple-element.107), channel_id=1, source_target_pairs={{0,4},{1,5},{2,6},{3,7},{8,12},{9,13},{10,14},{11,15},{16,20},{17,... | collective-permute-start | bytes 61448 | tf_op jit(solution)/shard_map/ppermute | solution.py:22
  67.9 1.3 collective-permute-start.3
  69.2 1.2 pad_maximum_fusion.6
  70.4 3.8 %collective-permute-done.3 = bf16[32,10,1,32]{0,3,2,1:T(8,128)(2,1)S(1)} collective-permute-done((bf16[32,10,1,32]{0,3,2,1:T(8,128)(2,1)S(1)}, bf16[32,10,1,32]{0,3,2,1:T(8,128)(2,1)S(1)}, u32[]{:S(2)}, u32[]{:S(2)}) %collective-permute-start.3) | collective-permute-done | bytes 20512 | tf_op jit(solution)/shard_map/ppermute | solution.py:23
  74.9 1.3 collective-permute-start.5
  76.2 3.7 %collective-permute-start.4 = (bf16[32,10,10,1]{0,3,2,1:T(2,128)(2,1)S(1)}, bf16[32,10,10,1]{0,3,2,1:T(2,128)(2,1)}, u32[]{:S(2)}, u32[]{:S(2)}) collective-permute-start(bf16[32,10,10,1]{0,3,2,1:T(2,128)(2,1)S(1)} %get-tuple-element.88), channel_id=1, source_target_pairs={{0,1},{1,2},{2,3},{4,5},{5,6},{6,7},{8,9},{9,10},{10,11},{12,13},{... | collective-permute-start | bytes 19208 | tf_op jit(solution)/shard_map/ppermute | solution.py:22
  80.1 1.3 fusion.33
  81.5 1.3 fusion.34
  83.6 0.8 copy.175
  84.5 2.1 pad_maximum_fusion
  86.6 2.8 %fusion.29 = (bf16[32,8,8,32]{0,3,2,1:T(8,128)(2,1)}, bf16[32,8,8,32]{0,3,2,1:T(8,128)(2,1)}, bf16[32,8,8,32]{0,3,2,1:T(8,128)(2,1)}, bf16[32,8,8,32]{0,3,2,1:T(...) fusion(bf16[32,10,10,33]{0,3,2,1:T(8,128)(2,1)S(1)} %get-tuple-, ...), kind=kLoop, calls=%fused_computation.112 | loop fusion | bytes 2359296 | tf_op jit(solution)/shard_map/slice | solution.py:38
  89.4 1.2 copy.181
  90.6 1.2 copy.178
  92.0 2.3 fusion.30
  94.3 1.3 copy.179
  95.6 1.3 copy.177
  97.4 1.1 fusion.23
  98.6 6.1 %concatenate.115 = bf16[288,2048]{0,1:T(8,128)(2,1)S(1)} concatenate(bf16[32,2048]{0,1:T(8,128)(2,1)} %bitcast.161, bf16[32,2048]{0,1:T(8,128)(2,1)} %bitcast.185, bf16[32,2048]{0,1:T(8,128)(2,1)} %bitcast.152, bf16[32,2048]{0,1:T(8,128)(2,1)} %bitcast.160, bf16[32,2048]{0,1:T(8,128)(2,1)} %bitcast.177, bf16[32,2048]{0,1:T(8,128)(2,1)} %bitcast.151, bf16[32,2048]{0,1:T(8,128)(2,1)} %bitcast.159, ...), dimensions={0} | concatenate | bytes 2359296 | tf_op jit(solution)/shard_map/concatenate | solution.py:45
  104.7 1.3 convolution_add_fusion.3
  106.0 6.1 %concatenate.118 = bf16[288,2048]{0,1:T(8,128)(2,1)S(1)} concatenate(bf16[32,2048]{0,1:T(8,128)(2,1)} %bitcast.155, bf16[32,2048]{0,1:T(8,128)(2,1)} %bitcast.181, bf16[32,2048]{0,1:T(8,128)(2,1)} %bitcast.143, bf16[32,2048]{0,1:T(8,128)(2,1)} %bitcast.154, bf16[32,2048]{0,1:T(8,128)(2,1)} %bitcast.175, bf16[32,2048]{0,1:T(8,128)(2,1)} %bitcast.142, bf16[32,2048]{0,1:T(8,128)(2,1)} %bitcast.153, ...), dimensions={0} | concatenate | bytes 2359296 | tf_op jit(solution)/shard_map/concatenate | solution.py:45
  112.1 1.7 fusion.15
  114.2 39.1 %all-reduce = (f32[8]{0:T(128)S(1)}, f32[8]{0:T(128)S(1)}) all-reduce(f32[8]{0:T(128)S(1)} %reduce_sum.96, f32[8]{0:T(128)S(1)} %reduce_sum.99), channel_id=1, replica_groups=mesh['gx'=4,'gy'=2,'gz'=4] {'gx','gy','gz'}, use_global_device_ids=true, to_apply=%region_10.11 | all-reduce | flops 16 | bytes 128 | tf_op jit(solution)/shard_map/psum | solution.py:57
  155.1 2.5 collective-permute-start.6
  157.7 1.5 collective-permute-start.7
  161.4 2.4 collective-permute-done.7
  163.9 4.2 %collective-permute-start.8 = (bf16[32,10,1,32]{0,3,2,1:T(8,128)(2,1)S(1)}, bf16[32,10,1,32]{0,3,2,1:T(8,128)(2,1)S(1)}, u32[]{:S(2)}, u32[]{:S(2)}) collective-permute-start(bf16[32,10,1,32]{0,3,2,1:T(8,128)(2,1)S(1)} %get-tuple-element.103), channel_id=1, source_target_pairs={{0,4},{1,5},{2,6},{3,7},{8,12},{9,13},{10,14},{11,15},{16,20},{17,... | collective-permute-start | bytes 61448 | tf_op jit(solution)/shard_map/ppermute | solution.py:22
  168.1 1.3 collective-permute-start.9
  169.4 1.2 pad_maximum_fusion.4
  170.6 3.8 %collective-permute-done.9 = bf16[32,10,1,32]{0,3,2,1:T(8,128)(2,1)S(1)} collective-permute-done((bf16[32,10,1,32]{0,3,2,1:T(8,128)(2,1)S(1)}, bf16[32,10,1,32]{0,3,2,1:T(8,128)(2,1)S(1)}, u32[]{:S(2)}, u32[]{:S(2)}) %collective-permute-start.9) | collective-permute-done | bytes 20512 | tf_op jit(solution)/shard_map/ppermute | solution.py:23
  175.2 1.3 collective-permute-start.11
  176.5 3.6 %collective-permute-start.10 = (bf16[32,10,10,1]{0,3,2,1:T(2,128)(2,1)}, bf16[32,10,10,1]{0,3,2,1:T(2,128)(2,1)}, u32[]{:S(2)}, u32[]{:S(2)}) collective-permute-start(bf16[32,10,10,1]{0,3,2,1:T(2,128)(2,1)} %get-tuple-element.84), channel_id=1, source_target_pairs={{0,1},{1,2},{2,3},{4,5},{5,6},{6,7},{8,9},{9,10},{10,11},{12,13},{... | collective-permute-start | bytes 19208 | tf_op jit(solution)/shard_map/ppermute | solution.py:22
  180.3 1.3 fusion.31
  181.7 1.3 fusion.32
  183.8 0.8 copy.184
  184.7 2.2 pad_maximum_fusion.1
  186.9 2.8 %fusion.27 = (bf16[32,8,8,32]{0,3,2,1:T(8,128)(2,1)}, bf16[32,8,8,32]{0,3,2,1:T(8,128)(2,1)}, bf16[32,8,8,32]{0,3,2,1:T(8,128)(2,1)}, bf16[32,8,8,32]{0,3,2,1:T(...) fusion(bf16[32,10,10,33]{0,3,2,1:T(8,128)(2,1)S(1)} %get-tuple-, ...), kind=kLoop, calls=%fused_computation.110 | loop fusion | bytes 2359296 | tf_op jit(solution)/shard_map/slice | solution.py:38
  189.7 1.2 copy.190
  190.9 1.9 copy.187
  192.8 0.8 copy.185
  193.6 2.3 fusion.28
  196.0 1.3 copy.188
  197.3 1.3 copy.186
  199.2 1.1 fusion.19
  200.3 6.1 %concatenate.126 = bf16[288,2048]{0,1:T(8,128)(2,1)S(1)} concatenate(bf16[32,2048]{0,1:T(8,128)(2,1)} %bitcast.158, bf16[32,2048]{0,1:T(8,128)(2,1)} %bitcast.184, bf16[32,2048]{0,1:T(8,128)(2,1)} %bitcast.146, bf16[32,2048]{0,1:T(8,128)(2,1)} %bitcast.157, bf16[32,2048]{0,1:T(8,128)(2,1)} %bitcast.176, bf16[32,2048]{0,1:T(8,128)(2,1)} %bitcast.145, bf16[32,2048]{0,1:T(8,128)(2,1)} %bitcast.156, ...), dimensions={0} | concatenate | bytes 2359296 | tf_op jit(solution)/shard_map/concatenate | solution.py:45
  206.4 1.3 convolution_add_fusion.1
  207.7 6.5 %concatenate.129 = bf16[288,2048]{0,1:T(8,128)(2,1)} concatenate(bf16[32,2048]{0,1:T(8,128)(2,1)} %bitcast.149, bf16[32,2048]{0,1:T(8,128)(2,1)} %bitcast.180, bf16[32,2048]{0,1:T(8,128)(2,1)} %bitcast.140, bf16[32,2048]{0,1:T(8,128)(2,1)} %bitcast.148, bf16[32,2048]{0,1:T(8,128)(2,1)} %bitcast.174, bf16[32,2048]{0,1:T(8,128)(2,1)} %bitcast.139, bf16[32,2048]{0,1:T(8,128)(2,1)} %bitcast.147, ...), dimensions={0} | concatenate | bytes 2359296 | tf_op jit(solution)/shard_map/concatenate | solution.py:45
  214.2 2.0 fusion
  216.7 1.3 fusion.12
  218.0 6.9 %copy.164 = bf16[4,2,8,32,2,4,4]{2,1,0,6,5,4,3:T(2,128)(2,1)} copy(bf16[4,2,8,32,2,4,4]{3,6,2,5,1,4,0:T(4,128)(2,1)} %fusion.12) | data formatting | bytes 262144 | tf_op jit(solution)/shard_map/transpose | solution.py:117
  224.9 6.4 %reshape.402 = bf16[64,1024]{0,1:T(8,128)(2,1)S(1)} reshape(bf16[4,2,8,32,2,4,4]{2,1,0,6,5,4,3:T(2,128)(2,1)} %copy.164) | data formatting | bytes 262144 | tf_op jit(solution)/shard_map/reshape | solution.py:118
  231.5 16.3 %all_gather.3 = bf16[256,1024]{1,0:T(8,128)(2,1)S(1)} all-gather(bf16[64,1024]{1,0:T(8,128)(2,1)S(1)} %copy.165), channel_id=1, replica_groups=mesh['gx'=4,'gy'=2,'gz'=4] {'gx'}, dimensions={0}, use_global_device_ids=true | all-gather | bytes 655360 | tf_op jit(solution)/shard_map/all_gather | solution.py:130
  247.8 1.4 convolution_convert_fusion
  249.1 1.2 copy.166
  252.2 3.3 %all-to-all-start = ((bf16[4,64,256]{2,1,0:T(8,128)(2,1)}), bf16[4,64,256]{2,1,0:T(8,128)(2,1)S(1)}, u32[]{:S(2)}, u32[]{:S(2)}) async-start(bf16[4,64,256]{2,1,0:T(8,128)(2,1)} %copy.192), calls=%async_computation | async-start | bytes 262144 | tf_op jit(solution)/shard_map/all_to_all | solution.py:167
  255.5 1.1 fusion.13
  256.6 2.7 %copy.191 = bf16[8,8,4,32,8]{4,3,2,1,0:T(8,128)(2,1)} copy(bf16[8,8,4,32,8]{3,4,2,1,0:T(8,128)(2,1)} %fusion.13) | data formatting | bytes 262144
  259.3 4.4 %reshape.406 = bf16[8,8,4,256]{3,2,1,0:T(4,128)(2,1)} reshape(bf16[8,8,4,32,8]{4,3,2,1,0:T(8,128)(2,1)} %copy.191) | data formatting | bytes 262144
  (179 shorter events, 18.2 us)
Async XLA Ops:
  0.6 247.1 %copy-start = (bf16[3,256,1024]{2,1,0:T(8,128)(2,1)S(1)}, bf16[3,256,1024]{2,1,0:T(8,128)(2,1)}, u32[]{:S(2)}) copy-start(bf16[3,256,1024]{2,1,0:T(8,128)(2,1)} %param.13) | copy-start | bytes 4718596
  1.5 7.1 %copy-start.30 = (bf16[4]{0:T(256)(128)(2,1)}, bf16[4]{0:T(256)(128)(2,1)S(1)}, u32[]{:S(2)}) copy-start(bf16[4]{0:T(256)(128)(2,1)S(1)} %get-tuple-element.43) | copy-start | bytes 28
  6.5 46.4 %copy-start.39 = (f32[2,32]{1,0:T(2,128)S(1)}, f32[2,32]{1,0:T(2,128)}, u32[]{:S(2)}) copy-start(f32[2,32]{1,0:T(2,128)} %param.10) | copy-start | bytes 772
  6.5 46.4 %copy-start.40 = (f32[2,32]{1,0:T(2,128)S(1)}, f32[2,32]{1,0:T(2,128)}, u32[]{:S(2)}) copy-start(f32[2,32]{1,0:T(2,128)} %param.9) | copy-start | bytes 772
  8.5 55.1 %copy-start.1 = (bf16[8,8,4,32,8]{3,4,2,1,0:T(8,128)(2,1)}, bf16[8,8,4,32,8]{3,4,2,1,0:T(8,128)(2,1)S(1)}, u32[]{:S(2)}) copy-start(bf16[8,8,4,32,8]{3,4,2,1,0:T(8,128)(2,1)S(1)} %copy.142) | copy-start | bytes 393220
  8.6 50.2 %copy-start.15 = (bf16[2,32,864]{2,1,0:T(8,128)(2,1)S(1)}, bf16[2,32,864]{2,1,0:T(8,128)(2,1)}, u32[]{:S(2)}) copy-start(bf16[2,32,864]{2,1,0:T(8,128)(2,1)} %param.11) | copy-start | bytes 331780
  8.6 50.9 %copy-start.38 = (f32[2,32]{1,0:T(2,128)S(1)}, f32[2,32]{1,0:T(2,128)}, u32[]{:S(2)}) copy-start(f32[2,32]{1,0:T(2,128)} %param.12) | copy-start | bytes 772
  53.5 6.6 %copy-start.17 = (f32[32]{0:T(128)}, f32[32]{0:T(128)S(1)}, u32[]{:S(2)}) copy-start(f32[32]{0:T(128)S(1)} %get-tuple-element.127) | copy-start | bytes 388
  53.5 6.6 %copy-start.19 = (f32[32]{0:T(128)}, f32[32]{0:T(128)S(1)}, u32[]{:S(2)}) copy-start(f32[32]{0:T(128)S(1)} %get-tuple-element.131) | copy-start | bytes 388
  54.1 7.0 %collective-permute-start = (bf16[32,1,8,32]{0,3,2,1:T(8,128)(2,1)S(1)}, bf16[32,1,8,32]{0,3,2,1:T(8,128)(2,1)S(1)}, u32[]{:S(2)}, u32[]{:S(2)}) collective-permute-start(bf16[32,1,8,32]{0,3,2,1:T(8,128)(2,1)S(1)} %get-tuple-element.115), channel_id=1, source_target_pairs={{0,8},{8,16},{16,24},{1,9},{9,17},{17,25},{2,10},{10,18},{18,26},{... | collective-permute-start | bytes 49160 | tf_op jit(solution)/shard_map/ppermute | solution.py:22
  57.5 6.2 %collective-permute-start.1 = (bf16[32,1,8,32]{0,3,2,1:T(8,128)(2,1)S(1)}, bf16[32,1,8,32]{0,3,2,1:T(8,128)(2,1)S(1)}, u32[]{:S(2)}, u32[]{:S(2)}) collective-permute-start(bf16[32,1,8,32]{0,3,2,1:T(8,128)(2,1)S(1)} %get-tuple-element.116), channel_id=1, source_target_pairs={{8,0},{16,8},{24,16},{9,1},{17,9},{25,17},{10,2},{18,10},{26,18},{... | collective-permute-start | bytes 49160 | tf_op jit(solution)/shard_map/ppermute | solution.py:23
  63.7 6.7 %collective-permute-start.2 = (bf16[32,10,1,32]{0,3,2,1:T(8,128)(2,1)S(1)}, bf16[32,10,1,32]{0,3,2,1:T(8,128)(2,1)S(1)}, u32[]{:S(2)}, u32[]{:S(2)}) collective-permute-start(bf16[32,10,1,32]{0,3,2,1:T(8,128)(2,1)S(1)} %get-tuple-element.107), channel_id=1, source_target_pairs={{0,4},{1,5},{2,6},{3,7},{8,12},{9,13},{10,14},{11,15},{16,20},{17,... | collective-permute-start | bytes 61448 | tf_op jit(solution)/shard_map/ppermute | solution.py:22
  67.9 6.3 %collective-permute-start.3 = (bf16[32,10,1,32]{0,3,2,1:T(8,128)(2,1)S(1)}, bf16[32,10,1,32]{0,3,2,1:T(8,128)(2,1)S(1)}, u32[]{:S(2)}, u32[]{:S(2)}) collective-permute-start(bf16[32,10,1,32]{0,3,2,1:T(8,128)(2,1)S(1)} %get-tuple-element.108), channel_id=1, source_target_pairs={{4,0},{5,1},{6,2},{7,3},{12,8},{13,9},{14,10},{15,11},{20,16},{21,... | collective-permute-start | bytes 61448 | tf_op jit(solution)/shard_map/ppermute | solution.py:23
  74.9 9.5 %collective-permute-start.5 = (bf16[32,10,10,1]{0,3,2,1:T(2,128)(2,1)}, bf16[32,10,10,1]{0,3,2,1:T(2,128)(2,1)}, u32[]{:S(2)}, u32[]{:S(2)}) collective-permute-start(bf16[32,10,10,1]{0,3,2,1:T(2,128)(2,1)} %get-tuple-element.87), channel_id=1, source_target_pairs={{1,0},{2,1},{3,2},{5,4},{6,5},{7,6},{9,8},{10,9},{11,10},{13,12},{... | collective-permute-start | bytes 19208 | tf_op jit(solution)/shard_map/ppermute | solution.py:23
  76.2 8.3 %collective-permute-start.4 = (bf16[32,10,10,1]{0,3,2,1:T(2,128)(2,1)S(1)}, bf16[32,10,10,1]{0,3,2,1:T(2,128)(2,1)}, u32[]{:S(2)}, u32[]{:S(2)}) collective-permute-start(bf16[32,10,10,1]{0,3,2,1:T(2,128)(2,1)S(1)} %get-tuple-element.88), channel_id=1, source_target_pairs={{0,1},{1,2},{2,3},{4,5},{5,6},{6,7},{8,9},{9,10},{10,11},{12,13},{... | collective-permute-start | bytes 19208 | tf_op jit(solution)/shard_map/ppermute | solution.py:22
  94.3 2.8 %copy-start.9 = (bf16[32,2048]{1,0:T(8,128)(2,1)S(1)}, bf16[32,2048]{1,0:T(8,128)(2,1)}, u32[]{:S(2)}) copy-start(bf16[32,2048]{1,0:T(8,128)(2,1)} %copy.175) | copy-start | bytes 393220
  94.3 2.8 %copy-start.6 = (bf16[32,2048]{1,0:T(8,128)(2,1)S(1)}, bf16[32,2048]{1,0:T(8,128)(2,1)}, u32[]{:S(2)}) copy-start(bf16[32,2048]{1,0:T(8,128)(2,1)} %copy.147) | copy-start | bytes 393220
  94.3 2.8 %copy-start.18 = (f32[32]{0:T(128)S(1)}, f32[32]{0:T(128)}, u32[]{:S(2)}) copy-start(f32[32]{0:T(128)} %copy-done.17) | copy-start | bytes 388
  94.3 2.8 %copy-start.20 = (f32[32]{0:T(128)S(1)}, f32[32]{0:T(128)}, u32[]{:S(2)}) copy-start(f32[32]{0:T(128)} %copy-done.19) | copy-start | bytes 388
  95.6 1.8 copy-start.8
  98.6 6.1 %copy-start.14 = (bf16[32,864]{1,0:T(8,128)(2,1)S(1)}, bf16[32,864]{1,0:T(8,128)(2,1)}, u32[]{:S(2)}) copy-start(bf16[32,864]{1,0:T(8,128)(2,1)} %get-tuple-element.121) | copy-start | bytes 165892
  112.1 42.5 %copy-start.26 = (f32[32]{0:T(128)S(1)}, f32[32]{0:T(128)}, u32[]{:S(2)}) copy-start(f32[32]{0:T(128)} %get-tuple-element.126) | copy-start | bytes 388
  112.1 42.5 %copy-start.28 = (f32[32]{0:T(128)S(1)}, f32[32]{0:T(128)}, u32[]{:S(2)}) copy-start(f32[32]{0:T(128)} %get-tuple-element.132) | copy-start | bytes 388
  154.0 1.1 copy-start.21
  154.2 0.9 copy-start.23
  154.5 4.6 %copy-start.16 = (s32[4,1,4]{2,1,0:T(1,128)S(1)}, s32[4,1,4]{2,1,0:T(1,128)}, u32[]{:S(2)}) copy-start(s32[4,1,4]{2,1,0:T(1,128)} %param.8) | copy-start | bytes 196
  155.1 6.3 %collective-permute-start.6 = (bf16[32,1,8,32]{0,3,2,1:T(8,128)(2,1)S(1)}, bf16[32,1,8,32]{0,3,2,1:T(8,128)(2,1)S(1)}, u32[]{:S(2)}, u32[]{:S(2)}) collective-permute-start(bf16[32,1,8,32]{0,3,2,1:T(8,128)(2,1)S(1)} %get-tuple-element.111), channel_id=1, source_target_pairs={{0,8},{8,16},{16,24},{1,9},{9,17},{17,25},{2,10},{10,18},{18,26},{... | collective-permute-start | bytes 49160 | tf_op jit(solution)/shard_map/ppermute | solution.py:22
  157.7 6.2 %collective-permute-start.7 = (bf16[32,1,8,32]{0,3,2,1:T(8,128)(2,1)S(1)}, bf16[32,1,8,32]{0,3,2,1:T(8,128)(2,1)S(1)}, u32[]{:S(2)}, u32[]{:S(2)}) collective-permute-start(bf16[32,1,8,32]{0,3,2,1:T(8,128)(2,1)S(1)} %get-tuple-element.112), channel_id=1, source_target_pairs={{8,0},{16,8},{24,16},{9,1},{17,9},{25,17},{10,2},{18,10},{26,18},{... | collective-permute-start | bytes 49160 | tf_op jit(solution)/shard_map/ppermute | solution.py:23
  159.5 0.6 copy-start.34
  159.5 8.6 %copy-start.36 = (bf16[8]{0:T(256)(128)(2,1)}, bf16[8]{0:T(256)(128)(2,1)S(1)}, u32[]{:S(2)}) copy-start(bf16[8]{0:T(256)(128)(2,1)S(1)} %convert_element_type.86) | copy-start | bytes 52
  163.9 6.7 %collective-permute-start.8 = (bf16[32,10,1,32]{0,3,2,1:T(8,128)(2,1)S(1)}, bf16[32,10,1,32]{0,3,2,1:T(8,128)(2,1)S(1)}, u32[]{:S(2)}, u32[]{:S(2)}) collective-permute-start(bf16[32,10,1,32]{0,3,2,1:T(8,128)(2,1)S(1)} %get-tuple-element.103), channel_id=1, source_target_pairs={{0,4},{1,5},{2,6},{3,7},{8,12},{9,13},{10,14},{11,15},{16,20},{17,... | collective-permute-start | bytes 61448 | tf_op jit(solution)/shard_map/ppermute | solution.py:22
  168.1 6.3 %collective-permute-start.9 = (bf16[32,10,1,32]{0,3,2,1:T(8,128)(2,1)S(1)}, bf16[32,10,1,32]{0,3,2,1:T(8,128)(2,1)S(1)}, u32[]{:S(2)}, u32[]{:S(2)}) collective-permute-start(bf16[32,10,1,32]{0,3,2,1:T(8,128)(2,1)S(1)} %get-tuple-element.104), channel_id=1, source_target_pairs={{4,0},{5,1},{6,2},{7,3},{12,8},{13,9},{14,10},{15,11},{20,16},{21,... | collective-permute-start | bytes 61448 | tf_op jit(solution)/shard_map/ppermute | solution.py:23
  170.6 9.8 %copy-start.4 = (bf16[32,10,1,32]{0,3,2,1:T(8,128)(2,1)}, bf16[32,10,1,32]{0,3,2,1:T(8,128)(2,1)S(1)}, u32[]{:S(2)}) copy-start(bf16[32,10,1,32]{0,3,2,1:T(8,128)(2,1)S(1)} %collective-permute-done.8) | copy-start | bytes 61444
  174.4 5.9 %copy-start.5 = (bf16[32,10,1,32]{0,3,2,1:T(8,128)(2,1)}, bf16[32,10,1,32]{0,3,2,1:T(8,128)(2,1)S(1)}, u32[]{:S(2)}) copy-start(bf16[32,10,1,32]{0,3,2,1:T(8,128)(2,1)S(1)} %collective-permute-done.9) | copy-start | bytes 61444
  175.2 9.5 %collective-permute-start.11 = (bf16[32,10,10,1]{0,3,2,1:T(2,128)(2,1)}, bf16[32,10,10,1]{0,3,2,1:T(2,128)(2,1)}, u32[]{:S(2)}, u32[]{:S(2)}) collective-permute-start(bf16[32,10,10,1]{0,3,2,1:T(2,128)(2,1)} %get-tuple-element.83), channel_id=1, source_target_pairs={{1,0},{2,1},{3,2},{5,4},{6,5},{7,6},{9,8},{10,9},{11,10},{13,12},{... | collective-permute-start | bytes 19208 | tf_op jit(solution)/shard_map/ppermute | solution.py:23
  176.5 8.2 %collective-permute-start.10 = (bf16[32,10,10,1]{0,3,2,1:T(2,128)(2,1)}, bf16[32,10,10,1]{0,3,2,1:T(2,128)(2,1)}, u32[]{:S(2)}, u32[]{:S(2)}) collective-permute-start(bf16[32,10,10,1]{0,3,2,1:T(2,128)(2,1)} %get-tuple-element.84), channel_id=1, source_target_pairs={{0,1},{1,2},{2,3},{4,5},{5,6},{6,7},{8,9},{9,10},{10,11},{12,13},{... | collective-permute-start | bytes 19208 | tf_op jit(solution)/shard_map/ppermute | solution.py:22
  195.9 2.8 %copy-start.10 = (bf16[32,2048]{1,0:T(8,128)(2,1)S(1)}, bf16[32,2048]{1,0:T(8,128)(2,1)}, u32[]{:S(2)}) copy-start(bf16[32,2048]{1,0:T(8,128)(2,1)} %copy.184) | copy-start | bytes 393220
  195.9 2.8 %copy-start.12 = (bf16[32,2048]{1,0:T(8,128)(2,1)S(1)}, bf16[32,2048]{1,0:T(8,128)(2,1)}, u32[]{:S(2)}) copy-start(bf16[32,2048]{1,0:T(8,128)(2,1)} %copy.185) | copy-start | bytes 393220
  195.9 2.9 %copy-start.22 = (f32[32]{0:T(128)S(1)}, f32[32]{0:T(128)}, u32[]{:S(2)}) copy-start(f32[32]{0:T(128)} %copy-done.21) | copy-start | bytes 388
  195.9 2.9 %copy-start.24 = (f32[32]{0:T(128)S(1)}, f32[32]{0:T(128)}, u32[]{:S(2)}) copy-start(f32[32]{0:T(128)} %copy-done.23) | copy-start | bytes 388
  196.0 2.9 %copy-start.27 = (f32[32]{0:T(128)S(1)}, f32[32]{0:T(128)}, u32[]{:S(2)}) copy-start(f32[32]{0:T(128)} %get-tuple-element.126) | copy-start | bytes 388
  196.0 2.9 %copy-start.29 = (f32[32]{0:T(128)S(1)}, f32[32]{0:T(128)}, u32[]{:S(2)}) copy-start(f32[32]{0:T(128)} %get-tuple-element.132) | copy-start | bytes 388
  196.0 3.1 %copy-start.11 = (bf16[32,2048]{1,0:T(8,128)(2,1)S(1)}, bf16[32,2048]{1,0:T(8,128)(2,1)}, u32[]{:S(2)}) copy-start(bf16[32,2048]{1,0:T(8,128)(2,1)} %copy.187) | copy-start | bytes 393220
  197.3 1.8 copy-start.7
  200.3 6.1 %copy-start.13 = (bf16[32,864]{1,0:T(8,128)(2,1)S(1)}, bf16[32,864]{1,0:T(8,128)(2,1)}, u32[]{:S(2)}) copy-start(bf16[32,864]{1,0:T(8,128)(2,1)} %get-tuple-element.120) | copy-start | bytes 165892
  207.7 6.5 %copy-start.3 = (f32[2048,32]{0,1:T(8,128)S(1)}, f32[2048,32]{0,1:T(8,128)}, u32[]{:S(2)}) copy-start(f32[2048,32]{0,1:T(8,128)} %convolution_add_fusion.1) | copy-start | bytes 786436
  214.2 2.4 copy-start.2
  214.2 2.4 copy-start.25
  214.2 2.4 copy-start.35
  214.2 2.4 copy-start.37
  247.7 2.6 copy-start.33
  250.9 4.6 %copy-start.31 = (bf16[4]{0:T(256)(128)(2,1)S(1)}, bf16[4]{0:T(256)(128)(2,1)}, u32[]{:S(2)}) copy-start(bf16[4]{0:T(256)(128)(2,1)} %copy-done.30) | copy-start | bytes 28
  252.2 11.5 %all-to-all-start = ((bf16[4,64,256]{2,1,0:T(8,128)(2,1)}), bf16[4,64,256]{2,1,0:T(8,128)(2,1)S(1)}, u32[]{:S(2)}, u32[]{:S(2)}) async-start(bf16[4,64,256]{2,1,0:T(8,128)(2,1)} %copy.192), calls=%async_computation | async-start | bytes 262144 | tf_op jit(solution)/shard_map/all_to_all | solution.py:167
  259.3 4.6 %copy-start.32 = (bf16[64]{0:T(256)(128)(2,1)S(1)}, bf16[64]{0:T(256)(128)(2,1)}, u32[]{:S(2)}) copy-start(bf16[64]{0:T(256)(128)(2,1)} %convert_element_type.92) | copy-start | bytes 388
where the time goes:
time: 267 us; the launch traced here: 265 us
  blocking collectives  97.4 us (36%)
  local copies, waits for them, and re-layouts  92.1 us (34%)
  starting transfers between devices  32.9 us (12%)
  other arithmetic  16.7 us (6%)
  waiting for transfers between devices  12.7 us (5%)
  matrix products  10.6 us (4%)
    psum x2, blocking collectives, moments(): lax.psum((jnp.sum(masked, axis=(1, 2)), jnp.sum(masked * shaped, axis=(1,...  81.2 us
    concatenate x6, local copies, waits for them, and re-layouts, convolve(): stacked = jnp.concatenate(pieces, axis=0)  24.8 us
    ppermute x6, starting transfers between devices, with_halo(): before = lax.ppermute(last, axis, up)  21.6 us
    all_gather x1, blocking collectives, body(): portion = lax.all_gather(tokens, 'gx', axis=0, tiled=True)  16.3 us
    slice x8, local copies, waits for them, and re-layouts, convolve(): padded[:, shift_x:shift_x + extent[0], shift_y:shift_y + extent[1], shift...  15.5 us
    reshape x16, local copies, waits for them, and re-layouts, convolve(): pieces.append(padded[:, shift_x:shift_x + extent[0], shift_y:shift_y + ex...  15.4 us
    ppermute x6, waiting for transfers between devices, with_halo(): after = lax.ppermute(first, axis, down)  12.7 us
    dot_general x6, matrix products, convolve(): jnp.dot(columns, stacked, preferred_element_type=jnp.float32)  8.54 us
  transfers between devices with their start and end apart: 13, of which 4 were waited for; matrix products, arithmetic and copies ran while one was open for 9% of the time, Pallas kernels for 0%

commit v1 on v0

v1 whole, which is shorter than its diff:
```python
import functools

import jax
import jax.numpy as jnp
from jax import lax
from jax.experimental import pallas as pl
from jax.experimental.pallas import tpu as pltpu
from jax.sharding import PartitionSpec as P

C = 32
GW = 4
HD = 64
BR = 8
EPS = 1e-05
SENT = 512.0
BIG = 1e30
ALL = ("gx", "gy", "gz")
F32, BF16 = jnp.float32, jnp.bfloat16
HIGHEST = lax.Precision.HIGHEST


def iota(shape, dim):
    return lax.broadcasted_iota(jnp.int32, shape, dim)


def onehot(cond, dtype=BF16):
    return jnp.where(cond, 1.0, 0.0).astype(dtype)


def exact_dot(a, b):
    return jnp.dot(a, b, precision=HIGHEST, preferred_element_type=F32)


def brick_rows(occ_ref, x, lanes):
    row = iota((8, lanes), 0)
    out = jnp.zeros((8, lanes), F32)
    for b in range(occ_ref.shape[2]):
        out = jnp.where(row == b, occ_ref[x, 0, b].astype(F32), out)
    return out


def pack_stats(total, second, count, out_ref):
    groups = C // GW
    lanes = total.shape[1]
    lane, col = iota((lanes, 128), 0), iota((lanes, 128), 1)
    to_mean = onehot(lane // (lanes // groups) == col, F32)
    to_second = onehot(lane // (lanes // groups) + groups == col, F32)
    row = exact_dot(jnp.broadcast_to(total, (8, lanes)), to_mean)
    row += exact_dot(jnp.broadcast_to(second, (8, lanes)), to_second)
    row = jnp.where(iota((8, 128), 1) == 2 * groups, count, row)
    out_ref[...] = jnp.broadcast_to(row[0:1], out_ref.shape)


def group_mean(total, count, lanes):
    same = onehot(iota((lanes, lanes), 0) // 32 == iota((lanes, lanes), 1) // 32, F32)
    return exact_dot(jnp.broadcast_to(total, (8, lanes)), same)[0:1] / count


def local_moments(shifted, total, keep, count, out_ref):
    lanes = total.shape[1]
    mean = group_mean(total, count, lanes)
    squares = jnp.sum(shifted(mean) * keep, axis=0, keepdims=True)
    pack_stats(total, squares, count, out_ref)


def combine(stats, lanes):
    groups = C // GW
    n = stats[:, 2 * groups : 2 * groups + 1]
    total = jnp.sum(n)
    centre = jnp.sum(stats, axis=0, keepdims=True) / total
    drift = stats / n - centre
    between = jnp.sum(drift * drift * n, axis=0, keepdims=True)
    within = jnp.sum(stats, axis=0, keepdims=True)
    col, lane = iota((128, lanes), 0), iota((128, lanes), 1)
    group = lane // (lanes // groups)
    pick, pick2 = onehot(group == col, F32), onehot(group + groups == col, F32)
    spread = exact_dot(jnp.broadcast_to(between, (8, 128)), pick)
    spread += exact_dot(jnp.broadcast_to(within, (8, 128)), pick2)
    centre = exact_dot(jnp.broadcast_to(centre, (8, 128)), pick)
    return centre[0:1], lax.rsqrt(spread[0:1] / total + EPS)


def silu(u):
    return 0.5 * u * (1.0 + jnp.tanh(0.5 * u))


def edges(act):
    z = iota(act.shape, 2) % BR
    before, after = pltpu.roll(act, 1, 1), pltpu.roll(act, 7, 1)
    return jnp.where(z == BR - 1, before, jnp.where(z == 0, after, 0.0))


def pre_kernel(swap, occ_ref, feat_ref, stats_ref, zlo_ref, zhi_ref, *rest):
    enc = rest[-1]
    faces = rest[:-1]
    sx, sy, sb, lanes = feat_ref.shape
    me = lax.axis_index("gx")
    keep = brick_rows(occ_ref, me, lanes)
    count = jnp.sum(keep[:, 0:1]) * float(sx * sy * BR * GW)
    field = feat_ref[...].astype(F32)
    total = jnp.sum(field.reshape(sx * sy, sb, lanes), axis=0) * keep[:sb]
    total = jnp.sum(total, axis=0, keepdims=True)

    def shifted(mean):
        d = field.reshape(sx * sy, sb, lanes) - mean[None]
        return jnp.sum(d * d, axis=0)

    local_moments(shifted, total, keep[:sb], count, stats_ref)
    coded = jnp.where((keep[:sb] > 0)[None, None], field, SENT)
    for h in range(lanes // 128):
        part = coded[:, :, :, h * 128 : (h + 1) * 128]
        blank = jnp.full((sx, sy, 8 - sb, 128), SENT, F32)
        enc[h] = jnp.concatenate([part, blank], axis=2).reshape(sx * sy * 8, 128)

    def pick(start, count, stride):
        halves = [
            enc[h, pl.ds(start, count, stride=stride), :]
            for h in range(lanes // 128)
        ]
        return jnp.concatenate(halves, axis=1)

    zlo_ref[...] = pick(0, sx * sy, 8).astype(BF16)
    zhi_ref[...] = pick(sb - 1, sx * sy, 8).astype(BF16)

    def face(y0):
        both = []
        for h in range(lanes // 128):
            block = enc[h].reshape(sx, sy, 8, 128)
            low, high = block[:, y0], pltpu.roll(block[:, y0 + 1], 4, 1)
            both.append(jnp.where(iota(low.shape, 1) < 4, low, high).reshape(sx * 8, 128))
        corner = [
            jnp.concatenate(
                [pick((y0 + i) * 8 + b, sx, sy * 8) for i in range(2)], axis=0
            )
            for b in (0, sb - 1)
        ]
        return [jnp.concatenate(both, axis=1)] + corner

    lo, hi = face(0), face(sy - 2)
    if swap:
        first = lax.axis_index("gy") == 0
        out = [jnp.where(first, h, l) for l, h in zip(lo, hi)]
    else:
        out = hi + lo
    for ref, value in zip(faces, out):
        ref[...] = value.astype(BF16)


def plane_kernel(swap, peers, occ_ref, feat_ref, zm_ref, zp_ref, *rest):
    faces = rest[:-4]
    ext_ref, xlo_ref, xhi_ref, buf = rest[-4:]
    sx, sy, sb, lanes = feat_ref.shape
    ey = sy + 4
    me = lax.axis_index("gx")
    keep = brick_rows(occ_ref, me, lanes)[:sb]
    own = jnp.where((keep > 0)[None, None], feat_ref[...].astype(F32), SENT)
    halves = range(lanes // 128)
    for h in halves:
        part = own[:, :, :, h * 128 : (h + 1) * 128]
        blank = jnp.full((sx, sy, 8 - sb, 128), SENT, F32)
        part = jnp.concatenate([part, blank], axis=2)
        for x in range(sx):
            buf[h, (x * ey + 2) * 8 : (x * ey + 2 + sy) * 8, :] = part[x].reshape(sy * 8, 128)

    def put(start, count, stride, value):
        for h in halves:
            buf[h, pl.ds(start, count, stride=stride), :] = value[:, h * 128 : (h + 1) * 128]

    gy, gz = lax.axis_index("gy"), lax.axis_index("gz")
    has_zm, has_zp = gz > 0, gz < peers[1] - 1
    zm = jnp.where(has_zm, zm_ref[...].astype(F32), SENT)
    zp = jnp.where(has_zp, zp_ref[...].astype(F32), SENT)
    for x in range(sx):
        part = slice(x * sy, (x + 1) * sy)
        put((x * ey + 2) * 8 + 7, sy, 8, zm[part])
        put((x * ey + 2) * 8 + sb, sy, 8, zp[part])

    def side(y0, there, face_ref, zm_corner, zp_corner):
        face = jnp.where(there, face_ref[...].astype(F32), SENT).reshape(sx, 8, lanes)
        for h in halves:
            part = face[:, :, h * 128 : (h + 1) * 128]
            inside = iota(part.shape, 1) < sb
            low = jnp.where(inside, part, SENT)
            high = jnp.where(inside, pltpu.roll(part, 4, 1), SENT)
            for x in range(sx):
                buf[h, (x * ey + y0) * 8 : (x * ey + y0 + 2) * 8, :] = jnp.concatenate(
                    [low[x], high[x]], axis=0
                )
        low = jnp.where(there & has_zm, zm_corner[...].astype(F32), SENT)
        high = jnp.where(there & has_zp, zp_corner[...].astype(F32), SENT)
        for i in range(2):
            put((y0 + i) * 8 + 7, sx, ey * 8, low[i * sx : (i + 1) * sx])
            put((y0 + i) * 8 + sb, sx, ey * 8, high[i * sx : (i + 1) * sx])

    if swap:
        side(0, gy == 1, faces[0], faces[1], faces[2])
        side(sy + 2, gy == 0, faces[0], faces[1], faces[2])
    else:
        side(0, gy > 0, faces[0], faces[1], faces[2])
        side(sy + 2, gy < peers[0] - 1, faces[3], faces[4], faces[5])
    slab = 2 * ey * 8
    rows = sx * ey * 8
    whole = jnp.concatenate([buf[h] for h in halves], axis=1).astype(BF16)
    ext_ref[...] = whole
    xlo_ref[...] = whole[0:slab]
    xhi_ref[...] = whole[rows - slab : rows]


def band_kernel(layer, weight_ref, pars_ref, out_ref, rows_ref=None):
    lanes = C * BR
    spread = onehot(iota((C, lanes), 0) == iota((C, lanes), 1) // BR)
    column = onehot(iota((lanes, C), 0) // BR == iota((lanes, C), 1))
    turned = jnp.transpose(weight_ref[layer].astype(F32)).astype(BF16)
    wide = jnp.dot(turned, spread, preferred_element_type=F32).astype(BF16)
    zi, zo = iota((lanes, lanes), 0) % BR, iota((lanes, lanes), 1) % BR
    for ex in range(3):
        for ey in range(3):
            terms = []
            for ez in range(3):
                q = (ex * 3 + ey) * 3 + ez
                terms.append(
                    jnp.dot(column, wide[q * C : (q + 1) * C], preferred_element_type=F32)
                )
            inner = jnp.where(zi == zo - 1, terms[0], 0.0)
            inner = jnp.where(zi == zo, terms[1], inner)
            inner = jnp.where(zi == zo + 1, terms[2], inner)
            outer = jnp.where((zi == BR - 1) & (zo == 0), terms[0], 0.0)
            outer = jnp.where((zi == 0) & (zo == BR - 1), terms[2], outer)
            out_ref[ex, ey * lanes : (ey + 1) * lanes, :] = inner.astype(BF16)
            out_ref[ex, (3 + ey) * lanes : (4 + ey) * lanes, :] = outer.astype(BF16)
    if rows_ref is not None:
        rows_ref[...] = exact_dot(
            pars_ref[...], onehot(iota((C, lanes), 0) == iota((C, lanes), 1) // BR, F32)
        )


def turn_kernel(weight_ref, out_ref):
    kinds, cols, feats = weight_ref.shape
    r = iota((feats, 1), 0)
    source = (r % 128) // 4 * 32 + r // 128 * 4 + r % 4
    pick = onehot(source == iota((feats, feats), 1))
    for k in range(kinds):
        out_ref[:, k * cols : (k + 1) * cols] = lax.dot_general(
            pick, weight_ref[k], (((1,), (1,)), ((), ())), preferred_element_type=F32
        ).astype(BF16)


def first_kernel(peers, stats_ref, ext_ref, xm_ref, xp_ref, weight_ref, rows_ref, occ_ref,
                 mid_ref, out_ref, lhs, msk):
    slab, lanes = xm_ref.shape
    ey = slab // 16
    oy = ey - 2
    sx = ext_ref.shape[0] // (ey * 8)
    centre, scale = combine(stats_ref[...], lanes)
    gain, shift, bias = rows_ref[0:1], rows_ref[1:2], rows_ref[2:3]
    scale = scale * gain
    me = lax.axis_index("gx")
    step = ey * 8
    for x in range(sx + 4):
        if x < 2:
            v = jnp.where(me > 0, xm_ref[x * step : (x + 1) * step].astype(F32), SENT)
        elif x < sx + 2:
            v = ext_ref[(x - 2) * step : (x - 1) * step].astype(F32)
        else:
            i = x - sx - 2
            v = jnp.where(me < peers - 1, xp_ref[i * step : (i + 1) * step].astype(F32), SENT)
        there = v != SENT
        msk[x * step : (x + 1) * step] = onehot(there[:, 0:128], F32)
        act = jnp.where(there, silu((v - centre) * scale + shift), 0.0).reshape(ey, 8, lanes)
        side = edges(act)
        for e in range(3):
            rows = slice(x * oy * 8, (x + 1) * oy * 8)
            lhs[rows, e * lanes : (e + 1) * lanes] = (
                act[e : e + oy].reshape(oy * 8, lanes).astype(BF16)
            )
            lhs[rows, (3 + e) * lanes : (4 + e) * lanes] = (
                side[e : e + oy].reshape(oy * 8, lanes).astype(BF16)
            )
    ox = sx + 2
    size = ox * oy * 8
    acc = bias
    for e in range(3):
        acc = acc + jnp.dot(
            lhs[e * oy * 8 : e * oy * 8 + size, :], weight_ref[e], preferred_element_type=F32
        )
    mid_ref[...] = acc
    keep = brick_rows(occ_ref, me, lanes)
    count = jnp.sum(keep[:, 0:1]) * float(sx * (oy - 2) * BR * GW)
    whole = jnp.zeros((8, lanes), F32)
    for x in range(ox):
        rows = slice(x * oy * 8, (x + 1) * oy * 8)
        own = mid_ref[rows].reshape(oy, 8, lanes)
        if 1 <= x <= sx:
            whole = whole + jnp.sum(own[1 : oy - 1], axis=0)
    total = jnp.sum(whole * keep, axis=0, keepdims=True)

    def shifted(mean):
        squares = jnp.zeros((8, lanes), F32)
        for x in range(1, sx + 1):
            d = mid_ref[(x * oy + 1) * 8 : (x * oy + oy - 1) * 8].reshape(oy - 2, 8, lanes)
            d = d - mean[None]
            squares = squares + jnp.sum(d * d, axis=0)
        return squares

    local_moments(shifted, total, keep, count, out_ref)
    for x in range(ox):
        rows = slice(x * oy * 8, (x + 1) * oy * 8)
        there = msk[(x + 1) * step + 8 : (x + 2) * step - 8] > 0
        there = jnp.concatenate([there.astype(F32)] * (lanes // 128), axis=1) > 0
        mid_ref[rows] = jnp.where(there, mid_ref[rows], BIG)


def second_kernel(stats_ref, mid_ref, weight_ref, rows_ref, occ_ref, feat_ref,
                  fine_ref, tok_ref, lhs, tmp):
    sx, sy, sb, lanes = feat_ref.shape
    ey = sy + 2
    step = ey * 8
    centre, scale = combine(stats_ref[...], lanes)
    gain, shift, bias = rows_ref[3:4], rows_ref[4:5], rows_ref[5:6]
    scale = scale * gain
    for x in range(sx + 2):
        v = mid_ref[x * step : (x + 1) * step]
        act = jnp.where(v < BIG, silu((v - centre) * scale + shift), 0.0).reshape(ey, 8, lanes)
        side = edges(act)
        rows = slice(x * sy * 8, (x + 1) * sy * 8)
        for e in range(3):
            lhs[rows, e * lanes : (e + 1) * lanes] = (
                act[e : e + sy].reshape(sy * 8, lanes).astype(BF16)
            )
            lhs[rows, (3 + e) * lanes : (4 + e) * lanes] = (
                side[e : e + sy].reshape(sy * 8, lanes).astype(BF16)
            )
    size = sx * sy * 8
    acc = bias
    for e in range(3):
        acc = acc + jnp.dot(
            lhs[e * sy * 8 : e * sy * 8 + size, :], weight_ref[e], preferred_element_type=F32
        )
    keep = brick_rows(occ_ref, lax.axis_index("gx"), lanes)[:sb]
    acc = acc.reshape(sx, sy, 8, lanes)
    out = (feat_ref[...].astype(F32) * keep + acc[:, :, :sb]) * keep
    out = out.astype(BF16)
    fine_ref[...] = out
    tmp[:, :, 0:sb, :] = out.astype(F32)
    tmp[:, :, sb:8, :] = jnp.zeros((sx, sy, 8 - sb, lanes), F32)
    i, j = iota((lanes, lanes), 0), iota((lanes, lanes), 1)
    pick = onehot(i == (j % 128) // 4 * 8 + j // 128 * 4 + j % 4)
    moved = jnp.dot(
        tmp[...].reshape(size, lanes).astype(BF16), pick, preferred_element_type=F32
    ).reshape(sx // 2, 2, sy // 4, 4, 8, lanes)
    count = sx // 2 * (sy // 4)
    parts = []
    for x in range(2):
        for y in range(4):
            piece = moved[:, x, :, y].reshape(count, 8, lanes)
            low, high = piece[:, :, :128], pltpu.roll(piece[:, :, 128:], 4, 1)
            both = jnp.where(iota(low.shape, 1) < 4, low, high).reshape(count * 8, 128)
            parts.append(both.astype(BF16))
    tokens = jnp.concatenate(parts, axis=1)
    n = count * 8
    i, j = iota((n, n), 0), iota((n, n), 1)
    order = onehot(j == i // 8 * 8 + i % 2 * 4 + i % 8 // 2)
    tok_ref[...] = jnp.dot(order, tokens, preferred_element_type=F32).astype(BF16)


def attend_kernel(members, occ_ref, weight_ref, *refs):
    tok_refs, out_refs, (toks, proj) = refs[:members], refs[members : 2 * members], refs[-2:]
    own = tok_refs[0].shape[0]
    seq = own * members
    cols = weight_ref.shape[1] // 3
    me = lax.axis_index("gx")
    for k in range(members):
        toks[k * own : (k + 1) * own, :] = tok_refs[k][...]
    proj[...] = jnp.dot(toks[...], weight_ref[...], preferred_element_type=F32).astype(BF16)
    lane, row = iota((1, seq), 1), iota((seq, 1), 0)
    key_keep, row_keep = jnp.zeros((1, seq), F32), jnp.zeros((seq, 1), F32)
    for k in range(members):
        for b in range(occ_ref.shape[2]):
            there = occ_ref[me ^ k, 0, b].astype(F32)
            key_keep = jnp.where((lane // own == k) & (lane % 8 // 2 == b), there, key_keep)
            row_keep = jnp.where((row // own == k) & (row % 8 // 2 == b), there, row_keep)
    width = min(128, cols)
    for t in range(cols // width):
        q = proj[:, t * width : (t + 1) * width]
        keys = proj[:, cols + t * width : cols + (t + 1) * width]
        values = proj[:, 2 * cols + t * width : 2 * cols + (t + 1) * width]
        head = iota((seq, width), 1) // HD
        merged = jnp.zeros((seq, width), F32)
        for h in range(width // HD):
            mine = jnp.where(head == h, q.astype(F32), 0.0).astype(BF16)
            scores = lax.dot_general(
                mine, keys, (((1,), (1,)), ((), ())), preferred_element_type=F32
            ) * float(HD) ** (-0.5)
            scores = jnp.where(key_keep > 0, scores, -BIG)
            probs = jnp.exp(scores - jnp.max(scores, axis=1, keepdims=True))
            total = jnp.sum(probs, axis=1, keepdims=True)
            mixed = jnp.dot(probs.astype(BF16), values, preferred_element_type=F32)
            merged = jnp.where(head == h, mixed * (row_keep / total), merged)
        merged = merged.astype(BF16)
        for k in range(members):
            out_refs[k][:, t * width : (t + 1) * width] = merged[k * own : (k + 1) * own]


def gather_kernel(members, *refs):
    out_ref = refs[-1]
    cols = refs[0].shape[1]
    me = lax.axis_index("gx")
    for k in range(members):
        out_ref[0, :, pl.ds(pl.multiple_of((me ^ k) * cols, cols), cols)] = refs[k][...]


VM = pl.BlockSpec(memory_space=pltpu.VMEM)
SM = pl.BlockSpec(memory_space=pltpu.SMEM)


def call(kernel, name, specs, out, args, scratch=(), flops=0, nbytes=0, mib=32):
    return pl.pallas_call(
        kernel,
        out_shape=out,
        in_specs=list(specs),
        out_specs=jax.tree.map(lambda _: VM, out),
        scratch_shapes=list(scratch),
        name=name,
        cost_estimate=pl.CostEstimate(flops=flops, bytes_accessed=nbytes, transcendentals=0),
        compiler_params=pltpu.CompilerParams(vmem_limit_bytes=mib * 2**20),
    )(*args)


def shape(*dims, dtype=BF16):
    return jax.ShapeDtypeStruct(dims, dtype)


def body(features, occupancy, norm_gain, norm_shift, conv_weight, conv_bias, qkv_weight):
    sx, sy, sb, lanes = features.shape
    nx, ny, nz = (lax.axis_size(a) for a in ALL)
    devices = nx * ny * nz
    swap = ny == 2
    plane = ("gy", "gz")

    def shift(x, dy, dz):
        pairs = []
        for y in range(ny):
            for z in range(nz):
                ty, tz = (y ^ 1 if swap and dy else y + dy), z + dz
                if 0 <= ty < ny and 0 <= tz < nz:
                    pairs.append((y * nz + z, ty * nz + tz))
        return lax.ppermute(x, plane, pairs)

    face = [shape(sx * 8, lanes)] + [shape(2 * sx, lanes)] * 2
    pre = call(
        functools.partial(pre_kernel, swap), "pre", (SM, VM),
        [shape(devices, 128, dtype=F32), shape(sx * sy, lanes), shape(sx * sy, lanes)]
        + face * (1 if swap else 2),
        (occupancy, features),
        [pltpu.VMEM((lanes // 128, sx * sy * 8, 128), F32)], nbytes=10**6,
    )
    stats, zlo, zhi = pre[:3]
    stats = lax.all_to_all(stats, ALL, 0, 0, tiled=True)
    received = [shift(zhi, 0, 1), shift(zlo, 0, -1)]
    for i, dy in enumerate((1,) if swap else (1, -1)):
        y_face, y_low, y_high = pre[3 + 3 * i : 6 + 3 * i]
        received += [shift(y_face, dy, 0), shift(y_high, dy, 1), shift(y_low, dy, -1)]
    ey = sy + 4
    slab = 2 * ey * 8
    ext, xlo, xhi = call(
        functools.partial(plane_kernel, swap, (ny, nz)), "plane", (SM,) + (VM,) * (1 + len(received)),
        [shape(sx * ey * 8, lanes), shape(slab, lanes), shape(slab, lanes)],
        (occupancy, features, *received),
        [pltpu.VMEM((lanes // 128, sx * ey * 8, 128), F32)], nbytes=10**6,
    )
    up = [(i, i + 1) for i in range(nx - 1)]
    down = [(j, i) for i, j in up]
    xm, xp = lax.ppermute(xhi, "gx", up), lax.ppermute(xlo, "gx", down)

    rows = jnp.stack([norm_gain[0], norm_shift[0], conv_bias[0], norm_gain[1], norm_shift[1],
                      conv_bias[1], conv_bias[0], conv_bias[1]])
    band = shape(3, 6 * lanes, lanes)
    band0, rows = call(
        functools.partial(band_kernel, 0), "band0", (VM, VM), [band, shape(8, lanes, dtype=F32)],
        (conv_weight, rows), nbytes=8 * 10**6,
    )
    band1 = call(
        functools.partial(band_kernel, 1), "band1", (VM, VM), band, (conv_weight, rows),
        nbytes=8 * 10**6,
    )
    cols, feats = qkv_weight.shape[1:]
    turned = call(
        turn_kernel, "turn", (VM,), shape(feats, 3 * cols), (qkv_weight,),
        flops=2 * 3 * cols * feats * feats, nbytes=6 * 10**6,
    )

    oy = sy + 2
    size = (sx + 2) * oy * 8
    mid, stats = call(
        functools.partial(first_kernel, nx), "first", (VM,) * 6 + (SM,),
        [shape(size, lanes, dtype=F32), shape(devices, 128, dtype=F32)],
        (stats, ext, xm, xp, band0, rows, occupancy),
        [pltpu.VMEM(((sx + 4) * oy * 8, 6 * lanes), BF16),
         pltpu.VMEM(((sx + 4) * ey * 8, 128), F32)],
        flops=3 * 10**9, nbytes=4 * 10**6,
    )
    stats = lax.all_to_all(stats, ALL, 0, 0, tiled=True)
    own = sx // 2 * (sy // 4) * sb * 2
    fine_out, tokens = call(
        second_kernel, "second", (VM,) * 4 + (SM, VM),
        [shape(*features.shape), shape(own, feats)],
        (stats, mid, band1, rows, occupancy, features),
        [pltpu.VMEM(((sx + 2) * sy * 8, 6 * lanes), BF16), pltpu.VMEM((sx, sy, 8, lanes), F32)],
        flops=2 * 10**9, nbytes=4 * 10**6,
    )
    swaps = [[(i, i ^ k) for i in range(nx)] for k in range(nx)]
    blocks = [tokens] + [lax.ppermute(tokens, "gx", swaps[k]) for k in range(1, nx)]
    outs = call(
        functools.partial(attend_kernel, nx), "attend", (SM,) + (VM,) * (1 + nx),
        [shape(own, cols)] * nx, (occupancy, turned, *blocks),
        [pltpu.VMEM((own * nx, feats), BF16), pltpu.VMEM((own * nx, 3 * cols), BF16)],
        flops=10**9, nbytes=3 * 10**6,
    )
    outs = [outs[0]] + [lax.ppermute(outs[k], "gx", swaps[k]) for k in range(1, nx)]
    if cols % 128 == 0:
        attention = call(
            functools.partial(gather_kernel, nx), "place", (VM,) * nx,
            shape(1, own, nx * cols), outs, nbytes=3 * 10**5, mib=16,
        )
    else:
        stacked, me = jnp.stack(outs), lax.axis_index("gx")
        attention = jnp.concatenate(
            [lax.dynamic_index_in_dim(stacked, me ^ j, 0, keepdims=False) for j in range(nx)],
            axis=1,
        )[None]
    return (fine_out, attention)


def solution(mesh):
    placed = (
        P("gx", "gy", "gz", None),
        P(None, "gy", "gz"),
        P(),
        P(),
        P(),
        P(),
        P(None, "gx", None),
    )
    return jax.shard_map(
        body,
        mesh=mesh,
        in_specs=placed,
        out_specs=(P("gx", "gy", "gz", None), P(("gy", "gz"), "gx", None)),
        check_vma=False,
    )
```

time: 267 us -> 84.6 us (0.32)
  blocking collectives: 97.4 us -> 0 us
  local copies, waits for them, and re-layouts: 92.1 us -> 7.88 us
  Pallas kernels: 0 us -> 18.9 us
  other arithmetic: 16.7 us -> 0 us
  matrix products: 10.6 us -> 0 us
  starting transfers between devices: 32.9 us -> 39.5 us
  waiting for transfers between devices: 12.7 us -> 17 us
    psum x2 -> x0, blocking collectives: 81.2 us -> none  [moments(): lax.psum((jnp.sum(masked, axis=(1, 2)), jnp.sum(masked * shaped, axis=(1,...]
    reshape x23 -> x0, local copies, waits for them, and re-layouts: 29.5 us -> none  [the longest x16 15.4 us: convolve(): pieces.append(padded[:, shift_x:shift_x + extent[0], shift_y:shift_y + ex...]
    concatenate x6 -> x0, local copies, waits for them, and re-layouts: 24.8 us -> none  [convolve(): stacked = jnp.concatenate(pieces, axis=0)]
    pallas_call x0 -> x9, Pallas kernels: none -> 18.9 us  [call(): pl.pallas_call(kernel, out_shape=out, in_specs=list(specs), out_specs=jax...]
    all_gather x1 -> x0, blocking collectives: 16.3 us -> none  [body(): portion = lax.all_gather(tokens, 'gx', axis=0, tiled=True)]
    slice x11 -> x2, local copies, waits for them, and re-layouts: 15.6 us -> 1.52 us  [the longest x1 0.76 us: body(): conv_bias[1]]
    all_to_all x1 -> x2, starting transfers between devices: 3.33 us -> 14.1 us  [body(): stats = lax.all_to_all(stats, ALL, 0, 0, tiled=True)]
    dot_general x9 -> x0, matrix products: 10.6 us -> none  [the longest x6 8.54 us: convolve(): jnp.dot(columns, stacked, preferred_element_type=jnp.float32)]
  transfers between devices with their start and end apart: 13 -> 15, of which waited for: 4 -> 6; matrix products, arithmetic and copies ran while one was open for 9% -> 3% of each run, Pallas kernels for 0% -> 7%
where the time goes in v1:
time: 84.6 us; the launch traced here: 84.1 us
  starting transfers between devices  39.5 us (47%)
  Pallas kernels  18.9 us (22%)
  waiting for transfers between devices  17 us (20%)
  local copies, waits for them, and re-layouts  7.88 us (9%)
    pallas_call x9, Pallas kernels, call(): pl.pallas_call(kernel, out_shape=out, in_specs=list(specs), out_specs=jax...  18.9 us
    all_to_all x2, starting transfers between devices, body(): stats = lax.all_to_all(stats, ALL, 0, 0, tiled=True)  14.1 us
    ppermute x5, starting transfers between devices, shift(): return lax.ppermute(x, plane, pairs)  11.5 us
    ppermute x3, waiting for transfers between devices, body(): lax.ppermute(tokens, 'gx', swaps[k])  6.97 us
    unnamed x24, local copies, waits for them, and re-layouts  5.65 us
    all_to_all x2, waiting for transfers between devices, body(): stats = lax.all_to_all(stats, ALL, 0, 0, tiled=True)  5.35 us
    ppermute x2, starting transfers between devices, body(): xm, xp = (lax.ppermute(xhi, 'gx', up), lax.ppermute(xlo, 'gx', down))  4.97 us
    ppermute x3, starting transfers between devices, body(): lax.ppermute(outs[k], 'gx', swaps[k])  4.59 us
  transfers between devices with their start and end apart: 15, of which 6 were waited for; matrix products, arithmetic and copies ran while one was open for 3% of the time, Pallas kernels for 7%

profile of v1, /device:TPU:0, one launch (start us, length us, event | category | flops | bytes accessed | tf_op | source)
XLA Modules:
  0.0 84.1 jit_solution(2955210462819513160)
XLA Ops:
  0.6 0.0 copy-start
  0.6 0.9 %copy-done = bf16[8,8,4,256]{3,2,1,0:T(4,128)(2,1)S(1)} copy-done((bf16[8,8,4,256]{3,2,1,0:T(4,128)(2,1)S(1)}, bf16[8,8,4,256]{3,2,1,0:T(4,128)(2,1)}, u32[]{:S(2)}) %copy-start) | copy-done | bytes 131096
  1.5 0.0 copy-start.5
  1.5 0.7 copy-done.5
  2.2 2.1 %pre.1 = (f32[32,128]{1,0:T(8,128)}, bf16[64,256]{1,0:T(8,128)(2,1)S(1)}, bf16[64,256]{1,0:T(8,128)(2,1)S(1)}, bf16[64,256]{1,0:T(8,128)(2,1)S(1)}, bf16[16,256]...) custom-call(s32[4,1,4]{2,1,0:T(1,128)S(1)} %copy-done.5, bf16[8,8,4,256]{3,2,1,0:T(4,128)(2,1)S(1)} %copy-done), custom_call_target="tpu_custom_call" | custom-call | bytes 1000000 | tf_op jit(solution)/shard_map/pre/pallas_call | solution.py:417
  4.4 2.3 %collective-permute-start = (bf16[64,256]{1,0:T(8,128)(2,1)S(1)}, bf16[64,256]{1,0:T(8,128)(2,1)S(1)}, u32[]{:S(2)}, u32[]{:S(2)}) collective-permute-start(bf16[64,256]{1,0:T(8,128)(2,1)S(1)} %get-tuple-element.22), channel_id=1, source_target_pairs={{0,1},{1,2},{2,3},{4,5},{5,6},{6,7},{8,9},{9,10},{10,11},{12,13},{... | collective-permute-start | bytes 98312 | tf_op jit(solution)/shard_map/ppermute | solution.py:447
  6.7 1.3 %collective-permute-start.1 = (bf16[64,256]{1,0:T(8,128)(2,1)S(1)}, bf16[64,256]{1,0:T(8,128)(2,1)S(1)}, u32[]{:S(2)}, u32[]{:S(2)}) collective-permute-start(bf16[64,256]{1,0:T(8,128)(2,1)S(1)} %get-tuple-element.23), channel_id=1, source_target_pairs={{1,0},{2,1},{3,2},{5,4},{6,5},{7,6},{9,8},{10,9},{11,10},{13,12},{... | collective-permute-start | bytes 98312 | tf_op jit(solution)/shard_map/ppermute | solution.py:447
  8.0 2.4 %collective-permute-start.2 = (bf16[64,256]{1,0:T(8,128)(2,1)S(1)}, bf16[64,256]{1,0:T(8,128)(2,1)S(1)}, u32[]{:S(2)}, u32[]{:S(2)}) collective-permute-start(bf16[64,256]{1,0:T(8,128)(2,1)S(1)} %get-tuple-element.24), channel_id=1, source_target_pairs={{0,4},{1,5},{2,6},{3,7},{4,0},{5,1},{6,2},{7,3},{8,12},{9,13},{10,... | collective-permute-start | bytes 98312 | tf_op jit(solution)/shard_map/ppermute | solution.py:447
  10.4 4.2 %collective-permute-start.3 = (bf16[16,256]{1,0:T(8,128)(2,1)S(1)}, bf16[16,256]{1,0:T(8,128)(2,1)S(1)}, u32[]{:S(2)}, u32[]{:S(2)}) collective-permute-start(bf16[16,256]{1,0:T(8,128)(2,1)S(1)} %get-tuple-element.25), channel_id=1, source_target_pairs={{0,5},{1,6},{2,7},{4,1},{5,2},{6,3},{8,13},{9,14},{10,15},{12,9},{... | collective-permute-start | bytes 24584 | tf_op jit(solution)/shard_map/ppermute | solution.py:447
  14.6 1.3 %collective-permute-start.4 = (bf16[16,256]{1,0:T(8,128)(2,1)S(1)}, bf16[16,256]{1,0:T(8,128)(2,1)S(1)}, u32[]{:S(2)}, u32[]{:S(2)}) collective-permute-start(bf16[16,256]{1,0:T(8,128)(2,1)S(1)} %get-tuple-element.26), channel_id=1, source_target_pairs={{1,4},{2,5},{3,6},{5,0},{6,1},{7,2},{9,12},{10,13},{11,14},{13,8},... | collective-permute-start | bytes 24584 | tf_op jit(solution)/shard_map/ppermute | solution.py:447
  15.9 8.4 %all-to-all-start = ((f32[32,1,128]{2,1,0:T(1,128)}), f32[32,1,128]{2,1,0:T(1,128)S(1)}, u32[]{:S(2)}, u32[]{:S(2)}) async-start(f32[32,1,128]{2,1,0:T(1,128)} %bitcast.1), calls=%async_computation | async-start | bytes 32768 | tf_op jit(solution)/shard_map/all_to_all | solution.py:458
  24.3 0.8 fusion
  25.1 0.0 collective-permute-done.3.rest_1_
  25.1 0.0 collective-permute-done.4.rest_2_
  25.1 0.0 collective-permute-done.zm_ref
  25.1 0.0 collective-permute-done.1.zp_ref
  25.1 0.0 collective-permute-done.2.rest_0_
  25.1 0.0 copy-start.1
  25.2 0.9 %copy-done.1 = bf16[8,8,4,256]{3,2,1,0:T(4,128)(2,1)S(1)} copy-done((bf16[8,8,4,256]{3,2,1,0:T(4,128)(2,1)S(1)}, bf16[8,8,4,256]{3,2,1,0:T(4,128)(2,1)}, u32[]{:S(2)}) %copy-start.1) | copy-done | bytes 131096
  26.1 0.0 copy-start.6
  26.1 0.7 copy-done.6
  26.7 0.8 plane.1
  27.5 3.7 %collective-permute-start.5 = (bf16[192,256]{1,0:T(8,128)(2,1)S(1)}, bf16[192,256]{1,0:T(8,128)(2,1)S(1)}, u32[]{:S(2)}, u32[]{:S(2)}) collective-permute-start(bf16[192,256]{1,0:T(8,128)(2,1)S(1)} %get-tuple-element.28), channel_id=1, source_target_pairs={{0,8},{8,16},{16,24},{1,9},{9,17},{17,25},{2,10},{10,18},{18,26},{... | collective-permute-start | bytes 294920 | tf_op jit(solution)/shard_map/ppermute | solution.py:473
  31.2 1.3 %collective-permute-start.6 = (bf16[192,256]{1,0:T(8,128)(2,1)S(1)}, bf16[192,256]{1,0:T(8,128)(2,1)S(1)}, u32[]{:S(2)}, u32[]{:S(2)}) collective-permute-start(bf16[192,256]{1,0:T(8,128)(2,1)S(1)} %get-tuple-element.29), channel_id=1, source_target_pairs={{8,0},{16,8},{24,16},{9,1},{17,9},{25,17},{10,2},{18,10},{26,18},{... | collective-permute-start | bytes 294920 | tf_op jit(solution)/shard_map/ppermute | solution.py:473
  32.5 0.8 fusion.2
  33.3 0.7 stack.3.pars_ref
  34.0 0.0 copy-start.3
  34.0 0.9 %copy-done.3 = bf16[2,32,864]{2,1,0:T(8,128)(2,1)S(1)} copy-done((bf16[2,32,864]{2,1,0:T(8,128)(2,1)S(1)}, bf16[2,32,864]{2,1,0:T(8,128)(2,1)}, u32[]{:S(2)}) %copy-start.3) | copy-done | bytes 110616
  34.9 1.6 %band0.1 = (bf16[3,1536,256]{2,1,0:T(8,128)(2,1)S(1)}, f32[8,256]{1,0:T(8,128)S(1)}) custom-call(bf16[2,32,864]{2,1,0:T(8,128)(2,1)S(1)} %copy-done.3, f32[8,32]{1,0:T(8,128)S(1)} %stack.3.pars_ref), custom_call_target="tpu_custom_call" | custom-call | bytes 8000000 | tf_op jit(solution)/shard_map/band0/pallas_call | solution.py:417
  36.5 0.0 all-to-all-done
  36.5 0.0 collective-permute-done.5.xm_ref
  36.5 1.3 %collective-permute-done.6.xp_ref = bf16[192,256]{1,0:T(8,128)(2,1)S(1)} collective-permute-done((bf16[192,256]{1,0:T(8,128)(2,1)S(1)}, bf16[192,256]{1,0:T(8,128)(2,1)S(1)}, u32[]{:S(2)}, u32[]{:S(2)}) %collective-permute-start.6) | collective-permute-done | bytes 98336 | tf_op jit(solution)/shard_map/ppermute | solution.py:473
  37.7 0.7 copy-done.7
  38.4 0.0 copy-start.4
  38.4 4.9 %first.1 = (f32[800,256]{1,0:T(8,128)S(1)}, f32[32,128]{1,0:T(8,128)}) custom-call(f32[32,128]{1,0:T(8,128)S(1)} %bitcast.8, bf16[768,256]{1,0:T(8,128)(2,1)S(1)} %get-tuple-element.27.ext_ref, bf16[192,256]{1,0:T(8,128)(2,1)S(1)} %collective-permute-done.5.xm_ref, bf16[192,256]{1,0:T(8,128)(2,1)S(1)} %collective-permute-done.6.xp_ref, ...), custom_call_target="tpu_custom_call" | custom-call | flops 3000000000 | bytes 4000000 | tf_op jit(solution)/shard_map/first/pallas_call | solution.py:417
  43.4 0.0 copy-start.10
  43.4 0.9 %copy-done.10 = f32[800,256]{1,0:T(8,128)} copy-done((f32[800,256]{1,0:T(8,128)}, f32[800,256]{1,0:T(8,128)S(1)}, u32[]{:S(2)}) %copy-start.10) | copy-done | bytes 819224
  44.2 0.0 copy-start.2
  44.3 0.0 copy-start.8
  44.3 5.6 %all-to-all-start.1 = ((f32[32,1,128]{2,1,0:T(1,128)}), f32[32,1,128]{2,1,0:T(1,128)S(1)}, u32[]{:S(2)}, u32[]{:S(2)}) async-start(f32[32,1,128]{2,1,0:T(1,128)} %bitcast.4), calls=%async_computation.1 | async-start | bytes 32768 | tf_op jit(solution)/shard_map/all_to_all | solution.py:502
  49.9 0.0 copy-done.4
  49.9 1.5 %band1.1.weight_ref = bf16[3,1536,256]{2,1,0:T(8,128)(2,1)S(1)} custom-call(bf16[2,32,864]{2,1,0:T(8,128)(2,1)S(1)} %copy-done.4, f32[8,256]{1,0:T(8,128)S(1)} %get-tuple-element.31.rows_ref.pars_ref), custom_call_target="tpu_custom_call" | custom-call | bytes 8000000 | tf_op jit(solution)/shard_map/band1/pallas_call | solution.py:417
  51.4 5.4 %all-to-all-done.1 = f32[32,1,128]{2,1,0:T(1,128)S(1)} async-done(((f32[32,1,128]{2,1,0:T(1,128)}), f32[32,1,128]{2,1,0:T(1,128)S(1)}, u32[]{:S(2)}, u32[]{:S(2)}) %all-to-all-start.1) | async-done | bytes 16416 | tf_op jit(solution)/shard_map/all_to_all | solution.py:502
  56.8 0.0 copy-done.2
  56.8 0.0 copy-done.8
  56.8 0.0 copy-done.11
  56.8 0.0 copy-start.9
  56.8 3.4 %second.1 = (bf16[8,8,4,256]{3,2,1,0:T(4,128)(2,1)}, bf16[64,1024]{1,0:T(8,128)(2,1)S(1)}) custom-call(f32[32,128]{1,0:T(8,128)S(1)} %bitcast.9, f32[800,256]{1,0:T(8,128)S(1)} %copy-done.11, bf16[3,1536,256]{2,1,0:T(8,128)(2,1)S(1)} %band1.1.weight_ref, f32[8,256]{1,0:T(8,128)S(1)} %get-tuple-element.31.rows_ref.pars_ref, s32[4,1,4]{2,1,0:T(1,128)S(1)} %copy-done.8, ...), custom_call_target="tpu_custom_call" | custom-call | flops 2000000000 | bytes 4000000 | tf_op jit(solution)/shard_map/second/pallas_call | solution.py:417
  60.2 0.6 collective-permute-start.7
  60.8 0.6 collective-permute-start.8
  61.4 3.2 %collective-permute-start.9 = (bf16[64,1024]{1,0:T(8,128)(2,1)S(1)}, bf16[64,1024]{1,0:T(8,128)(2,1)S(1)}, u32[]{:S(2)}, u32[]{:S(2)}) collective-permute-start(bf16[64,1024]{1,0:T(8,128)(2,1)S(1)} %get-tuple-element.35.refs_0_), channel_id=1, source_target_pairs={{0,24},{8,16},{16,8},{24,0},{1,25},{9,17},{17,9},{25,1},{2,26},{10... | collective-permute-start | bytes 393224 | tf_op jit(solution)/shard_map/ppermute | solution.py:512
  64.6 0.0 copy-done.9
  64.6 1.9 %turn.1.weight_ref = bf16[1024,768]{1,0:T(8,128)(2,1)S(1)} custom-call(bf16[3,256,1024]{2,1,0:T(8,128)(2,1)S(1)} %copy-done.9), custom_call_target="tpu_custom_call" | custom-call | flops 1610612736 | bytes 6000000 | tf_op jit(solution)/shard_map/turn/pallas_call | solution.py:417
  66.5 0.5 collective-permute-done.7.refs_1_
  67.1 6.4 %collective-permute-done.8.refs_2_ = bf16[64,1024]{1,0:T(8,128)(2,1)S(1)} collective-permute-done((bf16[64,1024]{1,0:T(8,128)(2,1)S(1)}, bf16[64,1024]{1,0:T(8,128)(2,1)S(1)}, u32[]{:S(2)}, u32[]{:S(2)}) %collective-permute-start.8) | collective-permute-done | bytes 131104 | tf_op jit(solution)/shard_map/ppermute | solution.py:512
  73.5 0.0 collective-permute-done.9.refs_3_
  73.5 1.9 %attend.1 = (bf16[64,256]{1,0:T(8,128)(2,1)S(1)}, bf16[64,256]{1,0:T(8,128)(2,1)S(1)}, bf16[64,256]{1,0:T(8,128)(2,1)S(1)}, bf16[64,256]{1,0:T(8,128)(2,1)S(1)}) custom-call(s32[4,1,4]{2,1,0:T(1,128)S(1)} %copy-done.8, bf16[1024,768]{1,0:T(8,128)(2,1)S(1)} %turn.1.weight_ref, bf16[64,1024]{1,0:T(8,128)(2,1)S(1)} %get-tuple-element.35.refs_0_, ...), custom_call_target="tpu_custom_call" | custom-call | flops 1000000000 | bytes 3000000 | tf_op jit(solution)/shard_map/attend/pallas_call | solution.py:417
  75.4 2.2 %collective-permute-start.10 = (bf16[64,256]{1,0:T(8,128)(2,1)S(1)}, bf16[64,256]{1,0:T(8,128)(2,1)S(1)}, u32[]{:S(2)}, u32[]{:S(2)}) collective-permute-start(bf16[64,256]{1,0:T(8,128)(2,1)S(1)} %get-tuple-element.37), channel_id=1, source_target_pairs={{0,8},{8,0},{16,24},{24,16},{1,9},{9,1},{17,25},{25,17},{2,10},{10... | collective-permute-start | bytes 98312 | tf_op jit(solution)/shard_map/ppermute | solution.py:519
  77.6 0.1 collective-permute-start.11
  77.7 2.3 %collective-permute-start.12 = (bf16[64,256]{1,0:T(8,128)(2,1)S(1)}, bf16[64,256]{1,0:T(8,128)(2,1)S(1)}, u32[]{:S(2)}, u32[]{:S(2)}) collective-permute-start(bf16[64,256]{1,0:T(8,128)(2,1)S(1)} %get-tuple-element.39), channel_id=1, source_target_pairs={{0,24},{8,16},{16,8},{24,0},{1,25},{9,17},{17,9},{25,1},{2,26},{10... | collective-permute-start | bytes 98312 | tf_op jit(solution)/shard_map/ppermute | solution.py:519
  80.0 0.0 collective-permute-done.10.refs_1_
  80.0 2.4 %collective-permute-done.11.refs_2_ = bf16[64,256]{1,0:T(8,128)(2,1)S(1)} collective-permute-done((bf16[64,256]{1,0:T(8,128)(2,1)S(1)}, bf16[64,256]{1,0:T(8,128)(2,1)S(1)}, u32[]{:S(2)}, u32[]{:S(2)}) %collective-permute-start.11) | collective-permute-done | bytes 32800 | tf_op jit(solution)/shard_map/ppermute | solution.py:519
  82.4 1.0 %collective-permute-done.12.refs_3_ = bf16[64,256]{1,0:T(8,128)(2,1)S(1)} collective-permute-done((bf16[64,256]{1,0:T(8,128)(2,1)S(1)}, bf16[64,256]{1,0:T(8,128)(2,1)S(1)}, u32[]{:S(2)}, u32[]{:S(2)}) %collective-permute-start.12) | collective-permute-done | bytes 32800 | tf_op jit(solution)/shard_map/ppermute | solution.py:519
  83.4 0.7 place.1
  (2 shorter events, 0.0 us)
Async XLA Ops:
  0.6 0.9 %copy-start = (bf16[8,8,4,256]{3,2,1,0:T(4,128)(2,1)S(1)}, bf16[8,8,4,256]{3,2,1,0:T(4,128)(2,1)}, u32[]{:S(2)}) copy-start(bf16[8,8,4,256]{3,2,1,0:T(4,128)(2,1)} %feat_ref.5) | copy-start | bytes 393220
  1.5 0.7 copy-start.5
  4.4 20.8 %collective-permute-start = (bf16[64,256]{1,0:T(8,128)(2,1)S(1)}, bf16[64,256]{1,0:T(8,128)(2,1)S(1)}, u32[]{:S(2)}, u32[]{:S(2)}) collective-permute-start(bf16[64,256]{1,0:T(8,128)(2,1)S(1)} %get-tuple-element.22), channel_id=1, source_target_pairs={{0,1},{1,2},{2,3},{4,5},{5,6},{6,7},{8,9},{9,10},{10,11},{12,13},{... | collective-permute-start | bytes 98312 | tf_op jit(solution)/shard_map/ppermute | solution.py:447
  6.7 18.4 %collective-permute-start.1 = (bf16[64,256]{1,0:T(8,128)(2,1)S(1)}, bf16[64,256]{1,0:T(8,128)(2,1)S(1)}, u32[]{:S(2)}, u32[]{:S(2)}) collective-permute-start(bf16[64,256]{1,0:T(8,128)(2,1)S(1)} %get-tuple-element.23), channel_id=1, source_target_pairs={{1,0},{2,1},{3,2},{5,4},{6,5},{7,6},{9,8},{10,9},{11,10},{13,12},{... | collective-permute-start | bytes 98312 | tf_op jit(solution)/shard_map/ppermute | solution.py:447
  8.0 17.1 %collective-permute-start.2 = (bf16[64,256]{1,0:T(8,128)(2,1)S(1)}, bf16[64,256]{1,0:T(8,128)(2,1)S(1)}, u32[]{:S(2)}, u32[]{:S(2)}) collective-permute-start(bf16[64,256]{1,0:T(8,128)(2,1)S(1)} %get-tuple-element.24), channel_id=1, source_target_pairs={{0,4},{1,5},{2,6},{3,7},{4,0},{5,1},{6,2},{7,3},{8,12},{9,13},{10,... | collective-permute-start | bytes 98312 | tf_op jit(solution)/shard_map/ppermute | solution.py:447
  10.4 14.7 %collective-permute-start.3 = (bf16[16,256]{1,0:T(8,128)(2,1)S(1)}, bf16[16,256]{1,0:T(8,128)(2,1)S(1)}, u32[]{:S(2)}, u32[]{:S(2)}) collective-permute-start(bf16[16,256]{1,0:T(8,128)(2,1)S(1)} %get-tuple-element.25), channel_id=1, source_target_pairs={{0,5},{1,6},{2,7},{4,1},{5,2},{6,3},{8,13},{9,14},{10,15},{12,9},{... | collective-permute-start | bytes 24584 | tf_op jit(solution)/shard_map/ppermute | solution.py:447
  14.6 10.5 %collective-permute-start.4 = (bf16[16,256]{1,0:T(8,128)(2,1)S(1)}, bf16[16,256]{1,0:T(8,128)(2,1)S(1)}, u32[]{:S(2)}, u32[]{:S(2)}) collective-permute-start(bf16[16,256]{1,0:T(8,128)(2,1)S(1)} %get-tuple-element.26), channel_id=1, source_target_pairs={{1,4},{2,5},{3,6},{5,0},{6,1},{7,2},{9,12},{10,13},{11,14},{13,8},... | collective-permute-start | bytes 24584 | tf_op jit(solution)/shard_map/ppermute | solution.py:447
  15.9 20.6 %all-to-all-start = ((f32[32,1,128]{2,1,0:T(1,128)}), f32[32,1,128]{2,1,0:T(1,128)S(1)}, u32[]{:S(2)}, u32[]{:S(2)}) async-start(f32[32,1,128]{2,1,0:T(1,128)} %bitcast.1), calls=%async_computation | async-start | bytes 32768 | tf_op jit(solution)/shard_map/all_to_all | solution.py:458
  25.1 0.9 %copy-start.1 = (bf16[8,8,4,256]{3,2,1,0:T(4,128)(2,1)S(1)}, bf16[8,8,4,256]{3,2,1,0:T(4,128)(2,1)}, u32[]{:S(2)}) copy-start(bf16[8,8,4,256]{3,2,1,0:T(4,128)(2,1)} %feat_ref.5) | copy-start | bytes 393220
  26.1 0.7 copy-start.6
  27.5 8.9 %collective-permute-start.5 = (bf16[192,256]{1,0:T(8,128)(2,1)S(1)}, bf16[192,256]{1,0:T(8,128)(2,1)S(1)}, u32[]{:S(2)}, u32[]{:S(2)}) collective-permute-start(bf16[192,256]{1,0:T(8,128)(2,1)S(1)} %get-tuple-element.28), channel_id=1, source_target_pairs={{0,8},{8,16},{16,24},{1,9},{9,17},{17,25},{2,10},{10,18},{18,26},{... | collective-permute-start | bytes 294920 | tf_op jit(solution)/shard_map/ppermute | solution.py:473
  31.2 6.5 %collective-permute-start.6 = (bf16[192,256]{1,0:T(8,128)(2,1)S(1)}, bf16[192,256]{1,0:T(8,128)(2,1)S(1)}, u32[]{:S(2)}, u32[]{:S(2)}) collective-permute-start(bf16[192,256]{1,0:T(8,128)(2,1)S(1)} %get-tuple-element.29), channel_id=1, source_target_pairs={{8,0},{16,8},{24,16},{9,1},{17,9},{25,17},{10,2},{18,10},{26,18},{... | collective-permute-start | bytes 294920 | tf_op jit(solution)/shard_map/ppermute | solution.py:473
  34.0 0.9 %copy-start.3 = (bf16[2,32,864]{2,1,0:T(8,128)(2,1)S(1)}, bf16[2,32,864]{2,1,0:T(8,128)(2,1)}, u32[]{:S(2)}) copy-start(bf16[2,32,864]{2,1,0:T(8,128)(2,1)} %weight_ref.4) | copy-start | bytes 331780
  37.7 0.7 copy-start.7
  38.4 11.5 %copy-start.4 = (bf16[2,32,864]{2,1,0:T(8,128)(2,1)S(1)}, bf16[2,32,864]{2,1,0:T(8,128)(2,1)}, u32[]{:S(2)}) copy-start(bf16[2,32,864]{2,1,0:T(8,128)(2,1)} %weight_ref.4) | copy-start | bytes 331780
  43.4 0.9 %copy-start.10 = (f32[800,256]{1,0:T(8,128)}, f32[800,256]{1,0:T(8,128)S(1)}, u32[]{:S(2)}) copy-start(f32[800,256]{1,0:T(8,128)S(1)} %get-tuple-element.33.mid_ref) | copy-start | bytes 2457604
  44.2 12.5 %copy-start.2 = (bf16[8,8,4,256]{3,2,1,0:T(4,128)(2,1)S(1)}, bf16[8,8,4,256]{3,2,1,0:T(4,128)(2,1)}, u32[]{:S(2)}) copy-start(bf16[8,8,4,256]{3,2,1,0:T(4,128)(2,1)} %feat_ref.5) | copy-start | bytes 393220
  44.3 12.5 %copy-start.8 = (s32[4,1,4]{2,1,0:T(1,128)S(1)}, s32[4,1,4]{2,1,0:T(1,128)}, u32[]{:S(2)}) copy-start(s32[4,1,4]{2,1,0:T(1,128)} %occ_ref.9) | copy-start | bytes 196
  44.3 12.5 %copy-start.11 = (f32[800,256]{1,0:T(8,128)S(1)}, f32[800,256]{1,0:T(8,128)}, u32[]{:S(2)}) copy-start(f32[800,256]{1,0:T(8,128)} %copy-done.10) | copy-start | bytes 2457604
  44.3 12.5 %all-to-all-start.1 = ((f32[32,1,128]{2,1,0:T(1,128)}), f32[32,1,128]{2,1,0:T(1,128)S(1)}, u32[]{:S(2)}, u32[]{:S(2)}) async-start(f32[32,1,128]{2,1,0:T(1,128)} %bitcast.4), calls=%async_computation.1 | async-start | bytes 32768 | tf_op jit(solution)/shard_map/all_to_all | solution.py:502
  56.8 7.8 %copy-start.9 = (bf16[3,256,1024]{2,1,0:T(8,128)(2,1)S(1)}, bf16[3,256,1024]{2,1,0:T(8,128)(2,1)}, u32[]{:S(2)}) copy-start(bf16[3,256,1024]{2,1,0:T(8,128)(2,1)} %weight_ref.5) | copy-start | bytes 4718596
  60.2 6.8 %collective-permute-start.7 = (bf16[64,1024]{1,0:T(8,128)(2,1)S(1)}, bf16[64,1024]{1,0:T(8,128)(2,1)S(1)}, u32[]{:S(2)}, u32[]{:S(2)}) collective-permute-start(bf16[64,1024]{1,0:T(8,128)(2,1)S(1)} %get-tuple-element.35.refs_0_), channel_id=1, source_target_pairs={{0,8},{8,0},{16,24},{24,16},{1,9},{9,1},{17,25},{25,17},{2,10},{10... | collective-permute-start | bytes 393224 | tf_op jit(solution)/shard_map/ppermute | solution.py:512
  60.8 12.7 %collective-permute-start.8 = (bf16[64,1024]{1,0:T(8,128)(2,1)S(1)}, bf16[64,1024]{1,0:T(8,128)(2,1)S(1)}, u32[]{:S(2)}, u32[]{:S(2)}) collective-permute-start(bf16[64,1024]{1,0:T(8,128)(2,1)S(1)} %get-tuple-element.35.refs_0_), channel_id=1, source_target_pairs={{0,16},{8,24},{16,0},{24,8},{1,17},{9,25},{17,1},{25,9},{2,18},{10... | collective-permute-start | bytes 393224 | tf_op jit(solution)/shard_map/ppermute | solution.py:512
  61.4 12.1 %collective-permute-start.9 = (bf16[64,1024]{1,0:T(8,128)(2,1)S(1)}, bf16[64,1024]{1,0:T(8,128)(2,1)S(1)}, u32[]{:S(2)}, u32[]{:S(2)}) collective-permute-start(bf16[64,1024]{1,0:T(8,128)(2,1)S(1)} %get-tuple-element.35.refs_0_), channel_id=1, source_target_pairs={{0,24},{8,16},{16,8},{24,0},{1,25},{9,17},{17,9},{25,1},{2,26},{10... | collective-permute-start | bytes 393224 | tf_op jit(solution)/shard_map/ppermute | solution.py:512
  75.4 4.6 %collective-permute-start.10 = (bf16[64,256]{1,0:T(8,128)(2,1)S(1)}, bf16[64,256]{1,0:T(8,128)(2,1)S(1)}, u32[]{:S(2)}, u32[]{:S(2)}) collective-permute-start(bf16[64,256]{1,0:T(8,128)(2,1)S(1)} %get-tuple-element.37), channel_id=1, source_target_pairs={{0,8},{8,0},{16,24},{24,16},{1,9},{9,1},{17,25},{25,17},{2,10},{10... | collective-permute-start | bytes 98312 | tf_op jit(solution)/shard_map/ppermute | solution.py:519
  77.6 4.8 %collective-permute-start.11 = (bf16[64,256]{1,0:T(8,128)(2,1)S(1)}, bf16[64,256]{1,0:T(8,128)(2,1)S(1)}, u32[]{:S(2)}, u32[]{:S(2)}) collective-permute-start(bf16[64,256]{1,0:T(8,128)(2,1)S(1)} %get-tuple-element.38), channel_id=1, source_target_pairs={{0,16},{8,24},{16,0},{24,8},{1,17},{9,25},{17,1},{25,9},{2,18},{10... | collective-permute-start | bytes 98312 | tf_op jit(solution)/shard_map/ppermute | solution.py:519
  77.7 5.7 %collective-permute-start.12 = (bf16[64,256]{1,0:T(8,128)(2,1)S(1)}, bf16[64,256]{1,0:T(8,128)(2,1)S(1)}, u32[]{:S(2)}, u32[]{:S(2)}) collective-permute-start(bf16[64,256]{1,0:T(8,128)(2,1)S(1)} %get-tuple-element.39), channel_id=1, source_target_pairs={{0,24},{8,16},{16,8},{24,0},{1,25},{9,17},{17,9},{25,1},{2,26},{10... | collective-permute-start | bytes 98312 | tf_op jit(solution)/shard_map/ppermute | solution.py:519

commit v2 on v1

v2 whole, which is shorter than its diff:
```python
import functools

import jax
import jax.numpy as jnp
from jax import lax
from jax.experimental import pallas as pl
from jax.experimental.pallas import tpu as pltpu
from jax.sharding import PartitionSpec as P

C = 32
GW = 4
HD = 64
BR = 8
EPS = 1e-05
SENT = 512.0
BIG = 1e30
ALL = ("gx", "gy", "gz")
F32, BF16 = jnp.float32, jnp.bfloat16
HIGHEST = lax.Precision.HIGHEST
GROUPS = C // GW
TAIL = 16


def iota(shape, dim):
    return lax.broadcasted_iota(jnp.int32, shape, dim)


def onehot(cond, dtype=BF16):
    return jnp.where(cond, 1.0, 0.0).astype(dtype)


def exact_dot(a, b):
    return jnp.dot(a, b, precision=HIGHEST, preferred_element_type=F32)


def group_of(lanes, dim, shape):
    return iota(shape, dim) // (lanes // GROUPS)


def moments(total, squares_about, count):
    lanes = total.shape[1]
    col = iota((lanes, 128), 1)
    group = group_of(lanes, 0, (lanes, 128))
    sums = exact_dot(jnp.broadcast_to(total, (8, lanes)), onehot(group == col, F32))
    back = onehot(iota((128, lanes), 0) == group_of(lanes, 1, (128, lanes)), F32)
    squares = squares_about(exact_dot(sums / count, back)[0:1])
    second = exact_dot(
        jnp.broadcast_to(squares, (8, lanes)), onehot(group + GROUPS == col, F32)
    )
    return jnp.where(iota((8, 128), 1) == 2 * GROUPS, count, sums + second)


def merge(rows):
    n = rows[:, 2 * GROUPS : 2 * GROUPS + 1]
    whole = jnp.sum(rows, axis=0, keepdims=True)
    drift = rows / jnp.maximum(n, 1.0) - whole / jnp.sum(n)
    between = jnp.sum(drift * drift * n, axis=0, keepdims=True)
    between = jnp.where(iota((8, 128), 1) < GROUPS, between, 0.0)
    return whole + pltpu.roll(between, GROUPS, 1)


def stack_rows(rows):
    index = iota((8, 128), 0)
    out = jnp.zeros((8, 128), F32)
    for i, row in enumerate(rows):
        out = jnp.where(index == i, row, out)
    return out


def centre_scale(merged, lanes):
    row = iota((128, lanes), 0)
    group = group_of(lanes, 1, (128, lanes))
    scaled = merged / merged[0:1, 2 * GROUPS : 2 * GROUPS + 1]
    centre = exact_dot(scaled, onehot(group == row, F32))
    spread = exact_dot(scaled, onehot(group + GROUPS == row, F32))
    return centre[0:1], lax.rsqrt(spread[0:1] + EPS)


def to_tail(row):
    high = row.astype(BF16).astype(F32)
    mid = (row - high).astype(BF16).astype(F32)
    low = row - high - mid
    index = iota((8, 128), 0)
    part = jnp.where(index == 0, high, jnp.where(index == 1, mid, jnp.where(index == 2, low, 0.0)))
    zero = jnp.zeros((8, 128), F32)
    top = jnp.concatenate([part, zero], axis=1)
    return jnp.concatenate([top, jnp.zeros((TAIL - 8, 256), F32)], axis=0).astype(BF16)


def from_tail(message_ref):
    rows = message_ref.shape[0]
    part = message_ref[rows - TAIL : rows, :].astype(F32)[:, 0:128]
    return jnp.broadcast_to(jnp.sum(part, axis=0, keepdims=True), (8, 128))


def silu(u):
    return 0.5 * u * (1.0 + jnp.tanh(0.5 * u))


def pack_pairs(v):
    n, m, _, lanes = v.shape
    v = v.reshape(n, m // 2, 2, 8, lanes)
    low, high = v[:, :, 0].reshape(-1, 8, lanes), v[:, :, 1].reshape(-1, 8, lanes)
    both = jnp.where(iota(low.shape, 1) < 4, low, pltpu.roll(high, 4, 1))
    return both.reshape(n, m // 2, 8, lanes)


def split_pairs(v, blank):
    inside = iota(v.shape, 1) < 4
    return [jnp.where(inside, v, blank), jnp.where(inside, pltpu.roll(v, 4, 1), blank)]


def edges(act):
    z = iota(act.shape, 2) % BR
    before, after = pltpu.roll(act, 1, 1), pltpu.roll(act, 7, 1)
    return jnp.where(z == BR - 1, before, jnp.where(z == 0, after, 0.0))


def columns(act, size):
    side = edges(act)
    z = iota((size,) + act.shape[1:], 2) % BR
    second = pltpu.roll(side, 2, 2)
    third = pltpu.roll(side, 4, 2)
    mixed = jnp.where(
        (z == 1) | (z == 2), second[1 : 1 + size],
        jnp.where((z == 3) | (z == 4), third[2 : 2 + size], side[0:size]),
    )
    return [act[e : e + size] for e in range(3)] + [mixed]


def halves(lanes):
    return range(lanes // 128)


def read(ref, start, count, stride):
    return jnp.concatenate(
        [ref[h, pl.ds(start, count, stride=stride), :] for h in range(ref.shape[0])], axis=1
    )


def write(ref, start, count, stride, value):
    for h in range(ref.shape[0]):
        ref[h, pl.ds(start, count, stride=stride), :] = value[:, h * 128 : (h + 1) * 128]


def write_block(ref, start, value):
    for h in range(ref.shape[0]):
        ref[h, start : start + value.shape[0], :] = value[:, h * 128 : (h + 1) * 128]


def even(axis):
    return lax.axis_index(axis) % 2 == 0


def sides(axis, first, second):
    i, n = lax.axis_index(axis), lax.axis_size(axis)
    blank = jnp.full(first.shape, SENT, F32)
    second = blank if second is None else second
    low, high = jnp.where(even(axis), second, first), jnp.where(even(axis), first, second)
    return jnp.where(i > 0, low, SENT), jnp.where(i < n - 1, high, SENT)


def coded(feat_ref, keep):
    sx, sy, sb, lanes = feat_ref.shape
    field = jnp.where((keep[:sb] > 0)[None, None], feat_ref[...].astype(F32), SENT)
    return jnp.concatenate([field, jnp.full((sx, sy, 8 - sb, lanes), SENT, F32)], axis=2)


def pre_kernel(members, occ_ref, feat_ref, keep_ref, keys_ref, first_ref, second_ref, tail_ref,
               rows_ref=None):
    sx, sy, sb, lanes = feat_ref.shape
    me = lax.axis_index("gx")
    row = iota((8, lanes), 0)
    keep = jnp.zeros((8, lanes), F32)
    count = 0.0
    for b in range(sb):
        there = occ_ref[me, 0, b].astype(F32)
        keep = jnp.where(row == b, there, keep)
        count = count + there
    count = count * float(sx * sy * BR * GW)
    keep_ref[...] = keep
    seq = keys_ref.shape[1]
    lane = iota(keys_ref.shape, 1)
    keys = jnp.zeros(keys_ref.shape, F32)
    for k in range(members):
        for b in range(sb):
            there = occ_ref[me ^ k, 0, b].astype(F32)
            keys = jnp.where(
                (lane // (seq // members) == k) & (lane % (2 * sb) // 2 == b), there, keys
            )
    keys_ref[...] = keys
    field = feat_ref[...].astype(F32).reshape(sx * sy, sb, lanes)
    total = jnp.sum(jnp.sum(field, axis=0) * keep[:sb], axis=0, keepdims=True)

    def squares_about(mean):
        d = field - mean[None]
        return jnp.sum(jnp.sum(d * d, axis=0) * keep[:sb], axis=0, keepdims=True)

    packed = pack_pairs(coded(feat_ref, keep))
    low = packed[0:2].reshape(-1, lanes)
    high = packed[sx - 2 : sx].reshape(-1, lanes)
    size = low.shape[0]
    first_ref[0:size, :] = jnp.where(even("gx"), high, low).astype(BF16)
    second_ref[0:size, :] = jnp.where(even("gx"), low, high).astype(BF16)
    mine = moments(total, squares_about, count)
    tail = to_tail(mine)
    first_ref[size : size + TAIL, :] = tail
    second_ref[size : size + TAIL, :] = tail
    tail_ref[...] = tail
    if rows_ref is not None:
        rows_ref[...] = jnp.broadcast_to(mine[0:1], rows_ref.shape)


def line_kernel(narrow, keep_ref, feat_ref, first_ref, second_ref, *rest):
    tails, (ext_ref, out_ref, buf) = rest[:-3], rest[-3:]
    sx, sy, sb, lanes = feat_ref.shape
    size = 2 * (sy // 2) * 8
    low, high = sides(
        "gx", first_ref[0:size].astype(F32), second_ref[0:size].astype(F32)
    )
    whole = coded(feat_ref, keep_ref[...]).reshape(sx * sy * 8, lanes)
    write_block(buf, 2 * sy * 8, whole)
    for x0, side in ((0, low), (sx + 2, high)):
        for i in range(2):
            part = side[i * (size // 2) : (i + 1) * (size // 2)].reshape(sy // 2, 8, lanes)
            pair = split_pairs(part, SENT)
            for y in range(sy):
                write_block(buf, ((x0 + i) * sy + y) * 8, pair[y % 2][y // 2])
    rows = (sx + 4) * sy * 8
    ext_ref[...] = jnp.concatenate([buf[h] for h in halves(lanes)], axis=1).astype(BF16)
    count = (sx + 4) * sy
    face = jnp.where(even("gz"), read(buf, sb - 1, count, 8), read(buf, 0, count, 8))
    out_ref[0:count, :] = face.astype(BF16)
    mine = [from_tail(ref) for ref in tails]
    if narrow:
        mine = mine + [from_tail(first_ref), from_tail(second_ref)]
    out_ref[count : count + TAIL, :] = to_tail(merge(stack_rows(mine)))


def corner_rows(count):
    return (count + 15) // 16 * 16


def chip_kernel(sb, sy, ext_ref, own_ref, other_ref, *rest):
    out, (buf, stage) = rest[:-2], rest[-2:]
    lanes = ext_ref.shape[1]
    ex = ext_ref.shape[0] // (sy * 8)
    block = ext_ref[...].astype(F32)
    write_block(buf, 0, block)
    write_block(stage, 0, other_ref[0 : ex * sy].astype(F32))
    gap = corner_rows(ex)
    pad = jnp.zeros((gap - ex, lanes), F32)
    tail = to_tail(merge(stack_rows([from_tail(own_ref), from_tail(other_ref)])))
    packed = pack_pairs(block.reshape(ex, sy, 8, lanes))

    def side(y0):
        face = packed[:, y0 // 2].reshape(ex * 8, lanes)
        inner, outer = [], []
        for i in range(2):
            inner += [read(stage, y0 + i, ex, sy), pad]
            start = (y0 + i) * 8
            outer += [
                jnp.where(
                    even("gz"),
                    read(buf, start, ex, sy * 8),
                    read(buf, start + sb - 1, ex, sy * 8),
                ),
                pad,
            ]
        return [face] + inner, outer

    (near_low, far_low), (near_high, far_high) = side(0), side(sy - 2)
    count = ex * sy
    z_face = jnp.where(even("gz"), read(buf, 0, count, 8), read(buf, sb - 1, count, 8))
    out[0][0:count, :] = z_face.astype(BF16)
    out[0][count : count + TAIL, :] = tail
    for k in range((len(out) - 1) // 2):
        up = even("gy") if k == 0 else jnp.logical_not(even("gy"))
        for ref, low, high in (
            (out[1 + 2 * k], near_low, near_high),
            (out[2 + 2 * k], far_low, far_high),
        ):
            value = jnp.where(
                up, jnp.concatenate(high, axis=0), jnp.concatenate(low, axis=0)
            ).astype(BF16)
            ref[0 : value.shape[0], :] = value
            ref[value.shape[0] : value.shape[0] + TAIL, :] = tail


def band_kernel(layer, weight_ref, *rest):
    pars, out_ref, rows_ref = (rest[:3], rest[3], rest[4]) if len(rest) > 1 else ((), rest[0], None)
    lanes = C * BR
    spread = onehot(iota((C, lanes), 0) == iota((C, lanes), 1) // BR)
    column = onehot(iota((lanes, C), 0) // BR == iota((lanes, C), 1))
    turned = jnp.transpose(weight_ref[layer].astype(F32)).astype(BF16)
    wide = jnp.dot(turned, spread, preferred_element_type=F32).astype(BF16)
    row = iota((lanes, lanes), 0)
    zi, zo = row % BR, iota((lanes, lanes), 1) % BR
    for ex in range(3):
        mixed = jnp.zeros((lanes, lanes), F32)
        for ey in range(3):
            terms = []
            for ez in range(3):
                q = (ex * 3 + ey) * 3 + ez
                terms.append(
                    jnp.dot(column, wide[q * C : (q + 1) * C], preferred_element_type=F32)
                )
            inner = jnp.where(zi == zo - 1, terms[0], 0.0)
            inner = jnp.where(zi == zo, terms[1], inner)
            inner = jnp.where(zi == zo + 1, terms[2], inner)
            outer = jnp.where((zi == BR - 1) & (zo == 0), terms[0], 0.0)
            outer = jnp.where((zi == 0) & (zo == BR - 1), terms[2], outer)
            mixed = mixed + (pltpu.roll(outer, 2 * ey, 0) if ey else outer)
            out_ref[ex, ey * lanes : (ey + 1) * lanes, :] = inner.astype(BF16)
        out_ref[ex, 3 * lanes : 4 * lanes, :] = mixed.astype(BF16)
    if rows_ref is not None:
        pick = onehot(iota((C, lanes), 0) == iota((C, lanes), 1) // BR, F32)
        for k, ref in enumerate(pars):
            rows_ref[2 * k : 2 * k + 2, :] = exact_dot(ref[...], pick)
        rows_ref[6:8, :] = jnp.zeros((2, lanes), F32)


def turn_kernel(weight_ref, out_ref):
    kinds, cols, feats = weight_ref.shape
    r = iota((feats, 1), 0)
    source = (r % 128) // 4 * 32 + r // 128 * 4 + r % 4
    pick = onehot(source == iota((feats, feats), 1))
    for k in range(kinds):
        out_ref[:, k * cols : (k + 1) * cols] = lax.dot_general(
            pick, weight_ref[k], (((1,), (1,)), ((), ())), preferred_element_type=F32
        ).astype(BF16)


def first_kernel(narrow, faces, sy, sb, ext_ref, own_ref, core_ref, zface_ref, *rest):
    near, far = rest[0 : 2 * faces : 2], rest[1 : 2 * faces : 2]
    rest = rest[2 * faces :]
    stats_ref = None
    if not narrow:
        stats_ref, rest = rest[0], rest[1:]
    keep_ref, weight_ref, rows_ref, mid_ref, out_ref, buf, lhs, msk = rest
    lanes = ext_ref.shape[1]
    ex = ext_ref.shape[0] // (sy * 8)
    ey = sy + 4
    count = ex * sy
    z_low, z_high = sides(
        "gz", core_ref[0:count].astype(F32), zface_ref[0:count].astype(F32)
    )
    for x in range(ex):
        write_block(
            buf, (x * ey + 2) * 8, ext_ref[x * sy * 8 : (x + 1) * sy * 8].astype(F32)
        )
        part = slice(x * sy, (x + 1) * sy)
        write(buf, (x * ey + 2) * 8 + 7, sy, 8, z_low[part])
        write(buf, (x * ey + 2) * 8 + sb, sy, 8, z_high[part])
    gap = corner_rows(ex)
    size = ex * 8
    face = sides("gy", *[
        near[k][0:size].astype(F32) if k < faces else None for k in range(2)
    ])
    inner = sides("gy", *[
        near[k][size : size + 2 * gap].astype(F32) if k < faces else None for k in range(2)
    ])
    outer = sides("gy", *[
        far[k][0 : 2 * gap].astype(F32) if k < faces else None for k in range(2)
    ])
    for s, y0 in enumerate((0, sy + 2)):
        pair = split_pairs(face[s].reshape(ex, 8, lanes), SENT)
        c_low, c_high = sides("gz", inner[s], outer[s])
        for i in range(2):
            for x in range(ex):
                write_block(buf, (x * ey + y0 + i) * 8, pair[i][x])
            write(buf, (y0 + i) * 8 + 7, ex, ey * 8, c_low[i * gap : i * gap + ex])
            write(buf, (y0 + i) * 8 + sb, ex, ey * 8, c_high[i * gap : i * gap + ex])
    if narrow:
        merged = merge(stack_rows(
            [from_tail(r) for r in (own_ref, zface_ref) + tuple(near) + tuple(far)]
        ))
    else:
        merged = merge(stats_ref[...])
    centre, scale = centre_scale(merged, lanes)
    gain, shift, bias = rows_ref[0:1], rows_ref[2:3], rows_ref[4:5]
    scale = scale * gain
    oy, sx = sy + 2, ex - 4
    step = ey * 8
    for x in range(ex):
        v = jnp.concatenate(
            [buf[h, x * step : (x + 1) * step, :] for h in halves(lanes)], axis=1
        )
        there = v != SENT
        msk[x * step : (x + 1) * step] = onehot(there[:, 0:128], F32)
        act = jnp.where(there, silu((v - centre) * scale + shift), 0.0).reshape(ey, 8, lanes)
        for e, part in enumerate(columns(act, oy)):
            lhs[x * oy * 8 : (x + 1) * oy * 8, e * lanes : (e + 1) * lanes] = (
                part.reshape(oy * 8, lanes).astype(BF16)
            )
    ox = sx + 2
    size = ox * oy * 8
    acc = bias
    for e in range(3):
        acc = acc + jnp.dot(
            lhs[e * oy * 8 : e * oy * 8 + size, :], weight_ref[e], preferred_element_type=F32
        )
    mid_ref[...] = acc
    keep = keep_ref[...]
    entries = jnp.sum(keep[:, 0:1]) * float(sx * sy * BR * GW)

    def over_cells(f):
        out = jnp.zeros((8, lanes), F32)
        for x in range(1, sx + 1):
            own = mid_ref[(x * oy + 1) * 8 : (x * oy + oy - 1) * 8].reshape(sy, 8, lanes)
            out = out + jnp.sum(f(own), axis=0)
        return jnp.sum(out * keep, axis=0, keepdims=True)

    def squares_about(mean):
        return over_cells(lambda v: (v - mean[None]) * (v - mean[None]))

    mine = moments(over_cells(lambda v: v), squares_about, entries)
    out_ref[...] = jnp.broadcast_to(mine[0:1], out_ref.shape)
    for x in range(ox):
        rows = slice(x * oy * 8, (x + 1) * oy * 8)
        there = msk[(x + 1) * step + 8 : (x + 2) * step - 8]
        there = jnp.concatenate([there] * (lanes // 128), axis=1) > 0
        mid_ref[rows] = jnp.where(there, mid_ref[rows], BIG)


def second_kernel(stats_ref, mid_ref, weight_ref, rows_ref, keep_ref, feat_ref,
                  fine_ref, tok_ref, lhs):
    sx, sy, sb, lanes = feat_ref.shape
    step = (sy + 2) * 8
    centre, scale = centre_scale(merge(stats_ref[...]), lanes)
    gain, shift, bias = rows_ref[1:2], rows_ref[3:4], rows_ref[5:6]
    scale = scale * gain
    half = sy // 2 * 8
    for x in range(sx + 2):
        v = mid_ref[x * step : (x + 1) * step]
        act = jnp.where(v < BIG, silu((v - centre) * scale + shift), 0.0)
        for e, part in enumerate(columns(act.reshape(sy + 2, 8, lanes), sy)):
            lhs[x * half : (x + 1) * half, e * lanes : (e + 1) * lanes] = (
                pack_pairs(part[None]).reshape(half, lanes).astype(BF16)
            )
    size = sx * half
    acc = bias
    for e in range(3):
        acc = acc + jnp.dot(
            lhs[e * half : e * half + size, :], weight_ref[e], preferred_element_type=F32
        )
    keep = keep_ref[...]
    keep = jnp.where(iota(keep.shape, 0) < sb, keep, pltpu.roll(keep, sb, 0))
    blank = jnp.zeros((sx, sy, 8 - sb, lanes), F32)
    field = pack_pairs(jnp.concatenate([feat_ref[...].astype(F32), blank], axis=2))
    out = (field.reshape(-1, 8, lanes) * keep + acc.reshape(-1, 8, lanes)) * keep
    out = out.astype(BF16)
    wide = out.astype(F32)
    other = pltpu.roll(wide, 4, 1)
    fine = jnp.stack([wide[:, :sb], other[:, :sb]], axis=1)
    fine_ref[...] = fine.reshape(sx, sy, sb, lanes).astype(BF16)
    i, j = iota((lanes, lanes), 0), iota((lanes, lanes), 1)
    pick = onehot(i == (j % 128) // 4 * 8 + j // 128 * 4 + j % 4)
    moved = jnp.dot(out.reshape(size, lanes), pick, preferred_element_type=F32).reshape(
        sx // 2, 2, sy // 4, 2, 8, lanes
    )
    count = sx // 2 * (sy // 4)
    parts = []
    for x in range(2):
        for y in range(2):
            piece = moved[:, x, :, y].reshape(count, 8, lanes)
            low, high = piece[:, :, :128], piece[:, :, 128:]
            inside = iota(low.shape, 1) < 4
            for both in (
                jnp.where(inside, low, pltpu.roll(high, 4, 1)),
                jnp.where(inside, pltpu.roll(low, 4, 1), high),
            ):
                parts.append(both.reshape(count * 8, 128).astype(BF16))
    tokens = jnp.concatenate(parts, axis=1)
    n = count * 8
    i, j = iota((n, n), 0), iota((n, n), 1)
    order = onehot(j == i // 8 * 8 + i % 2 * 4 + i % 8 // 2)
    tok_ref[...] = jnp.dot(order, tokens, preferred_element_type=F32).astype(BF16)


def attend_kernel(members, keys_ref, weight_ref, *refs):
    tok_refs, out_refs, (toks, proj) = refs[:members], refs[members : 2 * members], refs[-2:]
    own = tok_refs[0].shape[0]
    seq = own * members
    cols = weight_ref.shape[1] // 3
    for k in range(members):
        toks[k * own : (k + 1) * own, :] = tok_refs[k][...]
    proj[...] = jnp.dot(toks[...], weight_ref[...], preferred_element_type=F32).astype(BF16)
    there = keys_ref[0:1] > 0
    width = min(128, cols)
    for t in range(cols // width):
        q = proj[:, t * width : (t + 1) * width]
        keys = proj[:, cols + t * width : cols + (t + 1) * width]
        values = proj[:, 2 * cols + t * width : 2 * cols + (t + 1) * width]
        head = iota((seq, width), 1) // HD
        merged = jnp.zeros((seq, width), F32)
        for h in range(width // HD):
            mine = jnp.where(head == h, q.astype(F32), 0.0).astype(BF16)
            scores = lax.dot_general(
                mine, keys, (((1,), (1,)), ((), ())), preferred_element_type=F32
            ) * float(HD) ** (-0.5)
            scores = jnp.where(there, scores, -BIG)
            probs = jnp.exp(scores - jnp.max(scores, axis=1, keepdims=True))
            total = jnp.sum(probs, axis=1, keepdims=True)
            mixed = jnp.dot(probs.astype(BF16), values, preferred_element_type=F32)
            merged = jnp.where(head == h, mixed / total, merged)
        merged = merged.astype(BF16)
        for k in range(members):
            out_refs[k][:, t * width : (t + 1) * width] = merged[k * own : (k + 1) * own]


def place_kernel(members, keep_ref, *refs):
    out_ref = refs[-1]
    own, cols = refs[0].shape
    me = lax.axis_index("gx")
    row = iota((8, cols), 0)
    keep = jnp.zeros((8, cols), F32)
    for b in range(4):
        keep = jnp.where(row // 2 == b, jnp.broadcast_to(keep_ref[b : b + 1, :cols], (8, cols)), keep)
    for k in range(members):
        value = refs[k][...].astype(F32).reshape(own // 8, 8, cols)
        value = jnp.where((keep > 0)[None], value, 0.0).reshape(own, cols).astype(BF16)
        if cols % 128 == 0:
            out_ref[0, :, pl.ds(pl.multiple_of((me ^ k) * cols, cols), cols)] = value
        else:
            out_ref[k] = value


VM = pl.BlockSpec(memory_space=pltpu.VMEM)
SM = pl.BlockSpec(memory_space=pltpu.SMEM)


def call(kernel, name, specs, out, args, scratch=(), flops=0, nbytes=0, mib=16):
    return pl.pallas_call(
        kernel,
        out_shape=out,
        in_specs=list(specs),
        out_specs=jax.tree.map(lambda _: VM, out),
        scratch_shapes=list(scratch),
        name=name,
        cost_estimate=pl.CostEstimate(flops=flops, bytes_accessed=nbytes, transcendentals=0),
        compiler_params=pltpu.CompilerParams(vmem_limit_bytes=mib * 2**20),
    )(*args)


def shape(*dims, dtype=BF16):
    return jax.ShapeDtypeStruct(dims, dtype)


def pairing(n, odd, closed):
    partner = {i: (i ^ 1 if not odd else (i + 1 if i % 2 else i - 1)) for i in range(n)}
    if closed:
        partner = {i: j % n for i, j in partner.items()}
    return {i: j for i, j in partner.items() if 0 <= j < n and i != j}


def body(features, occupancy, norm_gain, norm_shift, conv_weight, conv_bias, qkv_weight):
    sx, sy, sb, lanes = features.shape
    nx, ny, nz = (lax.axis_size(a) for a in ALL)
    devices = nx * ny * nz
    narrow = nx == 4 and ny == 2 and nz == 4
    own = sx // 2 * (sy // 4) * sb * 2
    ex = sx + 4
    row_shape = [] if narrow else [shape(devices, 128, dtype=F32)]

    slab = sy * 8 + TAIL
    keep, keys, first, second, tail, *stats = call(
        functools.partial(pre_kernel, nx), "pre", (SM, VM),
        [shape(8, lanes, dtype=F32), shape(8, own * nx, dtype=F32), shape(slab, lanes),
         shape(slab, lanes), shape(TAIL, lanes)] + row_shape,
        (occupancy, features), nbytes=10**6,
    )
    stats = [lax.all_to_all(s, ALL, 0, 0, tiled=True) for s in stats]
    got = [
        lax.ppermute(first, "gx", list(pairing(nx, False, False).items())),
        lax.ppermute(second, "gx", list(pairing(nx, True, narrow).items())),
    ]
    tails = [tail]
    if narrow:
        tails.append(lax.ppermute(tail, "gx", [(i, i ^ 2) for i in range(nx)]))
    count = ex * sy
    ext, mine = call(
        functools.partial(line_kernel, narrow), "line", (VM,) * (4 + len(tails)),
        [shape(count * 8, lanes), shape(count + TAIL, lanes)],
        (keep, features, *got, *tails),
        [pltpu.VMEM((lanes // 128, count * 8, 128), F32)], nbytes=10**6,
    )
    core = lax.ppermute(mine, "gz", list(pairing(nz, False, False).items()))

    faces = 1 if ny == 2 else 2
    gap = corner_rows(ex)
    near, far = ex * 8 + 2 * gap + TAIL, 2 * gap + TAIL
    zface, *yfaces = call(
        functools.partial(chip_kernel, sb, sy), "chip", (VM,) * 3,
        [shape(count + TAIL, lanes)] + [shape(near, lanes), shape(far, lanes)] * faces,
        (ext, mine, core),
        [pltpu.VMEM((lanes // 128, count * 8, 128), F32),
         pltpu.VMEM((lanes // 128, count, 128), F32)], nbytes=10**6,
    )
    odd_z = pairing(nz, True, narrow)
    own_tail = zface
    zgot = lax.ppermute(zface, "gz", list(odd_z.items()))
    ygot = []
    for k in range(faces):
        along = pairing(ny, k == 1, False)
        ygot.append(lax.ppermute(yfaces[2 * k], "gy", list(along.items())))
        both = [
            (y * nz + z, along[y] * nz + odd_z[z]) for y in along for z in odd_z
        ]
        ygot.append(lax.ppermute(yfaces[2 * k + 1], ("gy", "gz"), both))

    band = shape(3, 4 * lanes, lanes)
    band0, rows = call(
        functools.partial(band_kernel, 0), "band0", (VM,) * 4, [band, shape(8, lanes, dtype=F32)],
        (conv_weight, norm_gain, norm_shift, conv_bias), nbytes=8 * 10**6,
    )
    band1 = call(
        functools.partial(band_kernel, 1), "band1", (VM,), band, (conv_weight,), nbytes=8 * 10**6,
    )
    cols, feats = qkv_weight.shape[1:]
    turned = call(
        turn_kernel, "turn", (VM,), shape(feats, 3 * cols), (qkv_weight,),
        flops=2 * 3 * cols * feats * feats, nbytes=6 * 10**6,
    )

    ey, oy = sy + 4, sy + 2
    size = (sx + 2) * oy * 8
    mid, mine = call(
        functools.partial(first_kernel, narrow, faces, sy, sb), "first",
        (VM,) * (7 + 2 * faces + len(stats)),
        [shape(size, lanes, dtype=F32), shape(devices, 128, dtype=F32)],
        (ext, own_tail, core, zgot, *ygot, *stats, keep, band0, rows),
        [pltpu.VMEM((lanes // 128, ex * ey * 8, 128), F32),
         pltpu.VMEM((ex * oy * 8, 4 * lanes), BF16),
         pltpu.VMEM((ex * ey * 8, 128), F32)],
        flops=2 * 10**9, nbytes=4 * 10**6, mib=20,
    )
    stats = lax.all_to_all(mine, ALL, 0, 0, tiled=True)
    fine_out, tokens = call(
        second_kernel, "second", (VM,) * 6,
        [shape(*features.shape), shape(own, feats)],
        (stats, mid, band1, rows, keep, features),
        [pltpu.VMEM(((sx + 2) * sy * 4, 4 * lanes), BF16)],
        flops=10**9, nbytes=4 * 10**6,
    )
    swaps = [[(i, i ^ k) for i in range(nx)] for k in range(nx)]
    blocks = [tokens] + [lax.ppermute(tokens, "gx", swaps[k]) for k in range(1, nx)]
    outs = call(
        functools.partial(attend_kernel, nx), "attend", (VM,) * (2 + nx),
        [shape(own, cols)] * nx, (keys, turned, *blocks),
        [pltpu.VMEM((own * nx, feats), BF16), pltpu.VMEM((own * nx, 3 * cols), BF16)],
        flops=10**9, nbytes=3 * 10**6, mib=16 if narrow else 40,
    )
    outs = [outs[0]] + [lax.ppermute(outs[k], "gx", swaps[k]) for k in range(1, nx)]
    lined = cols % 128 == 0
    attention = call(
        functools.partial(place_kernel, nx), "place", (VM,) * (1 + nx),
        shape(1, own, nx * cols) if lined else shape(nx, own, cols), (keep, *outs),
        nbytes=3 * 10**5, mib=8,
    )
    if not lined:
        me = lax.axis_index("gx")
        attention = jnp.concatenate(
            [lax.dynamic_index_in_dim(attention, me ^ j, 0, keepdims=False) for j in range(nx)],
            axis=1,
        )[None]
    return (fine_out, attention)


def solution(mesh):
    placed = (
        P("gx", "gy", "gz", None),
        P(None, "gy", "gz"),
        P(),
        P(),
        P(),
        P(),
        P(None, "gx", None),
    )
    return jax.shard_map(
        body,
        mesh=mesh,
        in_specs=placed,
        out_specs=(P("gx", "gy", "gz", None), P(("gy", "gz"), "gx", None)),
        check_vma=False,
    )
```

time: 84.6 us -> 65.5 us (0.77)
  starting transfers between devices: 39.5 us -> 21.8 us
  waiting for transfers between devices: 17 us -> 21.2 us
  Pallas kernels: 18.9 us -> 16 us
  local copies, waits for them, and re-layouts: 7.88 us -> 5.43 us
    all_to_all x2 -> x1, starting transfers between devices: 14.1 us -> 3.86 us  [body(): stats = lax.all_to_all(mine, ALL, 0, 0, tiled=True)]
    ppermute x7, starting transfers between devices: 16.5 us -> 8.96 us  [the longest x1 3.09 us: body(): lax.ppermute(first, 'gx', list(pairing(nx, False, False).items()))]
    ppermute x7, waiting for transfers between devices: 1.29 us -> 5.68 us  [the longest x1 4.43 us: body(): tails.append(lax.ppermute(tail, 'gx', [(i, i ^ 2) for i in range(nx)]))]
    pallas_call x9 -> x10, Pallas kernels: 18.9 us -> 16 us  [call(): pl.pallas_call(kernel, out_shape=out, in_specs=list(specs), out_specs=jax...]
    slice x2 -> x0, local copies, waits for them, and re-layouts: 1.52 us -> none  [the longest x1 0.76 us: body(): conv_bias[1]]
    unnamed x24 -> x20, local copies, waits for them, and re-layouts: 5.65 us -> 5.43 us
    all_to_all x2 -> x1, waiting for transfers between devices: 5.35 us -> 5.21 us  [body(): stats = lax.all_to_all(mine, ALL, 0, 0, tiled=True)]
  transfers between devices with their start and end apart: 15 -> 14, of which waited for: 6 -> 7; matrix products, arithmetic and copies ran while one was open for 3% -> 0% of each run, Pallas kernels for 7% -> 8%
where the time goes in v2:
time: 65.5 us; the launch traced here: 65.2 us
  starting transfers between devices  21.8 us (33%)
  waiting for transfers between devices  21.2 us (32%)
  Pallas kernels  16 us (24%)
  local copies, waits for them, and re-layouts  5.43 us (8%)
  between operations  0.74 us (1%)
    pallas_call x10, Pallas kernels, call(): pl.pallas_call(kernel, out_shape=out, in_specs=list(specs), out_specs=jax...  16 us
    ppermute x3, waiting for transfers between devices, body(): lax.ppermute(tokens, 'gx', swaps[k])  6.97 us
    unnamed x20, local copies, waits for them, and re-layouts  5.43 us
    all_to_all x1, waiting for transfers between devices, body(): stats = lax.all_to_all(mine, ALL, 0, 0, tiled=True)  5.21 us
    ppermute x3, starting transfers between devices, body(): lax.ppermute(outs[k], 'gx', swaps[k])  4.59 us
    ppermute x1, waiting for transfers between devices, body(): tails.append(lax.ppermute(tail, 'gx', [(i, i ^ 2) for i in range(nx)]))  4.43 us
    ppermute x3, starting transfers between devices, body(): lax.ppermute(tokens, 'gx', swaps[k])  4.39 us
    all_to_all x1, starting transfers between devices, body(): stats = lax.all_to_all(mine, ALL, 0, 0, tiled=True)  3.86 us
  transfers between devices with their start and end apart: 14, of which 7 were waited for; matrix products, arithmetic and copies ran while one was open for 0% of the time, Pallas kernels for 8%

profile of v2, /device:TPU:0, one launch (start us, length us, event | category | flops | bytes accessed | tf_op | source)
XLA Modules:
  0.0 65.2 jit_solution(5043722928575112917)
XLA Ops:
  0.6 0.0 copy-start
  0.6 0.9 %copy-done = bf16[8,8,4,256]{3,2,1,0:T(4,128)(2,1)S(1)} copy-done((bf16[8,8,4,256]{3,2,1,0:T(4,128)(2,1)S(1)}, bf16[8,8,4,256]{3,2,1,0:T(4,128)(2,1)}, u32[]{:S(2)}) %copy-start) | copy-done | bytes 131096
  1.5 0.0 copy-start.5
  1.5 0.7 %copy-done.5 = s32[4,1,4]{2,1,0:T(1,128)S(1)} copy-done((s32[4,1,4]{2,1,0:T(1,128)S(1)}, s32[4,1,4]{2,1,0:T(1,128)}, u32[]{:S(2)}) %copy-start.5) | copy-done | bytes 88
  2.2 1.4 %pre.1 = (f32[8,256]{1,0:T(8,128)S(1)}, f32[8,256]{1,0:T(8,128)S(1)}, bf16[80,256]{1,0:T(8,128)(2,1)S(1)}, bf16[80,256]{1,0:T(8,128)(2,1)S(1)}, bf16[16,256]{1,0:T(8,128)(2,1)S(1)}) custom-call(s32[4,1,4]{2,1,0:T(1,128)S(1)} %copy-done.5, bf16[8,8,4,256]{3,2,1,0:T(4,128)(2,1)S(1)} %copy-done), custom_call_target="tpu_custom_call" | custom-call | bytes 1000000 | tf_op jit(solution)/shard_map/pre/pallas_call | solution.py:534
  3.6 3.1 %collective-permute-start = (bf16[80,256]{1,0:T(8,128)(2,1)S(1)}, bf16[80,256]{1,0:T(8,128)(2,1)S(1)}, u32[]{:S(2)}, u32[]{:S(2)}) collective-permute-start(bf16[80,256]{1,0:T(8,128)(2,1)S(1)} %get-tuple-element.23), channel_id=1, source_target_pairs={{0,8},{8,0},{16,24},{24,16},{1,9},{9,1},{17,25},{25,17},{2,10},{10... | collective-permute-start | bytes 122888 | tf_op jit(solution)/shard_map/ppermute | solution.py:575
  6.7 2.5 %collective-permute-start.1 = (bf16[80,256]{1,0:T(8,128)(2,1)S(1)}, bf16[80,256]{1,0:T(8,128)(2,1)S(1)}, u32[]{:S(2)}, u32[]{:S(2)}) collective-permute-start(bf16[80,256]{1,0:T(8,128)(2,1)S(1)} %get-tuple-element.24), channel_id=1, source_target_pairs={{0,24},{8,16},{16,8},{24,0},{1,25},{9,17},{17,9},{25,1},{2,26},{10... | collective-permute-start | bytes 122888 | tf_op jit(solution)/shard_map/ppermute | solution.py:576
  9.2 0.1 collective-permute-start.2
  9.3 4.4 %collective-permute-done.2.rest_1_ = bf16[16,256]{1,0:T(8,128)(2,1)S(1)} collective-permute-done((bf16[16,256]{1,0:T(8,128)(2,1)S(1)}, bf16[16,256]{1,0:T(8,128)(2,1)S(1)}, u32[]{:S(2)}, u32[]{:S(2)}) %collective-permute-start.2) | collective-permute-done | bytes 8224 | tf_op jit(solution)/shard_map/ppermute | solution.py:580
  13.7 0.0 collective-permute-done.first_ref
  13.8 0.0 collective-permute-done.1.second_ref
  13.8 0.0 copy-start.1
  13.8 0.9 %copy-done.1 = bf16[8,8,4,256]{3,2,1,0:T(4,128)(2,1)S(1)} copy-done((bf16[8,8,4,256]{3,2,1,0:T(4,128)(2,1)S(1)}, bf16[8,8,4,256]{3,2,1,0:T(4,128)(2,1)}, u32[]{:S(2)}) %copy-start.1) | copy-done | bytes 131096
  14.7 0.4 line.1
  15.1 0.0 collective-permute-start.3
  15.1 1.2 %collective-permute-done.3.other_ref.core_ref = bf16[112,256]{1,0:T(8,128)(2,1)S(1)} collective-permute-done((bf16[112,256]{1,0:T(8,128)(2,1)S(1)}, bf16[112,256]{1,0:T(8,128)(2,1)S(1)}, u32[]{:S(2)}, u32[]{:S(2)}) %collective-permute-start.3) | collective-permute-done | bytes 57376 | tf_op jit(solution)/shard_map/ppermute | solution.py:588
  16.3 0.3 chip.1
  16.7 1.6 %collective-permute-start.5 = (bf16[144,256]{1,0:T(8,128)(2,1)S(1)}, bf16[144,256]{1,0:T(8,128)(2,1)S(1)}, u32[]{:S(2)}, u32[]{:S(2)}) collective-permute-start(bf16[144,256]{1,0:T(8,128)(2,1)S(1)} %get-tuple-element.29), channel_id=1, source_target_pairs={{0,4},{4,0},{1,5},{5,1},{2,6},{6,2},{3,7},{7,3},{8,12},{12,8},{9,1... | collective-permute-start | bytes 221192 | tf_op jit(solution)/shard_map/ppermute | solution.py:606
  18.2 1.0 %collective-permute-start.4 = (bf16[112,256]{1,0:T(8,128)(2,1)S(1)}, bf16[112,256]{1,0:T(8,128)(2,1)S(1)}, u32[]{:S(2)}, u32[]{:S(2)}) collective-permute-start(bf16[112,256]{1,0:T(8,128)(2,1)S(1)} %get-tuple-element.28.own_ref), channel_id=1, source_target_pairs={{0,3},{1,2},{2,1},{3,0},{4,7},{5,6},{6,5},{7,4},{8,11},{9,10},{10,... | collective-permute-start | bytes 172040 | tf_op jit(solution)/shard_map/ppermute | solution.py:602
  19.2 0.7 %collective-permute-start.6 = (bf16[48,256]{1,0:T(8,128)(2,1)S(1)}, bf16[48,256]{1,0:T(8,128)(2,1)S(1)}, u32[]{:S(2)}, u32[]{:S(2)}) collective-permute-start(bf16[48,256]{1,0:T(8,128)(2,1)S(1)} %get-tuple-element.30), channel_id=1, source_target_pairs={{0,7},{1,6},{2,5},{3,4},{4,3},{5,2},{6,1},{7,0},{8,15},{9,14},{10,... | collective-permute-start | bytes 73736 | tf_op jit(solution)/shard_map/ppermute | solution.py:610
  20.0 0.0 copy-start.3
  20.0 0.9 %copy-done.3 = bf16[2,32,864]{2,1,0:T(8,128)(2,1)S(1)} copy-done((bf16[2,32,864]{2,1,0:T(8,128)(2,1)S(1)}, bf16[2,32,864]{2,1,0:T(8,128)(2,1)}, u32[]{:S(2)}) %copy-start.3) | copy-done | bytes 110616
  20.9 0.0 copy-start.6
  20.9 0.7 %copy-done.6 = f32[2,32]{1,0:T(2,128)S(1)} copy-done((f32[2,32]{1,0:T(2,128)S(1)}, f32[2,32]{1,0:T(2,128)}, u32[]{:S(2)}) %copy-start.6) | copy-done | bytes 280
  21.5 0.0 copy-start.7
  21.5 0.7 %copy-done.7 = f32[2,32]{1,0:T(2,128)S(1)} copy-done((f32[2,32]{1,0:T(2,128)S(1)}, f32[2,32]{1,0:T(2,128)}, u32[]{:S(2)}) %copy-start.7) | copy-done | bytes 280
  22.2 0.0 copy-start.8
  22.2 0.7 %copy-done.8 = f32[2,32]{1,0:T(2,128)S(1)} copy-done((f32[2,32]{1,0:T(2,128)S(1)}, f32[2,32]{1,0:T(2,128)}, u32[]{:S(2)}) %copy-start.8) | copy-done | bytes 280
  22.9 1.8 %band0.1 = (bf16[3,1024,256]{2,1,0:T(8,128)(2,1)S(1)}, f32[8,256]{1,0:T(8,128)S(1)}) custom-call(bf16[2,32,864]{2,1,0:T(8,128)(2,1)S(1)} %copy-done.3, f32[2,32]{1,0:T(2,128)S(1)} %copy-done.6, f32[2,32]{1,0:T(2,128)S(1)} %copy-done.7, f32[2,32]{1,0:T(2,128)S(1)} %copy-done.8), custom_call_target="tpu_custom_call" | custom-call | bytes 8000000 | tf_op jit(solution)/shard_map/band0/pallas_call | solution.py:534
  24.6 0.0 collective-permute-done.6.rest_1_
  24.7 0.0 collective-permute-done.4.zface_ref
  24.7 0.0 collective-permute-done.5.rest_0_
  24.7 0.0 copy-start.4
  24.7 4.2 %first.1 = (f32[800,256]{1,0:T(8,128)S(1)}, f32[32,128]{1,0:T(8,128)}) custom-call(bf16[768,256]{1,0:T(8,128)(2,1)S(1)} %get-tuple-element.26.ext_ref, bf16[112,256]{1,0:T(8,128)(2,1)S(1)} %get-tuple-element.28.own_ref, bf16[112,256]{1,0:T(8,128)(2,1)S(1)} %collective-permute-done.3.other_ref.core_ref, ...), custom_call_target="tpu_custom_call" | custom-call | flops 2000000000 | bytes 4000000 | tf_op jit(solution)/shard_map/first/pallas_call | solution.py:534
  28.9 0.0 copy-start.2
  28.9 3.9 %all-to-all-start = ((f32[32,1,128]{2,1,0:T(1,128)}), f32[32,1,128]{2,1,0:T(1,128)S(1)}, u32[]{:S(2)}, u32[]{:S(2)}) async-start(f32[32,1,128]{2,1,0:T(1,128)} %bitcast.1), calls=%async_computation | async-start | bytes 32768 | tf_op jit(solution)/shard_map/all_to_all | solution.py:638
  32.8 0.0 copy-done.4
  32.8 1.7 %band1.1.weight_ref = bf16[3,1024,256]{2,1,0:T(8,128)(2,1)S(1)} custom-call(bf16[2,32,864]{2,1,0:T(8,128)(2,1)S(1)} %copy-done.4), custom_call_target="tpu_custom_call" | custom-call | bytes 8000000 | tf_op jit(solution)/shard_map/band1/pallas_call | solution.py:534
  34.4 5.2 %all-to-all-done = f32[32,1,128]{2,1,0:T(1,128)S(1)} async-done(((f32[32,1,128]{2,1,0:T(1,128)}), f32[32,1,128]{2,1,0:T(1,128)S(1)}, u32[]{:S(2)}, u32[]{:S(2)}) %all-to-all-start) | async-done | bytes 16416 | tf_op jit(solution)/shard_map/all_to_all | solution.py:638
  39.7 0.0 copy-done.2
  39.7 0.0 copy-start.9
  39.7 2.3 %second.1 = (bf16[8,8,4,256]{3,2,1,0:T(4,128)(2,1)}, bf16[64,1024]{1,0:T(8,128)(2,1)S(1)}) custom-call(f32[32,128]{1,0:T(8,128)S(1)} %bitcast.4, f32[800,256]{1,0:T(8,128)S(1)} %get-tuple-element.34.mid_ref, bf16[3,1024,256]{2,1,0:T(8,128)(2,1)S(1)} %band1.1.weight_ref, f32[8,256]{1,0:T(8,128)S(1)} %get-tuple-element.32.rest_4_.rows_ref, ...), custom_call_target="tpu_custom_call" | custom-call | flops 1000000000 | bytes 4000000 | tf_op jit(solution)/shard_map/second/pallas_call | solution.py:534
  41.9 0.6 collective-permute-start.7
  42.5 0.6 collective-permute-start.8
  43.1 3.2 %collective-permute-start.9 = (bf16[64,1024]{1,0:T(8,128)(2,1)S(1)}, bf16[64,1024]{1,0:T(8,128)(2,1)S(1)}, u32[]{:S(2)}, u32[]{:S(2)}) collective-permute-start(bf16[64,1024]{1,0:T(8,128)(2,1)S(1)} %get-tuple-element.37.refs_0_), channel_id=1, source_target_pairs={{0,24},{8,16},{16,8},{24,0},{1,25},{9,17},{17,9},{25,1},{2,26},{10... | collective-permute-start | bytes 393224 | tf_op jit(solution)/shard_map/ppermute | solution.py:647
  46.3 0.0 copy-done.9
  46.3 1.9 %turn.1.weight_ref = bf16[1024,768]{1,0:T(8,128)(2,1)S(1)} custom-call(bf16[3,256,1024]{2,1,0:T(8,128)(2,1)S(1)} %copy-done.9), custom_call_target="tpu_custom_call" | custom-call | flops 1610612736 | bytes 6000000 | tf_op jit(solution)/shard_map/turn/pallas_call | solution.py:534
  48.2 0.5 collective-permute-done.7.refs_1_
  48.8 6.4 %collective-permute-done.8.refs_2_ = bf16[64,1024]{1,0:T(8,128)(2,1)S(1)} collective-permute-done((bf16[64,1024]{1,0:T(8,128)(2,1)S(1)}, bf16[64,1024]{1,0:T(8,128)(2,1)S(1)}, u32[]{:S(2)}, u32[]{:S(2)}) %collective-permute-start.8) | collective-permute-done | bytes 131104 | tf_op jit(solution)/shard_map/ppermute | solution.py:647
  55.2 0.0 collective-permute-done.9.refs_3_
  55.2 1.4 %attend.1 = (bf16[64,256]{1,0:T(8,128)(2,1)S(1)}, bf16[64,256]{1,0:T(8,128)(2,1)S(1)}, bf16[64,256]{1,0:T(8,128)(2,1)S(1)}, bf16[64,256]{1,0:T(8,128)(2,1)S(1)}) custom-call(f32[8,256]{1,0:T(8,128)S(1)} %get-tuple-element.36.keys_ref, bf16[1024,768]{1,0:T(8,128)(2,1)S(1)} %turn.1.weight_ref, bf16[64,1024]{1,0:T(8,128)(2,1)S(1)} %get-tuple-element.37.refs_0_, ...), custom_call_target="tpu_custom_call" | custom-call | flops 1000000000 | bytes 3000000 | tf_op jit(solution)/shard_map/attend/pallas_call | solution.py:534
  56.6 2.2 %collective-permute-start.10 = (bf16[64,256]{1,0:T(8,128)(2,1)S(1)}, bf16[64,256]{1,0:T(8,128)(2,1)S(1)}, u32[]{:S(2)}, u32[]{:S(2)}) collective-permute-start(bf16[64,256]{1,0:T(8,128)(2,1)S(1)} %get-tuple-element.39), channel_id=1, source_target_pairs={{0,8},{8,0},{16,24},{24,16},{1,9},{9,1},{17,25},{25,17},{2,10},{10... | collective-permute-start | bytes 98312 | tf_op jit(solution)/shard_map/ppermute | solution.py:654
  58.7 0.1 collective-permute-start.11
  58.8 2.3 %collective-permute-start.12 = (bf16[64,256]{1,0:T(8,128)(2,1)S(1)}, bf16[64,256]{1,0:T(8,128)(2,1)S(1)}, u32[]{:S(2)}, u32[]{:S(2)}) collective-permute-start(bf16[64,256]{1,0:T(8,128)(2,1)S(1)} %get-tuple-element.41), channel_id=1, source_target_pairs={{0,24},{8,16},{16,8},{24,0},{1,25},{9,17},{17,9},{25,1},{2,26},{10... | collective-permute-start | bytes 98312 | tf_op jit(solution)/shard_map/ppermute | solution.py:654
  61.2 0.0 collective-permute-done.10.refs_1_
  61.2 2.4 %collective-permute-done.11.refs_2_ = bf16[64,256]{1,0:T(8,128)(2,1)S(1)} collective-permute-done((bf16[64,256]{1,0:T(8,128)(2,1)S(1)}, bf16[64,256]{1,0:T(8,128)(2,1)S(1)}, u32[]{:S(2)}, u32[]{:S(2)}) %collective-permute-start.11) | collective-permute-done | bytes 32800 | tf_op jit(solution)/shard_map/ppermute | solution.py:654
  63.5 1.0 %collective-permute-done.12.refs_3_ = bf16[64,256]{1,0:T(8,128)(2,1)S(1)} collective-permute-done((bf16[64,256]{1,0:T(8,128)(2,1)S(1)}, bf16[64,256]{1,0:T(8,128)(2,1)S(1)}, u32[]{:S(2)}, u32[]{:S(2)}) %collective-permute-start.12) | collective-permute-done | bytes 32800 | tf_op jit(solution)/shard_map/ppermute | solution.py:654
  64.5 0.7 %place.1 = bf16[1,64,1024]{2,1,0:T(8,128)(2,1)} custom-call(f32[8,256]{1,0:T(8,128)S(1)} %get-tuple-element.22.keep_ref.rest_2_, bf16[64,256]{1,0:T(8,128)(2,1)S(1)} %get-tuple-element.38.refs_0_, bf16[64,256]{1,0:T(8,128)(2,1)S(1)} %collective-permute-done.10.refs_1_, bf16[64,256]{1,0:T(8,128)(2,1)S(1)} %collective-permute-done.11.refs_2_, ...), custom_call_target="tpu_custom_call" | custom-call | bytes 300000 | tf_op jit(solution)/shard_map/place/pallas_call | solution.py:534
Async XLA Ops:
  0.6 0.9 %copy-start = (bf16[8,8,4,256]{3,2,1,0:T(4,128)(2,1)S(1)}, bf16[8,8,4,256]{3,2,1,0:T(4,128)(2,1)}, u32[]{:S(2)}) copy-start(bf16[8,8,4,256]{3,2,1,0:T(4,128)(2,1)} %feat_ref.5) | copy-start | bytes 393220
  1.5 0.7 %copy-start.5 = (s32[4,1,4]{2,1,0:T(1,128)S(1)}, s32[4,1,4]{2,1,0:T(1,128)}, u32[]{:S(2)}) copy-start(s32[4,1,4]{2,1,0:T(1,128)} %occ_ref.1) | copy-start | bytes 196
  3.6 10.1 %collective-permute-start = (bf16[80,256]{1,0:T(8,128)(2,1)S(1)}, bf16[80,256]{1,0:T(8,128)(2,1)S(1)}, u32[]{:S(2)}, u32[]{:S(2)}) collective-permute-start(bf16[80,256]{1,0:T(8,128)(2,1)S(1)} %get-tuple-element.23), channel_id=1, source_target_pairs={{0,8},{8,0},{16,24},{24,16},{1,9},{9,1},{17,25},{25,17},{2,10},{10... | collective-permute-start | bytes 122888 | tf_op jit(solution)/shard_map/ppermute | solution.py:575
  6.7 7.0 %collective-permute-start.1 = (bf16[80,256]{1,0:T(8,128)(2,1)S(1)}, bf16[80,256]{1,0:T(8,128)(2,1)S(1)}, u32[]{:S(2)}, u32[]{:S(2)}) collective-permute-start(bf16[80,256]{1,0:T(8,128)(2,1)S(1)} %get-tuple-element.24), channel_id=1, source_target_pairs={{0,24},{8,16},{16,8},{24,0},{1,25},{9,17},{17,9},{25,1},{2,26},{10... | collective-permute-start | bytes 122888 | tf_op jit(solution)/shard_map/ppermute | solution.py:576
  9.2 4.5 %collective-permute-start.2 = (bf16[16,256]{1,0:T(8,128)(2,1)S(1)}, bf16[16,256]{1,0:T(8,128)(2,1)S(1)}, u32[]{:S(2)}, u32[]{:S(2)}) collective-permute-start(bf16[16,256]{1,0:T(8,128)(2,1)S(1)} %get-tuple-element.25.rest_0_), channel_id=1, source_target_pairs={{0,16},{8,24},{16,0},{24,8},{1,17},{9,25},{17,1},{25,9},{2,18},{10... | collective-permute-start | bytes 24584 | tf_op jit(solution)/shard_map/ppermute | solution.py:580
  13.8 0.9 %copy-start.1 = (bf16[8,8,4,256]{3,2,1,0:T(4,128)(2,1)S(1)}, bf16[8,8,4,256]{3,2,1,0:T(4,128)(2,1)}, u32[]{:S(2)}) copy-start(bf16[8,8,4,256]{3,2,1,0:T(4,128)(2,1)} %feat_ref.5) | copy-start | bytes 393220
  15.1 1.2 %collective-permute-start.3 = (bf16[112,256]{1,0:T(8,128)(2,1)S(1)}, bf16[112,256]{1,0:T(8,128)(2,1)S(1)}, u32[]{:S(2)}, u32[]{:S(2)}) collective-permute-start(bf16[112,256]{1,0:T(8,128)(2,1)S(1)} %get-tuple-element.27.own_ref), channel_id=1, source_target_pairs={{0,1},{1,0},{2,3},{3,2},{4,5},{5,4},{6,7},{7,6},{8,9},{9,8},{10,11... | collective-permute-start | bytes 172040 | tf_op jit(solution)/shard_map/ppermute | solution.py:588
  16.7 8.0 %collective-permute-start.5 = (bf16[144,256]{1,0:T(8,128)(2,1)S(1)}, bf16[144,256]{1,0:T(8,128)(2,1)S(1)}, u32[]{:S(2)}, u32[]{:S(2)}) collective-permute-start(bf16[144,256]{1,0:T(8,128)(2,1)S(1)} %get-tuple-element.29), channel_id=1, source_target_pairs={{0,4},{4,0},{1,5},{5,1},{2,6},{6,2},{3,7},{7,3},{8,12},{12,8},{9,1... | collective-permute-start | bytes 221192 | tf_op jit(solution)/shard_map/ppermute | solution.py:606
  18.2 6.4 %collective-permute-start.4 = (bf16[112,256]{1,0:T(8,128)(2,1)S(1)}, bf16[112,256]{1,0:T(8,128)(2,1)S(1)}, u32[]{:S(2)}, u32[]{:S(2)}) collective-permute-start(bf16[112,256]{1,0:T(8,128)(2,1)S(1)} %get-tuple-element.28.own_ref), channel_id=1, source_target_pairs={{0,3},{1,2},{2,1},{3,0},{4,7},{5,6},{6,5},{7,4},{8,11},{9,10},{10,... | collective-permute-start | bytes 172040 | tf_op jit(solution)/shard_map/ppermute | solution.py:602
  19.2 5.4 %collective-permute-start.6 = (bf16[48,256]{1,0:T(8,128)(2,1)S(1)}, bf16[48,256]{1,0:T(8,128)(2,1)S(1)}, u32[]{:S(2)}, u32[]{:S(2)}) collective-permute-start(bf16[48,256]{1,0:T(8,128)(2,1)S(1)} %get-tuple-element.30), channel_id=1, source_target_pairs={{0,7},{1,6},{2,5},{3,4},{4,3},{5,2},{6,1},{7,0},{8,15},{9,14},{10,... | collective-permute-start | bytes 73736 | tf_op jit(solution)/shard_map/ppermute | solution.py:610
  20.0 0.9 %copy-start.3 = (bf16[2,32,864]{2,1,0:T(8,128)(2,1)S(1)}, bf16[2,32,864]{2,1,0:T(8,128)(2,1)}, u32[]{:S(2)}) copy-start(bf16[2,32,864]{2,1,0:T(8,128)(2,1)} %weight_ref.4) | copy-start | bytes 331780
  20.9 0.7 %copy-start.6 = (f32[2,32]{1,0:T(2,128)S(1)}, f32[2,32]{1,0:T(2,128)}, u32[]{:S(2)}) copy-start(f32[2,32]{1,0:T(2,128)} %rest_0_.1) | copy-start | bytes 772
  21.5 0.7 %copy-start.7 = (f32[2,32]{1,0:T(2,128)S(1)}, f32[2,32]{1,0:T(2,128)}, u32[]{:S(2)}) copy-start(f32[2,32]{1,0:T(2,128)} %rest_1_.1) | copy-start | bytes 772
  22.2 0.7 %copy-start.8 = (f32[2,32]{1,0:T(2,128)S(1)}, f32[2,32]{1,0:T(2,128)}, u32[]{:S(2)}) copy-start(f32[2,32]{1,0:T(2,128)} %rest_2_.1) | copy-start | bytes 772
  24.7 8.1 %copy-start.4 = (bf16[2,32,864]{2,1,0:T(8,128)(2,1)S(1)}, bf16[2,32,864]{2,1,0:T(8,128)(2,1)}, u32[]{:S(2)}) copy-start(bf16[2,32,864]{2,1,0:T(8,128)(2,1)} %weight_ref.4) | copy-start | bytes 331780
  28.9 10.8 %copy-start.2 = (bf16[8,8,4,256]{3,2,1,0:T(4,128)(2,1)S(1)}, bf16[8,8,4,256]{3,2,1,0:T(4,128)(2,1)}, u32[]{:S(2)}) copy-start(bf16[8,8,4,256]{3,2,1,0:T(4,128)(2,1)} %feat_ref.5) | copy-start | bytes 393220
  28.9 10.8 %all-to-all-start = ((f32[32,1,128]{2,1,0:T(1,128)}), f32[32,1,128]{2,1,0:T(1,128)S(1)}, u32[]{:S(2)}, u32[]{:S(2)}) async-start(f32[32,1,128]{2,1,0:T(1,128)} %bitcast.1), calls=%async_computation | async-start | bytes 32768 | tf_op jit(solution)/shard_map/all_to_all | solution.py:638
  39.7 6.7 %copy-start.9 = (bf16[3,256,1024]{2,1,0:T(8,128)(2,1)S(1)}, bf16[3,256,1024]{2,1,0:T(8,128)(2,1)}, u32[]{:S(2)}) copy-start(bf16[3,256,1024]{2,1,0:T(8,128)(2,1)} %weight_ref.5) | copy-start | bytes 4718596
  41.9 6.8 %collective-permute-start.7 = (bf16[64,1024]{1,0:T(8,128)(2,1)S(1)}, bf16[64,1024]{1,0:T(8,128)(2,1)S(1)}, u32[]{:S(2)}, u32[]{:S(2)}) collective-permute-start(bf16[64,1024]{1,0:T(8,128)(2,1)S(1)} %get-tuple-element.37.refs_0_), channel_id=1, source_target_pairs={{0,8},{8,0},{16,24},{24,16},{1,9},{9,1},{17,25},{25,17},{2,10},{10... | collective-permute-start | bytes 393224 | tf_op jit(solution)/shard_map/ppermute | solution.py:647
  42.5 12.7 %collective-permute-start.8 = (bf16[64,1024]{1,0:T(8,128)(2,1)S(1)}, bf16[64,1024]{1,0:T(8,128)(2,1)S(1)}, u32[]{:S(2)}, u32[]{:S(2)}) collective-permute-start(bf16[64,1024]{1,0:T(8,128)(2,1)S(1)} %get-tuple-element.37.refs_0_), channel_id=1, source_target_pairs={{0,16},{8,24},{16,0},{24,8},{1,17},{9,25},{17,1},{25,9},{2,18},{10... | collective-permute-start | bytes 393224 | tf_op jit(solution)/shard_map/ppermute | solution.py:647
  43.1 12.1 %collective-permute-start.9 = (bf16[64,1024]{1,0:T(8,128)(2,1)S(1)}, bf16[64,1024]{1,0:T(8,128)(2,1)S(1)}, u32[]{:S(2)}, u32[]{:S(2)}) collective-permute-start(bf16[64,1024]{1,0:T(8,128)(2,1)S(1)} %get-tuple-element.37.refs_0_), channel_id=1, source_target_pairs={{0,24},{8,16},{16,8},{24,0},{1,25},{9,17},{17,9},{25,1},{2,26},{10... | collective-permute-start | bytes 393224 | tf_op jit(solution)/shard_map/ppermute | solution.py:647
  56.6 4.6 %collective-permute-start.10 = (bf16[64,256]{1,0:T(8,128)(2,1)S(1)}, bf16[64,256]{1,0:T(8,128)(2,1)S(1)}, u32[]{:S(2)}, u32[]{:S(2)}) collective-permute-start(bf16[64,256]{1,0:T(8,128)(2,1)S(1)} %get-tuple-element.39), channel_id=1, source_target_pairs={{0,8},{8,0},{16,24},{24,16},{1,9},{9,1},{17,25},{25,17},{2,10},{10... | collective-permute-start | bytes 98312 | tf_op jit(solution)/shard_map/ppermute | solution.py:654
  58.7 4.8 %collective-permute-start.11 = (bf16[64,256]{1,0:T(8,128)(2,1)S(1)}, bf16[64,256]{1,0:T(8,128)(2,1)S(1)}, u32[]{:S(2)}, u32[]{:S(2)}) collective-permute-start(bf16[64,256]{1,0:T(8,128)(2,1)S(1)} %get-tuple-element.40), channel_id=1, source_target_pairs={{0,16},{8,24},{16,0},{24,8},{1,17},{9,25},{17,1},{25,9},{2,18},{10... | collective-permute-start | bytes 98312 | tf_op jit(solution)/shard_map/ppermute | solution.py:654
  58.8 5.7 %collective-permute-start.12 = (bf16[64,256]{1,0:T(8,128)(2,1)S(1)}, bf16[64,256]{1,0:T(8,128)(2,1)S(1)}, u32[]{:S(2)}, u32[]{:S(2)}) collective-permute-start(bf16[64,256]{1,0:T(8,128)(2,1)S(1)} %get-tuple-element.41), channel_id=1, source_target_pairs={{0,24},{8,16},{16,8},{24,0},{1,25},{9,17},{17,9},{25,1},{2,26},{10... | collective-permute-start | bytes 98312 | tf_op jit(solution)/shard_map/ppermute | solution.py:654

commit v3 on v2

--- a/solution.py
+++ b/solution.py
@@ -17,7 +17,6 @@
 ALL = ("gx", "gy", "gz")
 F32, BF16 = jnp.float32, jnp.bfloat16
 HIGHEST = lax.Precision.HIGHEST
-GROUPS = C // GW
 TAIL = 16
 
 
@@ -33,64 +32,87 @@
     return jnp.dot(a, b, precision=HIGHEST, preferred_element_type=F32)
 
 
-def group_of(lanes, dim, shape):
-    return iota(shape, dim) // (lanes // GROUPS)
+def spread_sum(v):
+    lane = iota(v.shape, 1)
+    s = 1
+    while s < GW * BR:
+        v = v + jnp.where(lane & s == 0, pltpu.roll(v, 128 - s, 1), pltpu.roll(v, s, 1))
+        s *= 2
+    return v
+
+
+def group_sum(total):
+    k = total.shape[1] // 128
+    rows = [jnp.broadcast_to(total[:, h * 128 : (h + 1) * 128], (8, 128)) for h in range(k)]
+    out = spread_sum(jnp.concatenate(rows, axis=0))
+    return jnp.concatenate([out[h * 8 : (h + 1) * 8] for h in range(k)], axis=1)
 
 
 def moments(total, squares_about, count):
-    lanes = total.shape[1]
-    col = iota((lanes, 128), 1)
-    group = group_of(lanes, 0, (lanes, 128))
-    sums = exact_dot(jnp.broadcast_to(total, (8, lanes)), onehot(group == col, F32))
-    back = onehot(iota((128, lanes), 0) == group_of(lanes, 1, (128, lanes)), F32)
-    squares = squares_about(exact_dot(sums / count, back)[0:1])
-    second = exact_dot(
-        jnp.broadcast_to(squares, (8, lanes)), onehot(group + GROUPS == col, F32)
-    )
-    return jnp.where(iota((8, 128), 1) == 2 * GROUPS, count, sums + second)
-
-
-def merge(rows):
-    n = rows[:, 2 * GROUPS : 2 * GROUPS + 1]
-    whole = jnp.sum(rows, axis=0, keepdims=True)
-    drift = rows / jnp.maximum(n, 1.0) - whole / jnp.sum(n)
-    between = jnp.sum(drift * drift * n, axis=0, keepdims=True)
-    between = jnp.where(iota((8, 128), 1) < GROUPS, between, 0.0)
-    return whole + pltpu.roll(between, GROUPS, 1)
-
-
-def stack_rows(rows):
-    index = iota((8, 128), 0)
-    out = jnp.zeros((8, 128), F32)
-    for i, row in enumerate(rows):
-        out = jnp.where(index == i, row, out)
-    return out
-
-
-def centre_scale(merged, lanes):
-    row = iota((128, lanes), 0)
-    group = group_of(lanes, 1, (128, lanes))
-    scaled = merged / merged[0:1, 2 * GROUPS : 2 * GROUPS + 1]
-    centre = exact_dot(scaled, onehot(group == row, F32))
-    spread = exact_dot(scaled, onehot(group + GROUPS == row, F32))
-    return centre[0:1], lax.rsqrt(spread[0:1] + EPS)
-
-
-def to_tail(row):
-    high = row.astype(BF16).astype(F32)
-    mid = (row - high).astype(BF16).astype(F32)
-    low = row - high - mid
-    index = iota((8, 128), 0)
-    part = jnp.where(index == 0, high, jnp.where(index == 1, mid, jnp.where(index == 2, low, 0.0)))
-    zero = jnp.zeros((8, 128), F32)
-    top = jnp.concatenate([part, zero], axis=1)
-    return jnp.concatenate([top, jnp.zeros((TAIL - 8, 256), F32)], axis=0).astype(BF16)
+    sums = group_sum(total)
+    squares = group_sum(squares_about((sums / count)[0:1]))
+    return sums, squares, jnp.zeros(sums.shape, F32) + count
+
+
+def merge(parts):
+    n = sum(p[2] for p in parts)
+    sums = sum(p[0] for p in parts)
+    centre = sums / n
+    squares = sum(p[1] + p[2] * (p[0] / p[2] - centre) ** 2 for p in parts)
+    return sums, squares, n
+
+
+def centre_scale(part):
+    return part[0] / part[2], lax.rsqrt(part[1] / part[2] + EPS)
+
+
+def to_row(part):
+    j = iota((8, 128), 1) % (GW * BR)
+    row = jnp.zeros((8, 128), F32)
+    for h in range(2):
+        for k in range(3):
+            row = jnp.where(j == 4 * h + k, part[k][:, h * 128 : (h + 1) * 128], row)
+    return row
+
+
+def from_rows(rows):
+    n = jnp.maximum(pltpu.roll(rows, 126, 1), 1.0)
+    total = jnp.sum(n, axis=0, keepdims=True)
+    centre = jnp.sum(rows, axis=0, keepdims=True) / total
+    drift = rows / n - centre
+    squares = pltpu.roll(rows, 127, 1) + n * drift * drift
+    spread = jnp.sum(squares, axis=0, keepdims=True) / total
+    j = iota((8, 128), 1) % (GW * BR)
+    blocks = [
+        jnp.where(j == 4 * h, jnp.broadcast_to(v, (8, 128)), 0.0)
+        for v in (centre, spread) for h in range(2)
+    ]
+    out = spread_sum(jnp.concatenate(blocks, axis=0))
+    out = [out[8 * i : 8 * i + 1] for i in range(4)]
+    return (
+        jnp.concatenate(out[:2], axis=1),
+        lax.rsqrt(jnp.concatenate(out[2:], axis=1) + EPS),
+    )
+
+
+def to_tail(part):
+    index = iota((8, 256), 0)
+    blocks = [jnp.zeros((8, 256), F32), jnp.zeros((8, 256), F32)]
+    for k, value in enumerate(part):
+        value = jnp.broadcast_to(value[0:1], (8, 256))
+        high = value.astype(BF16).astype(F32)
+        mid = (value - high).astype(BF16).astype(F32)
+        for i, piece in enumerate((high, mid, value - high - mid)):
+            blocks[k // 2] = jnp.where(index == 3 * (k % 2) + i, piece, blocks[k // 2])
+    return jnp.concatenate(blocks, axis=0).astype(BF16)
 
 
 def from_tail(message_ref):
     rows = message_ref.shape[0]
-    part = message_ref[rows - TAIL : rows, :].astype(F32)[:, 0:128]
-    return jnp.broadcast_to(jnp.sum(part, axis=0, keepdims=True), (8, 128))
+    part = message_ref[rows - TAIL : rows, :].astype(F32)
+    return [
+        jnp.sum(part[r : r + 3], axis=0, keepdims=True) for r in (0, 3, 8)
+    ]
 
 
 def silu(u):
@@ -160,14 +182,8 @@
     return jnp.where(i > 0, low, SENT), jnp.where(i < n - 1, high, SENT)
 
 
-def coded(feat_ref, keep):
-    sx, sy, sb, lanes = feat_ref.shape
-    field = jnp.where((keep[:sb] > 0)[None, None], feat_ref[...].astype(F32), SENT)
-    return jnp.concatenate([field, jnp.full((sx, sy, 8 - sb, lanes), SENT, F32)], axis=2)
-
-
-def pre_kernel(members, occ_ref, feat_ref, keep_ref, keys_ref, first_ref, second_ref, tail_ref,
-               rows_ref=None):
+def pre_kernel(members, occ_ref, feat_ref, keep_ref, keys_ref, coded_ref, first_ref, second_ref,
+               tail_ref, rows_ref=None):
     sx, sy, sb, lanes = feat_ref.shape
     me = lax.axis_index("gx")
     row = iota((8, lanes), 0)
@@ -189,14 +205,18 @@
                 (lane // (seq // members) == k) & (lane % (2 * sb) // 2 == b), there, keys
             )
     keys_ref[...] = keys
-    field = feat_ref[...].astype(F32).reshape(sx * sy, sb, lanes)
-    total = jnp.sum(jnp.sum(field, axis=0) * keep[:sb], axis=0, keepdims=True)
+    field = feat_ref[...].astype(F32)
+    wide = jnp.concatenate([field, jnp.zeros((sx, sy, 8 - sb, lanes), F32)], axis=2)
+    wide = wide.reshape(sx * sy, 8, lanes)
+    total = jnp.sum(jnp.sum(wide, axis=0) * keep, axis=0, keepdims=True)
 
     def squares_about(mean):
-        d = field - mean[None]
-        return jnp.sum(jnp.sum(d * d, axis=0) * keep[:sb], axis=0, keepdims=True)
-
-    packed = pack_pairs(coded(feat_ref, keep))
+        d = wide - mean[None]
+        return jnp.sum(jnp.sum(d * d, axis=0) * keep, axis=0, keepdims=True)
+
+    code = jnp.where((keep > 0)[None], wide, SENT)
+    coded_ref[...] = code.reshape(sx * sy * 8, lanes).astype(BF16)
+    packed = pack_pairs(code.reshape(sx, sy, 8, lanes))
     low = packed[0:2].reshape(-1, lanes)
     high = packed[sx - 2 : sx].reshape(-1, lanes)
     size = low.shape[0]
@@ -208,18 +228,18 @@
     second_ref[size : size + TAIL, :] = tail
     tail_ref[...] = tail
     if rows_ref is not None:
-        rows_ref[...] = jnp.broadcast_to(mine[0:1], rows_ref.shape)
-
-
-def line_kernel(narrow, keep_ref, feat_ref, first_ref, second_ref, *rest):
+        rows_ref[...] = jnp.broadcast_to(to_row(mine)[0:1], rows_ref.shape)
+
+
+def line_kernel(narrow, sy, sb, rows_ref, coded_ref, first_ref, second_ref, *rest):
     tails, (ext_ref, out_ref, buf) = rest[:-3], rest[-3:]
-    sx, sy, sb, lanes = feat_ref.shape
+    lanes = coded_ref.shape[1]
+    sx = coded_ref.shape[0] // (sy * 8)
     size = 2 * (sy // 2) * 8
     low, high = sides(
         "gx", first_ref[0:size].astype(F32), second_ref[0:size].astype(F32)
     )
-    whole = coded(feat_ref, keep_ref[...]).reshape(sx * sy * 8, lanes)
-    write_block(buf, 2 * sy * 8, whole)
+    write_block(buf, 2 * sy * 8, coded_ref[...].astype(F32))
     for x0, side in ((0, low), (sx + 2, high)):
         for i in range(2):
             part = side[i * (size // 2) : (i + 1) * (size // 2)].reshape(sy // 2, 8, lanes)
@@ -234,7 +254,7 @@
     mine = [from_tail(ref) for ref in tails]
     if narrow:
         mine = mine + [from_tail(first_ref), from_tail(second_ref)]
-    out_ref[count : count + TAIL, :] = to_tail(merge(stack_rows(mine)))
+    out_ref[count : count + TAIL, :] = to_tail(merge(mine))
 
 
 def corner_rows(count):
@@ -250,7 +270,7 @@
     write_block(stage, 0, other_ref[0 : ex * sy].astype(F32))
     gap = corner_rows(ex)
     pad = jnp.zeros((gap - ex, lanes), F32)
-    tail = to_tail(merge(stack_rows([from_tail(own_ref), from_tail(other_ref)])))
+    tail = to_tail(merge([from_tail(own_ref), from_tail(other_ref)]))
     packed = pack_pairs(block.reshape(ex, sy, 8, lanes))
 
     def side(y0):
@@ -287,12 +307,12 @@
             ref[value.shape[0] : value.shape[0] + TAIL, :] = tail
 
 
-def band_kernel(layer, weight_ref, *rest):
-    pars, out_ref, rows_ref = (rest[:3], rest[3], rest[4]) if len(rest) > 1 else ((), rest[0], None)
+def band_kernel(weight_ref, *rest):
+    out_ref, rows_ref = rest[-2:] if len(rest) == 2 else rest[1:3]
     lanes = C * BR
     spread = onehot(iota((C, lanes), 0) == iota((C, lanes), 1) // BR)
     column = onehot(iota((lanes, C), 0) // BR == iota((lanes, C), 1))
-    turned = jnp.transpose(weight_ref[layer].astype(F32)).astype(BF16)
+    turned = jnp.transpose(weight_ref[0].astype(F32)).astype(BF16)
     wide = jnp.dot(turned, spread, preferred_element_type=F32).astype(BF16)
     row = iota((lanes, lanes), 0)
     zi, zo = row % BR, iota((lanes, lanes), 1) % BR
@@ -313,11 +333,13 @@
             mixed = mixed + (pltpu.roll(outer, 2 * ey, 0) if ey else outer)
             out_ref[ex, ey * lanes : (ey + 1) * lanes, :] = inner.astype(BF16)
         out_ref[ex, 3 * lanes : 4 * lanes, :] = mixed.astype(BF16)
-    if rows_ref is not None:
+    if len(rest) > 2:
         pick = onehot(iota((C, lanes), 0) == iota((C, lanes), 1) // BR, F32)
-        for k, ref in enumerate(pars):
-            rows_ref[2 * k : 2 * k + 2, :] = exact_dot(ref[...], pick)
-        rows_ref[6:8, :] = jnp.zeros((2, lanes), F32)
+        rows_ref[...] = jnp.zeros(rows_ref.shape, F32)
+        rows_ref[0 : rest[0].shape[0], :] = exact_dot(rest[0][...], pick)
+        rest[3][...] = weight_ref[1:2]
+    else:
+        rows_ref[...] = jnp.zeros(rows_ref.shape, F32)
 
 
 def turn_kernel(weight_ref, out_ref):
@@ -337,7 +359,7 @@
     stats_ref = None
     if not narrow:
         stats_ref, rest = rest[0], rest[1:]
-    keep_ref, weight_ref, rows_ref, mid_ref, out_ref, buf, lhs, msk = rest
+    keep_ref, weight_ref, rows_ref, _, mid_ref, out_ref, buf, lhs, msk = rest
     lanes = ext_ref.shape[1]
     ex = ext_ref.shape[0] // (sy * 8)
     ey = sy + 4
@@ -372,12 +394,11 @@
             write(buf, (y0 + i) * 8 + 7, ex, ey * 8, c_low[i * gap : i * gap + ex])
             write(buf, (y0 + i) * 8 + sb, ex, ey * 8, c_high[i * gap : i * gap + ex])
     if narrow:
-        merged = merge(stack_rows(
+        centre, scale = centre_scale(merge(
             [from_tail(r) for r in (own_ref, zface_ref) + tuple(near) + tuple(far)]
         ))
     else:
-        merged = merge(stats_ref[...])
-    centre, scale = centre_scale(merged, lanes)
+        centre, scale = from_rows(stats_ref[...])
     gain, shift, bias = rows_ref[0:1], rows_ref[2:3], rows_ref[4:5]
     scale = scale * gain
     oy, sx = sy + 2, ex - 4
@@ -415,7 +436,7 @@
         return over_cells(lambda v: (v - mean[None]) * (v - mean[None]))
 
     mine = moments(over_cells(lambda v: v), squares_about, entries)
-    out_ref[...] = jnp.broadcast_to(mine[0:1], out_ref.shape)
+    out_ref[...] = jnp.broadcast_to(to_row(mine)[0:1], out_ref.shape)
     for x in range(ox):
         rows = slice(x * oy * 8, (x + 1) * oy * 8)
         there = msk[(x + 1) * step + 8 : (x + 2) * step - 8]
@@ -423,11 +444,10 @@
         mid_ref[rows] = jnp.where(there, mid_ref[rows], BIG)
 
 
-def second_kernel(stats_ref, mid_ref, weight_ref, rows_ref, keep_ref, feat_ref,
-                  fine_ref, tok_ref, lhs):
-    sx, sy, sb, lanes = feat_ref.shape
+def second_kernel(stats_ref, mid_ref, weight_ref, rows_ref, coded_ref, fine_ref, tok_ref, lhs):
+    sx, sy, sb, lanes = fine_ref.shape
     step = (sy + 2) * 8
-    centre, scale = centre_scale(merge(stats_ref[...]), lanes)
+    centre, scale = from_rows(stats_ref[...])
     gain, shift, bias = rows_ref[1:2], rows_ref[3:4], rows_ref[5:6]
     scale = scale * gain
     half = sy // 2 * 8
@@ -444,11 +464,9 @@
         acc = acc + jnp.dot(
             lhs[e * half : e * half + size, :], weight_ref[e], preferred_element_type=F32
         )
-    keep = keep_ref[...]
-    keep = jnp.where(iota(keep.shape, 0) < sb, keep, pltpu.roll(keep, sb, 0))
-    blank = jnp.zeros((sx, sy, 8 - sb, lanes), F32)
-    field = pack_pairs(jnp.concatenate([feat_ref[...].astype(F32), blank], axis=2))
-    out = (field.reshape(-1, 8, lanes) * keep + acc.reshape(-1, 8, lanes)) * keep
+    field = pack_pairs(coded_ref[...].astype(F32).reshape(sx, sy, 8, lanes))
+    field = field.reshape(size, lanes)
+    out = jnp.where(field != SENT, field + acc, 0.0).reshape(-1, 8, lanes)
     out = out.astype(BF16)
     wide = out.astype(F32)
     other = pltpu.roll(wide, 4, 1)
@@ -564,10 +582,11 @@
     row_shape = [] if narrow else [shape(devices, 128, dtype=F32)]
 
     slab = sy * 8 + TAIL
-    keep, keys, first, second, tail, *stats = call(
+    keep, keys, coded, first, second, tail, *stats = call(
         functools.partial(pre_kernel, nx), "pre", (SM, VM),
-        [shape(8, lanes, dtype=F32), shape(8, own * nx, dtype=F32), shape(slab, lanes),
-         shape(slab, lanes), shape(TAIL, lanes)] + row_shape,
+        [shape(8, lanes, dtype=F32), shape(8, own * nx, dtype=F32),
+         shape(sx * sy * 8, lanes), shape(slab, lanes), shape(slab, lanes), shape(TAIL, lanes)]
+        + row_shape,
         (occupancy, features), nbytes=10**6,
     )
     stats = [lax.all_to_all(s, ALL, 0, 0, tiled=True) for s in stats]
@@ -578,11 +597,21 @@
     tails = [tail]
     if narrow:
         tails.append(lax.ppermute(tail, "gx", [(i, i ^ 2) for i in range(nx)]))
+    band = shape(3, 4 * lanes, lanes)
+    pars = jnp.concatenate([norm_gain, norm_shift, conv_bias], axis=0)
+    later = shape(1, *conv_weight.shape[1:])
+    band0, rows, later = call(
+        band_kernel, "band0", (VM,) * 2, [band, shape(8, lanes, dtype=F32), later],
+        (conv_weight, pars), nbytes=8 * 10**6,
+    )
+    band1, mark = call(
+        band_kernel, "band1", (VM,), [band, shape(8, 128, dtype=F32)], (later,), nbytes=8 * 10**6,
+    )
     count = ex * sy
     ext, mine = call(
-        functools.partial(line_kernel, narrow), "line", (VM,) * (4 + len(tails)),
+        functools.partial(line_kernel, narrow, sy, sb), "line", (VM,) * (4 + len(tails)),
         [shape(count * 8, lanes), shape(count + TAIL, lanes)],
-        (keep, features, *got, *tails),
+        (rows, coded, *got, *tails),
         [pltpu.VMEM((lanes // 128, count * 8, 128), F32)], nbytes=10**6,
     )
     core = lax.ppermute(mine, "gz", list(pairing(nz, False, False).items()))
@@ -609,14 +638,6 @@
         ]
         ygot.append(lax.ppermute(yfaces[2 * k + 1], ("gy", "gz"), both))
 
-    band = shape(3, 4 * lanes, lanes)
-    band0, rows = call(
-        functools.partial(band_kernel, 0), "band0", (VM,) * 4, [band, shape(8, lanes, dtype=F32)],
-        (conv_weight, norm_gain, norm_shift, conv_bias), nbytes=8 * 10**6,
-    )
-    band1 = call(
-        functools.partial(band_kernel, 1), "band1", (VM,), band, (conv_weight,), nbytes=8 * 10**6,
-    )
     cols, feats = qkv_weight.shape[1:]
     turned = call(
         turn_kernel, "turn", (VM,), shape(feats, 3 * cols), (qkv_weight,),
@@ -627,9 +648,9 @@
     size = (sx + 2) * oy * 8
     mid, mine = call(
         functools.partial(first_kernel, narrow, faces, sy, sb), "first",
-        (VM,) * (7 + 2 * faces + len(stats)),
+        (VM,) * (8 + 2 * faces + len(stats)),
         [shape(size, lanes, dtype=F32), shape(devices, 128, dtype=F32)],
-        (ext, own_tail, core, zgot, *ygot, *stats, keep, band0, rows),
+        (ext, own_tail, core, zgot, *ygot, *stats, keep, band0, rows, mark),
         [pltpu.VMEM((lanes // 128, ex * ey * 8, 128), F32),
          pltpu.VMEM((ex * oy * 8, 4 * lanes), BF16),
          pltpu.VMEM((ex * ey * 8, 128), F32)],
@@ -637,14 +658,15 @@
     )
     stats = lax.all_to_all(mine, ALL, 0, 0, tiled=True)
     fine_out, tokens = call(
-        second_kernel, "second", (VM,) * 6,
+        second_kernel, "second", (VM,) * 5,
         [shape(*features.shape), shape(own, feats)],
-        (stats, mid, band1, rows, keep, features),
+        (stats, mid, band1, rows, coded),
         [pltpu.VMEM(((sx + 2) * sy * 4, 4 * lanes), BF16)],
         flops=10**9, nbytes=4 * 10**6,
     )
     swaps = [[(i, i ^ k) for i in range(nx)] for k in range(nx)]
-    blocks = [tokens] + [lax.ppermute(tokens, "gx", swaps[k]) for k in range(1, nx)]
+    blocks = {k: lax.ppermute(tokens, "gx", swaps[k]) for k in range(nx - 1, 0, -1)}
+    blocks = [tokens] + [blocks[k] for k in range(1, nx)]
     outs = call(
         functools.partial(attend_kernel, nx), "attend", (VM,) * (2 + nx),
         [shape(own, cols)] * nx, (keys, turned, *blocks),

time: 65.5 us -> 61.2 us (0.934)
  blocking collectives: 0 us -> 8.92 us
  waiting for transfers between devices: 21.2 us -> 15.8 us
  starting transfers between devices: 21.8 us -> 18 us
  local copies, waits for them, and re-layouts: 5.43 us -> 2.48 us
  Pallas kernels: 16 us -> 14.3 us
  other arithmetic: 0 us -> 0.72 us
    all_to_all x0 -> x1, blocking collectives: none -> 8.92 us  [body(): stats = lax.all_to_all(mine, ALL, 0, 0, tiled=True)]
    all_to_all x1 -> x0, waiting for transfers between devices: 5.21 us -> none  [body(): stats = lax.all_to_all(mine, ALL, 0, 0, tiled=True)]
    ppermute x1, waiting for transfers between devices: 4.43 us -> 0.01 us  [body(): tails.append(lax.ppermute(tail, 'gx', [(i, i ^ 2) for i in range(nx)]))]
    ppermute x1, starting transfers between devices: 0.12 us -> 4.11 us  [body(): tails.append(lax.ppermute(tail, 'gx', [(i, i ^ 2) for i in range(nx)]))]
    all_to_all x1 -> x0, starting transfers between devices: 3.86 us -> none  [body(): stats = lax.all_to_all(mine, ALL, 0, 0, tiled=True)]
    unnamed x20 -> x8, local copies, waits for them, and re-layouts: 5.43 us -> 2.48 us
    ppermute x1, starting transfers between devices: 2.47 us -> 0.01 us  [body(): lax.ppermute(second, 'gx', list(pairing(nx, True, narrow).items()))]
    ppermute x1, waiting for transfers between devices: 0.01 us -> 2.47 us  [body(): lax.ppermute(second, 'gx', list(pairing(nx, True, narrow).items()))]
  transfers between devices with their start and end apart: 14 -> 13, of which waited for: 7 -> 7; matrix products, arithmetic and copies ran while one was open for 0% -> 1% of each run, Pallas kernels for 8% -> 9%
where the time goes in v3:
time: 61.2 us; the launch traced here: 60.9 us
  starting transfers between devices  18 us (29%)
  waiting for transfers between devices  15.8 us (26%)
  Pallas kernels  14.3 us (23%)
  blocking collectives  8.92 us (15%)
  local copies, waits for them, and re-layouts  2.48 us (4%)
  other arithmetic  0.72 us (1%)
  between operations  0.71 us (1%)
    pallas_call x10, Pallas kernels, call(): pl.pallas_call(kernel, out_shape=out, in_specs=list(specs), out_specs=jax...  14.3 us
    all_to_all x1, blocking collectives, body(): stats = lax.all_to_all(mine, ALL, 0, 0, tiled=True)  8.92 us
    ppermute x3, waiting for transfers between devices, body(): lax.ppermute(tokens, 'gx', swaps[k])  6.97 us
    ppermute x3, starting transfers between devices, body(): lax.ppermute(outs[k], 'gx', swaps[k])  4.6 us
    ppermute x3, starting transfers between devices, body(): lax.ppermute(tokens, 'gx', swaps[k])  4.39 us
    ppermute x1, starting transfers between devices, body(): tails.append(lax.ppermute(tail, 'gx', [(i, i ^ 2) for i in range(nx)]))  4.11 us
    ppermute x3, waiting for transfers between devices, body(): lax.ppermute(outs[k], 'gx', swaps[k])  3.36 us
    unnamed x8, local copies, waits for them, and re-layouts  2.48 us
  transfers between devices with their start and end apart: 13, of which 7 were waited for; matrix products, arithmetic and copies ran while one was open for 1% of the time, Pallas kernels for 9%

profile of v3, /device:TPU:0, one launch (start us, length us, event | category | flops | bytes accessed | tf_op | source)
XLA Modules:
  0.0 60.9 jit_solution(147260500734241743)
XLA Ops:
  0.6 0.0 copy-start
  0.6 0.9 %copy-done = bf16[8,8,4,256]{3,2,1,0:T(4,128)(2,1)S(1)} copy-done((bf16[8,8,4,256]{3,2,1,0:T(4,128)(2,1)S(1)}, bf16[8,8,4,256]{3,2,1,0:T(4,128)(2,1)}, u32[]{:S(2)}) %copy-start) | copy-done | bytes 131096
  1.5 0.0 copy-start.2
  1.5 0.7 %copy-done.2 = s32[4,1,4]{2,1,0:T(1,128)S(1)} copy-done((s32[4,1,4]{2,1,0:T(1,128)S(1)}, s32[4,1,4]{2,1,0:T(1,128)}, u32[]{:S(2)}) %copy-start.2) | copy-done | bytes 88
  2.2 1.5 %pre.1 = (f32[8,256]{1,0:T(8,128)S(1)}, f32[8,256]{1,0:T(8,128)S(1)}, bf16[512,256]{1,0:T(8,128)(2,1)S(1)}, bf16[80,256]{1,0:T(8,128)(2,1)S(1)}, bf16[80,256]{1,...) custom-call(s32[4,1,4]{2,1,0:T(1,128)S(1)} %copy-done.2, bf16[8,8,4,256]{3,2,1,0:T(4,128)(2,1)S(1)} %copy-done), custom_call_target="tpu_custom_call" | custom-call | bytes 1000000 | tf_op jit(solution)/shard_map/pre/pallas_call | solution.py:552
  3.7 4.1 %collective-permute-start.2 = (bf16[16,256]{1,0:T(8,128)(2,1)S(1)}, bf16[16,256]{1,0:T(8,128)(2,1)S(1)}, u32[]{:S(2)}, u32[]{:S(2)}) collective-permute-start(bf16[16,256]{1,0:T(8,128)(2,1)S(1)} %get-tuple-element.30.rest_0_), channel_id=1, source_target_pairs={{0,16},{8,24},{16,0},{24,8},{1,17},{9,25},{17,1},{25,9},{2,18},{10... | collective-permute-start | bytes 24584 | tf_op jit(solution)/shard_map/ppermute | solution.py:599
  7.8 1.6 %collective-permute-start = (bf16[80,256]{1,0:T(8,128)(2,1)S(1)}, bf16[80,256]{1,0:T(8,128)(2,1)S(1)}, u32[]{:S(2)}, u32[]{:S(2)}) collective-permute-start(bf16[80,256]{1,0:T(8,128)(2,1)S(1)} %get-tuple-element.28), channel_id=1, source_target_pairs={{0,8},{8,0},{16,24},{24,16},{1,9},{9,1},{17,25},{25,17},{2,10},{10... | collective-permute-start | bytes 122888 | tf_op jit(solution)/shard_map/ppermute | solution.py:594
  9.4 0.0 collective-permute-start.1
  9.4 0.7 %pad_maximum_fusion.rest_0_ = f32[6,32]{1,0:T(8,128)S(1)} fusion(f32[2,32]{1,0:T(2,128)} %param.12, f32[2,32]{1,0:T(2,128)} %param.10, f32[2,32]{1,0:T(2,128)} %param.9), kind=kLoop, calls=%fused_computation | loop fusion | flops 384 | bytes 1536 | tf_op jit(solution)/shard_map/concatenate | solution.py:601
  10.1 0.0 copy-start.1
  10.1 0.9 %copy-done.1 = bf16[2,32,864]{2,1,0:T(8,128)(2,1)S(1)} copy-done((bf16[2,32,864]{2,1,0:T(8,128)(2,1)S(1)}, bf16[2,32,864]{2,1,0:T(8,128)(2,1)}, u32[]{:S(2)}) %copy-start.1) | copy-done | bytes 110616
  11.0 1.7 %band0.1 = (bf16[3,1024,256]{2,1,0:T(8,128)(2,1)S(1)}, f32[8,256]{1,0:T(8,128)S(1)}, bf16[1,32,864]{2,1,0:T(8,128)(2,1)S(1)}) custom-call(bf16[2,32,864]{2,1,0:T(8,128)(2,1)S(1)} %copy-done.1, f32[6,32]{1,0:T(8,128)S(1)} %pad_maximum_fusion.rest_0_), custom_call_target="tpu_custom_call" | custom-call | bytes 8000000 | tf_op jit(solution)/shard_map/band0/pallas_call | solution.py:552
  12.7 0.0 collective-permute-done.2.rest_1_
  12.7 0.0 collective-permute-done.first_ref
  12.7 2.5 %collective-permute-done.1.second_ref = bf16[80,256]{1,0:T(8,128)(2,1)S(1)} collective-permute-done((bf16[80,256]{1,0:T(8,128)(2,1)S(1)}, bf16[80,256]{1,0:T(8,128)(2,1)S(1)}, u32[]{:S(2)}, u32[]{:S(2)}) %collective-permute-start.1) | collective-permute-done | bytes 40992 | tf_op jit(solution)/shard_map/ppermute | solution.py:595
  15.2 0.2 line.1
  15.4 0.1 collective-permute-start.3
  15.5 1.2 %collective-permute-done.3.other_ref.core_ref = bf16[112,256]{1,0:T(8,128)(2,1)S(1)} collective-permute-done((bf16[112,256]{1,0:T(8,128)(2,1)S(1)}, bf16[112,256]{1,0:T(8,128)(2,1)S(1)}, u32[]{:S(2)}, u32[]{:S(2)}) %collective-permute-start.3) | collective-permute-done | bytes 57376 | tf_op jit(solution)/shard_map/ppermute | solution.py:617
  16.7 0.2 chip.1
  16.9 1.6 %collective-permute-start.5 = (bf16[144,256]{1,0:T(8,128)(2,1)S(1)}, bf16[144,256]{1,0:T(8,128)(2,1)S(1)}, u32[]{:S(2)}, u32[]{:S(2)}) collective-permute-start(bf16[144,256]{1,0:T(8,128)(2,1)S(1)} %get-tuple-element.34), channel_id=1, source_target_pairs={{0,4},{4,0},{1,5},{5,1},{2,6},{6,2},{3,7},{7,3},{8,12},{12,8},{9,1... | collective-permute-start | bytes 221192 | tf_op jit(solution)/shard_map/ppermute | solution.py:635
  18.5 1.0 %collective-permute-start.4 = (bf16[112,256]{1,0:T(8,128)(2,1)S(1)}, bf16[112,256]{1,0:T(8,128)(2,1)S(1)}, u32[]{:S(2)}, u32[]{:S(2)}) collective-permute-start(bf16[112,256]{1,0:T(8,128)(2,1)S(1)} %get-tuple-element.33.own_ref), channel_id=1, source_target_pairs={{0,3},{1,2},{2,1},{3,0},{4,7},{5,6},{6,5},{7,4},{8,11},{9,10},{10,... | collective-permute-start | bytes 172040 | tf_op jit(solution)/shard_map/ppermute | solution.py:631
  19.5 0.7 %collective-permute-start.6 = (bf16[48,256]{1,0:T(8,128)(2,1)S(1)}, bf16[48,256]{1,0:T(8,128)(2,1)S(1)}, u32[]{:S(2)}, u32[]{:S(2)}) collective-permute-start(bf16[48,256]{1,0:T(8,128)(2,1)S(1)} %get-tuple-element.35), channel_id=1, source_target_pairs={{0,7},{1,6},{2,5},{3,4},{4,3},{5,2},{6,1},{7,0},{8,15},{9,14},{10,... | collective-permute-start | bytes 73736 | tf_op jit(solution)/shard_map/ppermute | solution.py:639
  20.2 1.7 %band1.1 = (bf16[3,1024,256]{2,1,0:T(8,128)(2,1)S(1)}, f32[8,128]{1,0:T(8,128)S(1)}) custom-call(bf16[1,32,864]{2,1,0:T(8,128)(2,1)S(1)} %get-tuple-element.38.weight_ref), custom_call_target="tpu_custom_call" | custom-call | bytes 8000000 | tf_op jit(solution)/shard_map/band1/pallas_call | solution.py:552
  21.9 1.8 %collective-permute-done.6.rest_1_ = bf16[48,256]{1,0:T(8,128)(2,1)S(1)} collective-permute-done((bf16[48,256]{1,0:T(8,128)(2,1)S(1)}, bf16[48,256]{1,0:T(8,128)(2,1)S(1)}, u32[]{:S(2)}, u32[]{:S(2)}) %collective-permute-start.6) | collective-permute-done | bytes 24608 | tf_op jit(solution)/shard_map/ppermute | solution.py:639
  23.6 0.0 collective-permute-done.4.zface_ref
  23.6 0.0 collective-permute-done.5.rest_0_
  23.6 3.0 %first.1 = (f32[800,256]{1,0:T(8,128)S(1)}, f32[32,128]{1,0:T(8,128)S(1)}) custom-call(bf16[768,256]{1,0:T(8,128)(2,1)S(1)} %get-tuple-element.31.ext_ref, bf16[112,256]{1,0:T(8,128)(2,1)S(1)} %get-tuple-element.33.own_ref, bf16[112,256]{1,0:T(8,128)(2,1)S(1)} %collective-permute-done.3.other_ref.core_ref, ...), custom_call_target="tpu_custom_call" | custom-call | flops 2000000000 | bytes 4000000 | tf_op jit(solution)/shard_map/first/pallas_call | solution.py:552
  26.6 8.9 %all_to_all.11 = f32[32,1,128]{2,1,0:T(1,128)S(1)} all-to-all(f32[32,1,128]{2,1,0:T(1,128)S(1)} %bitcast.4), channel_id=1, replica_groups=mesh['gx'=4,'gy'=2,'gz'=4] {'gx','gy','gz'}, dimensions={0} | all-to-all | bytes 32768 | tf_op jit(solution)/shard_map/all_to_all | solution.py:659
  35.5 0.0 copy-start.3
  35.5 2.1 %second.1 = (bf16[8,8,4,256]{3,2,1,0:T(4,128)(2,1)}, bf16[64,1024]{1,0:T(8,128)(2,1)S(1)}) custom-call(f32[32,128]{1,0:T(8,128)S(1)} %bitcast.5, f32[800,256]{1,0:T(8,128)S(1)} %get-tuple-element.41.mid_ref, bf16[3,1024,256]{2,1,0:T(8,128)(2,1)S(1)} %get-tuple-element.42.weight_ref, f32[8,256]{1,0:T(8,128)S(1)} %get-tuple-element.26.rows_ref.rest_4_, ...), custom_call_target="tpu_custom_call" | custom-call | flops 1000000000 | bytes 4000000 | tf_op jit(solution)/shard_map/second/pallas_call | solution.py:552
  37.6 0.6 collective-permute-start.7
  38.2 0.6 collective-permute-start.8
  38.8 3.3 %collective-permute-start.9 = (bf16[64,1024]{1,0:T(8,128)(2,1)S(1)}, bf16[64,1024]{1,0:T(8,128)(2,1)S(1)}, u32[]{:S(2)}, u32[]{:S(2)}) collective-permute-start(bf16[64,1024]{1,0:T(8,128)(2,1)S(1)} %get-tuple-element.45.refs_0_), channel_id=1, source_target_pairs={{0,24},{8,16},{16,8},{24,0},{1,25},{9,17},{17,9},{25,1},{2,26},{10... | collective-permute-start | bytes 393224 | tf_op jit(solution)/shard_map/ppermute | solution.py:668
  42.0 0.0 copy-done.3
  42.0 1.9 %turn.1.weight_ref = bf16[1024,768]{1,0:T(8,128)(2,1)S(1)} custom-call(bf16[3,256,1024]{2,1,0:T(8,128)(2,1)S(1)} %copy-done.3), custom_call_target="tpu_custom_call" | custom-call | flops 1610612736 | bytes 6000000 | tf_op jit(solution)/shard_map/turn/pallas_call | solution.py:552
  44.0 0.5 collective-permute-done.7.refs_1_
  44.5 6.4 %collective-permute-done.8.refs_2_ = bf16[64,1024]{1,0:T(8,128)(2,1)S(1)} collective-permute-done((bf16[64,1024]{1,0:T(8,128)(2,1)S(1)}, bf16[64,1024]{1,0:T(8,128)(2,1)S(1)}, u32[]{:S(2)}, u32[]{:S(2)}) %collective-permute-start.8) | collective-permute-done | bytes 131104 | tf_op jit(solution)/shard_map/ppermute | solution.py:668
  50.9 0.0 collective-permute-done.9.refs_3_
  50.9 1.4 %attend.1 = (bf16[64,256]{1,0:T(8,128)(2,1)S(1)}, bf16[64,256]{1,0:T(8,128)(2,1)S(1)}, bf16[64,256]{1,0:T(8,128)(2,1)S(1)}, bf16[64,256]{1,0:T(8,128)(2,1)S(1)}) custom-call(f32[8,256]{1,0:T(8,128)S(1)} %get-tuple-element.44.keys_ref, bf16[1024,768]{1,0:T(8,128)(2,1)S(1)} %turn.1.weight_ref, bf16[64,1024]{1,0:T(8,128)(2,1)S(1)} %get-tuple-element.45.refs_0_, ...), custom_call_target="tpu_custom_call" | custom-call | flops 1000000000 | bytes 3000000 | tf_op jit(solution)/shard_map/attend/pallas_call | solution.py:552
  52.3 2.2 %collective-permute-start.10 = (bf16[64,256]{1,0:T(8,128)(2,1)S(1)}, bf16[64,256]{1,0:T(8,128)(2,1)S(1)}, u32[]{:S(2)}, u32[]{:S(2)}) collective-permute-start(bf16[64,256]{1,0:T(8,128)(2,1)S(1)} %get-tuple-element.47), channel_id=1, source_target_pairs={{0,8},{8,0},{16,24},{24,16},{1,9},{9,1},{17,25},{25,17},{2,10},{10... | collective-permute-start | bytes 98312 | tf_op jit(solution)/shard_map/ppermute | solution.py:676
  54.4 0.1 collective-permute-start.11
  54.5 2.3 %collective-permute-start.12 = (bf16[64,256]{1,0:T(8,128)(2,1)S(1)}, bf16[64,256]{1,0:T(8,128)(2,1)S(1)}, u32[]{:S(2)}, u32[]{:S(2)}) collective-permute-start(bf16[64,256]{1,0:T(8,128)(2,1)S(1)} %get-tuple-element.49), channel_id=1, source_target_pairs={{0,24},{8,16},{16,8},{24,0},{1,25},{9,17},{17,9},{25,1},{2,26},{10... | collective-permute-start | bytes 98312 | tf_op jit(solution)/shard_map/ppermute | solution.py:676
  56.9 0.0 collective-permute-done.10.refs_1_
  56.9 2.4 %collective-permute-done.11.refs_2_ = bf16[64,256]{1,0:T(8,128)(2,1)S(1)} collective-permute-done((bf16[64,256]{1,0:T(8,128)(2,1)S(1)}, bf16[64,256]{1,0:T(8,128)(2,1)S(1)}, u32[]{:S(2)}, u32[]{:S(2)}) %collective-permute-start.11) | collective-permute-done | bytes 32800 | tf_op jit(solution)/shard_map/ppermute | solution.py:676
  59.3 1.0 %collective-permute-done.12.refs_3_ = bf16[64,256]{1,0:T(8,128)(2,1)S(1)} collective-permute-done((bf16[64,256]{1,0:T(8,128)(2,1)S(1)}, bf16[64,256]{1,0:T(8,128)(2,1)S(1)}, u32[]{:S(2)}, u32[]{:S(2)}) %collective-permute-start.12) | collective-permute-done | bytes 32800 | tf_op jit(solution)/shard_map/ppermute | solution.py:676
  60.3 0.7 %place.1 = bf16[1,64,1024]{2,1,0:T(8,128)(2,1)} custom-call(f32[8,256]{1,0:T(8,128)S(1)} %get-tuple-element.36.rest_2_.keep_ref, bf16[64,256]{1,0:T(8,128)(2,1)S(1)} %get-tuple-element.46.refs_0_, bf16[64,256]{1,0:T(8,128)(2,1)S(1)} %collective-permute-done.10.refs_1_, bf16[64,256]{1,0:T(8,128)(2,1)S(1)} %collective-permute-done.11.refs_2_, ...), custom_call_target="tpu_custom_call" | custom-call | bytes 300000 | tf_op jit(solution)/shard_map/place/pallas_call | solution.py:552
Async XLA Ops:
  0.6 0.9 %copy-start = (bf16[8,8,4,256]{3,2,1,0:T(4,128)(2,1)S(1)}, bf16[8,8,4,256]{3,2,1,0:T(4,128)(2,1)}, u32[]{:S(2)}) copy-start(bf16[8,8,4,256]{3,2,1,0:T(4,128)(2,1)} %feat_ref.1) | copy-start | bytes 393220
  1.5 0.7 %copy-start.2 = (s32[4,1,4]{2,1,0:T(1,128)S(1)}, s32[4,1,4]{2,1,0:T(1,128)}, u32[]{:S(2)}) copy-start(s32[4,1,4]{2,1,0:T(1,128)} %occ_ref.1) | copy-start | bytes 196
  3.7 9.0 %collective-permute-start.2 = (bf16[16,256]{1,0:T(8,128)(2,1)S(1)}, bf16[16,256]{1,0:T(8,128)(2,1)S(1)}, u32[]{:S(2)}, u32[]{:S(2)}) collective-permute-start(bf16[16,256]{1,0:T(8,128)(2,1)S(1)} %get-tuple-element.30.rest_0_), channel_id=1, source_target_pairs={{0,16},{8,24},{16,0},{24,8},{1,17},{9,25},{17,1},{25,9},{2,18},{10... | collective-permute-start | bytes 24584 | tf_op jit(solution)/shard_map/ppermute | solution.py:599
  7.8 4.9 %collective-permute-start = (bf16[80,256]{1,0:T(8,128)(2,1)S(1)}, bf16[80,256]{1,0:T(8,128)(2,1)S(1)}, u32[]{:S(2)}, u32[]{:S(2)}) collective-permute-start(bf16[80,256]{1,0:T(8,128)(2,1)S(1)} %get-tuple-element.28), channel_id=1, source_target_pairs={{0,8},{8,0},{16,24},{24,16},{1,9},{9,1},{17,25},{25,17},{2,10},{10... | collective-permute-start | bytes 122888 | tf_op jit(solution)/shard_map/ppermute | solution.py:594
  9.4 5.8 %collective-permute-start.1 = (bf16[80,256]{1,0:T(8,128)(2,1)S(1)}, bf16[80,256]{1,0:T(8,128)(2,1)S(1)}, u32[]{:S(2)}, u32[]{:S(2)}) collective-permute-start(bf16[80,256]{1,0:T(8,128)(2,1)S(1)} %get-tuple-element.29), channel_id=1, source_target_pairs={{0,24},{8,16},{16,8},{24,0},{1,25},{9,17},{17,9},{25,1},{2,26},{10... | collective-permute-start | bytes 122888 | tf_op jit(solution)/shard_map/ppermute | solution.py:595
  10.1 0.9 %copy-start.1 = (bf16[2,32,864]{2,1,0:T(8,128)(2,1)S(1)}, bf16[2,32,864]{2,1,0:T(8,128)(2,1)}, u32[]{:S(2)}) copy-start(bf16[2,32,864]{2,1,0:T(8,128)(2,1)} %weight_ref.2) | copy-start | bytes 331780
  15.4 1.3 %collective-permute-start.3 = (bf16[112,256]{1,0:T(8,128)(2,1)S(1)}, bf16[112,256]{1,0:T(8,128)(2,1)S(1)}, u32[]{:S(2)}, u32[]{:S(2)}) collective-permute-start(bf16[112,256]{1,0:T(8,128)(2,1)S(1)} %get-tuple-element.32.own_ref), channel_id=1, source_target_pairs={{0,1},{1,0},{2,3},{3,2},{4,5},{5,4},{6,7},{7,6},{8,9},{9,8},{10,11... | collective-permute-start | bytes 172040 | tf_op jit(solution)/shard_map/ppermute | solution.py:617
  16.9 6.7 %collective-permute-start.5 = (bf16[144,256]{1,0:T(8,128)(2,1)S(1)}, bf16[144,256]{1,0:T(8,128)(2,1)S(1)}, u32[]{:S(2)}, u32[]{:S(2)}) collective-permute-start(bf16[144,256]{1,0:T(8,128)(2,1)S(1)} %get-tuple-element.34), channel_id=1, source_target_pairs={{0,4},{4,0},{1,5},{5,1},{2,6},{6,2},{3,7},{7,3},{8,12},{12,8},{9,1... | collective-permute-start | bytes 221192 | tf_op jit(solution)/shard_map/ppermute | solution.py:635
  18.5 5.2 %collective-permute-start.4 = (bf16[112,256]{1,0:T(8,128)(2,1)S(1)}, bf16[112,256]{1,0:T(8,128)(2,1)S(1)}, u32[]{:S(2)}, u32[]{:S(2)}) collective-permute-start(bf16[112,256]{1,0:T(8,128)(2,1)S(1)} %get-tuple-element.33.own_ref), channel_id=1, source_target_pairs={{0,3},{1,2},{2,1},{3,0},{4,7},{5,6},{6,5},{7,4},{8,11},{9,10},{10,... | collective-permute-start | bytes 172040 | tf_op jit(solution)/shard_map/ppermute | solution.py:631
  19.5 4.2 %collective-permute-start.6 = (bf16[48,256]{1,0:T(8,128)(2,1)S(1)}, bf16[48,256]{1,0:T(8,128)(2,1)S(1)}, u32[]{:S(2)}, u32[]{:S(2)}) collective-permute-start(bf16[48,256]{1,0:T(8,128)(2,1)S(1)} %get-tuple-element.35), channel_id=1, source_target_pairs={{0,7},{1,6},{2,5},{3,4},{4,3},{5,2},{6,1},{7,0},{8,15},{9,14},{10,... | collective-permute-start | bytes 73736 | tf_op jit(solution)/shard_map/ppermute | solution.py:639
  35.5 6.5 %copy-start.3 = (bf16[3,256,1024]{2,1,0:T(8,128)(2,1)S(1)}, bf16[3,256,1024]{2,1,0:T(8,128)(2,1)}, u32[]{:S(2)}) copy-start(bf16[3,256,1024]{2,1,0:T(8,128)(2,1)} %weight_ref.3) | copy-start | bytes 4718596
  37.6 6.8 %collective-permute-start.7 = (bf16[64,1024]{1,0:T(8,128)(2,1)S(1)}, bf16[64,1024]{1,0:T(8,128)(2,1)S(1)}, u32[]{:S(2)}, u32[]{:S(2)}) collective-permute-start(bf16[64,1024]{1,0:T(8,128)(2,1)S(1)} %get-tuple-element.45.refs_0_), channel_id=1, source_target_pairs={{0,8},{8,0},{16,24},{24,16},{1,9},{9,1},{17,25},{25,17},{2,10},{10... | collective-permute-start | bytes 393224 | tf_op jit(solution)/shard_map/ppermute | solution.py:668
  38.2 12.7 %collective-permute-start.8 = (bf16[64,1024]{1,0:T(8,128)(2,1)S(1)}, bf16[64,1024]{1,0:T(8,128)(2,1)S(1)}, u32[]{:S(2)}, u32[]{:S(2)}) collective-permute-start(bf16[64,1024]{1,0:T(8,128)(2,1)S(1)} %get-tuple-element.45.refs_0_), channel_id=1, source_target_pairs={{0,16},{8,24},{16,0},{24,8},{1,17},{9,25},{17,1},{25,9},{2,18},{10... | collective-permute-start | bytes 393224 | tf_op jit(solution)/shard_map/ppermute | solution.py:668
  38.8 12.1 %collective-permute-start.9 = (bf16[64,1024]{1,0:T(8,128)(2,1)S(1)}, bf16[64,1024]{1,0:T(8,128)(2,1)S(1)}, u32[]{:S(2)}, u32[]{:S(2)}) collective-permute-start(bf16[64,1024]{1,0:T(8,128)(2,1)S(1)} %get-tuple-element.45.refs_0_), channel_id=1, source_target_pairs={{0,24},{8,16},{16,8},{24,0},{1,25},{9,17},{17,9},{25,1},{2,26},{10... | collective-permute-start | bytes 393224 | tf_op jit(solution)/shard_map/ppermute | solution.py:668
  52.3 4.6 %collective-permute-start.10 = (bf16[64,256]{1,0:T(8,128)(2,1)S(1)}, bf16[64,256]{1,0:T(8,128)(2,1)S(1)}, u32[]{:S(2)}, u32[]{:S(2)}) collective-permute-start(bf16[64,256]{1,0:T(8,128)(2,1)S(1)} %get-tuple-element.47), channel_id=1, source_target_pairs={{0,8},{8,0},{16,24},{24,16},{1,9},{9,1},{17,25},{25,17},{2,10},{10... | collective-permute-start | bytes 98312 | tf_op jit(solution)/shard_map/ppermute | solution.py:676
  54.4 4.8 %collective-permute-start.11 = (bf16[64,256]{1,0:T(8,128)(2,1)S(1)}, bf16[64,256]{1,0:T(8,128)(2,1)S(1)}, u32[]{:S(2)}, u32[]{:S(2)}) collective-permute-start(bf16[64,256]{1,0:T(8,128)(2,1)S(1)} %get-tuple-element.48), channel_id=1, source_target_pairs={{0,16},{8,24},{16,0},{24,8},{1,17},{9,25},{17,1},{25,9},{2,18},{10... | collective-permute-start | bytes 98312 | tf_op jit(solution)/shard_map/ppermute | solution.py:676
  54.5 5.7 %collective-permute-start.12 = (bf16[64,256]{1,0:T(8,128)(2,1)S(1)}, bf16[64,256]{1,0:T(8,128)(2,1)S(1)}, u32[]{:S(2)}, u32[]{:S(2)}) collective-permute-start(bf16[64,256]{1,0:T(8,128)(2,1)S(1)} %get-tuple-element.49), channel_id=1, source_target_pairs={{0,24},{8,16},{16,8},{24,0},{1,25},{9,17},{17,9},{25,1},{2,26},{10... | collective-permute-start | bytes 98312 | tf_op jit(solution)/shard_map/ppermute | solution.py:676

commit v4 on v3

--- a/solution.py
+++ b/solution.py
@@ -186,25 +186,27 @@
                tail_ref, rows_ref=None):
     sx, sy, sb, lanes = feat_ref.shape
     me = lax.axis_index("gx")
-    row = iota((8, lanes), 0)
-    keep = jnp.zeros((8, lanes), F32)
-    count = 0.0
-    for b in range(sb):
-        there = occ_ref[me, 0, b].astype(F32)
-        keep = jnp.where(row == b, there, keep)
-        count = count + there
-    count = count * float(sx * sy * BR * GW)
+    bricks = [occ_ref[x].astype(F32) for x in range(members)]
+
+    def row_of(x):
+        return sum(jnp.where(x == i, v, 0.0) for i, v in enumerate(bricks))
+
+    mine = jnp.broadcast_to(row_of(me), (8, sb))
+    keep = jnp.where(iota((8, sb), 0) == iota((8, sb), 1), mine, 0.0)
+    keep = jnp.broadcast_to(jnp.sum(keep, axis=1, keepdims=True), (8, lanes))
+    count = jnp.sum(keep, axis=0, keepdims=True) * float(sx * sy * BR * GW)
     keep_ref[...] = keep
     seq = keys_ref.shape[1]
-    lane = iota(keys_ref.shape, 1)
-    keys = jnp.zeros(keys_ref.shape, F32)
+    lane = iota((1, seq), 1)
+    keys = jnp.zeros((1, seq), F32)
     for k in range(members):
+        there = row_of(me ^ k)
         for b in range(sb):
-            there = occ_ref[me ^ k, 0, b].astype(F32)
             keys = jnp.where(
-                (lane // (seq // members) == k) & (lane % (2 * sb) // 2 == b), there, keys
+                (lane // (seq // members) == k) & (lane % (2 * sb) // 2 == b),
+                there[:, b : b + 1], keys,
             )
-    keys_ref[...] = keys
+    keys_ref[...] = jnp.broadcast_to(keys, keys_ref.shape)
     field = feat_ref[...].astype(F32)
     wide = jnp.concatenate([field, jnp.zeros((sx, sy, 8 - sb, lanes), F32)], axis=2)
     wide = wide.reshape(sx * sy, 8, lanes)
@@ -231,7 +233,7 @@
         rows_ref[...] = jnp.broadcast_to(to_row(mine)[0:1], rows_ref.shape)
 
 
-def line_kernel(narrow, sy, sb, rows_ref, coded_ref, first_ref, second_ref, *rest):
+def line_kernel(narrow, sy, sb, _, coded_ref, first_ref, second_ref, *rest):
     tails, (ext_ref, out_ref, buf) = rest[:-3], rest[-3:]
     lanes = coded_ref.shape[1]
     sx = coded_ref.shape[0] // (sy * 8)
@@ -308,38 +310,39 @@
 
 
 def band_kernel(weight_ref, *rest):
-    out_ref, rows_ref = rest[-2:] if len(rest) == 2 else rest[1:3]
+    pars, (out_ref, more_ref) = rest[:-2], rest[-2:]
     lanes = C * BR
     spread = onehot(iota((C, lanes), 0) == iota((C, lanes), 1) // BR)
-    column = onehot(iota((lanes, C), 0) // BR == iota((lanes, C), 1))
     turned = jnp.transpose(weight_ref[0].astype(F32)).astype(BF16)
-    wide = jnp.dot(turned, spread, preferred_element_type=F32).astype(BF16)
-    row = iota((lanes, lanes), 0)
-    zi, zo = row % BR, iota((lanes, lanes), 1) % BR
+    wide = jnp.dot(turned, spread, preferred_element_type=F32)
+    full = (C, BR, lanes)
+    zi, zo = iota((1, BR, lanes), 1), iota((1, BR, lanes), 2) % BR
+
+    def rows(value):
+        return jnp.broadcast_to(value[:, None, :], full)
+
     for ex in range(3):
-        mixed = jnp.zeros((lanes, lanes), F32)
+        mixed = jnp.zeros(full, F32)
         for ey in range(3):
-            terms = []
-            for ez in range(3):
-                q = (ex * 3 + ey) * 3 + ez
-                terms.append(
-                    jnp.dot(column, wide[q * C : (q + 1) * C], preferred_element_type=F32)
-                )
-            inner = jnp.where(zi == zo - 1, terms[0], 0.0)
-            inner = jnp.where(zi == zo, terms[1], inner)
-            inner = jnp.where(zi == zo + 1, terms[2], inner)
-            outer = jnp.where((zi == BR - 1) & (zo == 0), terms[0], 0.0)
-            outer = jnp.where((zi == 0) & (zo == BR - 1), terms[2], outer)
-            mixed = mixed + (pltpu.roll(outer, 2 * ey, 0) if ey else outer)
-            out_ref[ex, ey * lanes : (ey + 1) * lanes, :] = inner.astype(BF16)
-        out_ref[ex, 3 * lanes : 4 * lanes, :] = mixed.astype(BF16)
-    if len(rest) > 2:
+            q = (ex * 3 + ey) * 3
+            terms = [wide[(q + e) * C : (q + e + 1) * C] for e in range(3)]
+            inner = jnp.where(zi == zo - 1, rows(terms[0]), 0.0)
+            inner = jnp.where(zi == zo, rows(terms[1]), inner)
+            inner = jnp.where(zi == zo + 1, rows(terms[2]), inner)
+            before = pltpu.roll(terms[0], 1, 0) if ey else terms[0]
+            low = 2 * ey - 1 if ey else BR - 1
+            mixed = jnp.where((zi == low) & (zo == 0), rows(before), mixed)
+            mixed = jnp.where((zi == 2 * ey) & (zo == BR - 1), rows(terms[2]), mixed)
+            out_ref[ex, ey * lanes : (ey + 1) * lanes, :] = (
+                inner.reshape(C * BR, lanes).astype(BF16)
+            )
+        out_ref[ex, 3 * lanes : 4 * lanes, :] = mixed.reshape(C * BR, lanes).astype(BF16)
+    if pars:
         pick = onehot(iota((C, lanes), 0) == iota((C, lanes), 1) // BR, F32)
-        rows_ref[...] = jnp.zeros(rows_ref.shape, F32)
-        rows_ref[0 : rest[0].shape[0], :] = exact_dot(rest[0][...], pick)
-        rest[3][...] = weight_ref[1:2]
+        more_ref[...] = jnp.zeros(more_ref.shape, F32)
+        more_ref[0 : pars[0].shape[0], :] = exact_dot(pars[0][...], pick)
     else:
-        rows_ref[...] = jnp.zeros(rows_ref.shape, F32)
+        more_ref[...] = weight_ref[1:2]
 
 
 def turn_kernel(weight_ref, out_ref):
@@ -359,7 +362,7 @@
     stats_ref = None
     if not narrow:
         stats_ref, rest = rest[0], rest[1:]
-    keep_ref, weight_ref, rows_ref, _, mid_ref, out_ref, buf, lhs, msk = rest
+    keep_ref, weight_ref, rows_ref, mid_ref, out_ref, buf, lhs, msk = rest
     lanes = ext_ref.shape[1]
     ex = ext_ref.shape[0] // (sy * 8)
     ey = sy + 4
@@ -545,7 +548,6 @@
 
 
 VM = pl.BlockSpec(memory_space=pltpu.VMEM)
-SM = pl.BlockSpec(memory_space=pltpu.SMEM)
 
 
 def call(kernel, name, specs, out, args, scratch=(), flops=0, nbytes=0, mib=16):
@@ -583,7 +585,7 @@
 
     slab = sy * 8 + TAIL
     keep, keys, coded, first, second, tail, *stats = call(
-        functools.partial(pre_kernel, nx), "pre", (SM, VM),
+        functools.partial(pre_kernel, nx), "pre", (VM, VM),
         [shape(8, lanes, dtype=F32), shape(8, own * nx, dtype=F32),
          shape(sx * sy * 8, lanes), shape(slab, lanes), shape(slab, lanes), shape(TAIL, lanes)]
         + row_shape,
@@ -600,18 +602,18 @@
     band = shape(3, 4 * lanes, lanes)
     pars = jnp.concatenate([norm_gain, norm_shift, conv_bias], axis=0)
     later = shape(1, *conv_weight.shape[1:])
-    band0, rows, later = call(
-        band_kernel, "band0", (VM,) * 2, [band, shape(8, lanes, dtype=F32), later],
-        (conv_weight, pars), nbytes=8 * 10**6,
-    )
-    band1, mark = call(
-        band_kernel, "band1", (VM,), [band, shape(8, 128, dtype=F32)], (later,), nbytes=8 * 10**6,
+    band0, later = call(
+        band_kernel, "band0", (VM,), [band, later], (conv_weight,), nbytes=8 * 10**6,
+    )
+    band1, rows = call(
+        band_kernel, "band1", (VM,) * 2, [band, shape(8, lanes, dtype=F32)], (later, pars),
+        nbytes=8 * 10**6,
     )
     count = ex * sy
     ext, mine = call(
         functools.partial(line_kernel, narrow, sy, sb), "line", (VM,) * (4 + len(tails)),
         [shape(count * 8, lanes), shape(count + TAIL, lanes)],
-        (rows, coded, *got, *tails),
+        (later, coded, *got, *tails),
         [pltpu.VMEM((lanes // 128, count * 8, 128), F32)], nbytes=10**6,
     )
     core = lax.ppermute(mine, "gz", list(pairing(nz, False, False).items()))
@@ -648,9 +650,9 @@
     size = (sx + 2) * oy * 8
     mid, mine = call(
         functools.partial(first_kernel, narrow, faces, sy, sb), "first",
-        (VM,) * (8 + 2 * faces + len(stats)),
+        (VM,) * (7 + 2 * faces + len(stats)),
         [shape(size, lanes, dtype=F32), shape(devices, 128, dtype=F32)],
-        (ext, own_tail, core, zgot, *ygot, *stats, keep, band0, rows, mark),
+        (ext, own_tail, core, zgot, *ygot, *stats, keep, band0, rows),
         [pltpu.VMEM((lanes // 128, ex * ey * 8, 128), F32),
          pltpu.VMEM((ex * oy * 8, 4 * lanes), BF16),
          pltpu.VMEM((ex * ey * 8, 128), F32)],
@@ -665,8 +667,11 @@
         flops=10**9, nbytes=4 * 10**6,
     )
     swaps = [[(i, i ^ k) for i in range(nx)] for k in range(nx)]
-    blocks = {k: lax.ppermute(tokens, "gx", swaps[k]) for k in range(nx - 1, 0, -1)}
-    blocks = [tokens] + [blocks[k] for k in range(1, nx)]
+    blocks = {0: tokens}
+    for k in sorted(range(1, nx), key=lambda k: (bin(k).count("1"), -k)):
+        low = k & -k
+        blocks[k] = lax.ppermute(blocks[k ^ low], "gx", swaps[low])
+    blocks = [blocks[k] for k in range(nx)]
     outs = call(
         functools.partial(attend_kernel, nx), "attend", (VM,) * (2 + nx),
         [shape(own, cols)] * nx, (keys, turned, *blocks),

time: 61.2 us -> 59.4 us (0.971)
  starting transfers between devices: 18 us -> 14.6 us
  waiting for transfers between devices: 15.8 us -> 18.2 us
  Pallas kernels: 14.3 us -> 13.1 us
    ppermute x3, waiting for transfers between devices: 6.97 us -> 11.2 us  [body(): blocks[k] = lax.ppermute(blocks[k ^ low], 'gx', swaps[low])]
    ppermute x1, starting transfers between devices: 4.11 us -> 0.12 us  [body(): tails.append(lax.ppermute(tail, 'gx', [(i, i ^ 2) for i in range(nx)]))]
    ppermute x3, starting transfers between devices: 4.39 us -> 1.14 us  [body(): blocks[k] = lax.ppermute(blocks[k ^ low], 'gx', swaps[low])]
    ppermute x1, starting transfers between devices: 0.01 us -> 2.47 us  [body(): lax.ppermute(second, 'gx', list(pairing(nx, True, narrow).items()))]
    ppermute x1, waiting for transfers between devices: 2.47 us -> 0.01 us  [body(): lax.ppermute(second, 'gx', list(pairing(nx, True, narrow).items()))]
    ppermute x1, waiting for transfers between devices: 0.01 us -> 2.16 us  [body(): tails.append(lax.ppermute(tail, 'gx', [(i, i ^ 2) for i in range(nx)]))]
    ppermute x1, starting transfers between devices: 1.58 us -> 3.09 us  [body(): lax.ppermute(first, 'gx', list(pairing(nx, False, False).items()))]
    pallas_call x10, Pallas kernels: 14.3 us -> 13.1 us  [call(): pl.pallas_call(kernel, out_shape=out, in_specs=list(specs), out_specs=jax...]
  transfers between devices with their start and end apart: 13 -> 13, of which waited for: 7 -> 7; matrix products, arithmetic and copies ran while one was open for 1% -> 1% of each run, Pallas kernels for 9% -> 8%
where the time goes in v4:
time: 59.4 us; the launch traced here: 59.1 us
  waiting for transfers between devices  18.2 us (31%)
  starting transfers between devices  14.6 us (25%)
  Pallas kernels  13.1 us (22%)
  blocking collectives  9.3 us (16%)
  local copies, waits for them, and re-layouts  2.48 us (4%)
  other arithmetic  0.72 us (1%)
  between operations  0.71 us (1%)
    pallas_call x10, Pallas kernels, call(): pl.pallas_call(kernel, out_shape=out, in_specs=list(specs), out_specs=jax...  13.1 us
    ppermute x3, waiting for transfers between devices, body(): blocks[k] = lax.ppermute(blocks[k ^ low], 'gx', swaps[low])  11.2 us
    all_to_all x1, blocking collectives, body(): stats = lax.all_to_all(mine, ALL, 0, 0, tiled=True)  9.3 us
    ppermute x3, starting transfers between devices, body(): lax.ppermute(outs[k], 'gx', swaps[k])  4.45 us
    ppermute x1, starting transfers between devices, body(): lax.ppermute(first, 'gx', list(pairing(nx, False, False).items()))  3.09 us
    unnamed x8, local copies, waits for them, and re-layouts  2.48 us
    ppermute x1, starting transfers between devices, body(): lax.ppermute(second, 'gx', list(pairing(nx, True, narrow).items()))  2.47 us
    ppermute x3, waiting for transfers between devices, body(): lax.ppermute(outs[k], 'gx', swaps[k])  2.24 us
  transfers between devices with their start and end apart: 13, of which 7 were waited for; matrix products, arithmetic and copies ran while one was open for 1% of the time, Pallas kernels for 8%

profile of v4, /device:TPU:0, one launch (start us, length us, event | category | flops | bytes accessed | tf_op | source)
XLA Modules:
  0.0 59.1 jit_solution(13854952634267861154)
XLA Ops:
  0.6 0.0 copy-start
  0.6 0.9 %copy-done = bf16[8,8,4,256]{3,2,1,0:T(4,128)(2,1)S(1)} copy-done((bf16[8,8,4,256]{3,2,1,0:T(4,128)(2,1)S(1)}, bf16[8,8,4,256]{3,2,1,0:T(4,128)(2,1)}, u32[]{:S(2)}) %copy-start) | copy-done | bytes 131096
  1.5 0.0 copy-start.2
  1.5 0.7 %copy-done.2 = s32[4,1,4]{2,1,0:T(1,128)S(1)} copy-done((s32[4,1,4]{2,1,0:T(1,128)S(1)}, s32[4,1,4]{2,1,0:T(1,128)}, u32[]{:S(2)}) %copy-start.2) | copy-done | bytes 88
  2.2 0.9 %pre.1 = (f32[8,256]{1,0:T(8,128)S(1)}, f32[8,256]{1,0:T(8,128)S(1)}, bf16[512,256]{1,0:T(8,128)(2,1)S(1)}, bf16[80,256]{1,0:T(8,128)(2,1)S(1)}, bf16[80,256]{1,...) custom-call(s32[4,1,4]{2,1,0:T(1,128)S(1)} %copy-done.2, bf16[8,8,4,256]{3,2,1,0:T(4,128)(2,1)S(1)} %copy-done), custom_call_target="tpu_custom_call" | custom-call | bytes 1000000 | tf_op jit(solution)/shard_map/pre/pallas_call | solution.py:554
  3.2 3.1 %collective-permute-start = (bf16[80,256]{1,0:T(8,128)(2,1)S(1)}, bf16[80,256]{1,0:T(8,128)(2,1)S(1)}, u32[]{:S(2)}, u32[]{:S(2)}) collective-permute-start(bf16[80,256]{1,0:T(8,128)(2,1)S(1)} %get-tuple-element.27), channel_id=1, source_target_pairs={{0,8},{8,0},{16,24},{24,16},{1,9},{9,1},{17,25},{25,17},{2,10},{10... | collective-permute-start | bytes 122888 | tf_op jit(solution)/shard_map/ppermute | solution.py:596
  6.3 2.5 %collective-permute-start.1 = (bf16[80,256]{1,0:T(8,128)(2,1)S(1)}, bf16[80,256]{1,0:T(8,128)(2,1)S(1)}, u32[]{:S(2)}, u32[]{:S(2)}) collective-permute-start(bf16[80,256]{1,0:T(8,128)(2,1)S(1)} %get-tuple-element.28), channel_id=1, source_target_pairs={{0,24},{8,16},{16,8},{24,0},{1,25},{9,17},{17,9},{25,1},{2,26},{10... | collective-permute-start | bytes 122888 | tf_op jit(solution)/shard_map/ppermute | solution.py:597
  8.7 0.1 collective-permute-start.2
  8.8 0.0 copy-start.1
  8.9 0.9 %copy-done.1 = bf16[2,32,864]{2,1,0:T(8,128)(2,1)S(1)} copy-done((bf16[2,32,864]{2,1,0:T(8,128)(2,1)S(1)}, bf16[2,32,864]{2,1,0:T(8,128)(2,1)}, u32[]{:S(2)}) %copy-start.1) | copy-done | bytes 110616
  9.7 1.4 %band0.1 = (bf16[3,1024,256]{2,1,0:T(8,128)(2,1)S(1)}, bf16[1,32,864]{2,1,0:T(8,128)(2,1)S(1)}) custom-call(bf16[2,32,864]{2,1,0:T(8,128)(2,1)S(1)} %copy-done.1), custom_call_target="tpu_custom_call" | custom-call | bytes 8000000 | tf_op jit(solution)/shard_map/band0/pallas_call | solution.py:554
  11.1 2.2 %collective-permute-done.2.rest_1_ = bf16[16,256]{1,0:T(8,128)(2,1)S(1)} collective-permute-done((bf16[16,256]{1,0:T(8,128)(2,1)S(1)}, bf16[16,256]{1,0:T(8,128)(2,1)S(1)}, u32[]{:S(2)}, u32[]{:S(2)}) %collective-permute-start.2) | collective-permute-done | bytes 8224 | tf_op jit(solution)/shard_map/ppermute | solution.py:601
  13.3 0.0 collective-permute-done.first_ref
  13.3 0.0 collective-permute-done.1.second_ref
  13.3 0.2 line.1
  13.5 0.1 collective-permute-start.3
  13.5 1.2 %collective-permute-done.3.other_ref.core_ref = bf16[112,256]{1,0:T(8,128)(2,1)S(1)} collective-permute-done((bf16[112,256]{1,0:T(8,128)(2,1)S(1)}, bf16[112,256]{1,0:T(8,128)(2,1)S(1)}, u32[]{:S(2)}, u32[]{:S(2)}) %collective-permute-start.3) | collective-permute-done | bytes 57376 | tf_op jit(solution)/shard_map/ppermute | solution.py:619
  14.8 0.2 chip.1
  15.0 1.6 %collective-permute-start.5 = (bf16[144,256]{1,0:T(8,128)(2,1)S(1)}, bf16[144,256]{1,0:T(8,128)(2,1)S(1)}, u32[]{:S(2)}, u32[]{:S(2)}) collective-permute-start(bf16[144,256]{1,0:T(8,128)(2,1)S(1)} %get-tuple-element.33), channel_id=1, source_target_pairs={{0,4},{4,0},{1,5},{5,1},{2,6},{6,2},{3,7},{7,3},{8,12},{12,8},{9,1... | collective-permute-start | bytes 221192 | tf_op jit(solution)/shard_map/ppermute | solution.py:637
  16.5 1.0 %collective-permute-start.4 = (bf16[112,256]{1,0:T(8,128)(2,1)S(1)}, bf16[112,256]{1,0:T(8,128)(2,1)S(1)}, u32[]{:S(2)}, u32[]{:S(2)}) collective-permute-start(bf16[112,256]{1,0:T(8,128)(2,1)S(1)} %get-tuple-element.32.own_ref), channel_id=1, source_target_pairs={{0,3},{1,2},{2,1},{3,0},{4,7},{5,6},{6,5},{7,4},{8,11},{9,10},{10,... | collective-permute-start | bytes 172040 | tf_op jit(solution)/shard_map/ppermute | solution.py:633
  17.5 0.7 %collective-permute-start.6 = (bf16[48,256]{1,0:T(8,128)(2,1)S(1)}, bf16[48,256]{1,0:T(8,128)(2,1)S(1)}, u32[]{:S(2)}, u32[]{:S(2)}) collective-permute-start(bf16[48,256]{1,0:T(8,128)(2,1)S(1)} %get-tuple-element.34), channel_id=1, source_target_pairs={{0,7},{1,6},{2,5},{3,4},{4,3},{5,2},{6,1},{7,0},{8,15},{9,14},{10,... | collective-permute-start | bytes 73736 | tf_op jit(solution)/shard_map/ppermute | solution.py:641
  18.3 0.7 %pad_maximum_fusion.rest_0_ = f32[6,32]{1,0:T(8,128)S(1)} fusion(f32[2,32]{1,0:T(2,128)} %param.12, f32[2,32]{1,0:T(2,128)} %param.10, f32[2,32]{1,0:T(2,128)} %param.9), kind=kLoop, calls=%fused_computation | loop fusion | flops 384 | bytes 1536 | tf_op jit(solution)/shard_map/concatenate | solution.py:603
  19.0 1.4 %band1.1 = (bf16[3,1024,256]{2,1,0:T(8,128)(2,1)S(1)}, f32[8,256]{1,0:T(8,128)S(1)}) custom-call(bf16[1,32,864]{2,1,0:T(8,128)(2,1)S(1)} %get-tuple-element.25._.weight_ref, f32[6,32]{1,0:T(8,128)S(1)} %pad_maximum_fusion.rest_0_), custom_call_target="tpu_custom_call" | custom-call | bytes 8000000 | tf_op jit(solution)/shard_map/band1/pallas_call | solution.py:554
  20.4 1.3 %collective-permute-done.6.rest_1_ = bf16[48,256]{1,0:T(8,128)(2,1)S(1)} collective-permute-done((bf16[48,256]{1,0:T(8,128)(2,1)S(1)}, bf16[48,256]{1,0:T(8,128)(2,1)S(1)}, u32[]{:S(2)}, u32[]{:S(2)}) %collective-permute-start.6) | collective-permute-done | bytes 24608 | tf_op jit(solution)/shard_map/ppermute | solution.py:641
  21.7 0.0 collective-permute-done.4.zface_ref
  21.7 0.0 collective-permute-done.5.rest_0_
  21.7 3.0 %first.1 = (f32[800,256]{1,0:T(8,128)S(1)}, f32[32,128]{1,0:T(8,128)S(1)}) custom-call(bf16[768,256]{1,0:T(8,128)(2,1)S(1)} %get-tuple-element.30.ext_ref, bf16[112,256]{1,0:T(8,128)(2,1)S(1)} %get-tuple-element.32.own_ref, bf16[112,256]{1,0:T(8,128)(2,1)S(1)} %collective-permute-done.3.other_ref.core_ref, ...), custom_call_target="tpu_custom_call" | custom-call | flops 2000000000 | bytes 4000000 | tf_op jit(solution)/shard_map/first/pallas_call | solution.py:554
  24.7 9.3 %all_to_all.11 = f32[32,1,128]{2,1,0:T(1,128)S(1)} all-to-all(f32[32,1,128]{2,1,0:T(1,128)S(1)} %bitcast.4), channel_id=1, replica_groups=mesh['gx'=4,'gy'=2,'gz'=4] {'gx','gy','gz'}, dimensions={0} | all-to-all | bytes 32768 | tf_op jit(solution)/shard_map/all_to_all | solution.py:661
  34.0 0.0 copy-start.3
  34.0 2.2 %second.1 = (bf16[8,8,4,256]{3,2,1,0:T(4,128)(2,1)}, bf16[64,1024]{1,0:T(8,128)(2,1)S(1)}) custom-call(f32[32,128]{1,0:T(8,128)S(1)} %bitcast.5, f32[800,256]{1,0:T(8,128)S(1)} %get-tuple-element.39.mid_ref, bf16[3,1024,256]{2,1,0:T(8,128)(2,1)S(1)} %get-tuple-element.40.weight_ref, f32[8,256]{1,0:T(8,128)S(1)} %get-tuple-element.37.rest_4_.rows_ref, ...), custom_call_target="tpu_custom_call" | custom-call | flops 1000000000 | bytes 4000000 | tf_op jit(solution)/shard_map/second/pallas_call | solution.py:554
  36.1 0.6 collective-permute-start.8
  36.7 0.5 collective-permute-start.7
  37.3 7.7 %collective-permute-done.8.refs_2_ = bf16[64,1024]{1,0:T(8,128)(2,1)S(1)} collective-permute-done((bf16[64,1024]{1,0:T(8,128)(2,1)S(1)}, bf16[64,1024]{1,0:T(8,128)(2,1)S(1)}, u32[]{:S(2)}, u32[]{:S(2)}) %collective-permute-start.8) | collective-permute-done | bytes 131104 | tf_op jit(solution)/shard_map/ppermute | solution.py:673
  45.0 0.0 collective-permute-start.9
  45.0 0.0 copy-done.3
  45.0 1.9 %turn.1.weight_ref = bf16[1024,768]{1,0:T(8,128)(2,1)S(1)} custom-call(bf16[3,256,1024]{2,1,0:T(8,128)(2,1)S(1)} %copy-done.3), custom_call_target="tpu_custom_call" | custom-call | flops 1610612736 | bytes 6000000 | tf_op jit(solution)/shard_map/turn/pallas_call | solution.py:554
  46.9 0.0 collective-permute-done.7.refs_1_
  46.9 3.5 %collective-permute-done.9.refs_3_ = bf16[64,1024]{1,0:T(8,128)(2,1)S(1)} collective-permute-done((bf16[64,1024]{1,0:T(8,128)(2,1)S(1)}, bf16[64,1024]{1,0:T(8,128)(2,1)S(1)}, u32[]{:S(2)}, u32[]{:S(2)}) %collective-permute-start.9) | collective-permute-done | bytes 131104 | tf_op jit(solution)/shard_map/ppermute | solution.py:673
  50.4 1.4 %attend.1 = (bf16[64,256]{1,0:T(8,128)(2,1)S(1)}, bf16[64,256]{1,0:T(8,128)(2,1)S(1)}, bf16[64,256]{1,0:T(8,128)(2,1)S(1)}, bf16[64,256]{1,0:T(8,128)(2,1)S(1)}) custom-call(f32[8,256]{1,0:T(8,128)S(1)} %get-tuple-element.42.keys_ref, bf16[1024,768]{1,0:T(8,128)(2,1)S(1)} %turn.1.weight_ref, bf16[64,1024]{1,0:T(8,128)(2,1)S(1)} %get-tuple-element.43.refs_0_, ...), custom_call_target="tpu_custom_call" | custom-call | flops 1000000000 | bytes 3000000 | tf_op jit(solution)/shard_map/attend/pallas_call | solution.py:554
  51.8 0.3 collective-permute-start.10
  52.1 0.5 collective-permute-start.11
  52.6 3.6 %collective-permute-start.12 = (bf16[64,256]{1,0:T(8,128)(2,1)S(1)}, bf16[64,256]{1,0:T(8,128)(2,1)S(1)}, u32[]{:S(2)}, u32[]{:S(2)}) collective-permute-start(bf16[64,256]{1,0:T(8,128)(2,1)S(1)} %get-tuple-element.47), channel_id=1, source_target_pairs={{0,24},{8,16},{16,8},{24,0},{1,25},{9,17},{17,9},{25,1},{2,26},{10... | collective-permute-start | bytes 98312 | tf_op jit(solution)/shard_map/ppermute | solution.py:681
  56.2 0.0 collective-permute-done.10.refs_1_
  56.2 0.7 %collective-permute-done.11.refs_2_ = bf16[64,256]{1,0:T(8,128)(2,1)S(1)} collective-permute-done((bf16[64,256]{1,0:T(8,128)(2,1)S(1)}, bf16[64,256]{1,0:T(8,128)(2,1)S(1)}, u32[]{:S(2)}, u32[]{:S(2)}) %collective-permute-start.11) | collective-permute-done | bytes 32800 | tf_op jit(solution)/shard_map/ppermute | solution.py:681
  56.9 1.5 %collective-permute-done.12.refs_3_ = bf16[64,256]{1,0:T(8,128)(2,1)S(1)} collective-permute-done((bf16[64,256]{1,0:T(8,128)(2,1)S(1)}, bf16[64,256]{1,0:T(8,128)(2,1)S(1)}, u32[]{:S(2)}, u32[]{:S(2)}) %collective-permute-start.12) | collective-permute-done | bytes 32800 | tf_op jit(solution)/shard_map/ppermute | solution.py:681
  58.5 0.7 %place.1 = bf16[1,64,1024]{2,1,0:T(8,128)(2,1)} custom-call(f32[8,256]{1,0:T(8,128)S(1)} %get-tuple-element.35.rest_2_.keep_ref, bf16[64,256]{1,0:T(8,128)(2,1)S(1)} %get-tuple-element.44.refs_0_, bf16[64,256]{1,0:T(8,128)(2,1)S(1)} %collective-permute-done.10.refs_1_, bf16[64,256]{1,0:T(8,128)(2,1)S(1)} %collective-permute-done.11.refs_2_, ...), custom_call_target="tpu_custom_call" | custom-call | bytes 300000 | tf_op jit(solution)/shard_map/place/pallas_call | solution.py:554
Async XLA Ops:
  0.6 0.9 %copy-start = (bf16[8,8,4,256]{3,2,1,0:T(4,128)(2,1)S(1)}, bf16[8,8,4,256]{3,2,1,0:T(4,128)(2,1)}, u32[]{:S(2)}) copy-start(bf16[8,8,4,256]{3,2,1,0:T(4,128)(2,1)} %feat_ref.1) | copy-start | bytes 393220
  1.5 0.7 %copy-start.2 = (s32[4,1,4]{2,1,0:T(1,128)S(1)}, s32[4,1,4]{2,1,0:T(1,128)}, u32[]{:S(2)}) copy-start(s32[4,1,4]{2,1,0:T(1,128)} %occ_ref.1) | copy-start | bytes 196
  3.2 10.1 %collective-permute-start = (bf16[80,256]{1,0:T(8,128)(2,1)S(1)}, bf16[80,256]{1,0:T(8,128)(2,1)S(1)}, u32[]{:S(2)}, u32[]{:S(2)}) collective-permute-start(bf16[80,256]{1,0:T(8,128)(2,1)S(1)} %get-tuple-element.27), channel_id=1, source_target_pairs={{0,8},{8,0},{16,24},{24,16},{1,9},{9,1},{17,25},{25,17},{2,10},{10... | collective-permute-start | bytes 122888 | tf_op jit(solution)/shard_map/ppermute | solution.py:596
  6.3 7.0 %collective-permute-start.1 = (bf16[80,256]{1,0:T(8,128)(2,1)S(1)}, bf16[80,256]{1,0:T(8,128)(2,1)S(1)}, u32[]{:S(2)}, u32[]{:S(2)}) collective-permute-start(bf16[80,256]{1,0:T(8,128)(2,1)S(1)} %get-tuple-element.28), channel_id=1, source_target_pairs={{0,24},{8,16},{16,8},{24,0},{1,25},{9,17},{17,9},{25,1},{2,26},{10... | collective-permute-start | bytes 122888 | tf_op jit(solution)/shard_map/ppermute | solution.py:597
  8.7 4.5 %collective-permute-start.2 = (bf16[16,256]{1,0:T(8,128)(2,1)S(1)}, bf16[16,256]{1,0:T(8,128)(2,1)S(1)}, u32[]{:S(2)}, u32[]{:S(2)}) collective-permute-start(bf16[16,256]{1,0:T(8,128)(2,1)S(1)} %get-tuple-element.29.rest_0_), channel_id=1, source_target_pairs={{0,16},{8,24},{16,0},{24,8},{1,17},{9,25},{17,1},{25,9},{2,18},{10... | collective-permute-start | bytes 24584 | tf_op jit(solution)/shard_map/ppermute | solution.py:601
  8.8 0.9 %copy-start.1 = (bf16[2,32,864]{2,1,0:T(8,128)(2,1)S(1)}, bf16[2,32,864]{2,1,0:T(8,128)(2,1)}, u32[]{:S(2)}) copy-start(bf16[2,32,864]{2,1,0:T(8,128)(2,1)} %weight_ref.2) | copy-start | bytes 331780
  13.5 1.3 %collective-permute-start.3 = (bf16[112,256]{1,0:T(8,128)(2,1)S(1)}, bf16[112,256]{1,0:T(8,128)(2,1)S(1)}, u32[]{:S(2)}, u32[]{:S(2)}) collective-permute-start(bf16[112,256]{1,0:T(8,128)(2,1)S(1)} %get-tuple-element.31.own_ref), channel_id=1, source_target_pairs={{0,1},{1,0},{2,3},{3,2},{4,5},{5,4},{6,7},{7,6},{8,9},{9,8},{10,11... | collective-permute-start | bytes 172040 | tf_op jit(solution)/shard_map/ppermute | solution.py:619
  15.0 6.7 %collective-permute-start.5 = (bf16[144,256]{1,0:T(8,128)(2,1)S(1)}, bf16[144,256]{1,0:T(8,128)(2,1)S(1)}, u32[]{:S(2)}, u32[]{:S(2)}) collective-permute-start(bf16[144,256]{1,0:T(8,128)(2,1)S(1)} %get-tuple-element.33), channel_id=1, source_target_pairs={{0,4},{4,0},{1,5},{5,1},{2,6},{6,2},{3,7},{7,3},{8,12},{12,8},{9,1... | collective-permute-start | bytes 221192 | tf_op jit(solution)/shard_map/ppermute | solution.py:637
  16.5 5.2 %collective-permute-start.4 = (bf16[112,256]{1,0:T(8,128)(2,1)S(1)}, bf16[112,256]{1,0:T(8,128)(2,1)S(1)}, u32[]{:S(2)}, u32[]{:S(2)}) collective-permute-start(bf16[112,256]{1,0:T(8,128)(2,1)S(1)} %get-tuple-element.32.own_ref), channel_id=1, source_target_pairs={{0,3},{1,2},{2,1},{3,0},{4,7},{5,6},{6,5},{7,4},{8,11},{9,10},{10,... | collective-permute-start | bytes 172040 | tf_op jit(solution)/shard_map/ppermute | solution.py:633
  17.5 4.2 %collective-permute-start.6 = (bf16[48,256]{1,0:T(8,128)(2,1)S(1)}, bf16[48,256]{1,0:T(8,128)(2,1)S(1)}, u32[]{:S(2)}, u32[]{:S(2)}) collective-permute-start(bf16[48,256]{1,0:T(8,128)(2,1)S(1)} %get-tuple-element.34), channel_id=1, source_target_pairs={{0,7},{1,6},{2,5},{3,4},{4,3},{5,2},{6,1},{7,0},{8,15},{9,14},{10,... | collective-permute-start | bytes 73736 | tf_op jit(solution)/shard_map/ppermute | solution.py:641
  34.0 11.0 %copy-start.3 = (bf16[3,256,1024]{2,1,0:T(8,128)(2,1)S(1)}, bf16[3,256,1024]{2,1,0:T(8,128)(2,1)}, u32[]{:S(2)}) copy-start(bf16[3,256,1024]{2,1,0:T(8,128)(2,1)} %weight_ref.3) | copy-start | bytes 4718596
  36.1 8.9 %collective-permute-start.8 = (bf16[64,1024]{1,0:T(8,128)(2,1)S(1)}, bf16[64,1024]{1,0:T(8,128)(2,1)S(1)}, u32[]{:S(2)}, u32[]{:S(2)}) collective-permute-start(bf16[64,1024]{1,0:T(8,128)(2,1)S(1)} %get-tuple-element.43.refs_0_), channel_id=1, source_target_pairs={{0,16},{8,24},{16,0},{24,8},{1,17},{9,25},{17,1},{25,9},{2,18},{10... | collective-permute-start | bytes 393224 | tf_op jit(solution)/shard_map/ppermute | solution.py:673
  36.7 10.2 %collective-permute-start.7 = (bf16[64,1024]{1,0:T(8,128)(2,1)S(1)}, bf16[64,1024]{1,0:T(8,128)(2,1)S(1)}, u32[]{:S(2)}, u32[]{:S(2)}) collective-permute-start(bf16[64,1024]{1,0:T(8,128)(2,1)S(1)} %get-tuple-element.43.refs_0_), channel_id=1, source_target_pairs={{0,8},{8,0},{16,24},{24,16},{1,9},{9,1},{17,25},{25,17},{2,10},{10... | collective-permute-start | bytes 393224 | tf_op jit(solution)/shard_map/ppermute | solution.py:673
  45.0 5.4 %collective-permute-start.9 = (bf16[64,1024]{1,0:T(8,128)(2,1)S(1)}, bf16[64,1024]{1,0:T(8,128)(2,1)S(1)}, u32[]{:S(2)}, u32[]{:S(2)}) collective-permute-start(bf16[64,1024]{1,0:T(8,128)(2,1)S(1)} %collective-permute-done.8.refs_2_), channel_id=1, source_target_pairs={{0,8},{8,0},{16,24},{24,16},{1,9},{9,1},{17,25},{25,17},{2,10},{10... | collective-permute-start | bytes 393224 | tf_op jit(solution)/shard_map/ppermute | solution.py:673
  51.8 4.5 %collective-permute-start.10 = (bf16[64,256]{1,0:T(8,128)(2,1)S(1)}, bf16[64,256]{1,0:T(8,128)(2,1)S(1)}, u32[]{:S(2)}, u32[]{:S(2)}) collective-permute-start(bf16[64,256]{1,0:T(8,128)(2,1)S(1)} %get-tuple-element.45), channel_id=1, source_target_pairs={{0,8},{8,0},{16,24},{24,16},{1,9},{9,1},{17,25},{25,17},{2,10},{10... | collective-permute-start | bytes 98312 | tf_op jit(solution)/shard_map/ppermute | solution.py:681
  52.1 4.8 %collective-permute-start.11 = (bf16[64,256]{1,0:T(8,128)(2,1)S(1)}, bf16[64,256]{1,0:T(8,128)(2,1)S(1)}, u32[]{:S(2)}, u32[]{:S(2)}) collective-permute-start(bf16[64,256]{1,0:T(8,128)(2,1)S(1)} %get-tuple-element.46), channel_id=1, source_target_pairs={{0,16},{8,24},{16,0},{24,8},{1,17},{9,25},{17,1},{25,9},{2,18},{10... | collective-permute-start | bytes 98312 | tf_op jit(solution)/shard_map/ppermute | solution.py:681
  52.6 5.8 %collective-permute-start.12 = (bf16[64,256]{1,0:T(8,128)(2,1)S(1)}, bf16[64,256]{1,0:T(8,128)(2,1)S(1)}, u32[]{:S(2)}, u32[]{:S(2)}) collective-permute-start(bf16[64,256]{1,0:T(8,128)(2,1)S(1)} %get-tuple-element.47), channel_id=1, source_target_pairs={{0,24},{8,16},{16,8},{24,0},{1,25},{9,17},{17,9},{25,1},{2,26},{10... | collective-permute-start | bytes 98312 | tf_op jit(solution)/shard_map/ppermute | solution.py:681

commit v5 on v4

--- a/solution.py
+++ b/solution.py
@@ -186,7 +186,7 @@
                tail_ref, rows_ref=None):
     sx, sy, sb, lanes = feat_ref.shape
     me = lax.axis_index("gx")
-    bricks = [occ_ref[x].astype(F32) for x in range(members)]
+    bricks = [occ_ref[x] for x in range(members)]
 
     def row_of(x):
         return sum(jnp.where(x == i, v, 0.0) for i, v in enumerate(bricks))
@@ -263,9 +263,12 @@
     return (count + 15) // 16 * 16
 
 
-def chip_kernel(sb, sy, ext_ref, own_ref, other_ref, *rest):
+def chip_kernel(sb, sy, pars_ref, ext_ref, own_ref, other_ref, rows_ref, *rest):
     out, (buf, stage) = rest[:-2], rest[-2:]
     lanes = ext_ref.shape[1]
+    pick = onehot(iota((C, lanes), 0) == iota((C, lanes), 1) // BR, F32)
+    rows_ref[...] = jnp.zeros(rows_ref.shape, F32)
+    rows_ref[0 : pars_ref.shape[0], :] = exact_dot(pars_ref[...], pick)
     ex = ext_ref.shape[0] // (sy * 8)
     block = ext_ref[...].astype(F32)
     write_block(buf, 0, block)
@@ -309,8 +312,7 @@
             ref[value.shape[0] : value.shape[0] + TAIL, :] = tail
 
 
-def band_kernel(weight_ref, *rest):
-    pars, (out_ref, more_ref) = rest[:-2], rest[-2:]
+def band_kernel(weight_ref, out_ref, *later):
     lanes = C * BR
     spread = onehot(iota((C, lanes), 0) == iota((C, lanes), 1) // BR)
     turned = jnp.transpose(weight_ref[0].astype(F32)).astype(BF16)
@@ -337,12 +339,8 @@
                 inner.reshape(C * BR, lanes).astype(BF16)
             )
         out_ref[ex, 3 * lanes : 4 * lanes, :] = mixed.reshape(C * BR, lanes).astype(BF16)
-    if pars:
-        pick = onehot(iota((C, lanes), 0) == iota((C, lanes), 1) // BR, F32)
-        more_ref[...] = jnp.zeros(more_ref.shape, F32)
-        more_ref[0 : pars[0].shape[0], :] = exact_dot(pars[0][...], pick)
-    else:
-        more_ref[...] = weight_ref[1:2]
+    if later:
+        later[0][...] = weight_ref[1:2]
 
 
 def turn_kernel(weight_ref, out_ref):
@@ -589,7 +587,7 @@
         [shape(8, lanes, dtype=F32), shape(8, own * nx, dtype=F32),
          shape(sx * sy * 8, lanes), shape(slab, lanes), shape(slab, lanes), shape(TAIL, lanes)]
         + row_shape,
-        (occupancy, features), nbytes=10**6,
+        (occupancy.astype(F32), features), nbytes=10**6,
     )
     stats = [lax.all_to_all(s, ALL, 0, 0, tiled=True) for s in stats]
     got = [
@@ -605,10 +603,7 @@
     band0, later = call(
         band_kernel, "band0", (VM,), [band, later], (conv_weight,), nbytes=8 * 10**6,
     )
-    band1, rows = call(
-        band_kernel, "band1", (VM,) * 2, [band, shape(8, lanes, dtype=F32)], (later, pars),
-        nbytes=8 * 10**6,
-    )
+    band1 = call(band_kernel, "band1", (VM,), band, (later,), nbytes=8 * 10**6)
     count = ex * sy
     ext, mine = call(
         functools.partial(line_kernel, narrow, sy, sb), "line", (VM,) * (4 + len(tails)),
@@ -621,10 +616,10 @@
     faces = 1 if ny == 2 else 2
     gap = corner_rows(ex)
     near, far = ex * 8 + 2 * gap + TAIL, 2 * gap + TAIL
-    zface, *yfaces = call(
-        functools.partial(chip_kernel, sb, sy), "chip", (VM,) * 3,
-        [shape(count + TAIL, lanes)] + [shape(near, lanes), shape(far, lanes)] * faces,
-        (ext, mine, core),
+    rows, zface, *yfaces = call(
+        functools.partial(chip_kernel, sb, sy), "chip", (VM,) * 4,
+        [shape(8, lanes, dtype=F32), shape(count + TAIL, lanes)] + [shape(near, lanes), shape(far, lanes)] * faces,
+        (pars, ext, mine, core),
         [pltpu.VMEM((lanes // 128, count * 8, 128), F32),
          pltpu.VMEM((lanes // 128, count, 128), F32)], nbytes=10**6,
     )
@@ -678,7 +673,8 @@
         [pltpu.VMEM((own * nx, feats), BF16), pltpu.VMEM((own * nx, 3 * cols), BF16)],
         flops=10**9, nbytes=3 * 10**6, mib=16 if narrow else 40,
     )
-    outs = [outs[0]] + [lax.ppermute(outs[k], "gx", swaps[k]) for k in range(1, nx)]
+    moved = {k: lax.ppermute(outs[k], "gx", swaps[k]) for k in range(nx - 1, 0, -1)}
+    outs = [outs[0]] + [moved[k] for k in range(1, nx)]
     lined = cols % 128 == 0
     attention = call(
         functools.partial(place_kernel, nx), "place", (VM,) * (1 + nx),

time: 59.4 us -> 60.4 us (1.017)
  blocking collectives: 9.3 us -> 0 us
  waiting for transfers between devices: 18.2 us -> 25.3 us
  starting transfers between devices: 14.6 us -> 17.1 us
  Pallas kernels: 13.1 us -> 13.8 us
  other arithmetic: 0.72 us -> 1.41 us
  local copies, waits for them, and re-layouts: 2.48 us -> 1.81 us
    all_to_all x1 -> x0, blocking collectives: 9.3 us -> none  [body(): stats = lax.all_to_all(mine, ALL, 0, 0, tiled=True)]
    all_to_all x0 -> x1, waiting for transfers between devices: none -> 5.7 us  [body(): stats = lax.all_to_all(mine, ALL, 0, 0, tiled=True)]
    all_to_all x0 -> x1, starting transfers between devices: none -> 2.54 us  [body(): stats = lax.all_to_all(mine, ALL, 0, 0, tiled=True)]
    ppermute x1, waiting for transfers between devices: 1.35 us -> 3.44 us  [body(): ygot.append(lax.ppermute(yfaces[2 * k + 1], ('gy', 'gz'), both))]
    pallas_call x10, Pallas kernels: 13.1 us -> 13.8 us  [call(): pl.pallas_call(kernel, out_shape=out, in_specs=list(specs), out_specs=jax...]
    ppermute x1, waiting for transfers between devices: 1.23 us -> 0.51 us  [body(): core = lax.ppermute(mine, 'gz', list(pairing(nz, False, False).items()))]
    convert_element_type x0 -> x1, other arithmetic: none -> 0.69 us  [body(): occupancy.astype(F32)]
    unnamed x8 -> x6, local copies, waits for them, and re-layouts: 2.48 us -> 1.81 us
  transfers between devices with their start and end apart: 13 -> 14, of which waited for: 7 -> 8; matrix products, arithmetic and copies ran while one was open for 1% -> 1% of each run, Pallas kernels for 8% -> 8%
where the time goes in v5:
time: 60.4 us; the launch traced here: 60.1 us
  waiting for transfers between devices  25.3 us (42%)
  starting transfers between devices  17.1 us (28%)
  Pallas kernels  13.8 us (23%)
  local copies, waits for them, and re-layouts  1.81 us (3%)
  other arithmetic  1.41 us (2%)
  between operations  0.71 us (1%)
    pallas_call x10, Pallas kernels, call(): pl.pallas_call(kernel, out_shape=out, in_specs=list(specs), out_specs=jax...  13.8 us
    ppermute x3, waiting for transfers between devices, body(): blocks[k] = lax.ppermute(blocks[k ^ low], 'gx', swaps[low])  11.2 us
    all_to_all x1, waiting for transfers between devices, body(): stats = lax.all_to_all(mine, ALL, 0, 0, tiled=True)  5.7 us
    ppermute x3, starting transfers between devices, body(): lax.ppermute(outs[k], 'gx', swaps[k])  4.45 us
    ppermute x1, waiting for transfers between devices, body(): ygot.append(lax.ppermute(yfaces[2 * k + 1], ('gy', 'gz'), both))  3.44 us
    ppermute x1, starting transfers between devices, body(): lax.ppermute(first, 'gx', list(pairing(nx, False, False).items()))  3.09 us
    all_to_all x1, starting transfers between devices, body(): stats = lax.all_to_all(mine, ALL, 0, 0, tiled=True)  2.54 us
    ppermute x1, starting transfers between devices, body(): lax.ppermute(second, 'gx', list(pairing(nx, True, narrow).items()))  2.47 us
  transfers between devices with their start and end apart: 14, of which 8 were waited for; matrix products, arithmetic and copies ran while one was open for 1% of the time, Pallas kernels for 8%

profile of v5, /device:TPU:0, one launch (start us, length us, event | category | flops | bytes accessed | tf_op | source)
XLA Modules:
  0.0 60.1 jit_solution(10569918250035866054)
XLA Ops:
  0.6 0.7 %convert_element_type.3.occ_ref = f32[4,1,4]{2,1,0:T(1,128)S(1)} convert(s32[4,1,4]{2,1,0:T(1,128)} %param.8) | non-fusion elementwise | flops 16 | bytes 128 | tf_op jit(solution)/shard_map/convert_element_type | solution.py:590
  1.3 0.0 copy-start
  1.3 0.9 %copy-done = bf16[8,8,4,256]{3,2,1,0:T(4,128)(2,1)S(1)} copy-done((bf16[8,8,4,256]{3,2,1,0:T(4,128)(2,1)S(1)}, bf16[8,8,4,256]{3,2,1,0:T(4,128)(2,1)}, u32[]{:S(2)}) %copy-start) | copy-done | bytes 131096
  2.2 0.9 %pre.1 = (f32[8,256]{1,0:T(8,128)S(1)}, f32[8,256]{1,0:T(8,128)S(1)}, bf16[512,256]{1,0:T(8,128)(2,1)S(1)}, bf16[80,256]{1,0:T(8,128)(2,1)S(1)}, bf16[80,256]{1,...) custom-call(f32[4,1,4]{2,1,0:T(1,128)S(1)} %convert_element_type.3.occ_ref, bf16[8,8,4,256]{3,2,1,0:T(4,128)(2,1)S(1)} %copy-done), custom_call_target="tpu_custom_call" | custom-call | bytes 1000000 | tf_op jit(solution)/shard_map/pre/pallas_call | solution.py:552
  3.2 3.1 %collective-permute-start = (bf16[80,256]{1,0:T(8,128)(2,1)S(1)}, bf16[80,256]{1,0:T(8,128)(2,1)S(1)}, u32[]{:S(2)}, u32[]{:S(2)}) collective-permute-start(bf16[80,256]{1,0:T(8,128)(2,1)S(1)} %get-tuple-element.26), channel_id=1, source_target_pairs={{0,8},{8,0},{16,24},{24,16},{1,9},{9,1},{17,25},{25,17},{2,10},{10... | collective-permute-start | bytes 122888 | tf_op jit(solution)/shard_map/ppermute | solution.py:594
  6.3 2.5 %collective-permute-start.1 = (bf16[80,256]{1,0:T(8,128)(2,1)S(1)}, bf16[80,256]{1,0:T(8,128)(2,1)S(1)}, u32[]{:S(2)}, u32[]{:S(2)}) collective-permute-start(bf16[80,256]{1,0:T(8,128)(2,1)S(1)} %get-tuple-element.27), channel_id=1, source_target_pairs={{0,24},{8,16},{16,8},{24,0},{1,25},{9,17},{17,9},{25,1},{2,26},{10... | collective-permute-start | bytes 122888 | tf_op jit(solution)/shard_map/ppermute | solution.py:595
  8.7 0.1 collective-permute-start.2
  8.9 0.0 copy-start.1
  8.9 0.9 %copy-done.1 = bf16[2,32,864]{2,1,0:T(8,128)(2,1)S(1)} copy-done((bf16[2,32,864]{2,1,0:T(8,128)(2,1)S(1)}, bf16[2,32,864]{2,1,0:T(8,128)(2,1)}, u32[]{:S(2)}) %copy-start.1) | copy-done | bytes 110616
  9.8 1.4 %band0.1 = (bf16[3,1024,256]{2,1,0:T(8,128)(2,1)S(1)}, bf16[1,32,864]{2,1,0:T(8,128)(2,1)S(1)}) custom-call(bf16[2,32,864]{2,1,0:T(8,128)(2,1)S(1)} %copy-done.1), custom_call_target="tpu_custom_call" | custom-call | bytes 8000000 | tf_op jit(solution)/shard_map/band0/pallas_call | solution.py:552
  11.1 2.2 %collective-permute-done.2.rest_1_ = bf16[16,256]{1,0:T(8,128)(2,1)S(1)} collective-permute-done((bf16[16,256]{1,0:T(8,128)(2,1)S(1)}, bf16[16,256]{1,0:T(8,128)(2,1)S(1)}, u32[]{:S(2)}, u32[]{:S(2)}) %collective-permute-start.2) | collective-permute-done | bytes 8224 | tf_op jit(solution)/shard_map/ppermute | solution.py:599
  13.3 0.0 collective-permute-done.first_ref
  13.3 0.0 collective-permute-done.1.second_ref
  13.3 0.2 line.1
  13.5 0.1 collective-permute-start.3
  13.5 0.7 %pad_maximum_fusion.pars_ref = f32[6,32]{1,0:T(8,128)S(1)} fusion(f32[2,32]{1,0:T(2,128)} %param.12, f32[2,32]{1,0:T(2,128)} %param.10, f32[2,32]{1,0:T(2,128)} %param.9), kind=kLoop, calls=%fused_computation | loop fusion | flops 384 | bytes 1536 | tf_op jit(solution)/shard_map/concatenate | solution.py:601
  14.3 0.5 collective-permute-done.3.other_ref.core_ref
  14.8 0.3 chip.1
  15.1 1.5 %collective-permute-start.5 = (bf16[144,256]{1,0:T(8,128)(2,1)S(1)}, bf16[144,256]{1,0:T(8,128)(2,1)S(1)}, u32[]{:S(2)}, u32[]{:S(2)}) collective-permute-start(bf16[144,256]{1,0:T(8,128)(2,1)S(1)} %get-tuple-element.32), channel_id=1, source_target_pairs={{0,4},{4,0},{1,5},{5,1},{2,6},{6,2},{3,7},{7,3},{8,12},{12,8},{9,1... | collective-permute-start | bytes 221192 | tf_op jit(solution)/shard_map/ppermute | solution.py:632
  16.6 1.0 %collective-permute-start.4 = (bf16[112,256]{1,0:T(8,128)(2,1)S(1)}, bf16[112,256]{1,0:T(8,128)(2,1)S(1)}, u32[]{:S(2)}, u32[]{:S(2)}) collective-permute-start(bf16[112,256]{1,0:T(8,128)(2,1)S(1)} %get-tuple-element.31.own_ref), channel_id=1, source_target_pairs={{0,3},{1,2},{2,1},{3,0},{4,7},{5,6},{6,5},{7,4},{8,11},{9,10},{10,... | collective-permute-start | bytes 172040 | tf_op jit(solution)/shard_map/ppermute | solution.py:628
  17.6 0.7 %collective-permute-start.6 = (bf16[48,256]{1,0:T(8,128)(2,1)S(1)}, bf16[48,256]{1,0:T(8,128)(2,1)S(1)}, u32[]{:S(2)}, u32[]{:S(2)}) collective-permute-start(bf16[48,256]{1,0:T(8,128)(2,1)S(1)} %get-tuple-element.33), channel_id=1, source_target_pairs={{0,7},{1,6},{2,5},{3,4},{4,3},{5,2},{6,1},{7,0},{8,15},{9,14},{10,... | collective-permute-start | bytes 73736 | tf_op jit(solution)/shard_map/ppermute | solution.py:636
  18.3 3.4 %collective-permute-done.6.rest_1_ = bf16[48,256]{1,0:T(8,128)(2,1)S(1)} collective-permute-done((bf16[48,256]{1,0:T(8,128)(2,1)S(1)}, bf16[48,256]{1,0:T(8,128)(2,1)S(1)}, u32[]{:S(2)}, u32[]{:S(2)}) %collective-permute-start.6) | collective-permute-done | bytes 24608 | tf_op jit(solution)/shard_map/ppermute | solution.py:636
  21.8 0.0 collective-permute-done.4.zface_ref
  21.8 0.0 collective-permute-done.5.rest_0_
  21.8 3.6 %first.1 = (f32[800,256]{1,0:T(8,128)S(1)}, f32[32,128]{1,0:T(8,128)}) custom-call(bf16[768,256]{1,0:T(8,128)(2,1)S(1)} %get-tuple-element.29.ext_ref, bf16[112,256]{1,0:T(8,128)(2,1)S(1)} %get-tuple-element.31.own_ref, bf16[112,256]{1,0:T(8,128)(2,1)S(1)} %collective-permute-done.3.other_ref.core_ref, ...), custom_call_target="tpu_custom_call" | custom-call | flops 2000000000 | bytes 4000000 | tf_op jit(solution)/shard_map/first/pallas_call | solution.py:552
  25.4 2.5 %all-to-all-start = ((f32[32,1,128]{2,1,0:T(1,128)}), f32[32,1,128]{2,1,0:T(1,128)S(1)}, u32[]{:S(2)}, u32[]{:S(2)}) async-start(f32[32,1,128]{2,1,0:T(1,128)} %bitcast.1), calls=%async_computation | async-start | bytes 32768 | tf_op jit(solution)/shard_map/all_to_all | solution.py:656
  27.9 1.4 %band1.1.weight_ref = bf16[3,1024,256]{2,1,0:T(8,128)(2,1)S(1)} custom-call(bf16[1,32,864]{2,1,0:T(8,128)(2,1)S(1)} %get-tuple-element.24._.weight_ref), custom_call_target="tpu_custom_call" | custom-call | bytes 8000000 | tf_op jit(solution)/shard_map/band1/pallas_call | solution.py:552
  29.3 5.7 %all-to-all-done = f32[32,1,128]{2,1,0:T(1,128)S(1)} async-done(((f32[32,1,128]{2,1,0:T(1,128)}), f32[32,1,128]{2,1,0:T(1,128)S(1)}, u32[]{:S(2)}, u32[]{:S(2)}) %all-to-all-start) | async-done | bytes 16416 | tf_op jit(solution)/shard_map/all_to_all | solution.py:656
  35.0 0.0 copy-start.2
  35.0 2.1 %second.1 = (bf16[8,8,4,256]{3,2,1,0:T(4,128)(2,1)}, bf16[64,1024]{1,0:T(8,128)(2,1)S(1)}) custom-call(f32[32,128]{1,0:T(8,128)S(1)} %bitcast.4, f32[800,256]{1,0:T(8,128)S(1)} %get-tuple-element.38.mid_ref, bf16[3,1024,256]{2,1,0:T(8,128)(2,1)S(1)} %band1.1.weight_ref, f32[8,256]{1,0:T(8,128)S(1)} %get-tuple-element.36.rest_4_.rows_ref, ...), custom_call_target="tpu_custom_call" | custom-call | flops 1000000000 | bytes 4000000 | tf_op jit(solution)/shard_map/second/pallas_call | solution.py:552
  37.1 0.6 collective-permute-start.8
  37.7 0.5 collective-permute-start.7
  38.3 7.7 %collective-permute-done.8.refs_2_ = bf16[64,1024]{1,0:T(8,128)(2,1)S(1)} collective-permute-done((bf16[64,1024]{1,0:T(8,128)(2,1)S(1)}, bf16[64,1024]{1,0:T(8,128)(2,1)S(1)}, u32[]{:S(2)}, u32[]{:S(2)}) %collective-permute-start.8) | collective-permute-done | bytes 131104 | tf_op jit(solution)/shard_map/ppermute | solution.py:668
  46.0 0.0 collective-permute-start.9
  46.0 0.0 copy-done.2
  46.0 1.9 %turn.1.weight_ref = bf16[1024,768]{1,0:T(8,128)(2,1)S(1)} custom-call(bf16[3,256,1024]{2,1,0:T(8,128)(2,1)S(1)} %copy-done.2), custom_call_target="tpu_custom_call" | custom-call | flops 1610612736 | bytes 6000000 | tf_op jit(solution)/shard_map/turn/pallas_call | solution.py:552
  47.9 0.0 collective-permute-done.7.refs_1_
  47.9 3.5 %collective-permute-done.9.refs_3_ = bf16[64,1024]{1,0:T(8,128)(2,1)S(1)} collective-permute-done((bf16[64,1024]{1,0:T(8,128)(2,1)S(1)}, bf16[64,1024]{1,0:T(8,128)(2,1)S(1)}, u32[]{:S(2)}, u32[]{:S(2)}) %collective-permute-start.9) | collective-permute-done | bytes 131104 | tf_op jit(solution)/shard_map/ppermute | solution.py:668
  51.4 1.4 %attend.1 = (bf16[64,256]{1,0:T(8,128)(2,1)S(1)}, bf16[64,256]{1,0:T(8,128)(2,1)S(1)}, bf16[64,256]{1,0:T(8,128)(2,1)S(1)}, bf16[64,256]{1,0:T(8,128)(2,1)S(1)}) custom-call(f32[8,256]{1,0:T(8,128)S(1)} %get-tuple-element.40.keys_ref, bf16[1024,768]{1,0:T(8,128)(2,1)S(1)} %turn.1.weight_ref, bf16[64,1024]{1,0:T(8,128)(2,1)S(1)} %get-tuple-element.41.refs_0_, ...), custom_call_target="tpu_custom_call" | custom-call | flops 1000000000 | bytes 3000000 | tf_op jit(solution)/shard_map/attend/pallas_call | solution.py:552
  52.8 0.4 collective-permute-start.10
  53.1 0.5 collective-permute-start.11
  53.6 3.6 %collective-permute-start.12 = (bf16[64,256]{1,0:T(8,128)(2,1)S(1)}, bf16[64,256]{1,0:T(8,128)(2,1)S(1)}, u32[]{:S(2)}, u32[]{:S(2)}) collective-permute-start(bf16[64,256]{1,0:T(8,128)(2,1)S(1)} %get-tuple-element.45), channel_id=1, source_target_pairs={{0,24},{8,16},{16,8},{24,0},{1,25},{9,17},{17,9},{25,1},{2,26},{10... | collective-permute-start | bytes 98312 | tf_op jit(solution)/shard_map/ppermute | solution.py:676
  57.2 0.0 collective-permute-done.10.refs_1_
  57.2 0.7 %collective-permute-done.11.refs_2_ = bf16[64,256]{1,0:T(8,128)(2,1)S(1)} collective-permute-done((bf16[64,256]{1,0:T(8,128)(2,1)S(1)}, bf16[64,256]{1,0:T(8,128)(2,1)S(1)}, u32[]{:S(2)}, u32[]{:S(2)}) %collective-permute-start.11) | collective-permute-done | bytes 32800 | tf_op jit(solution)/shard_map/ppermute | solution.py:676
  57.9 1.5 %collective-permute-done.12.refs_3_ = bf16[64,256]{1,0:T(8,128)(2,1)S(1)} collective-permute-done((bf16[64,256]{1,0:T(8,128)(2,1)S(1)}, bf16[64,256]{1,0:T(8,128)(2,1)S(1)}, u32[]{:S(2)}, u32[]{:S(2)}) %collective-permute-start.12) | collective-permute-done | bytes 32800 | tf_op jit(solution)/shard_map/ppermute | solution.py:676
  59.5 0.7 %place.1 = bf16[1,64,1024]{2,1,0:T(8,128)(2,1)} custom-call(f32[8,256]{1,0:T(8,128)S(1)} %get-tuple-element.34.rest_2_.keep_ref, bf16[64,256]{1,0:T(8,128)(2,1)S(1)} %get-tuple-element.42.refs_0_, bf16[64,256]{1,0:T(8,128)(2,1)S(1)} %collective-permute-done.10.refs_1_, bf16[64,256]{1,0:T(8,128)(2,1)S(1)} %collective-permute-done.11.refs_2_, ...), custom_call_target="tpu_custom_call" | custom-call | bytes 300000 | tf_op jit(solution)/shard_map/place/pallas_call | solution.py:552
Async XLA Ops:
  1.3 0.9 %copy-start = (bf16[8,8,4,256]{3,2,1,0:T(4,128)(2,1)S(1)}, bf16[8,8,4,256]{3,2,1,0:T(4,128)(2,1)}, u32[]{:S(2)}) copy-start(bf16[8,8,4,256]{3,2,1,0:T(4,128)(2,1)} %feat_ref.1) | copy-start | bytes 393220
  3.2 10.1 %collective-permute-start = (bf16[80,256]{1,0:T(8,128)(2,1)S(1)}, bf16[80,256]{1,0:T(8,128)(2,1)S(1)}, u32[]{:S(2)}, u32[]{:S(2)}) collective-permute-start(bf16[80,256]{1,0:T(8,128)(2,1)S(1)} %get-tuple-element.26), channel_id=1, source_target_pairs={{0,8},{8,0},{16,24},{24,16},{1,9},{9,1},{17,25},{25,17},{2,10},{10... | collective-permute-start | bytes 122888 | tf_op jit(solution)/shard_map/ppermute | solution.py:594
  6.3 7.0 %collective-permute-start.1 = (bf16[80,256]{1,0:T(8,128)(2,1)S(1)}, bf16[80,256]{1,0:T(8,128)(2,1)S(1)}, u32[]{:S(2)}, u32[]{:S(2)}) collective-permute-start(bf16[80,256]{1,0:T(8,128)(2,1)S(1)} %get-tuple-element.27), channel_id=1, source_target_pairs={{0,24},{8,16},{16,8},{24,0},{1,25},{9,17},{17,9},{25,1},{2,26},{10... | collective-permute-start | bytes 122888 | tf_op jit(solution)/shard_map/ppermute | solution.py:595
  8.7 4.5 %collective-permute-start.2 = (bf16[16,256]{1,0:T(8,128)(2,1)S(1)}, bf16[16,256]{1,0:T(8,128)(2,1)S(1)}, u32[]{:S(2)}, u32[]{:S(2)}) collective-permute-start(bf16[16,256]{1,0:T(8,128)(2,1)S(1)} %get-tuple-element.28.rest_0_), channel_id=1, source_target_pairs={{0,16},{8,24},{16,0},{24,8},{1,17},{9,25},{17,1},{25,9},{2,18},{10... | collective-permute-start | bytes 24584 | tf_op jit(solution)/shard_map/ppermute | solution.py:599
  8.9 0.9 %copy-start.1 = (bf16[2,32,864]{2,1,0:T(8,128)(2,1)S(1)}, bf16[2,32,864]{2,1,0:T(8,128)(2,1)}, u32[]{:S(2)}) copy-start(bf16[2,32,864]{2,1,0:T(8,128)(2,1)} %weight_ref.2) | copy-start | bytes 331780
  13.5 1.3 %collective-permute-start.3 = (bf16[112,256]{1,0:T(8,128)(2,1)S(1)}, bf16[112,256]{1,0:T(8,128)(2,1)S(1)}, u32[]{:S(2)}, u32[]{:S(2)}) collective-permute-start(bf16[112,256]{1,0:T(8,128)(2,1)S(1)} %get-tuple-element.30.own_ref), channel_id=1, source_target_pairs={{0,1},{1,0},{2,3},{3,2},{4,5},{5,4},{6,7},{7,6},{8,9},{9,8},{10,11... | collective-permute-start | bytes 172040 | tf_op jit(solution)/shard_map/ppermute | solution.py:614
  15.1 6.7 %collective-permute-start.5 = (bf16[144,256]{1,0:T(8,128)(2,1)S(1)}, bf16[144,256]{1,0:T(8,128)(2,1)S(1)}, u32[]{:S(2)}, u32[]{:S(2)}) collective-permute-start(bf16[144,256]{1,0:T(8,128)(2,1)S(1)} %get-tuple-element.32), channel_id=1, source_target_pairs={{0,4},{4,0},{1,5},{5,1},{2,6},{6,2},{3,7},{7,3},{8,12},{12,8},{9,1... | collective-permute-start | bytes 221192 | tf_op jit(solution)/shard_map/ppermute | solution.py:632
  16.6 5.2 %collective-permute-start.4 = (bf16[112,256]{1,0:T(8,128)(2,1)S(1)}, bf16[112,256]{1,0:T(8,128)(2,1)S(1)}, u32[]{:S(2)}, u32[]{:S(2)}) collective-permute-start(bf16[112,256]{1,0:T(8,128)(2,1)S(1)} %get-tuple-element.31.own_ref), channel_id=1, source_target_pairs={{0,3},{1,2},{2,1},{3,0},{4,7},{5,6},{6,5},{7,4},{8,11},{9,10},{10,... | collective-permute-start | bytes 172040 | tf_op jit(solution)/shard_map/ppermute | solution.py:628
  17.6 4.2 %collective-permute-start.6 = (bf16[48,256]{1,0:T(8,128)(2,1)S(1)}, bf16[48,256]{1,0:T(8,128)(2,1)S(1)}, u32[]{:S(2)}, u32[]{:S(2)}) collective-permute-start(bf16[48,256]{1,0:T(8,128)(2,1)S(1)} %get-tuple-element.33), channel_id=1, source_target_pairs={{0,7},{1,6},{2,5},{3,4},{4,3},{5,2},{6,1},{7,0},{8,15},{9,14},{10,... | collective-permute-start | bytes 73736 | tf_op jit(solution)/shard_map/ppermute | solution.py:636
  25.4 9.6 %all-to-all-start = ((f32[32,1,128]{2,1,0:T(1,128)}), f32[32,1,128]{2,1,0:T(1,128)S(1)}, u32[]{:S(2)}, u32[]{:S(2)}) async-start(f32[32,1,128]{2,1,0:T(1,128)} %bitcast.1), calls=%async_computation | async-start | bytes 32768 | tf_op jit(solution)/shard_map/all_to_all | solution.py:656
  35.0 11.0 %copy-start.2 = (bf16[3,256,1024]{2,1,0:T(8,128)(2,1)S(1)}, bf16[3,256,1024]{2,1,0:T(8,128)(2,1)}, u32[]{:S(2)}) copy-start(bf16[3,256,1024]{2,1,0:T(8,128)(2,1)} %weight_ref.3) | copy-start | bytes 4718596
  37.1 8.9 %collective-permute-start.8 = (bf16[64,1024]{1,0:T(8,128)(2,1)S(1)}, bf16[64,1024]{1,0:T(8,128)(2,1)S(1)}, u32[]{:S(2)}, u32[]{:S(2)}) collective-permute-start(bf16[64,1024]{1,0:T(8,128)(2,1)S(1)} %get-tuple-element.41.refs_0_), channel_id=1, source_target_pairs={{0,16},{8,24},{16,0},{24,8},{1,17},{9,25},{17,1},{25,9},{2,18},{10... | collective-permute-start | bytes 393224 | tf_op jit(solution)/shard_map/ppermute | solution.py:668
  37.7 10.2 %collective-permute-start.7 = (bf16[64,1024]{1,0:T(8,128)(2,1)S(1)}, bf16[64,1024]{1,0:T(8,128)(2,1)S(1)}, u32[]{:S(2)}, u32[]{:S(2)}) collective-permute-start(bf16[64,1024]{1,0:T(8,128)(2,1)S(1)} %get-tuple-element.41.refs_0_), channel_id=1, source_target_pairs={{0,8},{8,0},{16,24},{24,16},{1,9},{9,1},{17,25},{25,17},{2,10},{10... | collective-permute-start | bytes 393224 | tf_op jit(solution)/shard_map/ppermute | solution.py:668
  46.0 5.4 %collective-permute-start.9 = (bf16[64,1024]{1,0:T(8,128)(2,1)S(1)}, bf16[64,1024]{1,0:T(8,128)(2,1)S(1)}, u32[]{:S(2)}, u32[]{:S(2)}) collective-permute-start(bf16[64,1024]{1,0:T(8,128)(2,1)S(1)} %collective-permute-done.8.refs_2_), channel_id=1, source_target_pairs={{0,8},{8,0},{16,24},{24,16},{1,9},{9,1},{17,25},{25,17},{2,10},{10... | collective-permute-start | bytes 393224 | tf_op jit(solution)/shard_map/ppermute | solution.py:668
  52.8 4.5 %collective-permute-start.10 = (bf16[64,256]{1,0:T(8,128)(2,1)S(1)}, bf16[64,256]{1,0:T(8,128)(2,1)S(1)}, u32[]{:S(2)}, u32[]{:S(2)}) collective-permute-start(bf16[64,256]{1,0:T(8,128)(2,1)S(1)} %get-tuple-element.43), channel_id=1, source_target_pairs={{0,8},{8,0},{16,24},{24,16},{1,9},{9,1},{17,25},{25,17},{2,10},{10... | collective-permute-start | bytes 98312 | tf_op jit(solution)/shard_map/ppermute | solution.py:676
  53.1 4.8 %collective-permute-start.11 = (bf16[64,256]{1,0:T(8,128)(2,1)S(1)}, bf16[64,256]{1,0:T(8,128)(2,1)S(1)}, u32[]{:S(2)}, u32[]{:S(2)}) collective-permute-start(bf16[64,256]{1,0:T(8,128)(2,1)S(1)} %get-tuple-element.44), channel_id=1, source_target_pairs={{0,16},{8,24},{16,0},{24,8},{1,17},{9,25},{17,1},{25,9},{2,18},{10... | collective-permute-start | bytes 98312 | tf_op jit(solution)/shard_map/ppermute | solution.py:676
  53.6 5.8 %collective-permute-start.12 = (bf16[64,256]{1,0:T(8,128)(2,1)S(1)}, bf16[64,256]{1,0:T(8,128)(2,1)S(1)}, u32[]{:S(2)}, u32[]{:S(2)}) collective-permute-start(bf16[64,256]{1,0:T(8,128)(2,1)S(1)} %get-tuple-element.45), channel_id=1, source_target_pairs={{0,24},{8,16},{16,8},{24,0},{1,25},{9,17},{17,9},{25,1},{2,26},{10... | collective-permute-start | bytes 98312 | tf_op jit(solution)/shard_map/ppermute | solution.py:676

commit v6 on v4

--- a/solution.py
+++ b/solution.py
@@ -527,7 +527,7 @@
             merged = jnp.where(head == h, mixed / total, merged)
         merged = merged.astype(BF16)
         for k in range(members):
-            out_refs[k][:, t * width : (t + 1) * width] = merged[k * own : (k + 1) * own]
+            out_refs[-1 - k][:, t * width : (t + 1) * width] = merged[k * own : (k + 1) * own]
 
 
 def place_kernel(members, keep_ref, *refs):
@@ -539,7 +539,7 @@
     for b in range(4):
         keep = jnp.where(row // 2 == b, jnp.broadcast_to(keep_ref[b : b + 1, :cols], (8, cols)), keep)
     for k in range(members):
-        value = refs[k][...].astype(F32).reshape(own // 8, 8, cols)
+        value = refs[members - 1 - k][...].astype(F32).reshape(own // 8, 8, cols)
         value = jnp.where((keep > 0)[None], value, 0.0).reshape(own, cols).astype(BF16)
         if cols % 128 == 0:
             out_ref[0, :, pl.ds(pl.multiple_of((me ^ k) * cols, cols), cols)] = value
@@ -678,7 +678,8 @@
         [pltpu.VMEM((own * nx, feats), BF16), pltpu.VMEM((own * nx, 3 * cols), BF16)],
         flops=10**9, nbytes=3 * 10**6, mib=16 if narrow else 40,
     )
-    outs = [outs[0]] + [lax.ppermute(outs[k], "gx", swaps[k]) for k in range(1, nx)]
+    moved = [lax.ppermute(v, "gx", swaps[nx - 1 - i]) for i, v in enumerate(outs[:-1])]
+    outs = moved + [outs[-1]]
     lined = cols % 128 == 0
     attention = call(
         functools.partial(place_kernel, nx), "place", (VM,) * (1 + nx),

time: 59.4 us -> 59 us (level)
  no operation moved by 1% of the time
where the time goes in v6:
time: 59 us; the launch traced here: 58.8 us
  waiting for transfers between devices  17.9 us (30%)
  starting transfers between devices  14.6 us (25%)
  Pallas kernels  13.1 us (22%)
  blocking collectives  9.3 us (16%)
  local copies, waits for them, and re-layouts  2.48 us (4%)
  other arithmetic  0.72 us (1%)
  between operations  0.71 us (1%)
    pallas_call x10, Pallas kernels, call(): pl.pallas_call(kernel, out_shape=out, in_specs=list(specs), out_specs=jax...  13.1 us
    ppermute x3, waiting for transfers between devices, body(): blocks[k] = lax.ppermute(blocks[k ^ low], 'gx', swaps[low])  11.2 us
    all_to_all x1, blocking collectives, body(): stats = lax.all_to_all(mine, ALL, 0, 0, tiled=True)  9.3 us
    ppermute x3, starting transfers between devices, body(): lax.ppermute(v, 'gx', swaps[nx - 1 - i])  4.45 us
    ppermute x1, starting transfers between devices, body(): lax.ppermute(first, 'gx', list(pairing(nx, False, False).items()))  3.09 us
    unnamed x8, local copies, waits for them, and re-layouts  2.48 us
    ppermute x1, starting transfers between devices, body(): lax.ppermute(second, 'gx', list(pairing(nx, True, narrow).items()))  2.47 us
    ppermute x1, waiting for transfers between devices, body(): tails.append(lax.ppermute(tail, 'gx', [(i, i ^ 2) for i in range(nx)]))  2.16 us
  transfers between devices with their start and end apart: 13, of which 7 were waited for; matrix products, arithmetic and copies ran while one was open for 1% of the time, Pallas kernels for 8%

profile of v6, /device:TPU:0, one launch (start us, length us, event | category | flops | bytes accessed | tf_op | source)
XLA Modules:
  0.0 58.8 jit_solution(2758778859940439115)
XLA Ops:
  0.6 0.0 copy-start
  0.6 0.9 %copy-done = bf16[8,8,4,256]{3,2,1,0:T(4,128)(2,1)S(1)} copy-done((bf16[8,8,4,256]{3,2,1,0:T(4,128)(2,1)S(1)}, bf16[8,8,4,256]{3,2,1,0:T(4,128)(2,1)}, u32[]{:S(2)}) %copy-start) | copy-done | bytes 131096
  1.5 0.0 copy-start.2
  1.5 0.7 %copy-done.2 = s32[4,1,4]{2,1,0:T(1,128)S(1)} copy-done((s32[4,1,4]{2,1,0:T(1,128)S(1)}, s32[4,1,4]{2,1,0:T(1,128)}, u32[]{:S(2)}) %copy-start.2) | copy-done | bytes 88
  2.2 0.9 %pre.1 = (f32[8,256]{1,0:T(8,128)S(1)}, f32[8,256]{1,0:T(8,128)S(1)}, bf16[512,256]{1,0:T(8,128)(2,1)S(1)}, bf16[80,256]{1,0:T(8,128)(2,1)S(1)}, bf16[80,256]{1,...) custom-call(s32[4,1,4]{2,1,0:T(1,128)S(1)} %copy-done.2, bf16[8,8,4,256]{3,2,1,0:T(4,128)(2,1)S(1)} %copy-done), custom_call_target="tpu_custom_call" | custom-call | bytes 1000000 | tf_op jit(solution)/shard_map/pre/pallas_call | solution.py:554
  3.2 3.1 %collective-permute-start = (bf16[80,256]{1,0:T(8,128)(2,1)S(1)}, bf16[80,256]{1,0:T(8,128)(2,1)S(1)}, u32[]{:S(2)}, u32[]{:S(2)}) collective-permute-start(bf16[80,256]{1,0:T(8,128)(2,1)S(1)} %get-tuple-element.27), channel_id=1, source_target_pairs={{0,8},{8,0},{16,24},{24,16},{1,9},{9,1},{17,25},{25,17},{2,10},{10... | collective-permute-start | bytes 122888 | tf_op jit(solution)/shard_map/ppermute | solution.py:596
  6.3 2.5 %collective-permute-start.1 = (bf16[80,256]{1,0:T(8,128)(2,1)S(1)}, bf16[80,256]{1,0:T(8,128)(2,1)S(1)}, u32[]{:S(2)}, u32[]{:S(2)}) collective-permute-start(bf16[80,256]{1,0:T(8,128)(2,1)S(1)} %get-tuple-element.28), channel_id=1, source_target_pairs={{0,24},{8,16},{16,8},{24,0},{1,25},{9,17},{17,9},{25,1},{2,26},{10... | collective-permute-start | bytes 122888 | tf_op jit(solution)/shard_map/ppermute | solution.py:597
  8.7 0.1 collective-permute-start.2
  8.8 0.0 copy-start.1
  8.9 0.9 %copy-done.1 = bf16[2,32,864]{2,1,0:T(8,128)(2,1)S(1)} copy-done((bf16[2,32,864]{2,1,0:T(8,128)(2,1)S(1)}, bf16[2,32,864]{2,1,0:T(8,128)(2,1)}, u32[]{:S(2)}) %copy-start.1) | copy-done | bytes 110616
  9.7 1.4 %band0.1 = (bf16[3,1024,256]{2,1,0:T(8,128)(2,1)S(1)}, bf16[1,32,864]{2,1,0:T(8,128)(2,1)S(1)}) custom-call(bf16[2,32,864]{2,1,0:T(8,128)(2,1)S(1)} %copy-done.1), custom_call_target="tpu_custom_call" | custom-call | bytes 8000000 | tf_op jit(solution)/shard_map/band0/pallas_call | solution.py:554
  11.1 2.2 %collective-permute-done.2.rest_1_ = bf16[16,256]{1,0:T(8,128)(2,1)S(1)} collective-permute-done((bf16[16,256]{1,0:T(8,128)(2,1)S(1)}, bf16[16,256]{1,0:T(8,128)(2,1)S(1)}, u32[]{:S(2)}, u32[]{:S(2)}) %collective-permute-start.2) | collective-permute-done | bytes 8224 | tf_op jit(solution)/shard_map/ppermute | solution.py:601
  13.3 0.0 collective-permute-done.first_ref
  13.3 0.0 collective-permute-done.1.second_ref
  13.3 0.2 line.1
  13.5 0.1 collective-permute-start.3
  13.5 1.2 %collective-permute-done.3.other_ref.core_ref = bf16[112,256]{1,0:T(8,128)(2,1)S(1)} collective-permute-done((bf16[112,256]{1,0:T(8,128)(2,1)S(1)}, bf16[112,256]{1,0:T(8,128)(2,1)S(1)}, u32[]{:S(2)}, u32[]{:S(2)}) %collective-permute-start.3) | collective-permute-done | bytes 57376 | tf_op jit(solution)/shard_map/ppermute | solution.py:619
  14.8 0.2 chip.1
  15.0 1.6 %collective-permute-start.5 = (bf16[144,256]{1,0:T(8,128)(2,1)S(1)}, bf16[144,256]{1,0:T(8,128)(2,1)S(1)}, u32[]{:S(2)}, u32[]{:S(2)}) collective-permute-start(bf16[144,256]{1,0:T(8,128)(2,1)S(1)} %get-tuple-element.33), channel_id=1, source_target_pairs={{0,4},{4,0},{1,5},{5,1},{2,6},{6,2},{3,7},{7,3},{8,12},{12,8},{9,1... | collective-permute-start | bytes 221192 | tf_op jit(solution)/shard_map/ppermute | solution.py:637
  16.5 1.0 %collective-permute-start.4 = (bf16[112,256]{1,0:T(8,128)(2,1)S(1)}, bf16[112,256]{1,0:T(8,128)(2,1)S(1)}, u32[]{:S(2)}, u32[]{:S(2)}) collective-permute-start(bf16[112,256]{1,0:T(8,128)(2,1)S(1)} %get-tuple-element.32.own_ref), channel_id=1, source_target_pairs={{0,3},{1,2},{2,1},{3,0},{4,7},{5,6},{6,5},{7,4},{8,11},{9,10},{10,... | collective-permute-start | bytes 172040 | tf_op jit(solution)/shard_map/ppermute | solution.py:633
  17.5 0.7 %collective-permute-start.6 = (bf16[48,256]{1,0:T(8,128)(2,1)S(1)}, bf16[48,256]{1,0:T(8,128)(2,1)S(1)}, u32[]{:S(2)}, u32[]{:S(2)}) collective-permute-start(bf16[48,256]{1,0:T(8,128)(2,1)S(1)} %get-tuple-element.34), channel_id=1, source_target_pairs={{0,7},{1,6},{2,5},{3,4},{4,3},{5,2},{6,1},{7,0},{8,15},{9,14},{10,... | collective-permute-start | bytes 73736 | tf_op jit(solution)/shard_map/ppermute | solution.py:641
  18.3 0.7 %pad_maximum_fusion.rest_0_ = f32[6,32]{1,0:T(8,128)S(1)} fusion(f32[2,32]{1,0:T(2,128)} %param.12, f32[2,32]{1,0:T(2,128)} %param.10, f32[2,32]{1,0:T(2,128)} %param.9), kind=kLoop, calls=%fused_computation | loop fusion | flops 384 | bytes 1536 | tf_op jit(solution)/shard_map/concatenate | solution.py:603
  19.0 1.4 %band1.1 = (bf16[3,1024,256]{2,1,0:T(8,128)(2,1)S(1)}, f32[8,256]{1,0:T(8,128)S(1)}) custom-call(bf16[1,32,864]{2,1,0:T(8,128)(2,1)S(1)} %get-tuple-element.25._.weight_ref, f32[6,32]{1,0:T(8,128)S(1)} %pad_maximum_fusion.rest_0_), custom_call_target="tpu_custom_call" | custom-call | bytes 8000000 | tf_op jit(solution)/shard_map/band1/pallas_call | solution.py:554
  20.4 1.3 %collective-permute-done.6.rest_1_ = bf16[48,256]{1,0:T(8,128)(2,1)S(1)} collective-permute-done((bf16[48,256]{1,0:T(8,128)(2,1)S(1)}, bf16[48,256]{1,0:T(8,128)(2,1)S(1)}, u32[]{:S(2)}, u32[]{:S(2)}) %collective-permute-start.6) | collective-permute-done | bytes 24608 | tf_op jit(solution)/shard_map/ppermute | solution.py:641
  21.7 0.0 collective-permute-done.4.zface_ref
  21.7 0.0 collective-permute-done.5.rest_0_
  21.7 3.0 %first.1 = (f32[800,256]{1,0:T(8,128)S(1)}, f32[32,128]{1,0:T(8,128)S(1)}) custom-call(bf16[768,256]{1,0:T(8,128)(2,1)S(1)} %get-tuple-element.30.ext_ref, bf16[112,256]{1,0:T(8,128)(2,1)S(1)} %get-tuple-element.32.own_ref, bf16[112,256]{1,0:T(8,128)(2,1)S(1)} %collective-permute-done.3.other_ref.core_ref, ...), custom_call_target="tpu_custom_call" | custom-call | flops 2000000000 | bytes 4000000 | tf_op jit(solution)/shard_map/first/pallas_call | solution.py:554
  24.7 9.3 %all_to_all.11 = f32[32,1,128]{2,1,0:T(1,128)S(1)} all-to-all(f32[32,1,128]{2,1,0:T(1,128)S(1)} %bitcast.4), channel_id=1, replica_groups=mesh['gx'=4,'gy'=2,'gz'=4] {'gx','gy','gz'}, dimensions={0} | all-to-all | bytes 32768 | tf_op jit(solution)/shard_map/all_to_all | solution.py:661
  34.0 0.0 copy-start.3
  34.0 2.2 %second.1 = (bf16[8,8,4,256]{3,2,1,0:T(4,128)(2,1)}, bf16[64,1024]{1,0:T(8,128)(2,1)S(1)}) custom-call(f32[32,128]{1,0:T(8,128)S(1)} %bitcast.5, f32[800,256]{1,0:T(8,128)S(1)} %get-tuple-element.39.mid_ref, bf16[3,1024,256]{2,1,0:T(8,128)(2,1)S(1)} %get-tuple-element.40.weight_ref, f32[8,256]{1,0:T(8,128)S(1)} %get-tuple-element.37.rest_4_.rows_ref, ...), custom_call_target="tpu_custom_call" | custom-call | flops 1000000000 | bytes 4000000 | tf_op jit(solution)/shard_map/second/pallas_call | solution.py:554
  36.1 0.6 %collective-permute-start.8 = (bf16[64,1024]{1,0:T(8,128)(2,1)S(1)}, bf16[64,1024]{1,0:T(8,128)(2,1)S(1)}, u32[]{:S(2)}, u32[]{:S(2)}) collective-permute-start(bf16[64,1024]{1,0:T(8,128)(2,1)S(1)} %get-tuple-element.43.refs_0_), channel_id=1, source_target_pairs={{0,16},{8,24},{16,0},{24,8},{1,17},{9,25},{17,1},{25,9},{2,18},{10... | collective-permute-start | bytes 393224 | tf_op jit(solution)/shard_map/ppermute | solution.py:673
  36.7 0.5 collective-permute-start.7
  37.3 7.7 %collective-permute-done.8.refs_2_ = bf16[64,1024]{1,0:T(8,128)(2,1)S(1)} collective-permute-done((bf16[64,1024]{1,0:T(8,128)(2,1)S(1)}, bf16[64,1024]{1,0:T(8,128)(2,1)S(1)}, u32[]{:S(2)}, u32[]{:S(2)}) %collective-permute-start.8) | collective-permute-done | bytes 131104 | tf_op jit(solution)/shard_map/ppermute | solution.py:673
  45.0 0.0 collective-permute-start.9
  45.0 0.0 copy-done.3
  45.0 1.9 %turn.1.weight_ref = bf16[1024,768]{1,0:T(8,128)(2,1)S(1)} custom-call(bf16[3,256,1024]{2,1,0:T(8,128)(2,1)S(1)} %copy-done.3), custom_call_target="tpu_custom_call" | custom-call | flops 1610612736 | bytes 6000000 | tf_op jit(solution)/shard_map/turn/pallas_call | solution.py:554
  46.9 0.0 collective-permute-done.7.refs_1_
  46.9 3.5 %collective-permute-done.9.refs_3_ = bf16[64,1024]{1,0:T(8,128)(2,1)S(1)} collective-permute-done((bf16[64,1024]{1,0:T(8,128)(2,1)S(1)}, bf16[64,1024]{1,0:T(8,128)(2,1)S(1)}, u32[]{:S(2)}, u32[]{:S(2)}) %collective-permute-start.9) | collective-permute-done | bytes 131104 | tf_op jit(solution)/shard_map/ppermute | solution.py:673
  50.4 1.4 %attend.1 = (bf16[64,256]{1,0:T(8,128)(2,1)S(1)}, bf16[64,256]{1,0:T(8,128)(2,1)S(1)}, bf16[64,256]{1,0:T(8,128)(2,1)S(1)}, bf16[64,256]{1,0:T(8,128)(2,1)S(1)}) custom-call(f32[8,256]{1,0:T(8,128)S(1)} %get-tuple-element.42.keys_ref, bf16[1024,768]{1,0:T(8,128)(2,1)S(1)} %turn.1.weight_ref, bf16[64,1024]{1,0:T(8,128)(2,1)S(1)} %get-tuple-element.43.refs_0_, ...), custom_call_target="tpu_custom_call" | custom-call | flops 1000000000 | bytes 3000000 | tf_op jit(solution)/shard_map/attend/pallas_call | solution.py:554
  51.8 0.3 collective-permute-start.10
  52.1 1.5 %collective-permute-start.11 = (bf16[64,256]{1,0:T(8,128)(2,1)S(1)}, bf16[64,256]{1,0:T(8,128)(2,1)S(1)}, u32[]{:S(2)}, u32[]{:S(2)}) collective-permute-start(bf16[64,256]{1,0:T(8,128)(2,1)S(1)} %get-tuple-element.45), channel_id=1, source_target_pairs={{0,16},{8,24},{16,0},{24,8},{1,17},{9,25},{17,1},{25,9},{2,18},{10... | collective-permute-start | bytes 98312 | tf_op jit(solution)/shard_map/ppermute | solution.py:681
  53.6 2.6 %collective-permute-start.12 = (bf16[64,256]{1,0:T(8,128)(2,1)S(1)}, bf16[64,256]{1,0:T(8,128)(2,1)S(1)}, u32[]{:S(2)}, u32[]{:S(2)}) collective-permute-start(bf16[64,256]{1,0:T(8,128)(2,1)S(1)} %get-tuple-element.46), channel_id=1, source_target_pairs={{0,8},{8,0},{16,24},{24,16},{1,9},{9,1},{17,25},{25,17},{2,10},{10... | collective-permute-start | bytes 98312 | tf_op jit(solution)/shard_map/ppermute | solution.py:681
  56.2 1.3 %collective-permute-done.10.refs_0_ = bf16[64,256]{1,0:T(8,128)(2,1)S(1)} collective-permute-done((bf16[64,256]{1,0:T(8,128)(2,1)S(1)}, bf16[64,256]{1,0:T(8,128)(2,1)S(1)}, u32[]{:S(2)}, u32[]{:S(2)}) %collective-permute-start.10) | collective-permute-done | bytes 32800 | tf_op jit(solution)/shard_map/ppermute | solution.py:681
  57.5 0.0 collective-permute-done.11.refs_1_
  57.5 0.6 collective-permute-done.12.refs_2_
  58.1 0.7 %place.1 = bf16[1,64,1024]{2,1,0:T(8,128)(2,1)} custom-call(f32[8,256]{1,0:T(8,128)S(1)} %get-tuple-element.35.rest_2_.keep_ref, bf16[64,256]{1,0:T(8,128)(2,1)S(1)} %collective-permute-done.10.refs_0_, bf16[64,256]{1,0:T(8,128)(2,1)S(1)} %collective-permute-done.11.refs_1_, bf16[64,256]{1,0:T(8,128)(2,1)S(1)} %collective-permute-done.12.refs_2_, ...), custom_call_target="tpu_custom_call" | custom-call | bytes 300000 | tf_op jit(solution)/shard_map/place/pallas_call | solution.py:554
Async XLA Ops:
  0.6 0.9 %copy-start = (bf16[8,8,4,256]{3,2,1,0:T(4,128)(2,1)S(1)}, bf16[8,8,4,256]{3,2,1,0:T(4,128)(2,1)}, u32[]{:S(2)}) copy-start(bf16[8,8,4,256]{3,2,1,0:T(4,128)(2,1)} %feat_ref.1) | copy-start | bytes 393220
  1.5 0.7 %copy-start.2 = (s32[4,1,4]{2,1,0:T(1,128)S(1)}, s32[4,1,4]{2,1,0:T(1,128)}, u32[]{:S(2)}) copy-start(s32[4,1,4]{2,1,0:T(1,128)} %occ_ref.1) | copy-start | bytes 196
  3.2 10.1 %collective-permute-start = (bf16[80,256]{1,0:T(8,128)(2,1)S(1)}, bf16[80,256]{1,0:T(8,128)(2,1)S(1)}, u32[]{:S(2)}, u32[]{:S(2)}) collective-permute-start(bf16[80,256]{1,0:T(8,128)(2,1)S(1)} %get-tuple-element.27), channel_id=1, source_target_pairs={{0,8},{8,0},{16,24},{24,16},{1,9},{9,1},{17,25},{25,17},{2,10},{10... | collective-permute-start | bytes 122888 | tf_op jit(solution)/shard_map/ppermute | solution.py:596
  6.3 7.0 %collective-permute-start.1 = (bf16[80,256]{1,0:T(8,128)(2,1)S(1)}, bf16[80,256]{1,0:T(8,128)(2,1)S(1)}, u32[]{:S(2)}, u32[]{:S(2)}) collective-permute-start(bf16[80,256]{1,0:T(8,128)(2,1)S(1)} %get-tuple-element.28), channel_id=1, source_target_pairs={{0,24},{8,16},{16,8},{24,0},{1,25},{9,17},{17,9},{25,1},{2,26},{10... | collective-permute-start | bytes 122888 | tf_op jit(solution)/shard_map/ppermute | solution.py:597
  8.7 4.5 %collective-permute-start.2 = (bf16[16,256]{1,0:T(8,128)(2,1)S(1)}, bf16[16,256]{1,0:T(8,128)(2,1)S(1)}, u32[]{:S(2)}, u32[]{:S(2)}) collective-permute-start(bf16[16,256]{1,0:T(8,128)(2,1)S(1)} %get-tuple-element.29.rest_0_), channel_id=1, source_target_pairs={{0,16},{8,24},{16,0},{24,8},{1,17},{9,25},{17,1},{25,9},{2,18},{10... | collective-permute-start | bytes 24584 | tf_op jit(solution)/shard_map/ppermute | solution.py:601
  8.8 0.9 %copy-start.1 = (bf16[2,32,864]{2,1,0:T(8,128)(2,1)S(1)}, bf16[2,32,864]{2,1,0:T(8,128)(2,1)}, u32[]{:S(2)}) copy-start(bf16[2,32,864]{2,1,0:T(8,128)(2,1)} %weight_ref.2) | copy-start | bytes 331780
  13.5 1.3 %collective-permute-start.3 = (bf16[112,256]{1,0:T(8,128)(2,1)S(1)}, bf16[112,256]{1,0:T(8,128)(2,1)S(1)}, u32[]{:S(2)}, u32[]{:S(2)}) collective-permute-start(bf16[112,256]{1,0:T(8,128)(2,1)S(1)} %get-tuple-element.31.own_ref), channel_id=1, source_target_pairs={{0,1},{1,0},{2,3},{3,2},{4,5},{5,4},{6,7},{7,6},{8,9},{9,8},{10,11... | collective-permute-start | bytes 172040 | tf_op jit(solution)/shard_map/ppermute | solution.py:619
  15.0 6.7 %collective-permute-start.5 = (bf16[144,256]{1,0:T(8,128)(2,1)S(1)}, bf16[144,256]{1,0:T(8,128)(2,1)S(1)}, u32[]{:S(2)}, u32[]{:S(2)}) collective-permute-start(bf16[144,256]{1,0:T(8,128)(2,1)S(1)} %get-tuple-element.33), channel_id=1, source_target_pairs={{0,4},{4,0},{1,5},{5,1},{2,6},{6,2},{3,7},{7,3},{8,12},{12,8},{9,1... | collective-permute-start | bytes 221192 | tf_op jit(solution)/shard_map/ppermute | solution.py:637
  16.5 5.2 %collective-permute-start.4 = (bf16[112,256]{1,0:T(8,128)(2,1)S(1)}, bf16[112,256]{1,0:T(8,128)(2,1)S(1)}, u32[]{:S(2)}, u32[]{:S(2)}) collective-permute-start(bf16[112,256]{1,0:T(8,128)(2,1)S(1)} %get-tuple-element.32.own_ref), channel_id=1, source_target_pairs={{0,3},{1,2},{2,1},{3,0},{4,7},{5,6},{6,5},{7,4},{8,11},{9,10},{10,... | collective-permute-start | bytes 172040 | tf_op jit(solution)/shard_map/ppermute | solution.py:633
  17.5 4.2 %collective-permute-start.6 = (bf16[48,256]{1,0:T(8,128)(2,1)S(1)}, bf16[48,256]{1,0:T(8,128)(2,1)S(1)}, u32[]{:S(2)}, u32[]{:S(2)}) collective-permute-start(bf16[48,256]{1,0:T(8,128)(2,1)S(1)} %get-tuple-element.34), channel_id=1, source_target_pairs={{0,7},{1,6},{2,5},{3,4},{4,3},{5,2},{6,1},{7,0},{8,15},{9,14},{10,... | collective-permute-start | bytes 73736 | tf_op jit(solution)/shard_map/ppermute | solution.py:641
  34.0 11.0 %copy-start.3 = (bf16[3,256,1024]{2,1,0:T(8,128)(2,1)S(1)}, bf16[3,256,1024]{2,1,0:T(8,128)(2,1)}, u32[]{:S(2)}) copy-start(bf16[3,256,1024]{2,1,0:T(8,128)(2,1)} %weight_ref.3) | copy-start | bytes 4718596
  36.1 8.9 %collective-permute-start.8 = (bf16[64,1024]{1,0:T(8,128)(2,1)S(1)}, bf16[64,1024]{1,0:T(8,128)(2,1)S(1)}, u32[]{:S(2)}, u32[]{:S(2)}) collective-permute-start(bf16[64,1024]{1,0:T(8,128)(2,1)S(1)} %get-tuple-element.43.refs_0_), channel_id=1, source_target_pairs={{0,16},{8,24},{16,0},{24,8},{1,17},{9,25},{17,1},{25,9},{2,18},{10... | collective-permute-start | bytes 393224 | tf_op jit(solution)/shard_map/ppermute | solution.py:673
  36.7 10.2 %collective-permute-start.7 = (bf16[64,1024]{1,0:T(8,128)(2,1)S(1)}, bf16[64,1024]{1,0:T(8,128)(2,1)S(1)}, u32[]{:S(2)}, u32[]{:S(2)}) collective-permute-start(bf16[64,1024]{1,0:T(8,128)(2,1)S(1)} %get-tuple-element.43.refs_0_), channel_id=1, source_target_pairs={{0,8},{8,0},{16,24},{24,16},{1,9},{9,1},{17,25},{25,17},{2,10},{10... | collective-permute-start | bytes 393224 | tf_op jit(solution)/shard_map/ppermute | solution.py:673
  45.0 5.4 %collective-permute-start.9 = (bf16[64,1024]{1,0:T(8,128)(2,1)S(1)}, bf16[64,1024]{1,0:T(8,128)(2,1)S(1)}, u32[]{:S(2)}, u32[]{:S(2)}) collective-permute-start(bf16[64,1024]{1,0:T(8,128)(2,1)S(1)} %collective-permute-done.8.refs_2_), channel_id=1, source_target_pairs={{0,8},{8,0},{16,24},{24,16},{1,9},{9,1},{17,25},{25,17},{2,10},{10... | collective-permute-start | bytes 393224 | tf_op jit(solution)/shard_map/ppermute | solution.py:673
  51.8 5.8 %collective-permute-start.10 = (bf16[64,256]{1,0:T(8,128)(2,1)S(1)}, bf16[64,256]{1,0:T(8,128)(2,1)S(1)}, u32[]{:S(2)}, u32[]{:S(2)}) collective-permute-start(bf16[64,256]{1,0:T(8,128)(2,1)S(1)} %get-tuple-element.44), channel_id=1, source_target_pairs={{0,24},{8,16},{16,8},{24,0},{1,25},{9,17},{17,9},{25,1},{2,26},{10... | collective-permute-start | bytes 98312 | tf_op jit(solution)/shard_map/ppermute | solution.py:681
  52.1 5.5 %collective-permute-start.11 = (bf16[64,256]{1,0:T(8,128)(2,1)S(1)}, bf16[64,256]{1,0:T(8,128)(2,1)S(1)}, u32[]{:S(2)}, u32[]{:S(2)}) collective-permute-start(bf16[64,256]{1,0:T(8,128)(2,1)S(1)} %get-tuple-element.45), channel_id=1, source_target_pairs={{0,16},{8,24},{16,0},{24,8},{1,17},{9,25},{17,1},{25,9},{2,18},{10... | collective-permute-start | bytes 98312 | tf_op jit(solution)/shard_map/ppermute | solution.py:681
  53.6 4.5 %collective-permute-start.12 = (bf16[64,256]{1,0:T(8,128)(2,1)S(1)}, bf16[64,256]{1,0:T(8,128)(2,1)S(1)}, u32[]{:S(2)}, u32[]{:S(2)}) collective-permute-start(bf16[64,256]{1,0:T(8,128)(2,1)S(1)} %get-tuple-element.46), channel_id=1, source_target_pairs={{0,8},{8,0},{16,24},{24,16},{1,9},{9,1},{17,25},{25,17},{2,10},{10... | collective-permute-start | bytes 98312 | tf_op jit(solution)/shard_map/ppermute | solution.py:681

commit v7 on v4

--- a/solution.py
+++ b/solution.py
@@ -500,7 +500,7 @@
 
 
 def attend_kernel(members, keys_ref, weight_ref, *refs):
-    tok_refs, out_refs, (toks, proj) = refs[:members], refs[members : 2 * members], refs[-2:]
+    tok_refs, (out_ref, toks, proj) = refs[:members], refs[members:]
     own = tok_refs[0].shape[0]
     seq = own * members
     cols = weight_ref.shape[1] // 3
@@ -508,6 +508,7 @@
         toks[k * own : (k + 1) * own, :] = tok_refs[k][...]
     proj[...] = jnp.dot(toks[...], weight_ref[...], preferred_element_type=F32).astype(BF16)
     there = keys_ref[0:1] > 0
+    me = lax.axis_index("gx")
     width = min(128, cols)
     for t in range(cols // width):
         q = proj[:, t * width : (t + 1) * width]
@@ -527,24 +528,19 @@
             merged = jnp.where(head == h, mixed / total, merged)
         merged = merged.astype(BF16)
         for k in range(members):
-            out_refs[k][:, t * width : (t + 1) * width] = merged[k * own : (k + 1) * own]
-
-
-def place_kernel(members, keep_ref, *refs):
-    out_ref = refs[-1]
-    own, cols = refs[0].shape
-    me = lax.axis_index("gx")
+            out_ref[me ^ k, :, t * width : (t + 1) * width] = merged[k * own : (k + 1) * own]
+
+
+def place_kernel(keep_ref, got_ref, out_ref):
+    members, own, cols = got_ref.shape
     row = iota((8, cols), 0)
     keep = jnp.zeros((8, cols), F32)
     for b in range(4):
         keep = jnp.where(row // 2 == b, jnp.broadcast_to(keep_ref[b : b + 1, :cols], (8, cols)), keep)
     for k in range(members):
-        value = refs[k][...].astype(F32).reshape(own // 8, 8, cols)
+        value = got_ref[k].astype(F32).reshape(own // 8, 8, cols)
         value = jnp.where((keep > 0)[None], value, 0.0).reshape(own, cols).astype(BF16)
-        if cols % 128 == 0:
-            out_ref[0, :, pl.ds(pl.multiple_of((me ^ k) * cols, cols), cols)] = value
-        else:
-            out_ref[k] = value
+        out_ref[0, :, k * cols : (k + 1) * cols] = value
 
 
 VM = pl.BlockSpec(memory_space=pltpu.VMEM)
@@ -674,23 +670,15 @@
     blocks = [blocks[k] for k in range(nx)]
     outs = call(
         functools.partial(attend_kernel, nx), "attend", (VM,) * (2 + nx),
-        [shape(own, cols)] * nx, (keys, turned, *blocks),
+        shape(nx, own, cols), (keys, turned, *blocks),
         [pltpu.VMEM((own * nx, feats), BF16), pltpu.VMEM((own * nx, 3 * cols), BF16)],
         flops=10**9, nbytes=3 * 10**6, mib=16 if narrow else 40,
     )
-    outs = [outs[0]] + [lax.ppermute(outs[k], "gx", swaps[k]) for k in range(1, nx)]
-    lined = cols % 128 == 0
+    outs = lax.all_to_all(outs, "gx", 0, 0, tiled=True)
     attention = call(
-        functools.partial(place_kernel, nx), "place", (VM,) * (1 + nx),
-        shape(1, own, nx * cols) if lined else shape(nx, own, cols), (keep, *outs),
+        place_kernel, "place", (VM,) * 2, shape(1, own, nx * cols), (keep, outs),
         nbytes=3 * 10**5, mib=8,
     )
-    if not lined:
-        me = lax.axis_index("gx")
-        attention = jnp.concatenate(
-            [lax.dynamic_index_in_dim(attention, me ^ j, 0, keepdims=False) for j in range(nx)],
-            axis=1,
-        )[None]
     return (fine_out, attention)
 
 

time: 59.4 us -> 61 us (1.027)
  blocking collectives: 9.3 us -> 17.6 us
  starting transfers between devices: 14.6 us -> 10.2 us
  waiting for transfers between devices: 18.2 us -> 16 us
    all_to_all x0 -> x1, blocking collectives: none -> 8.31 us  [body(): outs = lax.all_to_all(outs, 'gx', 0, 0, tiled=True)]
    ppermute x3 -> x0, starting transfers between devices: 4.45 us -> none  [body(): lax.ppermute(outs[k], 'gx', swaps[k])]
    ppermute x3 -> x0, waiting for transfers between devices: 2.24 us -> none  [body(): lax.ppermute(outs[k], 'gx', swaps[k])]
  transfers between devices with their start and end apart: 13 -> 10, of which waited for: 7 -> 5; matrix products, arithmetic and copies ran while one was open for 1% -> 1% of each run, Pallas kernels for 8% -> 8%
where the time goes in v7:
time: 61 us; the launch traced here: 60.8 us
  blocking collectives  17.6 us (29%)
  waiting for transfers between devices  16 us (26%)
  Pallas kernels  13.1 us (21%)
  starting transfers between devices  10.2 us (17%)
  local copies, waits for them, and re-layouts  2.48 us (4%)
  other arithmetic  0.72 us (1%)
  between operations  0.71 us (1%)
    pallas_call x10, Pallas kernels, call(): pl.pallas_call(kernel, out_shape=out, in_specs=list(specs), out_specs=jax...  13.1 us
    ppermute x3, waiting for transfers between devices, body(): blocks[k] = lax.ppermute(blocks[k ^ low], 'gx', swaps[low])  11.2 us
    all_to_all x1, blocking collectives, body(): stats = lax.all_to_all(mine, ALL, 0, 0, tiled=True)  9.3 us
    all_to_all x1, blocking collectives, body(): outs = lax.all_to_all(outs, 'gx', 0, 0, tiled=True)  8.31 us
    ppermute x1, starting transfers between devices, body(): lax.ppermute(first, 'gx', list(pairing(nx, False, False).items()))  3.09 us
    unnamed x8, local copies, waits for them, and re-layouts  2.48 us
    ppermute x1, starting transfers between devices, body(): lax.ppermute(second, 'gx', list(pairing(nx, True, narrow).items()))  2.47 us
    ppermute x1, waiting for transfers between devices, body(): tails.append(lax.ppermute(tail, 'gx', [(i, i ^ 2) for i in range(nx)]))  2.16 us
  transfers between devices with their start and end apart: 10, of which 5 were waited for; matrix products, arithmetic and copies ran while one was open for 1% of the time, Pallas kernels for 8%

profile of v7, /device:TPU:0, one launch (start us, length us, event | category | flops | bytes accessed | tf_op | source)
XLA Modules:
  0.0 60.8 jit_solution(11753964981931041812)
XLA Ops:
  0.6 0.0 copy-start
  0.6 0.9 %copy-done = bf16[8,8,4,256]{3,2,1,0:T(4,128)(2,1)S(1)} copy-done((bf16[8,8,4,256]{3,2,1,0:T(4,128)(2,1)S(1)}, bf16[8,8,4,256]{3,2,1,0:T(4,128)(2,1)}, u32[]{:S(2)}) %copy-start) | copy-done | bytes 131096
  1.5 0.0 copy-start.2
  1.5 0.7 %copy-done.2 = s32[4,1,4]{2,1,0:T(1,128)S(1)} copy-done((s32[4,1,4]{2,1,0:T(1,128)S(1)}, s32[4,1,4]{2,1,0:T(1,128)}, u32[]{:S(2)}) %copy-start.2) | copy-done | bytes 88
  2.2 0.9 %pre.1 = (f32[8,256]{1,0:T(8,128)S(1)}, f32[8,256]{1,0:T(8,128)S(1)}, bf16[512,256]{1,0:T(8,128)(2,1)S(1)}, bf16[80,256]{1,0:T(8,128)(2,1)S(1)}, bf16[80,256]{1,...) custom-call(s32[4,1,4]{2,1,0:T(1,128)S(1)} %copy-done.2, bf16[8,8,4,256]{3,2,1,0:T(4,128)(2,1)S(1)} %copy-done), custom_call_target="tpu_custom_call" | custom-call | bytes 1000000 | tf_op jit(solution)/shard_map/pre/pallas_call | solution.py:550
  3.2 3.1 %collective-permute-start = (bf16[80,256]{1,0:T(8,128)(2,1)S(1)}, bf16[80,256]{1,0:T(8,128)(2,1)S(1)}, u32[]{:S(2)}, u32[]{:S(2)}) collective-permute-start(bf16[80,256]{1,0:T(8,128)(2,1)S(1)} %get-tuple-element.23), channel_id=1, source_target_pairs={{0,8},{8,0},{16,24},{24,16},{1,9},{9,1},{17,25},{25,17},{2,10},{10... | collective-permute-start | bytes 122888 | tf_op jit(solution)/shard_map/ppermute | solution.py:592
  6.3 2.5 %collective-permute-start.1 = (bf16[80,256]{1,0:T(8,128)(2,1)S(1)}, bf16[80,256]{1,0:T(8,128)(2,1)S(1)}, u32[]{:S(2)}, u32[]{:S(2)}) collective-permute-start(bf16[80,256]{1,0:T(8,128)(2,1)S(1)} %get-tuple-element.24), channel_id=1, source_target_pairs={{0,24},{8,16},{16,8},{24,0},{1,25},{9,17},{17,9},{25,1},{2,26},{10... | collective-permute-start | bytes 122888 | tf_op jit(solution)/shard_map/ppermute | solution.py:593
  8.7 0.1 collective-permute-start.2
  8.8 0.0 copy-start.1
  8.9 0.9 %copy-done.1 = bf16[2,32,864]{2,1,0:T(8,128)(2,1)S(1)} copy-done((bf16[2,32,864]{2,1,0:T(8,128)(2,1)S(1)}, bf16[2,32,864]{2,1,0:T(8,128)(2,1)}, u32[]{:S(2)}) %copy-start.1) | copy-done | bytes 110616
  9.7 1.4 %band0.1 = (bf16[3,1024,256]{2,1,0:T(8,128)(2,1)S(1)}, bf16[1,32,864]{2,1,0:T(8,128)(2,1)S(1)}) custom-call(bf16[2,32,864]{2,1,0:T(8,128)(2,1)S(1)} %copy-done.1), custom_call_target="tpu_custom_call" | custom-call | bytes 8000000 | tf_op jit(solution)/shard_map/band0/pallas_call | solution.py:550
  11.1 2.2 %collective-permute-done.2.rest_1_ = bf16[16,256]{1,0:T(8,128)(2,1)S(1)} collective-permute-done((bf16[16,256]{1,0:T(8,128)(2,1)S(1)}, bf16[16,256]{1,0:T(8,128)(2,1)S(1)}, u32[]{:S(2)}, u32[]{:S(2)}) %collective-permute-start.2) | collective-permute-done | bytes 8224 | tf_op jit(solution)/shard_map/ppermute | solution.py:597
  13.3 0.0 collective-permute-done.first_ref
  13.3 0.0 collective-permute-done.1.second_ref
  13.3 0.2 line.1
  13.5 0.1 collective-permute-start.3
  13.5 1.2 %collective-permute-done.3.other_ref.core_ref = bf16[112,256]{1,0:T(8,128)(2,1)S(1)} collective-permute-done((bf16[112,256]{1,0:T(8,128)(2,1)S(1)}, bf16[112,256]{1,0:T(8,128)(2,1)S(1)}, u32[]{:S(2)}, u32[]{:S(2)}) %collective-permute-start.3) | collective-permute-done | bytes 57376 | tf_op jit(solution)/shard_map/ppermute | solution.py:615
  14.8 0.2 chip.1
  15.0 1.6 %collective-permute-start.5 = (bf16[144,256]{1,0:T(8,128)(2,1)S(1)}, bf16[144,256]{1,0:T(8,128)(2,1)S(1)}, u32[]{:S(2)}, u32[]{:S(2)}) collective-permute-start(bf16[144,256]{1,0:T(8,128)(2,1)S(1)} %get-tuple-element.29), channel_id=1, source_target_pairs={{0,4},{4,0},{1,5},{5,1},{2,6},{6,2},{3,7},{7,3},{8,12},{12,8},{9,1... | collective-permute-start | bytes 221192 | tf_op jit(solution)/shard_map/ppermute | solution.py:633
  16.5 1.0 %collective-permute-start.4 = (bf16[112,256]{1,0:T(8,128)(2,1)S(1)}, bf16[112,256]{1,0:T(8,128)(2,1)S(1)}, u32[]{:S(2)}, u32[]{:S(2)}) collective-permute-start(bf16[112,256]{1,0:T(8,128)(2,1)S(1)} %get-tuple-element.28.own_ref), channel_id=1, source_target_pairs={{0,3},{1,2},{2,1},{3,0},{4,7},{5,6},{6,5},{7,4},{8,11},{9,10},{10,... | collective-permute-start | bytes 172040 | tf_op jit(solution)/shard_map/ppermute | solution.py:629
  17.5 0.7 %collective-permute-start.6 = (bf16[48,256]{1,0:T(8,128)(2,1)S(1)}, bf16[48,256]{1,0:T(8,128)(2,1)S(1)}, u32[]{:S(2)}, u32[]{:S(2)}) collective-permute-start(bf16[48,256]{1,0:T(8,128)(2,1)S(1)} %get-tuple-element.30), channel_id=1, source_target_pairs={{0,7},{1,6},{2,5},{3,4},{4,3},{5,2},{6,1},{7,0},{8,15},{9,14},{10,... | collective-permute-start | bytes 73736 | tf_op jit(solution)/shard_map/ppermute | solution.py:637
  18.3 0.7 %pad_maximum_fusion.rest_0_ = f32[6,32]{1,0:T(8,128)S(1)} fusion(f32[2,32]{1,0:T(2,128)} %param.12, f32[2,32]{1,0:T(2,128)} %param.10, f32[2,32]{1,0:T(2,128)} %param.9), kind=kLoop, calls=%fused_computation | loop fusion | flops 384 | bytes 1536 | tf_op jit(solution)/shard_map/concatenate | solution.py:599
  19.0 1.4 %band1.1 = (bf16[3,1024,256]{2,1,0:T(8,128)(2,1)S(1)}, f32[8,256]{1,0:T(8,128)S(1)}) custom-call(bf16[1,32,864]{2,1,0:T(8,128)(2,1)S(1)} %get-tuple-element.21._.weight_ref, f32[6,32]{1,0:T(8,128)S(1)} %pad_maximum_fusion.rest_0_), custom_call_target="tpu_custom_call" | custom-call | bytes 8000000 | tf_op jit(solution)/shard_map/band1/pallas_call | solution.py:550
  20.4 1.3 %collective-permute-done.6.rest_1_ = bf16[48,256]{1,0:T(8,128)(2,1)S(1)} collective-permute-done((bf16[48,256]{1,0:T(8,128)(2,1)S(1)}, bf16[48,256]{1,0:T(8,128)(2,1)S(1)}, u32[]{:S(2)}, u32[]{:S(2)}) %collective-permute-start.6) | collective-permute-done | bytes 24608 | tf_op jit(solution)/shard_map/ppermute | solution.py:637
  21.7 0.0 collective-permute-done.4.zface_ref
  21.7 0.0 collective-permute-done.5.rest_0_
  21.7 3.0 %first.1 = (f32[800,256]{1,0:T(8,128)S(1)}, f32[32,128]{1,0:T(8,128)S(1)}) custom-call(bf16[768,256]{1,0:T(8,128)(2,1)S(1)} %get-tuple-element.26.ext_ref, bf16[112,256]{1,0:T(8,128)(2,1)S(1)} %get-tuple-element.28.own_ref, bf16[112,256]{1,0:T(8,128)(2,1)S(1)} %collective-permute-done.3.other_ref.core_ref, ...), custom_call_target="tpu_custom_call" | custom-call | flops 2000000000 | bytes 4000000 | tf_op jit(solution)/shard_map/first/pallas_call | solution.py:550
  24.7 9.3 %all_to_all.16 = f32[32,1,128]{2,1,0:T(1,128)S(1)} all-to-all(f32[32,1,128]{2,1,0:T(1,128)S(1)} %bitcast.4), channel_id=1, replica_groups=mesh['gx'=4,'gy'=2,'gz'=4] {'gx','gy','gz'}, dimensions={0} | all-to-all | bytes 32768 | tf_op jit(solution)/shard_map/all_to_all | solution.py:657
  34.0 0.0 copy-start.3
  34.0 2.2 %second.1 = (bf16[8,8,4,256]{3,2,1,0:T(4,128)(2,1)}, bf16[64,1024]{1,0:T(8,128)(2,1)S(1)}) custom-call(f32[32,128]{1,0:T(8,128)S(1)} %bitcast.5, f32[800,256]{1,0:T(8,128)S(1)} %get-tuple-element.35.mid_ref, bf16[3,1024,256]{2,1,0:T(8,128)(2,1)S(1)} %get-tuple-element.36.weight_ref, f32[8,256]{1,0:T(8,128)S(1)} %get-tuple-element.33.rest_4_.rows_ref, ...), custom_call_target="tpu_custom_call" | custom-call | flops 1000000000 | bytes 4000000 | tf_op jit(solution)/shard_map/second/pallas_call | solution.py:550
  36.1 0.6 collective-permute-start.8
  36.7 0.5 collective-permute-start.7
  37.3 7.7 %collective-permute-done.8.refs_2_ = bf16[64,1024]{1,0:T(8,128)(2,1)S(1)} collective-permute-done((bf16[64,1024]{1,0:T(8,128)(2,1)S(1)}, bf16[64,1024]{1,0:T(8,128)(2,1)S(1)}, u32[]{:S(2)}, u32[]{:S(2)}) %collective-permute-start.8) | collective-permute-done | bytes 131104 | tf_op jit(solution)/shard_map/ppermute | solution.py:669
  45.0 0.0 collective-permute-start.9
  45.0 0.0 copy-done.3
  45.0 1.9 %turn.1.weight_ref = bf16[1024,768]{1,0:T(8,128)(2,1)S(1)} custom-call(bf16[3,256,1024]{2,1,0:T(8,128)(2,1)S(1)} %copy-done.3), custom_call_target="tpu_custom_call" | custom-call | flops 1610612736 | bytes 6000000 | tf_op jit(solution)/shard_map/turn/pallas_call | solution.py:550
  46.9 0.0 collective-permute-done.7.refs_1_
  46.9 3.5 %collective-permute-done.9.refs_3_ = bf16[64,1024]{1,0:T(8,128)(2,1)S(1)} collective-permute-done((bf16[64,1024]{1,0:T(8,128)(2,1)S(1)}, bf16[64,1024]{1,0:T(8,128)(2,1)S(1)}, u32[]{:S(2)}, u32[]{:S(2)}) %collective-permute-start.9) | collective-permute-done | bytes 131104 | tf_op jit(solution)/shard_map/ppermute | solution.py:669
  50.4 1.4 %attend.1 = bf16[4,64,256]{2,1,0:T(8,128)(2,1)S(1)} custom-call(f32[8,256]{1,0:T(8,128)S(1)} %get-tuple-element.38.keys_ref, bf16[1024,768]{1,0:T(8,128)(2,1)S(1)} %turn.1.weight_ref, bf16[64,1024]{1,0:T(8,128)(2,1)S(1)} %get-tuple-element.39.refs_0_, bf16[64,1024]{1,0:T(8,128)(2,1)S(1)} %collective-permute-done.7.refs_1_, ...), custom_call_target="tpu_custom_call" | custom-call | flops 1000000000 | bytes 3000000 | tf_op jit(solution)/shard_map/attend/pallas_call | solution.py:550
  51.8 8.3 %all_to_all.17.got_ref = bf16[4,64,256]{2,1,0:T(8,128)(2,1)S(1)} all-to-all(bf16[4,64,256]{2,1,0:T(8,128)(2,1)S(1)} %attend.1), channel_id=1, replica_groups=mesh['gx'=4,'gy'=2,'gz'=4] {'gx'}, dimensions={0} | all-to-all | bytes 262144 | tf_op jit(solution)/shard_map/all_to_all | solution.py:677
  60.1 0.7 %place.1 = bf16[1,64,1024]{2,1,0:T(8,128)(2,1)} custom-call(f32[8,256]{1,0:T(8,128)S(1)} %get-tuple-element.31.rest_2_.keep_ref, bf16[4,64,256]{2,1,0:T(8,128)(2,1)S(1)} %all_to_all.17.got_ref), custom_call_target="tpu_custom_call" | custom-call | bytes 300000 | tf_op jit(solution)/shard_map/place/pallas_call | solution.py:550
Async XLA Ops:
  0.6 0.9 %copy-start = (bf16[8,8,4,256]{3,2,1,0:T(4,128)(2,1)S(1)}, bf16[8,8,4,256]{3,2,1,0:T(4,128)(2,1)}, u32[]{:S(2)}) copy-start(bf16[8,8,4,256]{3,2,1,0:T(4,128)(2,1)} %feat_ref.1) | copy-start | bytes 393220
  1.5 0.7 %copy-start.2 = (s32[4,1,4]{2,1,0:T(1,128)S(1)}, s32[4,1,4]{2,1,0:T(1,128)}, u32[]{:S(2)}) copy-start(s32[4,1,4]{2,1,0:T(1,128)} %occ_ref.1) | copy-start | bytes 196
  3.2 10.1 %collective-permute-start = (bf16[80,256]{1,0:T(8,128)(2,1)S(1)}, bf16[80,256]{1,0:T(8,128)(2,1)S(1)}, u32[]{:S(2)}, u32[]{:S(2)}) collective-permute-start(bf16[80,256]{1,0:T(8,128)(2,1)S(1)} %get-tuple-element.23), channel_id=1, source_target_pairs={{0,8},{8,0},{16,24},{24,16},{1,9},{9,1},{17,25},{25,17},{2,10},{10... | collective-permute-start | bytes 122888 | tf_op jit(solution)/shard_map/ppermute | solution.py:592
  6.3 7.0 %collective-permute-start.1 = (bf16[80,256]{1,0:T(8,128)(2,1)S(1)}, bf16[80,256]{1,0:T(8,128)(2,1)S(1)}, u32[]{:S(2)}, u32[]{:S(2)}) collective-permute-start(bf16[80,256]{1,0:T(8,128)(2,1)S(1)} %get-tuple-element.24), channel_id=1, source_target_pairs={{0,24},{8,16},{16,8},{24,0},{1,25},{9,17},{17,9},{25,1},{2,26},{10... | collective-permute-start | bytes 122888 | tf_op jit(solution)/shard_map/ppermute | solution.py:593
  8.7 4.5 %collective-permute-start.2 = (bf16[16,256]{1,0:T(8,128)(2,1)S(1)}, bf16[16,256]{1,0:T(8,128)(2,1)S(1)}, u32[]{:S(2)}, u32[]{:S(2)}) collective-permute-start(bf16[16,256]{1,0:T(8,128)(2,1)S(1)} %get-tuple-element.25.rest_0_), channel_id=1, source_target_pairs={{0,16},{8,24},{16,0},{24,8},{1,17},{9,25},{17,1},{25,9},{2,18},{10... | collective-permute-start | bytes 24584 | tf_op jit(solution)/shard_map/ppermute | solution.py:597
  8.8 0.9 %copy-start.1 = (bf16[2,32,864]{2,1,0:T(8,128)(2,1)S(1)}, bf16[2,32,864]{2,1,0:T(8,128)(2,1)}, u32[]{:S(2)}) copy-start(bf16[2,32,864]{2,1,0:T(8,128)(2,1)} %weight_ref.2) | copy-start | bytes 331780
  13.5 1.3 %collective-permute-start.3 = (bf16[112,256]{1,0:T(8,128)(2,1)S(1)}, bf16[112,256]{1,0:T(8,128)(2,1)S(1)}, u32[]{:S(2)}, u32[]{:S(2)}) collective-permute-start(bf16[112,256]{1,0:T(8,128)(2,1)S(1)} %get-tuple-element.27.own_ref), channel_id=1, source_target_pairs={{0,1},{1,0},{2,3},{3,2},{4,5},{5,4},{6,7},{7,6},{8,9},{9,8},{10,11... | collective-permute-start | bytes 172040 | tf_op jit(solution)/shard_map/ppermute | solution.py:615
  15.0 6.7 %collective-permute-start.5 = (bf16[144,256]{1,0:T(8,128)(2,1)S(1)}, bf16[144,256]{1,0:T(8,128)(2,1)S(1)}, u32[]{:S(2)}, u32[]{:S(2)}) collective-permute-start(bf16[144,256]{1,0:T(8,128)(2,1)S(1)} %get-tuple-element.29), channel_id=1, source_target_pairs={{0,4},{4,0},{1,5},{5,1},{2,6},{6,2},{3,7},{7,3},{8,12},{12,8},{9,1... | collective-permute-start | bytes 221192 | tf_op jit(solution)/shard_map/ppermute | solution.py:633
  16.5 5.2 %collective-permute-start.4 = (bf16[112,256]{1,0:T(8,128)(2,1)S(1)}, bf16[112,256]{1,0:T(8,128)(2,1)S(1)}, u32[]{:S(2)}, u32[]{:S(2)}) collective-permute-start(bf16[112,256]{1,0:T(8,128)(2,1)S(1)} %get-tuple-element.28.own_ref), channel_id=1, source_target_pairs={{0,3},{1,2},{2,1},{3,0},{4,7},{5,6},{6,5},{7,4},{8,11},{9,10},{10,... | collective-permute-start | bytes 172040 | tf_op jit(solution)/shard_map/ppermute | solution.py:629
  17.5 4.2 %collective-permute-start.6 = (bf16[48,256]{1,0:T(8,128)(2,1)S(1)}, bf16[48,256]{1,0:T(8,128)(2,1)S(1)}, u32[]{:S(2)}, u32[]{:S(2)}) collective-permute-start(bf16[48,256]{1,0:T(8,128)(2,1)S(1)} %get-tuple-element.30), channel_id=1, source_target_pairs={{0,7},{1,6},{2,5},{3,4},{4,3},{5,2},{6,1},{7,0},{8,15},{9,14},{10,... | collective-permute-start | bytes 73736 | tf_op jit(solution)/shard_map/ppermute | solution.py:637
  34.0 11.0 %copy-start.3 = (bf16[3,256,1024]{2,1,0:T(8,128)(2,1)S(1)}, bf16[3,256,1024]{2,1,0:T(8,128)(2,1)}, u32[]{:S(2)}) copy-start(bf16[3,256,1024]{2,1,0:T(8,128)(2,1)} %weight_ref.3) | copy-start | bytes 4718596
  36.1 8.9 %collective-permute-start.8 = (bf16[64,1024]{1,0:T(8,128)(2,1)S(1)}, bf16[64,1024]{1,0:T(8,128)(2,1)S(1)}, u32[]{:S(2)}, u32[]{:S(2)}) collective-permute-start(bf16[64,1024]{1,0:T(8,128)(2,1)S(1)} %get-tuple-element.39.refs_0_), channel_id=1, source_target_pairs={{0,16},{8,24},{16,0},{24,8},{1,17},{9,25},{17,1},{25,9},{2,18},{10... | collective-permute-start | bytes 393224 | tf_op jit(solution)/shard_map/ppermute | solution.py:669
  36.7 10.2 %collective-permute-start.7 = (bf16[64,1024]{1,0:T(8,128)(2,1)S(1)}, bf16[64,1024]{1,0:T(8,128)(2,1)S(1)}, u32[]{:S(2)}, u32[]{:S(2)}) collective-permute-start(bf16[64,1024]{1,0:T(8,128)(2,1)S(1)} %get-tuple-element.39.refs_0_), channel_id=1, source_target_pairs={{0,8},{8,0},{16,24},{24,16},{1,9},{9,1},{17,25},{25,17},{2,10},{10... | collective-permute-start | bytes 393224 | tf_op jit(solution)/shard_map/ppermute | solution.py:669
  45.0 5.4 %collective-permute-start.9 = (bf16[64,1024]{1,0:T(8,128)(2,1)S(1)}, bf16[64,1024]{1,0:T(8,128)(2,1)S(1)}, u32[]{:S(2)}, u32[]{:S(2)}) collective-permute-start(bf16[64,1024]{1,0:T(8,128)(2,1)S(1)} %collective-permute-done.8.refs_2_), channel_id=1, source_target_pairs={{0,8},{8,0},{16,24},{24,16},{1,9},{9,1},{17,25},{25,17},{2,10},{10... | collective-permute-start | bytes 393224 | tf_op jit(solution)/shard_map/ppermute | solution.py:669

commit v8 on v6

--- a/solution.py
+++ b/solution.py
@@ -362,7 +362,7 @@
     stats_ref = None
     if not narrow:
         stats_ref, rest = rest[0], rest[1:]
-    keep_ref, weight_ref, rows_ref, mid_ref, out_ref, buf, lhs, msk = rest
+    keep_ref, weight_ref, rows_ref, mid_ref, out_ref, msk, buf, lhs = rest
     lanes = ext_ref.shape[1]
     ex = ext_ref.shape[0] // (sy * 8)
     ey = sy + 4
@@ -440,23 +440,21 @@
 
     mine = moments(over_cells(lambda v: v), squares_about, entries)
     out_ref[...] = jnp.broadcast_to(to_row(mine)[0:1], out_ref.shape)
-    for x in range(ox):
-        rows = slice(x * oy * 8, (x + 1) * oy * 8)
-        there = msk[(x + 1) * step + 8 : (x + 2) * step - 8]
-        there = jnp.concatenate([there] * (lanes // 128), axis=1) > 0
-        mid_ref[rows] = jnp.where(there, mid_ref[rows], BIG)
-
-
-def second_kernel(stats_ref, mid_ref, weight_ref, rows_ref, coded_ref, fine_ref, tok_ref, lhs):
-    sx, sy, sb, lanes = fine_ref.shape
-    step = (sy + 2) * 8
+
+
+def second_kernel(sx, sy, sb, stats_ref, mid_ref, msk_ref, weight_ref, rows_ref, coded_ref,
+                  field_ref, tok_ref, lhs):
+    lanes = coded_ref.shape[1]
+    step, ext = (sy + 2) * 8, (sy + 4) * 8
     centre, scale = from_rows(stats_ref[...])
     gain, shift, bias = rows_ref[1:2], rows_ref[3:4], rows_ref[5:6]
     scale = scale * gain
     half = sy // 2 * 8
     for x in range(sx + 2):
         v = mid_ref[x * step : (x + 1) * step]
-        act = jnp.where(v < BIG, silu((v - centre) * scale + shift), 0.0)
+        there = msk_ref[(x + 1) * ext + 8 : (x + 2) * ext - 8]
+        there = jnp.concatenate([there] * (lanes // 128), axis=1) > 0
+        act = jnp.where(there, silu((v - centre) * scale + shift), 0.0)
         for e, part in enumerate(columns(act.reshape(sy + 2, 8, lanes), sy)):
             lhs[x * half : (x + 1) * half, e * lanes : (e + 1) * lanes] = (
                 pack_pairs(part[None]).reshape(half, lanes).astype(BF16)
@@ -471,10 +469,7 @@
     field = field.reshape(size, lanes)
     out = jnp.where(field != SENT, field + acc, 0.0).reshape(-1, 8, lanes)
     out = out.astype(BF16)
-    wide = out.astype(F32)
-    other = pltpu.roll(wide, 4, 1)
-    fine = jnp.stack([wide[:, :sb], other[:, :sb]], axis=1)
-    fine_ref[...] = fine.reshape(sx, sy, sb, lanes).astype(BF16)
+    field_ref[...] = out.reshape(size, lanes)
     i, j = iota((lanes, lanes), 0), iota((lanes, lanes), 1)
     pick = onehot(i == (j % 128) // 4 * 8 + j // 128 * 4 + j % 4)
     moved = jnp.dot(out.reshape(size, lanes), pick, preferred_element_type=F32).reshape(
@@ -497,6 +492,14 @@
     i, j = iota((n, n), 0), iota((n, n), 1)
     order = onehot(j == i // 8 * 8 + i % 2 * 4 + i % 8 // 2)
     tok_ref[...] = jnp.dot(order, tokens, preferred_element_type=F32).astype(BF16)
+
+
+def fine_kernel(field_ref, fine_ref):
+    sx, sy, sb, lanes = fine_ref.shape
+    wide = field_ref[...].astype(F32).reshape(-1, 8, lanes)
+    other = pltpu.roll(wide, 4, 1)
+    fine = jnp.stack([wide[:, :sb], other[:, :sb]], axis=1)
+    fine_ref[...] = fine.reshape(sx, sy, sb, lanes).astype(BF16)
 
 
 def attend_kernel(members, keys_ref, weight_ref, *refs):
@@ -648,23 +651,26 @@
 
     ey, oy = sy + 4, sy + 2
     size = (sx + 2) * oy * 8
-    mid, mine = call(
+    mid, mine, there = call(
         functools.partial(first_kernel, narrow, faces, sy, sb), "first",
         (VM,) * (7 + 2 * faces + len(stats)),
-        [shape(size, lanes, dtype=F32), shape(devices, 128, dtype=F32)],
+        [shape(size, lanes, dtype=F32), shape(devices, 128, dtype=F32),
+         shape(ex * ey * 8, 128, dtype=F32)],
         (ext, own_tail, core, zgot, *ygot, *stats, keep, band0, rows),
         [pltpu.VMEM((lanes // 128, ex * ey * 8, 128), F32),
-         pltpu.VMEM((ex * oy * 8, 4 * lanes), BF16),
-         pltpu.VMEM((ex * ey * 8, 128), F32)],
+         pltpu.VMEM((ex * oy * 8, 4 * lanes), BF16)],
         flops=2 * 10**9, nbytes=4 * 10**6, mib=20,
     )
     stats = lax.all_to_all(mine, ALL, 0, 0, tiled=True)
-    fine_out, tokens = call(
-        second_kernel, "second", (VM,) * 5,
-        [shape(*features.shape), shape(own, feats)],
-        (stats, mid, band1, rows, coded),
+    field, tokens = call(
+        functools.partial(second_kernel, sx, sy, sb), "second", (VM,) * 6,
+        [shape(sx * sy * 4, lanes), shape(own, feats)],
+        (stats, mid, there, band1, rows, coded),
         [pltpu.VMEM(((sx + 2) * sy * 4, 4 * lanes), BF16)],
         flops=10**9, nbytes=4 * 10**6,
+    )
+    fine_out = call(
+        fine_kernel, "fine", (VM,), shape(*features.shape), (field,), nbytes=4 * 10**6, mib=8,
     )
     swaps = [[(i, i ^ k) for i in range(nx)] for k in range(nx)]
     blocks = {0: tokens}

time: 59 us -> 58.8 us (level)
  waiting for transfers between devices: 17.9 us -> 17.2 us
    ppermute x3, waiting for transfers between devices: 1.89 us -> 1.2 us  [body(): lax.ppermute(v, 'gx', swaps[nx - 1 - i])]
    pallas_call x10 -> x11, Pallas kernels: 13.1 us -> 13.5 us  [call(): pl.pallas_call(kernel, out_shape=out, in_specs=list(specs), out_specs=jax...]
  transfers between devices with their start and end apart: 13 -> 13, of which waited for: 7 -> 7; matrix products, arithmetic and copies ran while one was open for 1% -> 1% of each run, Pallas kernels for 8% -> 9%
where the time goes in v8:
time: 58.8 us; the launch traced here: 58.5 us
  waiting for transfers between devices  17.2 us (29%)
  starting transfers between devices  14.7 us (25%)
  Pallas kernels  13.5 us (23%)
  blocking collectives  9.3 us (16%)
  local copies, waits for them, and re-layouts  2.48 us (4%)
  other arithmetic  0.72 us (1%)
  between operations  0.72 us (1%)
    pallas_call x11, Pallas kernels, call(): pl.pallas_call(kernel, out_shape=out, in_specs=list(specs), out_specs=jax...  13.5 us
    ppermute x3, waiting for transfers between devices, body(): blocks[k] = lax.ppermute(blocks[k ^ low], 'gx', swaps[low])  11.2 us
    all_to_all x1, blocking collectives, body(): stats = lax.all_to_all(mine, ALL, 0, 0, tiled=True)  9.3 us
    ppermute x3, starting transfers between devices, body(): lax.ppermute(v, 'gx', swaps[nx - 1 - i])  4.45 us
    ppermute x1, starting transfers between devices, body(): lax.ppermute(first, 'gx', list(pairing(nx, False, False).items()))  3.09 us
    unnamed x8, local copies, waits for them, and re-layouts  2.48 us
    ppermute x1, starting transfers between devices, body(): lax.ppermute(second, 'gx', list(pairing(nx, True, narrow).items()))  2.47 us
    ppermute x1, waiting for transfers between devices, body(): tails.append(lax.ppermute(tail, 'gx', [(i, i ^ 2) for i in range(nx)]))  2.16 us
  transfers between devices with their start and end apart: 13, of which 7 were waited for; matrix products, arithmetic and copies ran while one was open for 1% of the time, Pallas kernels for 9%

profile of v8, /device:TPU:0, one launch (start us, length us, event | category | flops | bytes accessed | tf_op | source)
XLA Modules:
  0.0 58.5 jit_solution(7110733060983941487)
XLA Ops:
  0.6 0.0 copy-start
  0.6 0.9 %copy-done = bf16[8,8,4,256]{3,2,1,0:T(4,128)(2,1)S(1)} copy-done((bf16[8,8,4,256]{3,2,1,0:T(4,128)(2,1)S(1)}, bf16[8,8,4,256]{3,2,1,0:T(4,128)(2,1)}, u32[]{:S(2)}) %copy-start) | copy-done | bytes 131096
  1.5 0.0 copy-start.2
  1.5 0.7 %copy-done.2 = s32[4,1,4]{2,1,0:T(1,128)S(1)} copy-done((s32[4,1,4]{2,1,0:T(1,128)S(1)}, s32[4,1,4]{2,1,0:T(1,128)}, u32[]{:S(2)}) %copy-start.2) | copy-done | bytes 88
  2.2 0.9 %pre.1 = (f32[8,256]{1,0:T(8,128)S(1)}, f32[8,256]{1,0:T(8,128)S(1)}, bf16[512,256]{1,0:T(8,128)(2,1)S(1)}, bf16[80,256]{1,0:T(8,128)(2,1)S(1)}, bf16[80,256]{1,...) custom-call(s32[4,1,4]{2,1,0:T(1,128)S(1)} %copy-done.2, bf16[8,8,4,256]{3,2,1,0:T(4,128)(2,1)S(1)} %copy-done), custom_call_target="tpu_custom_call" | custom-call | bytes 1000000 | tf_op jit(solution)/shard_map/pre/pallas_call | solution.py:557
  3.2 3.1 %collective-permute-start = (bf16[80,256]{1,0:T(8,128)(2,1)S(1)}, bf16[80,256]{1,0:T(8,128)(2,1)S(1)}, u32[]{:S(2)}, u32[]{:S(2)}) collective-permute-start(bf16[80,256]{1,0:T(8,128)(2,1)S(1)} %get-tuple-element.28), channel_id=1, source_target_pairs={{0,8},{8,0},{16,24},{24,16},{1,9},{9,1},{17,25},{25,17},{2,10},{10... | collective-permute-start | bytes 122888 | tf_op jit(solution)/shard_map/ppermute | solution.py:599
  6.3 2.5 %collective-permute-start.1 = (bf16[80,256]{1,0:T(8,128)(2,1)S(1)}, bf16[80,256]{1,0:T(8,128)(2,1)S(1)}, u32[]{:S(2)}, u32[]{:S(2)}) collective-permute-start(bf16[80,256]{1,0:T(8,128)(2,1)S(1)} %get-tuple-element.29), channel_id=1, source_target_pairs={{0,24},{8,16},{16,8},{24,0},{1,25},{9,17},{17,9},{25,1},{2,26},{10... | collective-permute-start | bytes 122888 | tf_op jit(solution)/shard_map/ppermute | solution.py:600
  8.7 0.1 collective-permute-start.2
  8.8 0.0 copy-start.1
  8.9 0.9 %copy-done.1 = bf16[2,32,864]{2,1,0:T(8,128)(2,1)S(1)} copy-done((bf16[2,32,864]{2,1,0:T(8,128)(2,1)S(1)}, bf16[2,32,864]{2,1,0:T(8,128)(2,1)}, u32[]{:S(2)}) %copy-start.1) | copy-done | bytes 110616
  9.7 1.4 %band0.1 = (bf16[3,1024,256]{2,1,0:T(8,128)(2,1)S(1)}, bf16[1,32,864]{2,1,0:T(8,128)(2,1)S(1)}) custom-call(bf16[2,32,864]{2,1,0:T(8,128)(2,1)S(1)} %copy-done.1), custom_call_target="tpu_custom_call" | custom-call | bytes 8000000 | tf_op jit(solution)/shard_map/band0/pallas_call | solution.py:557
  11.1 2.2 %collective-permute-done.2.rest_1_ = bf16[16,256]{1,0:T(8,128)(2,1)S(1)} collective-permute-done((bf16[16,256]{1,0:T(8,128)(2,1)S(1)}, bf16[16,256]{1,0:T(8,128)(2,1)S(1)}, u32[]{:S(2)}, u32[]{:S(2)}) %collective-permute-start.2) | collective-permute-done | bytes 8224 | tf_op jit(solution)/shard_map/ppermute | solution.py:604
  13.3 0.0 collective-permute-done.first_ref
  13.3 0.0 collective-permute-done.1.second_ref
  13.3 0.2 line.1
  13.5 0.1 collective-permute-start.3
  13.5 1.2 %collective-permute-done.3.other_ref.core_ref = bf16[112,256]{1,0:T(8,128)(2,1)S(1)} collective-permute-done((bf16[112,256]{1,0:T(8,128)(2,1)S(1)}, bf16[112,256]{1,0:T(8,128)(2,1)S(1)}, u32[]{:S(2)}, u32[]{:S(2)}) %collective-permute-start.3) | collective-permute-done | bytes 57376 | tf_op jit(solution)/shard_map/ppermute | solution.py:622
  14.8 0.2 chip.1
  15.0 1.6 %collective-permute-start.5 = (bf16[144,256]{1,0:T(8,128)(2,1)S(1)}, bf16[144,256]{1,0:T(8,128)(2,1)S(1)}, u32[]{:S(2)}, u32[]{:S(2)}) collective-permute-start(bf16[144,256]{1,0:T(8,128)(2,1)S(1)} %get-tuple-element.34), channel_id=1, source_target_pairs={{0,4},{4,0},{1,5},{5,1},{2,6},{6,2},{3,7},{7,3},{8,12},{12,8},{9,1... | collective-permute-start | bytes 221192 | tf_op jit(solution)/shard_map/ppermute | solution.py:640
  16.5 1.0 %collective-permute-start.4 = (bf16[112,256]{1,0:T(8,128)(2,1)S(1)}, bf16[112,256]{1,0:T(8,128)(2,1)S(1)}, u32[]{:S(2)}, u32[]{:S(2)}) collective-permute-start(bf16[112,256]{1,0:T(8,128)(2,1)S(1)} %get-tuple-element.33.own_ref), channel_id=1, source_target_pairs={{0,3},{1,2},{2,1},{3,0},{4,7},{5,6},{6,5},{7,4},{8,11},{9,10},{10,... | collective-permute-start | bytes 172040 | tf_op jit(solution)/shard_map/ppermute | solution.py:636
  17.5 0.7 %collective-permute-start.6 = (bf16[48,256]{1,0:T(8,128)(2,1)S(1)}, bf16[48,256]{1,0:T(8,128)(2,1)S(1)}, u32[]{:S(2)}, u32[]{:S(2)}) collective-permute-start(bf16[48,256]{1,0:T(8,128)(2,1)S(1)} %get-tuple-element.35), channel_id=1, source_target_pairs={{0,7},{1,6},{2,5},{3,4},{4,3},{5,2},{6,1},{7,0},{8,15},{9,14},{10,... | collective-permute-start | bytes 73736 | tf_op jit(solution)/shard_map/ppermute | solution.py:644
  18.3 0.7 %pad_maximum_fusion.rest_0_ = f32[6,32]{1,0:T(8,128)S(1)} fusion(f32[2,32]{1,0:T(2,128)} %param.12, f32[2,32]{1,0:T(2,128)} %param.10, f32[2,32]{1,0:T(2,128)} %param.9), kind=kLoop, calls=%fused_computation | loop fusion | flops 384 | bytes 1536 | tf_op jit(solution)/shard_map/concatenate | solution.py:606
  19.0 1.4 %band1.1 = (bf16[3,1024,256]{2,1,0:T(8,128)(2,1)S(1)}, f32[8,256]{1,0:T(8,128)S(1)}) custom-call(bf16[1,32,864]{2,1,0:T(8,128)(2,1)S(1)} %get-tuple-element.26._.weight_ref, f32[6,32]{1,0:T(8,128)S(1)} %pad_maximum_fusion.rest_0_), custom_call_target="tpu_custom_call" | custom-call | bytes 8000000 | tf_op jit(solution)/shard_map/band1/pallas_call | solution.py:557
  20.4 1.3 %collective-permute-done.6.rest_1_ = bf16[48,256]{1,0:T(8,128)(2,1)S(1)} collective-permute-done((bf16[48,256]{1,0:T(8,128)(2,1)S(1)}, bf16[48,256]{1,0:T(8,128)(2,1)S(1)}, u32[]{:S(2)}, u32[]{:S(2)}) %collective-permute-start.6) | collective-permute-done | bytes 24608 | tf_op jit(solution)/shard_map/ppermute | solution.py:644
  21.7 0.0 collective-permute-done.4.zface_ref
  21.7 0.0 collective-permute-done.5.rest_0_
  21.7 3.0 %first.1 = (f32[800,256]{1,0:T(8,128)S(1)}, f32[32,128]{1,0:T(8,128)S(1)}, f32[1152,128]{1,0:T(8,128)S(1)}) custom-call(bf16[768,256]{1,0:T(8,128)(2,1)S(1)} %get-tuple-element.31.ext_ref, bf16[112,256]{1,0:T(8,128)(2,1)S(1)} %get-tuple-element.33.own_ref, bf16[112,256]{1,0:T(8,128)(2,1)S(1)} %collective-permute-done.3.other_ref.core_ref, ...), custom_call_target="tpu_custom_call" | custom-call | flops 2000000000 | bytes 4000000 | tf_op jit(solution)/shard_map/first/pallas_call | solution.py:557
  24.7 9.3 %all_to_all.11 = f32[32,1,128]{2,1,0:T(1,128)S(1)} all-to-all(f32[32,1,128]{2,1,0:T(1,128)S(1)} %bitcast.4), channel_id=1, replica_groups=mesh['gx'=4,'gy'=2,'gz'=4] {'gx','gy','gz'}, dimensions={0} | all-to-all | bytes 32768 | tf_op jit(solution)/shard_map/all_to_all | solution.py:664
  34.0 0.0 copy-start.3
  34.0 1.8 %second.1 = (bf16[256,256]{1,0:T(8,128)(2,1)S(1)}, bf16[64,1024]{1,0:T(8,128)(2,1)S(1)}) custom-call(f32[32,128]{1,0:T(8,128)S(1)} %bitcast.5, f32[800,256]{1,0:T(8,128)S(1)} %get-tuple-element.40.mid_ref, f32[1152,128]{1,0:T(8,128)S(1)} %get-tuple-element.41.msk_ref, bf16[3,1024,256]{2,1,0:T(8,128)(2,1)S(1)} %get-tuple-element.42.weight_ref, ...), custom_call_target="tpu_custom_call" | custom-call | flops 1000000000 | bytes 4000000 | tf_op jit(solution)/shard_map/second/pallas_call | solution.py:557
  35.8 0.7 %collective-permute-start.8 = (bf16[64,1024]{1,0:T(8,128)(2,1)S(1)}, bf16[64,1024]{1,0:T(8,128)(2,1)S(1)}, u32[]{:S(2)}, u32[]{:S(2)}) collective-permute-start(bf16[64,1024]{1,0:T(8,128)(2,1)S(1)} %get-tuple-element.45.refs_0_), channel_id=1, source_target_pairs={{0,16},{8,24},{16,0},{24,8},{1,17},{9,25},{17,1},{25,9},{2,18},{10... | collective-permute-start | bytes 393224 | tf_op jit(solution)/shard_map/ppermute | solution.py:679
  36.5 0.5 collective-permute-start.7
  37.0 7.7 %collective-permute-done.8.refs_2_ = bf16[64,1024]{1,0:T(8,128)(2,1)S(1)} collective-permute-done((bf16[64,1024]{1,0:T(8,128)(2,1)S(1)}, bf16[64,1024]{1,0:T(8,128)(2,1)S(1)}, u32[]{:S(2)}, u32[]{:S(2)}) %collective-permute-start.8) | collective-permute-done | bytes 131104 | tf_op jit(solution)/shard_map/ppermute | solution.py:679
  44.7 0.0 collective-permute-start.9
  44.7 0.0 copy-done.3
  44.7 1.9 %turn.1.weight_ref = bf16[1024,768]{1,0:T(8,128)(2,1)S(1)} custom-call(bf16[3,256,1024]{2,1,0:T(8,128)(2,1)S(1)} %copy-done.3), custom_call_target="tpu_custom_call" | custom-call | flops 1610612736 | bytes 6000000 | tf_op jit(solution)/shard_map/turn/pallas_call | solution.py:557
  46.6 0.0 collective-permute-done.7.refs_1_
  46.7 3.5 %collective-permute-done.9.refs_3_ = bf16[64,1024]{1,0:T(8,128)(2,1)S(1)} collective-permute-done((bf16[64,1024]{1,0:T(8,128)(2,1)S(1)}, bf16[64,1024]{1,0:T(8,128)(2,1)S(1)}, u32[]{:S(2)}, u32[]{:S(2)}) %collective-permute-start.9) | collective-permute-done | bytes 131104 | tf_op jit(solution)/shard_map/ppermute | solution.py:679
  50.1 1.4 %attend.1 = (bf16[64,256]{1,0:T(8,128)(2,1)S(1)}, bf16[64,256]{1,0:T(8,128)(2,1)S(1)}, bf16[64,256]{1,0:T(8,128)(2,1)S(1)}, bf16[64,256]{1,0:T(8,128)(2,1)S(1)}) custom-call(f32[8,256]{1,0:T(8,128)S(1)} %get-tuple-element.44.keys_ref, bf16[1024,768]{1,0:T(8,128)(2,1)S(1)} %turn.1.weight_ref, bf16[64,1024]{1,0:T(8,128)(2,1)S(1)} %get-tuple-element.45.refs_0_, ...), custom_call_target="tpu_custom_call" | custom-call | flops 1000000000 | bytes 3000000 | tf_op jit(solution)/shard_map/attend/pallas_call | solution.py:557
  51.5 0.3 collective-permute-start.10
  51.8 1.5 %collective-permute-start.11 = (bf16[64,256]{1,0:T(8,128)(2,1)S(1)}, bf16[64,256]{1,0:T(8,128)(2,1)S(1)}, u32[]{:S(2)}, u32[]{:S(2)}) collective-permute-start(bf16[64,256]{1,0:T(8,128)(2,1)S(1)} %get-tuple-element.47), channel_id=1, source_target_pairs={{0,16},{8,24},{16,0},{24,8},{1,17},{9,25},{17,1},{25,9},{2,18},{10... | collective-permute-start | bytes 98312 | tf_op jit(solution)/shard_map/ppermute | solution.py:687
  53.3 2.6 %collective-permute-start.12 = (bf16[64,256]{1,0:T(8,128)(2,1)S(1)}, bf16[64,256]{1,0:T(8,128)(2,1)S(1)}, u32[]{:S(2)}, u32[]{:S(2)}) collective-permute-start(bf16[64,256]{1,0:T(8,128)(2,1)S(1)} %get-tuple-element.48), channel_id=1, source_target_pairs={{0,8},{8,0},{16,24},{24,16},{1,9},{9,1},{17,25},{25,17},{2,10},{10... | collective-permute-start | bytes 98312 | tf_op jit(solution)/shard_map/ppermute | solution.py:687
  55.9 0.7 %fine.1 = bf16[8,8,4,256]{3,2,1,0:T(4,128)(2,1)} custom-call(bf16[256,256]{1,0:T(8,128)(2,1)S(1)} %get-tuple-element.43.field_ref), custom_call_target="tpu_custom_call" | custom-call | bytes 4000000 | tf_op jit(solution)/shard_map/fine/pallas_call | solution.py:557
  56.6 0.6 %collective-permute-done.10.refs_0_ = bf16[64,256]{1,0:T(8,128)(2,1)S(1)} collective-permute-done((bf16[64,256]{1,0:T(8,128)(2,1)S(1)}, bf16[64,256]{1,0:T(8,128)(2,1)S(1)}, u32[]{:S(2)}, u32[]{:S(2)}) %collective-permute-start.10) | collective-permute-done | bytes 32800 | tf_op jit(solution)/shard_map/ppermute | solution.py:687
  57.3 0.0 collective-permute-done.11.refs_1_
  57.3 0.6 collective-permute-done.12.refs_2_
  57.8 0.7 %place.1 = bf16[1,64,1024]{2,1,0:T(8,128)(2,1)} custom-call(f32[8,256]{1,0:T(8,128)S(1)} %get-tuple-element.36.rest_2_.keep_ref, bf16[64,256]{1,0:T(8,128)(2,1)S(1)} %collective-permute-done.10.refs_0_, bf16[64,256]{1,0:T(8,128)(2,1)S(1)} %collective-permute-done.11.refs_1_, bf16[64,256]{1,0:T(8,128)(2,1)S(1)} %collective-permute-done.12.refs_2_, ...), custom_call_target="tpu_custom_call" | custom-call | bytes 300000 | tf_op jit(solution)/shard_map/place/pallas_call | solution.py:557
Async XLA Ops:
  0.6 0.9 %copy-start = (bf16[8,8,4,256]{3,2,1,0:T(4,128)(2,1)S(1)}, bf16[8,8,4,256]{3,2,1,0:T(4,128)(2,1)}, u32[]{:S(2)}) copy-start(bf16[8,8,4,256]{3,2,1,0:T(4,128)(2,1)} %feat_ref.1) | copy-start | bytes 393220
  1.5 0.7 %copy-start.2 = (s32[4,1,4]{2,1,0:T(1,128)S(1)}, s32[4,1,4]{2,1,0:T(1,128)}, u32[]{:S(2)}) copy-start(s32[4,1,4]{2,1,0:T(1,128)} %occ_ref.1) | copy-start | bytes 196
  3.2 10.1 %collective-permute-start = (bf16[80,256]{1,0:T(8,128)(2,1)S(1)}, bf16[80,256]{1,0:T(8,128)(2,1)S(1)}, u32[]{:S(2)}, u32[]{:S(2)}) collective-permute-start(bf16[80,256]{1,0:T(8,128)(2,1)S(1)} %get-tuple-element.28), channel_id=1, source_target_pairs={{0,8},{8,0},{16,24},{24,16},{1,9},{9,1},{17,25},{25,17},{2,10},{10... | collective-permute-start | bytes 122888 | tf_op jit(solution)/shard_map/ppermute | solution.py:599
  6.3 7.0 %collective-permute-start.1 = (bf16[80,256]{1,0:T(8,128)(2,1)S(1)}, bf16[80,256]{1,0:T(8,128)(2,1)S(1)}, u32[]{:S(2)}, u32[]{:S(2)}) collective-permute-start(bf16[80,256]{1,0:T(8,128)(2,1)S(1)} %get-tuple-element.29), channel_id=1, source_target_pairs={{0,24},{8,16},{16,8},{24,0},{1,25},{9,17},{17,9},{25,1},{2,26},{10... | collective-permute-start | bytes 122888 | tf_op jit(solution)/shard_map/ppermute | solution.py:600
  8.7 4.5 %collective-permute-start.2 = (bf16[16,256]{1,0:T(8,128)(2,1)S(1)}, bf16[16,256]{1,0:T(8,128)(2,1)S(1)}, u32[]{:S(2)}, u32[]{:S(2)}) collective-permute-start(bf16[16,256]{1,0:T(8,128)(2,1)S(1)} %get-tuple-element.30.rest_0_), channel_id=1, source_target_pairs={{0,16},{8,24},{16,0},{24,8},{1,17},{9,25},{17,1},{25,9},{2,18},{10... | collective-permute-start | bytes 24584 | tf_op jit(solution)/shard_map/ppermute | solution.py:604
  8.8 0.9 %copy-start.1 = (bf16[2,32,864]{2,1,0:T(8,128)(2,1)S(1)}, bf16[2,32,864]{2,1,0:T(8,128)(2,1)}, u32[]{:S(2)}) copy-start(bf16[2,32,864]{2,1,0:T(8,128)(2,1)} %weight_ref.2) | copy-start | bytes 331780
  13.5 1.3 %collective-permute-start.3 = (bf16[112,256]{1,0:T(8,128)(2,1)S(1)}, bf16[112,256]{1,0:T(8,128)(2,1)S(1)}, u32[]{:S(2)}, u32[]{:S(2)}) collective-permute-start(bf16[112,256]{1,0:T(8,128)(2,1)S(1)} %get-tuple-element.32.own_ref), channel_id=1, source_target_pairs={{0,1},{1,0},{2,3},{3,2},{4,5},{5,4},{6,7},{7,6},{8,9},{9,8},{10,11... | collective-permute-start | bytes 172040 | tf_op jit(solution)/shard_map/ppermute | solution.py:622
  15.0 6.7 %collective-permute-start.5 = (bf16[144,256]{1,0:T(8,128)(2,1)S(1)}, bf16[144,256]{1,0:T(8,128)(2,1)S(1)}, u32[]{:S(2)}, u32[]{:S(2)}) collective-permute-start(bf16[144,256]{1,0:T(8,128)(2,1)S(1)} %get-tuple-element.34), channel_id=1, source_target_pairs={{0,4},{4,0},{1,5},{5,1},{2,6},{6,2},{3,7},{7,3},{8,12},{12,8},{9,1... | collective-permute-start | bytes 221192 | tf_op jit(solution)/shard_map/ppermute | solution.py:640
  16.5 5.2 %collective-permute-start.4 = (bf16[112,256]{1,0:T(8,128)(2,1)S(1)}, bf16[112,256]{1,0:T(8,128)(2,1)S(1)}, u32[]{:S(2)}, u32[]{:S(2)}) collective-permute-start(bf16[112,256]{1,0:T(8,128)(2,1)S(1)} %get-tuple-element.33.own_ref), channel_id=1, source_target_pairs={{0,3},{1,2},{2,1},{3,0},{4,7},{5,6},{6,5},{7,4},{8,11},{9,10},{10,... | collective-permute-start | bytes 172040 | tf_op jit(solution)/shard_map/ppermute | solution.py:636
  17.5 4.2 %collective-permute-start.6 = (bf16[48,256]{1,0:T(8,128)(2,1)S(1)}, bf16[48,256]{1,0:T(8,128)(2,1)S(1)}, u32[]{:S(2)}, u32[]{:S(2)}) collective-permute-start(bf16[48,256]{1,0:T(8,128)(2,1)S(1)} %get-tuple-element.35), channel_id=1, source_target_pairs={{0,7},{1,6},{2,5},{3,4},{4,3},{5,2},{6,1},{7,0},{8,15},{9,14},{10,... | collective-permute-start | bytes 73736 | tf_op jit(solution)/shard_map/ppermute | solution.py:644
  34.0 10.7 %copy-start.3 = (bf16[3,256,1024]{2,1,0:T(8,128)(2,1)S(1)}, bf16[3,256,1024]{2,1,0:T(8,128)(2,1)}, u32[]{:S(2)}) copy-start(bf16[3,256,1024]{2,1,0:T(8,128)(2,1)} %weight_ref.3) | copy-start | bytes 4718596
  35.8 8.9 %collective-permute-start.8 = (bf16[64,1024]{1,0:T(8,128)(2,1)S(1)}, bf16[64,1024]{1,0:T(8,128)(2,1)S(1)}, u32[]{:S(2)}, u32[]{:S(2)}) collective-permute-start(bf16[64,1024]{1,0:T(8,128)(2,1)S(1)} %get-tuple-element.45.refs_0_), channel_id=1, source_target_pairs={{0,16},{8,24},{16,0},{24,8},{1,17},{9,25},{17,1},{25,9},{2,18},{10... | collective-permute-start | bytes 393224 | tf_op jit(solution)/shard_map/ppermute | solution.py:679
  36.5 10.2 %collective-permute-start.7 = (bf16[64,1024]{1,0:T(8,128)(2,1)S(1)}, bf16[64,1024]{1,0:T(8,128)(2,1)S(1)}, u32[]{:S(2)}, u32[]{:S(2)}) collective-permute-start(bf16[64,1024]{1,0:T(8,128)(2,1)S(1)} %get-tuple-element.45.refs_0_), channel_id=1, source_target_pairs={{0,8},{8,0},{16,24},{24,16},{1,9},{9,1},{17,25},{25,17},{2,10},{10... | collective-permute-start | bytes 393224 | tf_op jit(solution)/shard_map/ppermute | solution.py:679
  44.7 5.4 %collective-permute-start.9 = (bf16[64,1024]{1,0:T(8,128)(2,1)S(1)}, bf16[64,1024]{1,0:T(8,128)(2,1)S(1)}, u32[]{:S(2)}, u32[]{:S(2)}) collective-permute-start(bf16[64,1024]{1,0:T(8,128)(2,1)S(1)} %collective-permute-done.8.refs_2_), channel_id=1, source_target_pairs={{0,8},{8,0},{16,24},{24,16},{1,9},{9,1},{17,25},{25,17},{2,10},{10... | collective-permute-start | bytes 393224 | tf_op jit(solution)/shard_map/ppermute | solution.py:679
  51.5 5.8 %collective-permute-start.10 = (bf16[64,256]{1,0:T(8,128)(2,1)S(1)}, bf16[64,256]{1,0:T(8,128)(2,1)S(1)}, u32[]{:S(2)}, u32[]{:S(2)}) collective-permute-start(bf16[64,256]{1,0:T(8,128)(2,1)S(1)} %get-tuple-element.46), channel_id=1, source_target_pairs={{0,24},{8,16},{16,8},{24,0},{1,25},{9,17},{17,9},{25,1},{2,26},{10... | collective-permute-start | bytes 98312 | tf_op jit(solution)/shard_map/ppermute | solution.py:687
  51.8 5.5 %collective-permute-start.11 = (bf16[64,256]{1,0:T(8,128)(2,1)S(1)}, bf16[64,256]{1,0:T(8,128)(2,1)S(1)}, u32[]{:S(2)}, u32[]{:S(2)}) collective-permute-start(bf16[64,256]{1,0:T(8,128)(2,1)S(1)} %get-tuple-element.47), channel_id=1, source_target_pairs={{0,16},{8,24},{16,0},{24,8},{1,17},{9,25},{17,1},{25,9},{2,18},{10... | collective-permute-start | bytes 98312 | tf_op jit(solution)/shard_map/ppermute | solution.py:687
  53.3 4.5 %collective-permute-start.12 = (bf16[64,256]{1,0:T(8,128)(2,1)S(1)}, bf16[64,256]{1,0:T(8,128)(2,1)S(1)}, u32[]{:S(2)}, u32[]{:S(2)}) collective-permute-start(bf16[64,256]{1,0:T(8,128)(2,1)S(1)} %get-tuple-element.48), channel_id=1, source_target_pairs={{0,8},{8,0},{16,24},{24,16},{1,9},{9,1},{17,25},{25,17},{2,10},{10... | collective-permute-start | bytes 98312 | tf_op jit(solution)/shard_map/ppermute | solution.py:687

commit v9 on v8

--- a/solution.py
+++ b/solution.py
@@ -443,7 +443,7 @@
 
 
 def second_kernel(sx, sy, sb, stats_ref, mid_ref, msk_ref, weight_ref, rows_ref, coded_ref,
-                  field_ref, tok_ref, lhs):
+                  field_ref, tok_ref, low_ref, high_ref, lhs):
     lanes = coded_ref.shape[1]
     step, ext = (sy + 2) * 8, (sy + 4) * 8
     centre, scale = from_rows(stats_ref[...])
@@ -491,7 +491,10 @@
     n = count * 8
     i, j = iota((n, n), 0), iota((n, n), 1)
     order = onehot(j == i // 8 * 8 + i % 2 * 4 + i % 8 // 2)
-    tok_ref[...] = jnp.dot(order, tokens, preferred_element_type=F32).astype(BF16)
+    tokens = jnp.dot(order, tokens, preferred_element_type=F32).astype(BF16)
+    tok_ref[...] = tokens
+    low_ref[...] = tokens[0 : n // 2]
+    high_ref[...] = tokens[n // 2 : n]
 
 
 def fine_kernel(field_ref, fine_ref):
@@ -503,12 +506,13 @@
 
 
 def attend_kernel(members, keys_ref, weight_ref, *refs):
-    tok_refs, out_refs, (toks, proj) = refs[:members], refs[members : 2 * members], refs[-2:]
-    own = tok_refs[0].shape[0]
+    tok_refs, out_refs, (toks, proj) = refs[: -2 - members], refs[-2 - members : -2], refs[-2:]
+    own, cols = tok_refs[0].shape[0], weight_ref.shape[1] // 3
     seq = own * members
-    cols = weight_ref.shape[1] // 3
-    for k in range(members):
-        toks[k * own : (k + 1) * own, :] = tok_refs[k][...]
+    start = 0
+    for ref in tok_refs:
+        toks[start : start + ref.shape[0], :] = ref[...]
+        start += ref.shape[0]
     proj[...] = jnp.dot(toks[...], weight_ref[...], preferred_element_type=F32).astype(BF16)
     there = keys_ref[0:1] > 0
     width = min(128, cols)
@@ -662,9 +666,9 @@
         flops=2 * 10**9, nbytes=4 * 10**6, mib=20,
     )
     stats = lax.all_to_all(mine, ALL, 0, 0, tiled=True)
-    field, tokens = call(
+    field, tokens, *parts = call(
         functools.partial(second_kernel, sx, sy, sb), "second", (VM,) * 6,
-        [shape(sx * sy * 4, lanes), shape(own, feats)],
+        [shape(sx * sy * 4, lanes), shape(own, feats)] + [shape(own // 2, feats)] * 2,
         (stats, mid, there, band1, rows, coded),
         [pltpu.VMEM(((sx + 2) * sy * 4, 4 * lanes), BF16)],
         flops=10**9, nbytes=4 * 10**6,
@@ -673,13 +677,14 @@
         fine_kernel, "fine", (VM,), shape(*features.shape), (field,), nbytes=4 * 10**6, mib=8,
     )
     swaps = [[(i, i ^ k) for i in range(nx)] for k in range(nx)]
-    blocks = {0: tokens}
+    blocks = {0: parts}
     for k in sorted(range(1, nx), key=lambda k: (bin(k).count("1"), -k)):
         low = k & -k
-        blocks[k] = lax.ppermute(blocks[k ^ low], "gx", swaps[low])
-    blocks = [blocks[k] for k in range(nx)]
+        source = [tokens] if k == 1 else blocks[k ^ low]
+        blocks[k] = [lax.ppermute(v, "gx", swaps[low]) for v in source]
+    blocks = [tokens] + [v for k in range(1, nx) for v in blocks[k]]
     outs = call(
-        functools.partial(attend_kernel, nx), "attend", (VM,) * (2 + nx),
+        functools.partial(attend_kernel, nx), "attend", (VM,) * (2 + len(blocks)),
         [shape(own, cols)] * nx, (keys, turned, *blocks),
         [pltpu.VMEM((own * nx, feats), BF16), pltpu.VMEM((own * nx, 3 * cols), BF16)],
         flops=10**9, nbytes=3 * 10**6, mib=16 if narrow else 40,

time: 58.8 us -> 57.8 us (0.983)
  waiting for transfers between devices: 17.2 us -> 13.1 us
  starting transfers between devices: 14.7 us -> 17.8 us
    ppermute x3 -> x5, waiting for transfers between devices: 11.2 us -> 7.17 us  [body(): blocks[k] = [lax.ppermute(v, 'gx', swaps[low]) for v in source]]
    ppermute x3 -> x5, starting transfers between devices: 1.2 us -> 4.28 us  [body(): blocks[k] = [lax.ppermute(v, 'gx', swaps[low]) for v in source]]
  transfers between devices with their start and end apart: 13 -> 15, of which waited for: 7 -> 9; matrix products, arithmetic and copies ran while one was open for 1% -> 1% of each run, Pallas kernels for 9% -> 9%
where the time goes in v9:
time: 57.8 us; the launch traced here: 57.6 us
  starting transfers between devices  17.8 us (31%)
  Pallas kernels  13.5 us (23%)
  waiting for transfers between devices  13.1 us (23%)
  blocking collectives  9.3 us (16%)
  local copies, waits for them, and re-layouts  2.48 us (4%)
  other arithmetic  0.72 us (1%)
  between operations  0.72 us (1%)
    pallas_call x11, Pallas kernels, call(): pl.pallas_call(kernel, out_shape=out, in_specs=list(specs), out_specs=jax...  13.5 us
    all_to_all x1, blocking collectives, body(): stats = lax.all_to_all(mine, ALL, 0, 0, tiled=True)  9.3 us
    ppermute x5, waiting for transfers between devices, body(): blocks[k] = [lax.ppermute(v, 'gx', swaps[low]) for v in source]  7.17 us
    ppermute x3, starting transfers between devices, body(): lax.ppermute(v, 'gx', swaps[nx - 1 - i])  4.45 us
    ppermute x5, starting transfers between devices, body(): blocks[k] = [lax.ppermute(v, 'gx', swaps[low]) for v in source]  4.28 us
    ppermute x1, starting transfers between devices, body(): lax.ppermute(first, 'gx', list(pairing(nx, False, False).items()))  3.09 us
    unnamed x8, local copies, waits for them, and re-layouts  2.48 us
    ppermute x1, starting transfers between devices, body(): lax.ppermute(second, 'gx', list(pairing(nx, True, narrow).items()))  2.47 us
  transfers between devices with their start and end apart: 15, of which 9 were waited for; matrix products, arithmetic and copies ran while one was open for 1% of the time, Pallas kernels for 9%

profile of v9, /device:TPU:0, one launch (start us, length us, event | category | flops | bytes accessed | tf_op | source)
XLA Modules:
  0.0 57.6 jit_solution(54777648671280850)
XLA Ops:
  0.6 0.0 copy-start
  0.6 0.9 %copy-done = bf16[8,8,4,256]{3,2,1,0:T(4,128)(2,1)S(1)} copy-done((bf16[8,8,4,256]{3,2,1,0:T(4,128)(2,1)S(1)}, bf16[8,8,4,256]{3,2,1,0:T(4,128)(2,1)}, u32[]{:S(2)}) %copy-start) | copy-done | bytes 131096
  1.5 0.0 copy-start.2
  1.5 0.7 %copy-done.2 = s32[4,1,4]{2,1,0:T(1,128)S(1)} copy-done((s32[4,1,4]{2,1,0:T(1,128)S(1)}, s32[4,1,4]{2,1,0:T(1,128)}, u32[]{:S(2)}) %copy-start.2) | copy-done | bytes 88
  2.2 0.9 %pre.1 = (f32[8,256]{1,0:T(8,128)S(1)}, f32[8,256]{1,0:T(8,128)S(1)}, bf16[512,256]{1,0:T(8,128)(2,1)S(1)}, bf16[80,256]{1,0:T(8,128)(2,1)S(1)}, bf16[80,256]{1,...) custom-call(s32[4,1,4]{2,1,0:T(1,128)S(1)} %copy-done.2, bf16[8,8,4,256]{3,2,1,0:T(4,128)(2,1)S(1)} %copy-done), custom_call_target="tpu_custom_call" | custom-call | bytes 1000000 | tf_op jit(solution)/shard_map/pre/pallas_call | solution.py:561
  3.2 3.1 %collective-permute-start = (bf16[80,256]{1,0:T(8,128)(2,1)S(1)}, bf16[80,256]{1,0:T(8,128)(2,1)S(1)}, u32[]{:S(2)}, u32[]{:S(2)}) collective-permute-start(bf16[80,256]{1,0:T(8,128)(2,1)S(1)} %get-tuple-element.30), channel_id=1, source_target_pairs={{0,8},{8,0},{16,24},{24,16},{1,9},{9,1},{17,25},{25,17},{2,10},{10... | collective-permute-start | bytes 122888 | tf_op jit(solution)/shard_map/ppermute | solution.py:603
  6.3 2.5 %collective-permute-start.1 = (bf16[80,256]{1,0:T(8,128)(2,1)S(1)}, bf16[80,256]{1,0:T(8,128)(2,1)S(1)}, u32[]{:S(2)}, u32[]{:S(2)}) collective-permute-start(bf16[80,256]{1,0:T(8,128)(2,1)S(1)} %get-tuple-element.31), channel_id=1, source_target_pairs={{0,24},{8,16},{16,8},{24,0},{1,25},{9,17},{17,9},{25,1},{2,26},{10... | collective-permute-start | bytes 122888 | tf_op jit(solution)/shard_map/ppermute | solution.py:604
  8.7 0.1 collective-permute-start.2
  8.8 0.0 copy-start.1
  8.9 0.9 %copy-done.1 = bf16[2,32,864]{2,1,0:T(8,128)(2,1)S(1)} copy-done((bf16[2,32,864]{2,1,0:T(8,128)(2,1)S(1)}, bf16[2,32,864]{2,1,0:T(8,128)(2,1)}, u32[]{:S(2)}) %copy-start.1) | copy-done | bytes 110616
  9.7 1.4 %band0.1 = (bf16[3,1024,256]{2,1,0:T(8,128)(2,1)S(1)}, bf16[1,32,864]{2,1,0:T(8,128)(2,1)S(1)}) custom-call(bf16[2,32,864]{2,1,0:T(8,128)(2,1)S(1)} %copy-done.1), custom_call_target="tpu_custom_call" | custom-call | bytes 8000000 | tf_op jit(solution)/shard_map/band0/pallas_call | solution.py:561
  11.1 2.2 %collective-permute-done.2.rest_1_ = bf16[16,256]{1,0:T(8,128)(2,1)S(1)} collective-permute-done((bf16[16,256]{1,0:T(8,128)(2,1)S(1)}, bf16[16,256]{1,0:T(8,128)(2,1)S(1)}, u32[]{:S(2)}, u32[]{:S(2)}) %collective-permute-start.2) | collective-permute-done | bytes 8224 | tf_op jit(solution)/shard_map/ppermute | solution.py:608
  13.3 0.0 collective-permute-done.first_ref
  13.3 0.0 collective-permute-done.1.second_ref
  13.3 0.2 line.1
  13.5 0.1 collective-permute-start.3
  13.5 1.2 %collective-permute-done.3.other_ref.core_ref = bf16[112,256]{1,0:T(8,128)(2,1)S(1)} collective-permute-done((bf16[112,256]{1,0:T(8,128)(2,1)S(1)}, bf16[112,256]{1,0:T(8,128)(2,1)S(1)}, u32[]{:S(2)}, u32[]{:S(2)}) %collective-permute-start.3) | collective-permute-done | bytes 57376 | tf_op jit(solution)/shard_map/ppermute | solution.py:626
  14.8 0.2 chip.1
  15.0 1.6 %collective-permute-start.5 = (bf16[144,256]{1,0:T(8,128)(2,1)S(1)}, bf16[144,256]{1,0:T(8,128)(2,1)S(1)}, u32[]{:S(2)}, u32[]{:S(2)}) collective-permute-start(bf16[144,256]{1,0:T(8,128)(2,1)S(1)} %get-tuple-element.36), channel_id=1, source_target_pairs={{0,4},{4,0},{1,5},{5,1},{2,6},{6,2},{3,7},{7,3},{8,12},{12,8},{9,1... | collective-permute-start | bytes 221192 | tf_op jit(solution)/shard_map/ppermute | solution.py:644
  16.5 1.0 %collective-permute-start.4 = (bf16[112,256]{1,0:T(8,128)(2,1)S(1)}, bf16[112,256]{1,0:T(8,128)(2,1)S(1)}, u32[]{:S(2)}, u32[]{:S(2)}) collective-permute-start(bf16[112,256]{1,0:T(8,128)(2,1)S(1)} %get-tuple-element.35.own_ref), channel_id=1, source_target_pairs={{0,3},{1,2},{2,1},{3,0},{4,7},{5,6},{6,5},{7,4},{8,11},{9,10},{10,... | collective-permute-start | bytes 172040 | tf_op jit(solution)/shard_map/ppermute | solution.py:640
  17.5 0.7 %collective-permute-start.6 = (bf16[48,256]{1,0:T(8,128)(2,1)S(1)}, bf16[48,256]{1,0:T(8,128)(2,1)S(1)}, u32[]{:S(2)}, u32[]{:S(2)}) collective-permute-start(bf16[48,256]{1,0:T(8,128)(2,1)S(1)} %get-tuple-element.37), channel_id=1, source_target_pairs={{0,7},{1,6},{2,5},{3,4},{4,3},{5,2},{6,1},{7,0},{8,15},{9,14},{10,... | collective-permute-start | bytes 73736 | tf_op jit(solution)/shard_map/ppermute | solution.py:648
  18.3 0.7 %pad_maximum_fusion.rest_0_ = f32[6,32]{1,0:T(8,128)S(1)} fusion(f32[2,32]{1,0:T(2,128)} %param.12, f32[2,32]{1,0:T(2,128)} %param.10, f32[2,32]{1,0:T(2,128)} %param.9), kind=kLoop, calls=%fused_computation | loop fusion | flops 384 | bytes 1536 | tf_op jit(solution)/shard_map/concatenate | solution.py:610
  19.0 1.4 %band1.1 = (bf16[3,1024,256]{2,1,0:T(8,128)(2,1)S(1)}, f32[8,256]{1,0:T(8,128)S(1)}) custom-call(bf16[1,32,864]{2,1,0:T(8,128)(2,1)S(1)} %get-tuple-element.28._.weight_ref, f32[6,32]{1,0:T(8,128)S(1)} %pad_maximum_fusion.rest_0_), custom_call_target="tpu_custom_call" | custom-call | bytes 8000000 | tf_op jit(solution)/shard_map/band1/pallas_call | solution.py:561
  20.4 1.3 %collective-permute-done.6.rest_1_ = bf16[48,256]{1,0:T(8,128)(2,1)S(1)} collective-permute-done((bf16[48,256]{1,0:T(8,128)(2,1)S(1)}, bf16[48,256]{1,0:T(8,128)(2,1)S(1)}, u32[]{:S(2)}, u32[]{:S(2)}) %collective-permute-start.6) | collective-permute-done | bytes 24608 | tf_op jit(solution)/shard_map/ppermute | solution.py:648
  21.7 0.0 collective-permute-done.4.zface_ref
  21.7 0.0 collective-permute-done.5.rest_0_
  21.7 3.0 %first.1 = (f32[800,256]{1,0:T(8,128)S(1)}, f32[32,128]{1,0:T(8,128)S(1)}, f32[1152,128]{1,0:T(8,128)S(1)}) custom-call(bf16[768,256]{1,0:T(8,128)(2,1)S(1)} %get-tuple-element.33.ext_ref, bf16[112,256]{1,0:T(8,128)(2,1)S(1)} %get-tuple-element.35.own_ref, bf16[112,256]{1,0:T(8,128)(2,1)S(1)} %collective-permute-done.3.other_ref.core_ref, ...), custom_call_target="tpu_custom_call" | custom-call | flops 2000000000 | bytes 4000000 | tf_op jit(solution)/shard_map/first/pallas_call | solution.py:561
  24.7 9.3 %all_to_all.11 = f32[32,1,128]{2,1,0:T(1,128)S(1)} all-to-all(f32[32,1,128]{2,1,0:T(1,128)S(1)} %bitcast.5), channel_id=1, replica_groups=mesh['gx'=4,'gy'=2,'gz'=4] {'gx','gy','gz'}, dimensions={0} | all-to-all | bytes 32768 | tf_op jit(solution)/shard_map/all_to_all | solution.py:668
  34.0 0.0 copy-start.3
  34.0 1.8 %second.1 = (bf16[256,256]{1,0:T(8,128)(2,1)S(1)}, bf16[64,1024]{1,0:T(8,128)(2,1)S(1)}, bf16[32,1024]{1,0:T(8,128)(2,1)S(1)}, bf16[32,1024]{1,0:T(8,128)(2,1)S(1)}) custom-call(f32[32,128]{1,0:T(8,128)S(1)} %bitcast.4, f32[800,256]{1,0:T(8,128)S(1)} %get-tuple-element.42.mid_ref, f32[1152,128]{1,0:T(8,128)S(1)} %get-tuple-element.43.msk_ref, ...), custom_call_target="tpu_custom_call" | custom-call | flops 1000000000 | bytes 4000000 | tf_op jit(solution)/shard_map/second/pallas_call | solution.py:561
  35.8 0.7 %collective-permute-start.8 = (bf16[32,1024]{1,0:T(8,128)(2,1)S(1)}, bf16[32,1024]{1,0:T(8,128)(2,1)S(1)}, u32[]{:S(2)}, u32[]{:S(2)}) collective-permute-start(bf16[32,1024]{1,0:T(8,128)(2,1)S(1)} %get-tuple-element.48), channel_id=1, source_target_pairs={{0,16},{8,24},{16,0},{24,8},{1,17},{9,25},{17,1},{25,9},{2,18},{10... | collective-permute-start | bytes 196616 | tf_op jit(solution)/shard_map/ppermute | solution.py:684
  36.5 2.3 %collective-permute-start.9 = (bf16[32,1024]{1,0:T(8,128)(2,1)S(1)}, bf16[32,1024]{1,0:T(8,128)(2,1)S(1)}, u32[]{:S(2)}, u32[]{:S(2)}) collective-permute-start(bf16[32,1024]{1,0:T(8,128)(2,1)S(1)} %get-tuple-element.49), channel_id=1, source_target_pairs={{0,16},{8,24},{16,0},{24,8},{1,17},{9,25},{17,1},{25,9},{2,18},{10... | collective-permute-start | bytes 196616 | tf_op jit(solution)/shard_map/ppermute | solution.py:684
  38.8 0.6 collective-permute-start.7
  39.4 4.1 %collective-permute-done.8.refs_2_ = bf16[32,1024]{1,0:T(8,128)(2,1)S(1)} collective-permute-done((bf16[32,1024]{1,0:T(8,128)(2,1)S(1)}, bf16[32,1024]{1,0:T(8,128)(2,1)S(1)}, u32[]{:S(2)}, u32[]{:S(2)}) %collective-permute-start.8) | collective-permute-done | bytes 65568 | tf_op jit(solution)/shard_map/ppermute | solution.py:684
  43.5 0.0 collective-permute-start.10
  43.5 1.3 %collective-permute-done.9.refs_3_ = bf16[32,1024]{1,0:T(8,128)(2,1)S(1)} collective-permute-done((bf16[32,1024]{1,0:T(8,128)(2,1)S(1)}, bf16[32,1024]{1,0:T(8,128)(2,1)S(1)}, u32[]{:S(2)}, u32[]{:S(2)}) %collective-permute-start.9) | collective-permute-done | bytes 65568 | tf_op jit(solution)/shard_map/ppermute | solution.py:684
  44.8 0.7 %collective-permute-start.11 = (bf16[32,1024]{1,0:T(8,128)(2,1)S(1)}, bf16[32,1024]{1,0:T(8,128)(2,1)S(1)}, u32[]{:S(2)}, u32[]{:S(2)}) collective-permute-start(bf16[32,1024]{1,0:T(8,128)(2,1)S(1)} %collective-permute-done.9.refs_3_), channel_id=1, source_target_pairs={{0,8},{8,0},{16,24},{24,16},{1,9},{9,1},{17,25},{25,17},{2,10},{10... | collective-permute-start | bytes 196616 | tf_op jit(solution)/shard_map/ppermute | solution.py:684
  45.5 0.0 copy-done.3
  45.5 1.9 %turn.1.weight_ref = bf16[1024,768]{1,0:T(8,128)(2,1)S(1)} custom-call(bf16[3,256,1024]{2,1,0:T(8,128)(2,1)S(1)} %copy-done.3), custom_call_target="tpu_custom_call" | custom-call | flops 1610612736 | bytes 6000000 | tf_op jit(solution)/shard_map/turn/pallas_call | solution.py:561
  47.5 0.7 %collective-permute-done.10.refs_4_ = bf16[32,1024]{1,0:T(8,128)(2,1)S(1)} collective-permute-done((bf16[32,1024]{1,0:T(8,128)(2,1)S(1)}, bf16[32,1024]{1,0:T(8,128)(2,1)S(1)}, u32[]{:S(2)}, u32[]{:S(2)}) %collective-permute-start.10) | collective-permute-done | bytes 65568 | tf_op jit(solution)/shard_map/ppermute | solution.py:684
  48.2 1.0 %collective-permute-done.11.refs_5_ = bf16[32,1024]{1,0:T(8,128)(2,1)S(1)} collective-permute-done((bf16[32,1024]{1,0:T(8,128)(2,1)S(1)}, bf16[32,1024]{1,0:T(8,128)(2,1)S(1)}, u32[]{:S(2)}, u32[]{:S(2)}) %collective-permute-start.11) | collective-permute-done | bytes 65568 | tf_op jit(solution)/shard_map/ppermute | solution.py:684
  49.2 0.0 collective-permute-done.7.refs_1_
  49.2 1.3 %attend.1 = (bf16[64,256]{1,0:T(8,128)(2,1)S(1)}, bf16[64,256]{1,0:T(8,128)(2,1)S(1)}, bf16[64,256]{1,0:T(8,128)(2,1)S(1)}, bf16[64,256]{1,0:T(8,128)(2,1)S(1)}) custom-call(f32[8,256]{1,0:T(8,128)S(1)} %get-tuple-element.46.keys_ref, bf16[1024,768]{1,0:T(8,128)(2,1)S(1)} %turn.1.weight_ref, bf16[64,1024]{1,0:T(8,128)(2,1)S(1)} %get-tuple-element.47.refs_0_, ...), custom_call_target="tpu_custom_call" | custom-call | flops 1000000000 | bytes 3000000 | tf_op jit(solution)/shard_map/attend/pallas_call | solution.py:561
  50.5 0.6 collective-permute-start.12
  51.1 1.6 %collective-permute-start.13 = (bf16[64,256]{1,0:T(8,128)(2,1)S(1)}, bf16[64,256]{1,0:T(8,128)(2,1)S(1)}, u32[]{:S(2)}, u32[]{:S(2)}) collective-permute-start(bf16[64,256]{1,0:T(8,128)(2,1)S(1)} %get-tuple-element.51), channel_id=1, source_target_pairs={{0,16},{8,24},{16,0},{24,8},{1,17},{9,25},{17,1},{25,9},{2,18},{10... | collective-permute-start | bytes 98312 | tf_op jit(solution)/shard_map/ppermute | solution.py:692
  52.7 2.3 %collective-permute-start.14 = (bf16[64,256]{1,0:T(8,128)(2,1)S(1)}, bf16[64,256]{1,0:T(8,128)(2,1)S(1)}, u32[]{:S(2)}, u32[]{:S(2)}) collective-permute-start(bf16[64,256]{1,0:T(8,128)(2,1)S(1)} %get-tuple-element.52), channel_id=1, source_target_pairs={{0,8},{8,0},{16,24},{24,16},{1,9},{9,1},{17,25},{25,17},{2,10},{10... | collective-permute-start | bytes 98312 | tf_op jit(solution)/shard_map/ppermute | solution.py:692
  55.0 0.7 %fine.1 = bf16[8,8,4,256]{3,2,1,0:T(4,128)(2,1)} custom-call(bf16[256,256]{1,0:T(8,128)(2,1)S(1)} %get-tuple-element.45.field_ref), custom_call_target="tpu_custom_call" | custom-call | bytes 4000000 | tf_op jit(solution)/shard_map/fine/pallas_call | solution.py:561
  55.7 0.6 %collective-permute-done.12.refs_0_ = bf16[64,256]{1,0:T(8,128)(2,1)S(1)} collective-permute-done((bf16[64,256]{1,0:T(8,128)(2,1)S(1)}, bf16[64,256]{1,0:T(8,128)(2,1)S(1)}, u32[]{:S(2)}, u32[]{:S(2)}) %collective-permute-start.12) | collective-permute-done | bytes 32800 | tf_op jit(solution)/shard_map/ppermute | solution.py:692
  56.3 0.0 collective-permute-done.13.refs_1_
  56.3 0.6 collective-permute-done.14.refs_2_
  56.9 0.7 %place.1 = bf16[1,64,1024]{2,1,0:T(8,128)(2,1)} custom-call(f32[8,256]{1,0:T(8,128)S(1)} %get-tuple-element.38.rest_2_.keep_ref, bf16[64,256]{1,0:T(8,128)(2,1)S(1)} %collective-permute-done.12.refs_0_, bf16[64,256]{1,0:T(8,128)(2,1)S(1)} %collective-permute-done.13.refs_1_, bf16[64,256]{1,0:T(8,128)(2,1)S(1)} %collective-permute-done.14.refs_2_, ...), custom_call_target="tpu_custom_call" | custom-call | bytes 300000 | tf_op jit(solution)/shard_map/place/pallas_call | solution.py:561
Async XLA Ops:
  0.6 0.9 %copy-start = (bf16[8,8,4,256]{3,2,1,0:T(4,128)(2,1)S(1)}, bf16[8,8,4,256]{3,2,1,0:T(4,128)(2,1)}, u32[]{:S(2)}) copy-start(bf16[8,8,4,256]{3,2,1,0:T(4,128)(2,1)} %feat_ref.1) | copy-start | bytes 393220
  1.5 0.7 %copy-start.2 = (s32[4,1,4]{2,1,0:T(1,128)S(1)}, s32[4,1,4]{2,1,0:T(1,128)}, u32[]{:S(2)}) copy-start(s32[4,1,4]{2,1,0:T(1,128)} %occ_ref.1) | copy-start | bytes 196
  3.2 10.1 %collective-permute-start = (bf16[80,256]{1,0:T(8,128)(2,1)S(1)}, bf16[80,256]{1,0:T(8,128)(2,1)S(1)}, u32[]{:S(2)}, u32[]{:S(2)}) collective-permute-start(bf16[80,256]{1,0:T(8,128)(2,1)S(1)} %get-tuple-element.30), channel_id=1, source_target_pairs={{0,8},{8,0},{16,24},{24,16},{1,9},{9,1},{17,25},{25,17},{2,10},{10... | collective-permute-start | bytes 122888 | tf_op jit(solution)/shard_map/ppermute | solution.py:603
  6.3 7.0 %collective-permute-start.1 = (bf16[80,256]{1,0:T(8,128)(2,1)S(1)}, bf16[80,256]{1,0:T(8,128)(2,1)S(1)}, u32[]{:S(2)}, u32[]{:S(2)}) collective-permute-start(bf16[80,256]{1,0:T(8,128)(2,1)S(1)} %get-tuple-element.31), channel_id=1, source_target_pairs={{0,24},{8,16},{16,8},{24,0},{1,25},{9,17},{17,9},{25,1},{2,26},{10... | collective-permute-start | bytes 122888 | tf_op jit(solution)/shard_map/ppermute | solution.py:604
  8.7 4.5 %collective-permute-start.2 = (bf16[16,256]{1,0:T(8,128)(2,1)S(1)}, bf16[16,256]{1,0:T(8,128)(2,1)S(1)}, u32[]{:S(2)}, u32[]{:S(2)}) collective-permute-start(bf16[16,256]{1,0:T(8,128)(2,1)S(1)} %get-tuple-element.32.rest_0_), channel_id=1, source_target_pairs={{0,16},{8,24},{16,0},{24,8},{1,17},{9,25},{17,1},{25,9},{2,18},{10... | collective-permute-start | bytes 24584 | tf_op jit(solution)/shard_map/ppermute | solution.py:608
  8.8 0.9 %copy-start.1 = (bf16[2,32,864]{2,1,0:T(8,128)(2,1)S(1)}, bf16[2,32,864]{2,1,0:T(8,128)(2,1)}, u32[]{:S(2)}) copy-start(bf16[2,32,864]{2,1,0:T(8,128)(2,1)} %weight_ref.2) | copy-start | bytes 331780
  13.5 1.3 %collective-permute-start.3 = (bf16[112,256]{1,0:T(8,128)(2,1)S(1)}, bf16[112,256]{1,0:T(8,128)(2,1)S(1)}, u32[]{:S(2)}, u32[]{:S(2)}) collective-permute-start(bf16[112,256]{1,0:T(8,128)(2,1)S(1)} %get-tuple-element.34.own_ref), channel_id=1, source_target_pairs={{0,1},{1,0},{2,3},{3,2},{4,5},{5,4},{6,7},{7,6},{8,9},{9,8},{10,11... | collective-permute-start | bytes 172040 | tf_op jit(solution)/shard_map/ppermute | solution.py:626
  15.0 6.7 %collective-permute-start.5 = (bf16[144,256]{1,0:T(8,128)(2,1)S(1)}, bf16[144,256]{1,0:T(8,128)(2,1)S(1)}, u32[]{:S(2)}, u32[]{:S(2)}) collective-permute-start(bf16[144,256]{1,0:T(8,128)(2,1)S(1)} %get-tuple-element.36), channel_id=1, source_target_pairs={{0,4},{4,0},{1,5},{5,1},{2,6},{6,2},{3,7},{7,3},{8,12},{12,8},{9,1... | collective-permute-start | bytes 221192 | tf_op jit(solution)/shard_map/ppermute | solution.py:644
  16.5 5.2 %collective-permute-start.4 = (bf16[112,256]{1,0:T(8,128)(2,1)S(1)}, bf16[112,256]{1,0:T(8,128)(2,1)S(1)}, u32[]{:S(2)}, u32[]{:S(2)}) collective-permute-start(bf16[112,256]{1,0:T(8,128)(2,1)S(1)} %get-tuple-element.35.own_ref), channel_id=1, source_target_pairs={{0,3},{1,2},{2,1},{3,0},{4,7},{5,6},{6,5},{7,4},{8,11},{9,10},{10,... | collective-permute-start | bytes 172040 | tf_op jit(solution)/shard_map/ppermute | solution.py:640
  17.5 4.2 %collective-permute-start.6 = (bf16[48,256]{1,0:T(8,128)(2,1)S(1)}, bf16[48,256]{1,0:T(8,128)(2,1)S(1)}, u32[]{:S(2)}, u32[]{:S(2)}) collective-permute-start(bf16[48,256]{1,0:T(8,128)(2,1)S(1)} %get-tuple-element.37), channel_id=1, source_target_pairs={{0,7},{1,6},{2,5},{3,4},{4,3},{5,2},{6,1},{7,0},{8,15},{9,14},{10,... | collective-permute-start | bytes 73736 | tf_op jit(solution)/shard_map/ppermute | solution.py:648
  34.0 11.5 %copy-start.3 = (bf16[3,256,1024]{2,1,0:T(8,128)(2,1)S(1)}, bf16[3,256,1024]{2,1,0:T(8,128)(2,1)}, u32[]{:S(2)}) copy-start(bf16[3,256,1024]{2,1,0:T(8,128)(2,1)} %weight_ref.3) | copy-start | bytes 4718596
  35.8 7.7 %collective-permute-start.8 = (bf16[32,1024]{1,0:T(8,128)(2,1)S(1)}, bf16[32,1024]{1,0:T(8,128)(2,1)S(1)}, u32[]{:S(2)}, u32[]{:S(2)}) collective-permute-start(bf16[32,1024]{1,0:T(8,128)(2,1)S(1)} %get-tuple-element.48), channel_id=1, source_target_pairs={{0,16},{8,24},{16,0},{24,8},{1,17},{9,25},{17,1},{25,9},{2,18},{10... | collective-permute-start | bytes 196616 | tf_op jit(solution)/shard_map/ppermute | solution.py:684
  36.5 8.4 %collective-permute-start.9 = (bf16[32,1024]{1,0:T(8,128)(2,1)S(1)}, bf16[32,1024]{1,0:T(8,128)(2,1)S(1)}, u32[]{:S(2)}, u32[]{:S(2)}) collective-permute-start(bf16[32,1024]{1,0:T(8,128)(2,1)S(1)} %get-tuple-element.49), channel_id=1, source_target_pairs={{0,16},{8,24},{16,0},{24,8},{1,17},{9,25},{17,1},{25,9},{2,18},{10... | collective-permute-start | bytes 196616 | tf_op jit(solution)/shard_map/ppermute | solution.py:684
  38.8 10.4 %collective-permute-start.7 = (bf16[64,1024]{1,0:T(8,128)(2,1)S(1)}, bf16[64,1024]{1,0:T(8,128)(2,1)S(1)}, u32[]{:S(2)}, u32[]{:S(2)}) collective-permute-start(bf16[64,1024]{1,0:T(8,128)(2,1)S(1)} %get-tuple-element.47.refs_0_), channel_id=1, source_target_pairs={{0,8},{8,0},{16,24},{24,16},{1,9},{9,1},{17,25},{25,17},{2,10},{10... | collective-permute-start | bytes 393224 | tf_op jit(solution)/shard_map/ppermute | solution.py:684
  43.5 4.7 %collective-permute-start.10 = (bf16[32,1024]{1,0:T(8,128)(2,1)S(1)}, bf16[32,1024]{1,0:T(8,128)(2,1)S(1)}, u32[]{:S(2)}, u32[]{:S(2)}) collective-permute-start(bf16[32,1024]{1,0:T(8,128)(2,1)S(1)} %collective-permute-done.8.refs_2_), channel_id=1, source_target_pairs={{0,8},{8,0},{16,24},{24,16},{1,9},{9,1},{17,25},{25,17},{2,10},{10... | collective-permute-start | bytes 196616 | tf_op jit(solution)/shard_map/ppermute | solution.py:684
  44.8 4.4 %collective-permute-start.11 = (bf16[32,1024]{1,0:T(8,128)(2,1)S(1)}, bf16[32,1024]{1,0:T(8,128)(2,1)S(1)}, u32[]{:S(2)}, u32[]{:S(2)}) collective-permute-start(bf16[32,1024]{1,0:T(8,128)(2,1)S(1)} %collective-permute-done.9.refs_3_), channel_id=1, source_target_pairs={{0,8},{8,0},{16,24},{24,16},{1,9},{9,1},{17,25},{25,17},{2,10},{10... | collective-permute-start | bytes 196616 | tf_op jit(solution)/shard_map/ppermute | solution.py:684
  50.5 5.8 %collective-permute-start.12 = (bf16[64,256]{1,0:T(8,128)(2,1)S(1)}, bf16[64,256]{1,0:T(8,128)(2,1)S(1)}, u32[]{:S(2)}, u32[]{:S(2)}) collective-permute-start(bf16[64,256]{1,0:T(8,128)(2,1)S(1)} %get-tuple-element.50), channel_id=1, source_target_pairs={{0,24},{8,16},{16,8},{24,0},{1,25},{9,17},{17,9},{25,1},{2,26},{10... | collective-permute-start | bytes 98312 | tf_op jit(solution)/shard_map/ppermute | solution.py:692
  51.1 5.2 %collective-permute-start.13 = (bf16[64,256]{1,0:T(8,128)(2,1)S(1)}, bf16[64,256]{1,0:T(8,128)(2,1)S(1)}, u32[]{:S(2)}, u32[]{:S(2)}) collective-permute-start(bf16[64,256]{1,0:T(8,128)(2,1)S(1)} %get-tuple-element.51), channel_id=1, source_target_pairs={{0,16},{8,24},{16,0},{24,8},{1,17},{9,25},{17,1},{25,9},{2,18},{10... | collective-permute-start | bytes 98312 | tf_op jit(solution)/shard_map/ppermute | solution.py:692
  52.7 4.2 %collective-permute-start.14 = (bf16[64,256]{1,0:T(8,128)(2,1)S(1)}, bf16[64,256]{1,0:T(8,128)(2,1)S(1)}, u32[]{:S(2)}, u32[]{:S(2)}) collective-permute-start(bf16[64,256]{1,0:T(8,128)(2,1)S(1)} %get-tuple-element.52), channel_id=1, source_target_pairs={{0,8},{8,0},{16,24},{24,16},{1,9},{9,1},{17,25},{25,17},{2,10},{10... | collective-permute-start | bytes 98312 | tf_op jit(solution)/shard_map/ppermute | solution.py:692

commit v10 on v9

--- a/solution.py
+++ b/solution.py
@@ -681,6 +681,9 @@
     for k in sorted(range(1, nx), key=lambda k: (bin(k).count("1"), -k)):
         low = k & -k
         source = [tokens] if k == 1 else blocks[k ^ low]
+        if k & (k - 1):
+            first, turned = lax.optimization_barrier((source[0], turned))
+            source = [first] + source[1:]
         blocks[k] = [lax.ppermute(v, "gx", swaps[low]) for v in source]
     blocks = [tokens] + [v for k in range(1, nx) for v in blocks[k]]
     outs = call(

time: 57.8 us -> 57.8 us (level)
  no operation moved by 1% of the time
where the time goes in v10:
time: 57.8 us; the launch traced here: 57.6 us
  starting transfers between devices  17.8 us (31%)
  Pallas kernels  13.5 us (23%)
  waiting for transfers between devices  13.1 us (23%)
  blocking collectives  9.3 us (16%)
  local copies, waits for them, and re-layouts  2.48 us (4%)
  other arithmetic  0.72 us (1%)
  between operations  0.72 us (1%)
    pallas_call x11, Pallas kernels, call(): pl.pallas_call(kernel, out_shape=out, in_specs=list(specs), out_specs=jax...  13.5 us
    all_to_all x1, blocking collectives, body(): stats = lax.all_to_all(mine, ALL, 0, 0, tiled=True)  9.3 us
    ppermute x5, waiting for transfers between devices, body(): blocks[k] = [lax.ppermute(v, 'gx', swaps[low]) for v in source]  7.17 us
    ppermute x3, starting transfers between devices, body(): lax.ppermute(v, 'gx', swaps[nx - 1 - i])  4.45 us
    ppermute x5, starting transfers between devices, body(): blocks[k] = [lax.ppermute(v, 'gx', swaps[low]) for v in source]  4.28 us
    ppermute x1, starting transfers between devices, body(): lax.ppermute(first, 'gx', list(pairing(nx, False, False).items()))  3.09 us
    unnamed x8, local copies, waits for them, and re-layouts  2.48 us
    ppermute x1, starting transfers between devices, body(): lax.ppermute(second, 'gx', list(pairing(nx, True, narrow).items()))  2.47 us
  transfers between devices with their start and end apart: 15, of which 9 were waited for; matrix products, arithmetic and copies ran while one was open for 1% of the time, Pallas kernels for 9%

profile of v10, /device:TPU:0, one launch (start us, length us, event | category | flops | bytes accessed | tf_op | source)
XLA Modules:
  0.0 57.6 jit_solution(13048958069531745733)
XLA Ops:
  0.6 0.0 copy-start
  0.6 0.9 %copy-done = bf16[8,8,4,256]{3,2,1,0:T(4,128)(2,1)S(1)} copy-done((bf16[8,8,4,256]{3,2,1,0:T(4,128)(2,1)S(1)}, bf16[8,8,4,256]{3,2,1,0:T(4,128)(2,1)}, u32[]{:S(2)}) %copy-start) | copy-done | bytes 131096
  1.5 0.0 copy-start.2
  1.5 0.7 %copy-done.2 = s32[4,1,4]{2,1,0:T(1,128)S(1)} copy-done((s32[4,1,4]{2,1,0:T(1,128)S(1)}, s32[4,1,4]{2,1,0:T(1,128)}, u32[]{:S(2)}) %copy-start.2) | copy-done | bytes 88
  2.2 0.9 %pre.1 = (f32[8,256]{1,0:T(8,128)S(1)}, f32[8,256]{1,0:T(8,128)S(1)}, bf16[512,256]{1,0:T(8,128)(2,1)S(1)}, bf16[80,256]{1,0:T(8,128)(2,1)S(1)}, bf16[80,256]{1,...) custom-call(s32[4,1,4]{2,1,0:T(1,128)S(1)} %copy-done.2, bf16[8,8,4,256]{3,2,1,0:T(4,128)(2,1)S(1)} %copy-done), custom_call_target="tpu_custom_call" | custom-call | bytes 1000000 | tf_op jit(solution)/shard_map/pre/pallas_call | solution.py:561
  3.2 3.1 %collective-permute-start = (bf16[80,256]{1,0:T(8,128)(2,1)S(1)}, bf16[80,256]{1,0:T(8,128)(2,1)S(1)}, u32[]{:S(2)}, u32[]{:S(2)}) collective-permute-start(bf16[80,256]{1,0:T(8,128)(2,1)S(1)} %get-tuple-element.32), channel_id=1, source_target_pairs={{0,8},{8,0},{16,24},{24,16},{1,9},{9,1},{17,25},{25,17},{2,10},{10... | collective-permute-start | bytes 122888 | tf_op jit(solution)/shard_map/ppermute | solution.py:603
  6.3 2.5 %collective-permute-start.1 = (bf16[80,256]{1,0:T(8,128)(2,1)S(1)}, bf16[80,256]{1,0:T(8,128)(2,1)S(1)}, u32[]{:S(2)}, u32[]{:S(2)}) collective-permute-start(bf16[80,256]{1,0:T(8,128)(2,1)S(1)} %get-tuple-element.33), channel_id=1, source_target_pairs={{0,24},{8,16},{16,8},{24,0},{1,25},{9,17},{17,9},{25,1},{2,26},{10... | collective-permute-start | bytes 122888 | tf_op jit(solution)/shard_map/ppermute | solution.py:604
  8.7 0.1 collective-permute-start.2
  8.8 0.0 copy-start.1
  8.9 0.9 %copy-done.1 = bf16[2,32,864]{2,1,0:T(8,128)(2,1)S(1)} copy-done((bf16[2,32,864]{2,1,0:T(8,128)(2,1)S(1)}, bf16[2,32,864]{2,1,0:T(8,128)(2,1)}, u32[]{:S(2)}) %copy-start.1) | copy-done | bytes 110616
  9.7 1.4 %band0.1 = (bf16[3,1024,256]{2,1,0:T(8,128)(2,1)S(1)}, bf16[1,32,864]{2,1,0:T(8,128)(2,1)S(1)}) custom-call(bf16[2,32,864]{2,1,0:T(8,128)(2,1)S(1)} %copy-done.1), custom_call_target="tpu_custom_call" | custom-call | bytes 8000000 | tf_op jit(solution)/shard_map/band0/pallas_call | solution.py:561
  11.1 2.2 %collective-permute-done.2.rest_1_ = bf16[16,256]{1,0:T(8,128)(2,1)S(1)} collective-permute-done((bf16[16,256]{1,0:T(8,128)(2,1)S(1)}, bf16[16,256]{1,0:T(8,128)(2,1)S(1)}, u32[]{:S(2)}, u32[]{:S(2)}) %collective-permute-start.2) | collective-permute-done | bytes 8224 | tf_op jit(solution)/shard_map/ppermute | solution.py:608
  13.3 0.0 collective-permute-done.first_ref
  13.3 0.0 collective-permute-done.1.second_ref
  13.3 0.2 line.1
  13.5 0.1 collective-permute-start.3
  13.5 1.2 %collective-permute-done.3.other_ref.core_ref = bf16[112,256]{1,0:T(8,128)(2,1)S(1)} collective-permute-done((bf16[112,256]{1,0:T(8,128)(2,1)S(1)}, bf16[112,256]{1,0:T(8,128)(2,1)S(1)}, u32[]{:S(2)}, u32[]{:S(2)}) %collective-permute-start.3) | collective-permute-done | bytes 57376 | tf_op jit(solution)/shard_map/ppermute | solution.py:626
  14.8 0.2 chip.1
  15.0 1.6 %collective-permute-start.5 = (bf16[144,256]{1,0:T(8,128)(2,1)S(1)}, bf16[144,256]{1,0:T(8,128)(2,1)S(1)}, u32[]{:S(2)}, u32[]{:S(2)}) collective-permute-start(bf16[144,256]{1,0:T(8,128)(2,1)S(1)} %get-tuple-element.38), channel_id=1, source_target_pairs={{0,4},{4,0},{1,5},{5,1},{2,6},{6,2},{3,7},{7,3},{8,12},{12,8},{9,1... | collective-permute-start | bytes 221192 | tf_op jit(solution)/shard_map/ppermute | solution.py:644
  16.5 1.0 %collective-permute-start.4 = (bf16[112,256]{1,0:T(8,128)(2,1)S(1)}, bf16[112,256]{1,0:T(8,128)(2,1)S(1)}, u32[]{:S(2)}, u32[]{:S(2)}) collective-permute-start(bf16[112,256]{1,0:T(8,128)(2,1)S(1)} %get-tuple-element.37.own_ref), channel_id=1, source_target_pairs={{0,3},{1,2},{2,1},{3,0},{4,7},{5,6},{6,5},{7,4},{8,11},{9,10},{10,... | collective-permute-start | bytes 172040 | tf_op jit(solution)/shard_map/ppermute | solution.py:640
  17.5 0.7 %collective-permute-start.6 = (bf16[48,256]{1,0:T(8,128)(2,1)S(1)}, bf16[48,256]{1,0:T(8,128)(2,1)S(1)}, u32[]{:S(2)}, u32[]{:S(2)}) collective-permute-start(bf16[48,256]{1,0:T(8,128)(2,1)S(1)} %get-tuple-element.39), channel_id=1, source_target_pairs={{0,7},{1,6},{2,5},{3,4},{4,3},{5,2},{6,1},{7,0},{8,15},{9,14},{10,... | collective-permute-start | bytes 73736 | tf_op jit(solution)/shard_map/ppermute | solution.py:648
  18.3 0.7 %pad_maximum_fusion.rest_0_ = f32[6,32]{1,0:T(8,128)S(1)} fusion(f32[2,32]{1,0:T(2,128)} %param.12, f32[2,32]{1,0:T(2,128)} %param.10, f32[2,32]{1,0:T(2,128)} %param.9), kind=kLoop, calls=%fused_computation | loop fusion | flops 384 | bytes 1536 | tf_op jit(solution)/shard_map/concatenate | solution.py:610
  19.0 1.4 %band1.1 = (bf16[3,1024,256]{2,1,0:T(8,128)(2,1)S(1)}, f32[8,256]{1,0:T(8,128)S(1)}) custom-call(bf16[1,32,864]{2,1,0:T(8,128)(2,1)S(1)} %get-tuple-element.30._.weight_ref, f32[6,32]{1,0:T(8,128)S(1)} %pad_maximum_fusion.rest_0_), custom_call_target="tpu_custom_call" | custom-call | bytes 8000000 | tf_op jit(solution)/shard_map/band1/pallas_call | solution.py:561
  20.4 1.3 %collective-permute-done.6.rest_1_ = bf16[48,256]{1,0:T(8,128)(2,1)S(1)} collective-permute-done((bf16[48,256]{1,0:T(8,128)(2,1)S(1)}, bf16[48,256]{1,0:T(8,128)(2,1)S(1)}, u32[]{:S(2)}, u32[]{:S(2)}) %collective-permute-start.6) | collective-permute-done | bytes 24608 | tf_op jit(solution)/shard_map/ppermute | solution.py:648
  21.7 0.0 collective-permute-done.4.zface_ref
  21.7 0.0 collective-permute-done.5.rest_0_
  21.7 3.0 %first.1 = (f32[800,256]{1,0:T(8,128)S(1)}, f32[32,128]{1,0:T(8,128)S(1)}, f32[1152,128]{1,0:T(8,128)S(1)}) custom-call(bf16[768,256]{1,0:T(8,128)(2,1)S(1)} %get-tuple-element.35.ext_ref, bf16[112,256]{1,0:T(8,128)(2,1)S(1)} %get-tuple-element.37.own_ref, bf16[112,256]{1,0:T(8,128)(2,1)S(1)} %collective-permute-done.3.other_ref.core_ref, ...), custom_call_target="tpu_custom_call" | custom-call | flops 2000000000 | bytes 4000000 | tf_op jit(solution)/shard_map/first/pallas_call | solution.py:561
  24.7 9.3 %all_to_all.11 = f32[32,1,128]{2,1,0:T(1,128)S(1)} all-to-all(f32[32,1,128]{2,1,0:T(1,128)S(1)} %bitcast.5), channel_id=1, replica_groups=mesh['gx'=4,'gy'=2,'gz'=4] {'gx','gy','gz'}, dimensions={0} | all-to-all | bytes 32768 | tf_op jit(solution)/shard_map/all_to_all | solution.py:668
  34.0 0.0 copy-start.3
  34.0 1.8 %second.1 = (bf16[256,256]{1,0:T(8,128)(2,1)S(1)}, bf16[64,1024]{1,0:T(8,128)(2,1)S(1)}, bf16[32,1024]{1,0:T(8,128)(2,1)S(1)}, bf16[32,1024]{1,0:T(8,128)(2,1)S(1)}) custom-call(f32[32,128]{1,0:T(8,128)S(1)} %bitcast.4, f32[800,256]{1,0:T(8,128)S(1)} %get-tuple-element.44.mid_ref, f32[1152,128]{1,0:T(8,128)S(1)} %get-tuple-element.45.msk_ref, ...), custom_call_target="tpu_custom_call" | custom-call | flops 1000000000 | bytes 4000000 | tf_op jit(solution)/shard_map/second/pallas_call | solution.py:561
  35.8 0.7 %collective-permute-start.7 = (bf16[32,1024]{1,0:T(8,128)(2,1)S(1)}, bf16[32,1024]{1,0:T(8,128)(2,1)S(1)}, u32[]{:S(2)}, u32[]{:S(2)}) collective-permute-start(bf16[32,1024]{1,0:T(8,128)(2,1)S(1)} %get-tuple-element.49), channel_id=1, source_target_pairs={{0,16},{8,24},{16,0},{24,8},{1,17},{9,25},{17,1},{25,9},{2,18},{10... | collective-permute-start | bytes 196616 | tf_op jit(solution)/shard_map/ppermute | solution.py:687
  36.5 2.3 %collective-permute-start.9 = (bf16[32,1024]{1,0:T(8,128)(2,1)S(1)}, bf16[32,1024]{1,0:T(8,128)(2,1)S(1)}, u32[]{:S(2)}, u32[]{:S(2)}) collective-permute-start(bf16[32,1024]{1,0:T(8,128)(2,1)S(1)} %get-tuple-element.52), channel_id=1, source_target_pairs={{0,16},{8,24},{16,0},{24,8},{1,17},{9,25},{17,1},{25,9},{2,18},{10... | collective-permute-start | bytes 196616 | tf_op jit(solution)/shard_map/ppermute | solution.py:687
  38.8 0.6 collective-permute-start.8
  39.4 0.0 copy-done.3
  39.4 1.9 %turn.1.weight_ref = bf16[1024,768]{1,0:T(8,128)(2,1)S(1)} custom-call(bf16[3,256,1024]{2,1,0:T(8,128)(2,1)S(1)} %copy-done.3), custom_call_target="tpu_custom_call" | custom-call | flops 1610612736 | bytes 6000000 | tf_op jit(solution)/shard_map/turn/pallas_call | solution.py:561
  41.3 2.2 %collective-permute-done.7.refs_2_ = bf16[32,1024]{1,0:T(8,128)(2,1)S(1)} collective-permute-done((bf16[32,1024]{1,0:T(8,128)(2,1)S(1)}, bf16[32,1024]{1,0:T(8,128)(2,1)S(1)}, u32[]{:S(2)}, u32[]{:S(2)}) %collective-permute-start.7) | collective-permute-done | bytes 65568 | tf_op jit(solution)/shard_map/ppermute | solution.py:687
  43.5 0.0 collective-permute-start.10
  43.5 1.3 %collective-permute-done.9.refs_3_ = bf16[32,1024]{1,0:T(8,128)(2,1)S(1)} collective-permute-done((bf16[32,1024]{1,0:T(8,128)(2,1)S(1)}, bf16[32,1024]{1,0:T(8,128)(2,1)S(1)}, u32[]{:S(2)}, u32[]{:S(2)}) %collective-permute-start.9) | collective-permute-done | bytes 65568 | tf_op jit(solution)/shard_map/ppermute | solution.py:687
  44.8 0.7 %collective-permute-start.11 = (bf16[32,1024]{1,0:T(8,128)(2,1)S(1)}, bf16[32,1024]{1,0:T(8,128)(2,1)S(1)}, u32[]{:S(2)}, u32[]{:S(2)}) collective-permute-start(bf16[32,1024]{1,0:T(8,128)(2,1)S(1)} %collective-permute-done.9.refs_3_), channel_id=1, source_target_pairs={{0,8},{8,0},{16,24},{24,16},{1,9},{9,1},{17,25},{25,17},{2,10},{10... | collective-permute-start | bytes 196616 | tf_op jit(solution)/shard_map/ppermute | solution.py:687
  45.5 2.6 %collective-permute-done.10.refs_4_ = bf16[32,1024]{1,0:T(8,128)(2,1)S(1)} collective-permute-done((bf16[32,1024]{1,0:T(8,128)(2,1)S(1)}, bf16[32,1024]{1,0:T(8,128)(2,1)S(1)}, u32[]{:S(2)}, u32[]{:S(2)}) %collective-permute-start.10) | collective-permute-done | bytes 65568 | tf_op jit(solution)/shard_map/ppermute | solution.py:687
  48.2 1.0 %collective-permute-done.11.refs_5_ = bf16[32,1024]{1,0:T(8,128)(2,1)S(1)} collective-permute-done((bf16[32,1024]{1,0:T(8,128)(2,1)S(1)}, bf16[32,1024]{1,0:T(8,128)(2,1)S(1)}, u32[]{:S(2)}, u32[]{:S(2)}) %collective-permute-start.11) | collective-permute-done | bytes 65568 | tf_op jit(solution)/shard_map/ppermute | solution.py:687
  49.2 0.0 collective-permute-done.8.refs_1_
  49.2 1.3 %attend.1 = (bf16[64,256]{1,0:T(8,128)(2,1)S(1)}, bf16[64,256]{1,0:T(8,128)(2,1)S(1)}, bf16[64,256]{1,0:T(8,128)(2,1)S(1)}, bf16[64,256]{1,0:T(8,128)(2,1)S(1)}) custom-call(f32[8,256]{1,0:T(8,128)S(1)} %get-tuple-element.48.keys_ref, bf16[1024,768]{1,0:T(8,128)(2,1)S(1)} %turn.1.weight_ref, bf16[64,1024]{1,0:T(8,128)(2,1)S(1)} %get-tuple-element.51.refs_0_, ...), custom_call_target="tpu_custom_call" | custom-call | flops 1000000000 | bytes 3000000 | tf_op jit(solution)/shard_map/attend/pallas_call | solution.py:561
  50.5 0.6 collective-permute-start.12
  51.1 1.6 %collective-permute-start.13 = (bf16[64,256]{1,0:T(8,128)(2,1)S(1)}, bf16[64,256]{1,0:T(8,128)(2,1)S(1)}, u32[]{:S(2)}, u32[]{:S(2)}) collective-permute-start(bf16[64,256]{1,0:T(8,128)(2,1)S(1)} %get-tuple-element.55), channel_id=1, source_target_pairs={{0,16},{8,24},{16,0},{24,8},{1,17},{9,25},{17,1},{25,9},{2,18},{10... | collective-permute-start | bytes 98312 | tf_op jit(solution)/shard_map/ppermute | solution.py:695
  52.7 2.3 %collective-permute-start.14 = (bf16[64,256]{1,0:T(8,128)(2,1)S(1)}, bf16[64,256]{1,0:T(8,128)(2,1)S(1)}, u32[]{:S(2)}, u32[]{:S(2)}) collective-permute-start(bf16[64,256]{1,0:T(8,128)(2,1)S(1)} %get-tuple-element.56), channel_id=1, source_target_pairs={{0,8},{8,0},{16,24},{24,16},{1,9},{9,1},{17,25},{25,17},{2,10},{10... | collective-permute-start | bytes 98312 | tf_op jit(solution)/shard_map/ppermute | solution.py:695
  55.0 0.7 %fine.1 = bf16[8,8,4,256]{3,2,1,0:T(4,128)(2,1)} custom-call(bf16[256,256]{1,0:T(8,128)(2,1)S(1)} %get-tuple-element.47.field_ref), custom_call_target="tpu_custom_call" | custom-call | bytes 4000000 | tf_op jit(solution)/shard_map/fine/pallas_call | solution.py:561
  55.7 0.6 %collective-permute-done.12.refs_0_ = bf16[64,256]{1,0:T(8,128)(2,1)S(1)} collective-permute-done((bf16[64,256]{1,0:T(8,128)(2,1)S(1)}, bf16[64,256]{1,0:T(8,128)(2,1)S(1)}, u32[]{:S(2)}, u32[]{:S(2)}) %collective-permute-start.12) | collective-permute-done | bytes 32800 | tf_op jit(solution)/shard_map/ppermute | solution.py:695
  56.3 0.0 collective-permute-done.13.refs_1_
  56.3 0.6 collective-permute-done.14.refs_2_
  56.9 0.7 %place.1 = bf16[1,64,1024]{2,1,0:T(8,128)(2,1)} custom-call(f32[8,256]{1,0:T(8,128)S(1)} %get-tuple-element.40.rest_2_.keep_ref, bf16[64,256]{1,0:T(8,128)(2,1)S(1)} %collective-permute-done.12.refs_0_, bf16[64,256]{1,0:T(8,128)(2,1)S(1)} %collective-permute-done.13.refs_1_, bf16[64,256]{1,0:T(8,128)(2,1)S(1)} %collective-permute-done.14.refs_2_, ...), custom_call_target="tpu_custom_call" | custom-call | bytes 300000 | tf_op jit(solution)/shard_map/place/pallas_call | solution.py:561
Async XLA Ops:
  0.6 0.9 %copy-start = (bf16[8,8,4,256]{3,2,1,0:T(4,128)(2,1)S(1)}, bf16[8,8,4,256]{3,2,1,0:T(4,128)(2,1)}, u32[]{:S(2)}) copy-start(bf16[8,8,4,256]{3,2,1,0:T(4,128)(2,1)} %feat_ref.1) | copy-start | bytes 393220
  1.5 0.7 %copy-start.2 = (s32[4,1,4]{2,1,0:T(1,128)S(1)}, s32[4,1,4]{2,1,0:T(1,128)}, u32[]{:S(2)}) copy-start(s32[4,1,4]{2,1,0:T(1,128)} %occ_ref.1) | copy-start | bytes 196
  3.2 10.1 %collective-permute-start = (bf16[80,256]{1,0:T(8,128)(2,1)S(1)}, bf16[80,256]{1,0:T(8,128)(2,1)S(1)}, u32[]{:S(2)}, u32[]{:S(2)}) collective-permute-start(bf16[80,256]{1,0:T(8,128)(2,1)S(1)} %get-tuple-element.32), channel_id=1, source_target_pairs={{0,8},{8,0},{16,24},{24,16},{1,9},{9,1},{17,25},{25,17},{2,10},{10... | collective-permute-start | bytes 122888 | tf_op jit(solution)/shard_map/ppermute | solution.py:603
  6.3 7.0 %collective-permute-start.1 = (bf16[80,256]{1,0:T(8,128)(2,1)S(1)}, bf16[80,256]{1,0:T(8,128)(2,1)S(1)}, u32[]{:S(2)}, u32[]{:S(2)}) collective-permute-start(bf16[80,256]{1,0:T(8,128)(2,1)S(1)} %get-tuple-element.33), channel_id=1, source_target_pairs={{0,24},{8,16},{16,8},{24,0},{1,25},{9,17},{17,9},{25,1},{2,26},{10... | collective-permute-start | bytes 122888 | tf_op jit(solution)/shard_map/ppermute | solution.py:604
  8.7 4.5 %collective-permute-start.2 = (bf16[16,256]{1,0:T(8,128)(2,1)S(1)}, bf16[16,256]{1,0:T(8,128)(2,1)S(1)}, u32[]{:S(2)}, u32[]{:S(2)}) collective-permute-start(bf16[16,256]{1,0:T(8,128)(2,1)S(1)} %get-tuple-element.34.rest_0_), channel_id=1, source_target_pairs={{0,16},{8,24},{16,0},{24,8},{1,17},{9,25},{17,1},{25,9},{2,18},{10... | collective-permute-start | bytes 24584 | tf_op jit(solution)/shard_map/ppermute | solution.py:608
  8.8 0.9 %copy-start.1 = (bf16[2,32,864]{2,1,0:T(8,128)(2,1)S(1)}, bf16[2,32,864]{2,1,0:T(8,128)(2,1)}, u32[]{:S(2)}) copy-start(bf16[2,32,864]{2,1,0:T(8,128)(2,1)} %weight_ref.2) | copy-start | bytes 331780
  13.5 1.3 %collective-permute-start.3 = (bf16[112,256]{1,0:T(8,128)(2,1)S(1)}, bf16[112,256]{1,0:T(8,128)(2,1)S(1)}, u32[]{:S(2)}, u32[]{:S(2)}) collective-permute-start(bf16[112,256]{1,0:T(8,128)(2,1)S(1)} %get-tuple-element.36.own_ref), channel_id=1, source_target_pairs={{0,1},{1,0},{2,3},{3,2},{4,5},{5,4},{6,7},{7,6},{8,9},{9,8},{10,11... | collective-permute-start | bytes 172040 | tf_op jit(solution)/shard_map/ppermute | solution.py:626
  15.0 6.7 %collective-permute-start.5 = (bf16[144,256]{1,0:T(8,128)(2,1)S(1)}, bf16[144,256]{1,0:T(8,128)(2,1)S(1)}, u32[]{:S(2)}, u32[]{:S(2)}) collective-permute-start(bf16[144,256]{1,0:T(8,128)(2,1)S(1)} %get-tuple-element.38), channel_id=1, source_target_pairs={{0,4},{4,0},{1,5},{5,1},{2,6},{6,2},{3,7},{7,3},{8,12},{12,8},{9,1... | collective-permute-start | bytes 221192 | tf_op jit(solution)/shard_map/ppermute | solution.py:644
  16.5 5.2 %collective-permute-start.4 = (bf16[112,256]{1,0:T(8,128)(2,1)S(1)}, bf16[112,256]{1,0:T(8,128)(2,1)S(1)}, u32[]{:S(2)}, u32[]{:S(2)}) collective-permute-start(bf16[112,256]{1,0:T(8,128)(2,1)S(1)} %get-tuple-element.37.own_ref), channel_id=1, source_target_pairs={{0,3},{1,2},{2,1},{3,0},{4,7},{5,6},{6,5},{7,4},{8,11},{9,10},{10,... | collective-permute-start | bytes 172040 | tf_op jit(solution)/shard_map/ppermute | solution.py:640
  17.5 4.2 %collective-permute-start.6 = (bf16[48,256]{1,0:T(8,128)(2,1)S(1)}, bf16[48,256]{1,0:T(8,128)(2,1)S(1)}, u32[]{:S(2)}, u32[]{:S(2)}) collective-permute-start(bf16[48,256]{1,0:T(8,128)(2,1)S(1)} %get-tuple-element.39), channel_id=1, source_target_pairs={{0,7},{1,6},{2,5},{3,4},{4,3},{5,2},{6,1},{7,0},{8,15},{9,14},{10,... | collective-permute-start | bytes 73736 | tf_op jit(solution)/shard_map/ppermute | solution.py:648
  34.0 5.3 %copy-start.3 = (bf16[3,256,1024]{2,1,0:T(8,128)(2,1)S(1)}, bf16[3,256,1024]{2,1,0:T(8,128)(2,1)}, u32[]{:S(2)}) copy-start(bf16[3,256,1024]{2,1,0:T(8,128)(2,1)} %weight_ref.3) | copy-start | bytes 4718596
  35.8 7.7 %collective-permute-start.7 = (bf16[32,1024]{1,0:T(8,128)(2,1)S(1)}, bf16[32,1024]{1,0:T(8,128)(2,1)S(1)}, u32[]{:S(2)}, u32[]{:S(2)}) collective-permute-start(bf16[32,1024]{1,0:T(8,128)(2,1)S(1)} %get-tuple-element.49), channel_id=1, source_target_pairs={{0,16},{8,24},{16,0},{24,8},{1,17},{9,25},{17,1},{25,9},{2,18},{10... | collective-permute-start | bytes 196616 | tf_op jit(solution)/shard_map/ppermute | solution.py:687
  36.5 8.4 %collective-permute-start.9 = (bf16[32,1024]{1,0:T(8,128)(2,1)S(1)}, bf16[32,1024]{1,0:T(8,128)(2,1)S(1)}, u32[]{:S(2)}, u32[]{:S(2)}) collective-permute-start(bf16[32,1024]{1,0:T(8,128)(2,1)S(1)} %get-tuple-element.52), channel_id=1, source_target_pairs={{0,16},{8,24},{16,0},{24,8},{1,17},{9,25},{17,1},{25,9},{2,18},{10... | collective-permute-start | bytes 196616 | tf_op jit(solution)/shard_map/ppermute | solution.py:687
  38.8 10.4 %collective-permute-start.8 = (bf16[64,1024]{1,0:T(8,128)(2,1)S(1)}, bf16[64,1024]{1,0:T(8,128)(2,1)S(1)}, u32[]{:S(2)}, u32[]{:S(2)}) collective-permute-start(bf16[64,1024]{1,0:T(8,128)(2,1)S(1)} %get-tuple-element.51.refs_0_), channel_id=1, source_target_pairs={{0,8},{8,0},{16,24},{24,16},{1,9},{9,1},{17,25},{25,17},{2,10},{10... | collective-permute-start | bytes 393224 | tf_op jit(solution)/shard_map/ppermute | solution.py:687
  43.5 4.7 %collective-permute-start.10 = (bf16[32,1024]{1,0:T(8,128)(2,1)S(1)}, bf16[32,1024]{1,0:T(8,128)(2,1)S(1)}, u32[]{:S(2)}, u32[]{:S(2)}) collective-permute-start(bf16[32,1024]{1,0:T(8,128)(2,1)S(1)} %collective-permute-done.7.refs_2_), channel_id=1, source_target_pairs={{0,8},{8,0},{16,24},{24,16},{1,9},{9,1},{17,25},{25,17},{2,10},{10... | collective-permute-start | bytes 196616 | tf_op jit(solution)/shard_map/ppermute | solution.py:687
  44.8 4.4 %collective-permute-start.11 = (bf16[32,1024]{1,0:T(8,128)(2,1)S(1)}, bf16[32,1024]{1,0:T(8,128)(2,1)S(1)}, u32[]{:S(2)}, u32[]{:S(2)}) collective-permute-start(bf16[32,1024]{1,0:T(8,128)(2,1)S(1)} %collective-permute-done.9.refs_3_), channel_id=1, source_target_pairs={{0,8},{8,0},{16,24},{24,16},{1,9},{9,1},{17,25},{25,17},{2,10},{10... | collective-permute-start | bytes 196616 | tf_op jit(solution)/shard_map/ppermute | solution.py:687
  50.5 5.8 %collective-permute-start.12 = (bf16[64,256]{1,0:T(8,128)(2,1)S(1)}, bf16[64,256]{1,0:T(8,128)(2,1)S(1)}, u32[]{:S(2)}, u32[]{:S(2)}) collective-permute-start(bf16[64,256]{1,0:T(8,128)(2,1)S(1)} %get-tuple-element.54), channel_id=1, source_target_pairs={{0,24},{8,16},{16,8},{24,0},{1,25},{9,17},{17,9},{25,1},{2,26},{10... | collective-permute-start | bytes 98312 | tf_op jit(solution)/shard_map/ppermute | solution.py:695
  51.1 5.2 %collective-permute-start.13 = (bf16[64,256]{1,0:T(8,128)(2,1)S(1)}, bf16[64,256]{1,0:T(8,128)(2,1)S(1)}, u32[]{:S(2)}, u32[]{:S(2)}) collective-permute-start(bf16[64,256]{1,0:T(8,128)(2,1)S(1)} %get-tuple-element.55), channel_id=1, source_target_pairs={{0,16},{8,24},{16,0},{24,8},{1,17},{9,25},{17,1},{25,9},{2,18},{10... | collective-permute-start | bytes 98312 | tf_op jit(solution)/shard_map/ppermute | solution.py:695
  52.7 4.2 %collective-permute-start.14 = (bf16[64,256]{1,0:T(8,128)(2,1)S(1)}, bf16[64,256]{1,0:T(8,128)(2,1)S(1)}, u32[]{:S(2)}, u32[]{:S(2)}) collective-permute-start(bf16[64,256]{1,0:T(8,128)(2,1)S(1)} %get-tuple-element.56), channel_id=1, source_target_pairs={{0,8},{8,0},{16,24},{24,16},{1,9},{9,1},{17,25},{25,17},{2,10},{10... | collective-permute-start | bytes 98312 | tf_op jit(solution)/shard_map/ppermute | solution.py:695

commit v11 on v9

--- a/solution.py
+++ b/solution.py
@@ -681,6 +681,9 @@
     for k in sorted(range(1, nx), key=lambda k: (bin(k).count("1"), -k)):
         low = k & -k
         source = [tokens] if k == 1 else blocks[k ^ low]
+        if k == 1 and nx > 2:
+            part, source[0], turned = lax.optimization_barrier((blocks[2][0], tokens, turned))
+            blocks[2] = [part] + blocks[2][1:]
         blocks[k] = [lax.ppermute(v, "gx", swaps[low]) for v in source]
     blocks = [tokens] + [v for k in range(1, nx) for v in blocks[k]]
     outs = call(

time: 57.8 us -> 58.9 us (1.019)
  starting transfers between devices: 17.8 us -> 18.6 us
    ppermute x5, starting transfers between devices: 4.28 us -> 5.13 us  [body(): blocks[k] = [lax.ppermute(v, 'gx', swaps[low]) for v in source]]
  transfers between devices with their start and end apart: 15 -> 15, of which waited for: 9 -> 8; matrix products, arithmetic and copies ran while one was open for 1% -> 1% of each run, Pallas kernels for 9% -> 9%
where the time goes in v11:
time: 58.9 us; the launch traced here: 58.7 us
  starting transfers between devices  18.6 us (32%)
  Pallas kernels  13.5 us (23%)
  waiting for transfers between devices  13.4 us (23%)
  blocking collectives  9.3 us (16%)
  local copies, waits for them, and re-layouts  2.48 us (4%)
  other arithmetic  0.72 us (1%)
  between operations  0.72 us (1%)
    pallas_call x11, Pallas kernels, call(): pl.pallas_call(kernel, out_shape=out, in_specs=list(specs), out_specs=jax...  13.5 us
    all_to_all x1, blocking collectives, body(): stats = lax.all_to_all(mine, ALL, 0, 0, tiled=True)  9.3 us
    ppermute x5, waiting for transfers between devices, body(): blocks[k] = [lax.ppermute(v, 'gx', swaps[low]) for v in source]  7.48 us
    ppermute x5, starting transfers between devices, body(): blocks[k] = [lax.ppermute(v, 'gx', swaps[low]) for v in source]  5.13 us
    ppermute x3, starting transfers between devices, body(): lax.ppermute(v, 'gx', swaps[nx - 1 - i])  4.45 us
    ppermute x1, starting transfers between devices, body(): lax.ppermute(first, 'gx', list(pairing(nx, False, False).items()))  3.09 us
    unnamed x8, local copies, waits for them, and re-layouts  2.48 us
    ppermute x1, starting transfers between devices, body(): lax.ppermute(second, 'gx', list(pairing(nx, True, narrow).items()))  2.47 us
  transfers between devices with their start and end apart: 15, of which 8 were waited for; matrix products, arithmetic and copies ran while one was open for 1% of the time, Pallas kernels for 9%

profile of v11, /device:TPU:0, one launch (start us, length us, event | category | flops | bytes accessed | tf_op | source)
XLA Modules:
  0.0 58.7 jit_solution(5465694440455590687)
XLA Ops:
  0.6 0.0 copy-start
  0.6 0.9 %copy-done = bf16[8,8,4,256]{3,2,1,0:T(4,128)(2,1)S(1)} copy-done((bf16[8,8,4,256]{3,2,1,0:T(4,128)(2,1)S(1)}, bf16[8,8,4,256]{3,2,1,0:T(4,128)(2,1)}, u32[]{:S(2)}) %copy-start) | copy-done | bytes 131096
  1.5 0.0 copy-start.2
  1.5 0.7 %copy-done.2 = s32[4,1,4]{2,1,0:T(1,128)S(1)} copy-done((s32[4,1,4]{2,1,0:T(1,128)S(1)}, s32[4,1,4]{2,1,0:T(1,128)}, u32[]{:S(2)}) %copy-start.2) | copy-done | bytes 88
  2.2 0.9 %pre.1 = (f32[8,256]{1,0:T(8,128)S(1)}, f32[8,256]{1,0:T(8,128)S(1)}, bf16[512,256]{1,0:T(8,128)(2,1)S(1)}, bf16[80,256]{1,0:T(8,128)(2,1)S(1)}, bf16[80,256]{1,...) custom-call(s32[4,1,4]{2,1,0:T(1,128)S(1)} %copy-done.2, bf16[8,8,4,256]{3,2,1,0:T(4,128)(2,1)S(1)} %copy-done), custom_call_target="tpu_custom_call" | custom-call | bytes 1000000 | tf_op jit(solution)/shard_map/pre/pallas_call | solution.py:561
  3.2 3.1 %collective-permute-start = (bf16[80,256]{1,0:T(8,128)(2,1)S(1)}, bf16[80,256]{1,0:T(8,128)(2,1)S(1)}, u32[]{:S(2)}, u32[]{:S(2)}) collective-permute-start(bf16[80,256]{1,0:T(8,128)(2,1)S(1)} %get-tuple-element.33), channel_id=1, source_target_pairs={{0,8},{8,0},{16,24},{24,16},{1,9},{9,1},{17,25},{25,17},{2,10},{10... | collective-permute-start | bytes 122888 | tf_op jit(solution)/shard_map/ppermute | solution.py:603
  6.3 2.5 %collective-permute-start.1 = (bf16[80,256]{1,0:T(8,128)(2,1)S(1)}, bf16[80,256]{1,0:T(8,128)(2,1)S(1)}, u32[]{:S(2)}, u32[]{:S(2)}) collective-permute-start(bf16[80,256]{1,0:T(8,128)(2,1)S(1)} %get-tuple-element.34), channel_id=1, source_target_pairs={{0,24},{8,16},{16,8},{24,0},{1,25},{9,17},{17,9},{25,1},{2,26},{10... | collective-permute-start | bytes 122888 | tf_op jit(solution)/shard_map/ppermute | solution.py:604
  8.7 0.1 collective-permute-start.2
  8.8 0.0 copy-start.1
  8.9 0.9 %copy-done.1 = bf16[2,32,864]{2,1,0:T(8,128)(2,1)S(1)} copy-done((bf16[2,32,864]{2,1,0:T(8,128)(2,1)S(1)}, bf16[2,32,864]{2,1,0:T(8,128)(2,1)}, u32[]{:S(2)}) %copy-start.1) | copy-done | bytes 110616
  9.7 1.4 %band0.1 = (bf16[3,1024,256]{2,1,0:T(8,128)(2,1)S(1)}, bf16[1,32,864]{2,1,0:T(8,128)(2,1)S(1)}) custom-call(bf16[2,32,864]{2,1,0:T(8,128)(2,1)S(1)} %copy-done.1), custom_call_target="tpu_custom_call" | custom-call | bytes 8000000 | tf_op jit(solution)/shard_map/band0/pallas_call | solution.py:561
  11.1 2.2 %collective-permute-done.2.rest_1_ = bf16[16,256]{1,0:T(8,128)(2,1)S(1)} collective-permute-done((bf16[16,256]{1,0:T(8,128)(2,1)S(1)}, bf16[16,256]{1,0:T(8,128)(2,1)S(1)}, u32[]{:S(2)}, u32[]{:S(2)}) %collective-permute-start.2) | collective-permute-done | bytes 8224 | tf_op jit(solution)/shard_map/ppermute | solution.py:608
  13.3 0.0 collective-permute-done.first_ref
  13.3 0.0 collective-permute-done.1.second_ref
  13.3 0.2 line.1
  13.5 0.1 collective-permute-start.3
  13.5 1.2 %collective-permute-done.3.other_ref.core_ref = bf16[112,256]{1,0:T(8,128)(2,1)S(1)} collective-permute-done((bf16[112,256]{1,0:T(8,128)(2,1)S(1)}, bf16[112,256]{1,0:T(8,128)(2,1)S(1)}, u32[]{:S(2)}, u32[]{:S(2)}) %collective-permute-start.3) | collective-permute-done | bytes 57376 | tf_op jit(solution)/shard_map/ppermute | solution.py:626
  14.8 0.2 chip.1
  15.0 1.6 %collective-permute-start.5 = (bf16[144,256]{1,0:T(8,128)(2,1)S(1)}, bf16[144,256]{1,0:T(8,128)(2,1)S(1)}, u32[]{:S(2)}, u32[]{:S(2)}) collective-permute-start(bf16[144,256]{1,0:T(8,128)(2,1)S(1)} %get-tuple-element.39), channel_id=1, source_target_pairs={{0,4},{4,0},{1,5},{5,1},{2,6},{6,2},{3,7},{7,3},{8,12},{12,8},{9,1... | collective-permute-start | bytes 221192 | tf_op jit(solution)/shard_map/ppermute | solution.py:644
  16.5 1.0 %collective-permute-start.4 = (bf16[112,256]{1,0:T(8,128)(2,1)S(1)}, bf16[112,256]{1,0:T(8,128)(2,1)S(1)}, u32[]{:S(2)}, u32[]{:S(2)}) collective-permute-start(bf16[112,256]{1,0:T(8,128)(2,1)S(1)} %get-tuple-element.38.own_ref), channel_id=1, source_target_pairs={{0,3},{1,2},{2,1},{3,0},{4,7},{5,6},{6,5},{7,4},{8,11},{9,10},{10,... | collective-permute-start | bytes 172040 | tf_op jit(solution)/shard_map/ppermute | solution.py:640
  17.5 0.7 %collective-permute-start.6 = (bf16[48,256]{1,0:T(8,128)(2,1)S(1)}, bf16[48,256]{1,0:T(8,128)(2,1)S(1)}, u32[]{:S(2)}, u32[]{:S(2)}) collective-permute-start(bf16[48,256]{1,0:T(8,128)(2,1)S(1)} %get-tuple-element.40), channel_id=1, source_target_pairs={{0,7},{1,6},{2,5},{3,4},{4,3},{5,2},{6,1},{7,0},{8,15},{9,14},{10,... | collective-permute-start | bytes 73736 | tf_op jit(solution)/shard_map/ppermute | solution.py:648
  18.3 0.7 %pad_maximum_fusion.rest_0_ = f32[6,32]{1,0:T(8,128)S(1)} fusion(f32[2,32]{1,0:T(2,128)} %param.12, f32[2,32]{1,0:T(2,128)} %param.10, f32[2,32]{1,0:T(2,128)} %param.9), kind=kLoop, calls=%fused_computation | loop fusion | flops 384 | bytes 1536 | tf_op jit(solution)/shard_map/concatenate | solution.py:610
  19.0 1.4 %band1.1 = (bf16[3,1024,256]{2,1,0:T(8,128)(2,1)S(1)}, f32[8,256]{1,0:T(8,128)S(1)}) custom-call(bf16[1,32,864]{2,1,0:T(8,128)(2,1)S(1)} %get-tuple-element.31._.weight_ref, f32[6,32]{1,0:T(8,128)S(1)} %pad_maximum_fusion.rest_0_), custom_call_target="tpu_custom_call" | custom-call | bytes 8000000 | tf_op jit(solution)/shard_map/band1/pallas_call | solution.py:561
  20.4 1.3 %collective-permute-done.6.rest_1_ = bf16[48,256]{1,0:T(8,128)(2,1)S(1)} collective-permute-done((bf16[48,256]{1,0:T(8,128)(2,1)S(1)}, bf16[48,256]{1,0:T(8,128)(2,1)S(1)}, u32[]{:S(2)}, u32[]{:S(2)}) %collective-permute-start.6) | collective-permute-done | bytes 24608 | tf_op jit(solution)/shard_map/ppermute | solution.py:648
  21.7 0.0 collective-permute-done.4.zface_ref
  21.7 0.0 collective-permute-done.5.rest_0_
  21.7 3.0 %first.1 = (f32[800,256]{1,0:T(8,128)S(1)}, f32[32,128]{1,0:T(8,128)S(1)}, f32[1152,128]{1,0:T(8,128)S(1)}) custom-call(bf16[768,256]{1,0:T(8,128)(2,1)S(1)} %get-tuple-element.36.ext_ref, bf16[112,256]{1,0:T(8,128)(2,1)S(1)} %get-tuple-element.38.own_ref, bf16[112,256]{1,0:T(8,128)(2,1)S(1)} %collective-permute-done.3.other_ref.core_ref, ...), custom_call_target="tpu_custom_call" | custom-call | flops 2000000000 | bytes 4000000 | tf_op jit(solution)/shard_map/first/pallas_call | solution.py:561
  24.7 9.3 %all_to_all.11 = f32[32,1,128]{2,1,0:T(1,128)S(1)} all-to-all(f32[32,1,128]{2,1,0:T(1,128)S(1)} %bitcast.5), channel_id=1, replica_groups=mesh['gx'=4,'gy'=2,'gz'=4] {'gx','gy','gz'}, dimensions={0} | all-to-all | bytes 32768 | tf_op jit(solution)/shard_map/all_to_all | solution.py:668
  34.0 0.0 copy-start.3
  34.0 1.8 %second.1 = (bf16[256,256]{1,0:T(8,128)(2,1)S(1)}, bf16[64,1024]{1,0:T(8,128)(2,1)S(1)}, bf16[32,1024]{1,0:T(8,128)(2,1)S(1)}, bf16[32,1024]{1,0:T(8,128)(2,1)S(1)}) custom-call(f32[32,128]{1,0:T(8,128)S(1)} %bitcast.4, f32[800,256]{1,0:T(8,128)S(1)} %get-tuple-element.45.mid_ref, f32[1152,128]{1,0:T(8,128)S(1)} %get-tuple-element.46.msk_ref, ...), custom_call_target="tpu_custom_call" | custom-call | flops 1000000000 | bytes 4000000 | tf_op jit(solution)/shard_map/second/pallas_call | solution.py:561
  35.8 0.7 %collective-permute-start.7 = (bf16[32,1024]{1,0:T(8,128)(2,1)S(1)}, bf16[32,1024]{1,0:T(8,128)(2,1)S(1)}, u32[]{:S(2)}, u32[]{:S(2)}) collective-permute-start(bf16[32,1024]{1,0:T(8,128)(2,1)S(1)} %get-tuple-element.50), channel_id=1, source_target_pairs={{0,16},{8,24},{16,0},{24,8},{1,17},{9,25},{17,1},{25,9},{2,18},{10... | collective-permute-start | bytes 196616 | tf_op jit(solution)/shard_map/ppermute | solution.py:687
  36.5 0.0 copy-done.3
  36.5 1.9 %turn.1.weight_ref = bf16[1024,768]{1,0:T(8,128)(2,1)S(1)} custom-call(bf16[3,256,1024]{2,1,0:T(8,128)(2,1)S(1)} %copy-done.3), custom_call_target="tpu_custom_call" | custom-call | flops 1610612736 | bytes 6000000 | tf_op jit(solution)/shard_map/turn/pallas_call | solution.py:561
  38.4 2.4 %collective-permute-start.9 = (bf16[32,1024]{1,0:T(8,128)(2,1)S(1)}, bf16[32,1024]{1,0:T(8,128)(2,1)S(1)}, u32[]{:S(2)}, u32[]{:S(2)}) collective-permute-start(bf16[32,1024]{1,0:T(8,128)(2,1)S(1)} %get-tuple-element.55), channel_id=1, source_target_pairs={{0,16},{8,24},{16,0},{24,8},{1,17},{9,25},{17,1},{25,9},{2,18},{10... | collective-permute-start | bytes 196616 | tf_op jit(solution)/shard_map/ppermute | solution.py:687
  40.8 2.6 %collective-permute-done.7.refs_2_ = bf16[32,1024]{1,0:T(8,128)(2,1)S(1)} collective-permute-done((bf16[32,1024]{1,0:T(8,128)(2,1)S(1)}, bf16[32,1024]{1,0:T(8,128)(2,1)S(1)}, u32[]{:S(2)}, u32[]{:S(2)}) %collective-permute-start.7) | collective-permute-done | bytes 65568 | tf_op jit(solution)/shard_map/ppermute | solution.py:687
  43.4 0.0 collective-permute-start.8
  43.4 2.0 %collective-permute-start.10 = (bf16[32,1024]{1,0:T(8,128)(2,1)S(1)}, bf16[32,1024]{1,0:T(8,128)(2,1)S(1)}, u32[]{:S(2)}, u32[]{:S(2)}) collective-permute-start(bf16[32,1024]{1,0:T(8,128)(2,1)S(1)} %collective-permute-done.7.refs_2_), channel_id=1, source_target_pairs={{0,8},{8,0},{16,24},{24,16},{1,9},{9,1},{17,25},{25,17},{2,10},{10... | collective-permute-start | bytes 196616 | tf_op jit(solution)/shard_map/ppermute | solution.py:687
  45.4 0.0 collective-permute-done.9.refs_3_
  45.4 0.0 collective-permute-start.11
  45.4 4.2 %collective-permute-done.10.refs_4_ = bf16[32,1024]{1,0:T(8,128)(2,1)S(1)} collective-permute-done((bf16[32,1024]{1,0:T(8,128)(2,1)S(1)}, bf16[32,1024]{1,0:T(8,128)(2,1)S(1)}, u32[]{:S(2)}, u32[]{:S(2)}) %collective-permute-start.10) | collective-permute-done | bytes 65568 | tf_op jit(solution)/shard_map/ppermute | solution.py:687
  49.6 0.7 %collective-permute-done.11.refs_5_ = bf16[32,1024]{1,0:T(8,128)(2,1)S(1)} collective-permute-done((bf16[32,1024]{1,0:T(8,128)(2,1)S(1)}, bf16[32,1024]{1,0:T(8,128)(2,1)S(1)}, u32[]{:S(2)}, u32[]{:S(2)}) %collective-permute-start.11) | collective-permute-done | bytes 65568 | tf_op jit(solution)/shard_map/ppermute | solution.py:687
  50.3 0.0 collective-permute-done.8.refs_1_
  50.3 1.3 %attend.1 = (bf16[64,256]{1,0:T(8,128)(2,1)S(1)}, bf16[64,256]{1,0:T(8,128)(2,1)S(1)}, bf16[64,256]{1,0:T(8,128)(2,1)S(1)}, bf16[64,256]{1,0:T(8,128)(2,1)S(1)}) custom-call(f32[8,256]{1,0:T(8,128)S(1)} %get-tuple-element.49.keys_ref, bf16[1024,768]{1,0:T(8,128)(2,1)S(1)} %turn.1.weight_ref, bf16[64,1024]{1,0:T(8,128)(2,1)S(1)} %get-tuple-element.53.refs_0_, ...), custom_call_target="tpu_custom_call" | custom-call | flops 1000000000 | bytes 3000000 | tf_op jit(solution)/shard_map/attend/pallas_call | solution.py:561
  51.7 0.3 collective-permute-start.12
  52.0 1.6 %collective-permute-start.13 = (bf16[64,256]{1,0:T(8,128)(2,1)S(1)}, bf16[64,256]{1,0:T(8,128)(2,1)S(1)}, u32[]{:S(2)}, u32[]{:S(2)}) collective-permute-start(bf16[64,256]{1,0:T(8,128)(2,1)S(1)} %get-tuple-element.57), channel_id=1, source_target_pairs={{0,16},{8,24},{16,0},{24,8},{1,17},{9,25},{17,1},{25,9},{2,18},{10... | collective-permute-start | bytes 98312 | tf_op jit(solution)/shard_map/ppermute | solution.py:695
  53.5 2.6 %collective-permute-start.14 = (bf16[64,256]{1,0:T(8,128)(2,1)S(1)}, bf16[64,256]{1,0:T(8,128)(2,1)S(1)}, u32[]{:S(2)}, u32[]{:S(2)}) collective-permute-start(bf16[64,256]{1,0:T(8,128)(2,1)S(1)} %get-tuple-element.58), channel_id=1, source_target_pairs={{0,8},{8,0},{16,24},{24,16},{1,9},{9,1},{17,25},{25,17},{2,10},{10... | collective-permute-start | bytes 98312 | tf_op jit(solution)/shard_map/ppermute | solution.py:695
  56.1 0.7 %fine.1 = bf16[8,8,4,256]{3,2,1,0:T(4,128)(2,1)} custom-call(bf16[256,256]{1,0:T(8,128)(2,1)S(1)} %get-tuple-element.48.field_ref), custom_call_target="tpu_custom_call" | custom-call | bytes 4000000 | tf_op jit(solution)/shard_map/fine/pallas_call | solution.py:561
  56.8 0.6 %collective-permute-done.12.refs_0_ = bf16[64,256]{1,0:T(8,128)(2,1)S(1)} collective-permute-done((bf16[64,256]{1,0:T(8,128)(2,1)S(1)}, bf16[64,256]{1,0:T(8,128)(2,1)S(1)}, u32[]{:S(2)}, u32[]{:S(2)}) %collective-permute-start.12) | collective-permute-done | bytes 32800 | tf_op jit(solution)/shard_map/ppermute | solution.py:695
  57.5 0.0 collective-permute-done.13.refs_1_
  57.5 0.6 collective-permute-done.14.refs_2_
  58.0 0.7 %place.1 = bf16[1,64,1024]{2,1,0:T(8,128)(2,1)} custom-call(f32[8,256]{1,0:T(8,128)S(1)} %get-tuple-element.41.rest_2_.keep_ref, bf16[64,256]{1,0:T(8,128)(2,1)S(1)} %collective-permute-done.12.refs_0_, bf16[64,256]{1,0:T(8,128)(2,1)S(1)} %collective-permute-done.13.refs_1_, bf16[64,256]{1,0:T(8,128)(2,1)S(1)} %collective-permute-done.14.refs_2_, ...), custom_call_target="tpu_custom_call" | custom-call | bytes 300000 | tf_op jit(solution)/shard_map/place/pallas_call | solution.py:561
Async XLA Ops:
  0.6 0.9 %copy-start = (bf16[8,8,4,256]{3,2,1,0:T(4,128)(2,1)S(1)}, bf16[8,8,4,256]{3,2,1,0:T(4,128)(2,1)}, u32[]{:S(2)}) copy-start(bf16[8,8,4,256]{3,2,1,0:T(4,128)(2,1)} %feat_ref.1) | copy-start | bytes 393220
  1.5 0.7 %copy-start.2 = (s32[4,1,4]{2,1,0:T(1,128)S(1)}, s32[4,1,4]{2,1,0:T(1,128)}, u32[]{:S(2)}) copy-start(s32[4,1,4]{2,1,0:T(1,128)} %occ_ref.1) | copy-start | bytes 196
  3.2 10.1 %collective-permute-start = (bf16[80,256]{1,0:T(8,128)(2,1)S(1)}, bf16[80,256]{1,0:T(8,128)(2,1)S(1)}, u32[]{:S(2)}, u32[]{:S(2)}) collective-permute-start(bf16[80,256]{1,0:T(8,128)(2,1)S(1)} %get-tuple-element.33), channel_id=1, source_target_pairs={{0,8},{8,0},{16,24},{24,16},{1,9},{9,1},{17,25},{25,17},{2,10},{10... | collective-permute-start | bytes 122888 | tf_op jit(solution)/shard_map/ppermute | solution.py:603
  6.3 7.0 %collective-permute-start.1 = (bf16[80,256]{1,0:T(8,128)(2,1)S(1)}, bf16[80,256]{1,0:T(8,128)(2,1)S(1)}, u32[]{:S(2)}, u32[]{:S(2)}) collective-permute-start(bf16[80,256]{1,0:T(8,128)(2,1)S(1)} %get-tuple-element.34), channel_id=1, source_target_pairs={{0,24},{8,16},{16,8},{24,0},{1,25},{9,17},{17,9},{25,1},{2,26},{10... | collective-permute-start | bytes 122888 | tf_op jit(solution)/shard_map/ppermute | solution.py:604
  8.7 4.5 %collective-permute-start.2 = (bf16[16,256]{1,0:T(8,128)(2,1)S(1)}, bf16[16,256]{1,0:T(8,128)(2,1)S(1)}, u32[]{:S(2)}, u32[]{:S(2)}) collective-permute-start(bf16[16,256]{1,0:T(8,128)(2,1)S(1)} %get-tuple-element.35.rest_0_), channel_id=1, source_target_pairs={{0,16},{8,24},{16,0},{24,8},{1,17},{9,25},{17,1},{25,9},{2,18},{10... | collective-permute-start | bytes 24584 | tf_op jit(solution)/shard_map/ppermute | solution.py:608
  8.8 0.9 %copy-start.1 = (bf16[2,32,864]{2,1,0:T(8,128)(2,1)S(1)}, bf16[2,32,864]{2,1,0:T(8,128)(2,1)}, u32[]{:S(2)}) copy-start(bf16[2,32,864]{2,1,0:T(8,128)(2,1)} %weight_ref.2) | copy-start | bytes 331780
  13.5 1.3 %collective-permute-start.3 = (bf16[112,256]{1,0:T(8,128)(2,1)S(1)}, bf16[112,256]{1,0:T(8,128)(2,1)S(1)}, u32[]{:S(2)}, u32[]{:S(2)}) collective-permute-start(bf16[112,256]{1,0:T(8,128)(2,1)S(1)} %get-tuple-element.37.own_ref), channel_id=1, source_target_pairs={{0,1},{1,0},{2,3},{3,2},{4,5},{5,4},{6,7},{7,6},{8,9},{9,8},{10,11... | collective-permute-start | bytes 172040 | tf_op jit(solution)/shard_map/ppermute | solution.py:626
  15.0 6.7 %collective-permute-start.5 = (bf16[144,256]{1,0:T(8,128)(2,1)S(1)}, bf16[144,256]{1,0:T(8,128)(2,1)S(1)}, u32[]{:S(2)}, u32[]{:S(2)}) collective-permute-start(bf16[144,256]{1,0:T(8,128)(2,1)S(1)} %get-tuple-element.39), channel_id=1, source_target_pairs={{0,4},{4,0},{1,5},{5,1},{2,6},{6,2},{3,7},{7,3},{8,12},{12,8},{9,1... | collective-permute-start | bytes 221192 | tf_op jit(solution)/shard_map/ppermute | solution.py:644
  16.5 5.2 %collective-permute-start.4 = (bf16[112,256]{1,0:T(8,128)(2,1)S(1)}, bf16[112,256]{1,0:T(8,128)(2,1)S(1)}, u32[]{:S(2)}, u32[]{:S(2)}) collective-permute-start(bf16[112,256]{1,0:T(8,128)(2,1)S(1)} %get-tuple-element.38.own_ref), channel_id=1, source_target_pairs={{0,3},{1,2},{2,1},{3,0},{4,7},{5,6},{6,5},{7,4},{8,11},{9,10},{10,... | collective-permute-start | bytes 172040 | tf_op jit(solution)/shard_map/ppermute | solution.py:640
  17.5 4.2 %collective-permute-start.6 = (bf16[48,256]{1,0:T(8,128)(2,1)S(1)}, bf16[48,256]{1,0:T(8,128)(2,1)S(1)}, u32[]{:S(2)}, u32[]{:S(2)}) collective-permute-start(bf16[48,256]{1,0:T(8,128)(2,1)S(1)} %get-tuple-element.40), channel_id=1, source_target_pairs={{0,7},{1,6},{2,5},{3,4},{4,3},{5,2},{6,1},{7,0},{8,15},{9,14},{10,... | collective-permute-start | bytes 73736 | tf_op jit(solution)/shard_map/ppermute | solution.py:648
  34.0 2.4 %copy-start.3 = (bf16[3,256,1024]{2,1,0:T(8,128)(2,1)S(1)}, bf16[3,256,1024]{2,1,0:T(8,128)(2,1)}, u32[]{:S(2)}) copy-start(bf16[3,256,1024]{2,1,0:T(8,128)(2,1)} %weight_ref.3) | copy-start | bytes 4718596
  35.8 7.6 %collective-permute-start.7 = (bf16[32,1024]{1,0:T(8,128)(2,1)S(1)}, bf16[32,1024]{1,0:T(8,128)(2,1)S(1)}, u32[]{:S(2)}, u32[]{:S(2)}) collective-permute-start(bf16[32,1024]{1,0:T(8,128)(2,1)S(1)} %get-tuple-element.50), channel_id=1, source_target_pairs={{0,16},{8,24},{16,0},{24,8},{1,17},{9,25},{17,1},{25,9},{2,18},{10... | collective-permute-start | bytes 196616 | tf_op jit(solution)/shard_map/ppermute | solution.py:687
  38.4 7.0 %collective-permute-start.9 = (bf16[32,1024]{1,0:T(8,128)(2,1)S(1)}, bf16[32,1024]{1,0:T(8,128)(2,1)S(1)}, u32[]{:S(2)}, u32[]{:S(2)}) collective-permute-start(bf16[32,1024]{1,0:T(8,128)(2,1)S(1)} %get-tuple-element.55), channel_id=1, source_target_pairs={{0,16},{8,24},{16,0},{24,8},{1,17},{9,25},{17,1},{25,9},{2,18},{10... | collective-permute-start | bytes 196616 | tf_op jit(solution)/shard_map/ppermute | solution.py:687
  43.4 7.0 %collective-permute-start.8 = (bf16[64,1024]{1,0:T(8,128)(2,1)S(1)}, bf16[64,1024]{1,0:T(8,128)(2,1)S(1)}, u32[]{:S(2)}, u32[]{:S(2)}) collective-permute-start(bf16[64,1024]{1,0:T(8,128)(2,1)S(1)} %get-tuple-element.53.refs_0_), channel_id=1, source_target_pairs={{0,8},{8,0},{16,24},{24,16},{1,9},{9,1},{17,25},{25,17},{2,10},{10... | collective-permute-start | bytes 393224 | tf_op jit(solution)/shard_map/ppermute | solution.py:687
  43.4 6.2 %collective-permute-start.10 = (bf16[32,1024]{1,0:T(8,128)(2,1)S(1)}, bf16[32,1024]{1,0:T(8,128)(2,1)S(1)}, u32[]{:S(2)}, u32[]{:S(2)}) collective-permute-start(bf16[32,1024]{1,0:T(8,128)(2,1)S(1)} %collective-permute-done.7.refs_2_), channel_id=1, source_target_pairs={{0,8},{8,0},{16,24},{24,16},{1,9},{9,1},{17,25},{25,17},{2,10},{10... | collective-permute-start | bytes 196616 | tf_op jit(solution)/shard_map/ppermute | solution.py:687
  45.4 4.9 %collective-permute-start.11 = (bf16[32,1024]{1,0:T(8,128)(2,1)S(1)}, bf16[32,1024]{1,0:T(8,128)(2,1)S(1)}, u32[]{:S(2)}, u32[]{:S(2)}) collective-permute-start(bf16[32,1024]{1,0:T(8,128)(2,1)S(1)} %collective-permute-done.9.refs_3_), channel_id=1, source_target_pairs={{0,8},{8,0},{16,24},{24,16},{1,9},{9,1},{17,25},{25,17},{2,10},{10... | collective-permute-start | bytes 196616 | tf_op jit(solution)/shard_map/ppermute | solution.py:687
  51.7 5.8 %collective-permute-start.12 = (bf16[64,256]{1,0:T(8,128)(2,1)S(1)}, bf16[64,256]{1,0:T(8,128)(2,1)S(1)}, u32[]{:S(2)}, u32[]{:S(2)}) collective-permute-start(bf16[64,256]{1,0:T(8,128)(2,1)S(1)} %get-tuple-element.56), channel_id=1, source_target_pairs={{0,24},{8,16},{16,8},{24,0},{1,25},{9,17},{17,9},{25,1},{2,26},{10... | collective-permute-start | bytes 98312 | tf_op jit(solution)/shard_map/ppermute | solution.py:695
  52.0 5.5 %collective-permute-start.13 = (bf16[64,256]{1,0:T(8,128)(2,1)S(1)}, bf16[64,256]{1,0:T(8,128)(2,1)S(1)}, u32[]{:S(2)}, u32[]{:S(2)}) collective-permute-start(bf16[64,256]{1,0:T(8,128)(2,1)S(1)} %get-tuple-element.57), channel_id=1, source_target_pairs={{0,16},{8,24},{16,0},{24,8},{1,17},{9,25},{17,1},{25,9},{2,18},{10... | collective-permute-start | bytes 98312 | tf_op jit(solution)/shard_map/ppermute | solution.py:695
  53.5 4.5 %collective-permute-start.14 = (bf16[64,256]{1,0:T(8,128)(2,1)S(1)}, bf16[64,256]{1,0:T(8,128)(2,1)S(1)}, u32[]{:S(2)}, u32[]{:S(2)}) collective-permute-start(bf16[64,256]{1,0:T(8,128)(2,1)S(1)} %get-tuple-element.58), channel_id=1, source_target_pairs={{0,8},{8,0},{16,24},{24,16},{1,9},{9,1},{17,25},{25,17},{2,10},{10... | collective-permute-start | bytes 98312 | tf_op jit(solution)/shard_map/ppermute | solution.py:695

commit v12 on v11

--- a/solution.py
+++ b/solution.py
@@ -682,7 +682,7 @@
         low = k & -k
         source = [tokens] if k == 1 else blocks[k ^ low]
         if k == 1 and nx > 2:
-            part, source[0], turned = lax.optimization_barrier((blocks[2][0], tokens, turned))
+            part, source[0] = lax.optimization_barrier((blocks[2][0], tokens))
             blocks[2] = [part] + blocks[2][1:]
         blocks[k] = [lax.ppermute(v, "gx", swaps[low]) for v in source]
     blocks = [tokens] + [v for k in range(1, nx) for v in blocks[k]]

time: 58.9 us -> 60.2 us (1.022)
  waiting for transfers between devices: 13.4 us -> 14.7 us
    ppermute x5, waiting for transfers between devices: 7.48 us -> 8.76 us  [body(): blocks[k] = [lax.ppermute(v, 'gx', swaps[low]) for v in source]]
where the time goes in v12:
time: 60.2 us; the launch traced here: 59.9 us
  starting transfers between devices  18.5 us (31%)
  waiting for transfers between devices  14.7 us (24%)
  Pallas kernels  13.5 us (22%)
  blocking collectives  9.3 us (15%)
  local copies, waits for them, and re-layouts  2.48 us (4%)
  other arithmetic  0.72 us (1%)
  between operations  0.72 us (1%)
    pallas_call x11, Pallas kernels, call(): pl.pallas_call(kernel, out_shape=out, in_specs=list(specs), out_specs=jax...  13.5 us
    all_to_all x1, blocking collectives, body(): stats = lax.all_to_all(mine, ALL, 0, 0, tiled=True)  9.3 us
    ppermute x5, waiting for transfers between devices, body(): blocks[k] = [lax.ppermute(v, 'gx', swaps[low]) for v in source]  8.76 us
    ppermute x5, starting transfers between devices, body(): blocks[k] = [lax.ppermute(v, 'gx', swaps[low]) for v in source]  5.06 us
    ppermute x3, starting transfers between devices, body(): lax.ppermute(v, 'gx', swaps[nx - 1 - i])  4.45 us
    ppermute x1, starting transfers between devices, body(): lax.ppermute(first, 'gx', list(pairing(nx, False, False).items()))  3.09 us
    unnamed x8, local copies, waits for them, and re-layouts  2.48 us
    ppermute x1, starting transfers between devices, body(): lax.ppermute(second, 'gx', list(pairing(nx, True, narrow).items()))  2.47 us
  transfers between devices with their start and end apart: 15, of which 8 were waited for; matrix products, arithmetic and copies ran while one was open for 1% of the time, Pallas kernels for 9%

profile of v12, /device:TPU:0, one launch (start us, length us, event | category | flops | bytes accessed | tf_op | source)
XLA Modules:
  0.0 59.9 jit_solution(17783668233428510506)
XLA Ops:
  0.6 0.0 copy-start
  0.6 0.9 %copy-done = bf16[8,8,4,256]{3,2,1,0:T(4,128)(2,1)S(1)} copy-done((bf16[8,8,4,256]{3,2,1,0:T(4,128)(2,1)S(1)}, bf16[8,8,4,256]{3,2,1,0:T(4,128)(2,1)}, u32[]{:S(2)}) %copy-start) | copy-done | bytes 131096
  1.5 0.0 copy-start.2
  1.5 0.7 %copy-done.2 = s32[4,1,4]{2,1,0:T(1,128)S(1)} copy-done((s32[4,1,4]{2,1,0:T(1,128)S(1)}, s32[4,1,4]{2,1,0:T(1,128)}, u32[]{:S(2)}) %copy-start.2) | copy-done | bytes 88
  2.2 0.9 %pre.1 = (f32[8,256]{1,0:T(8,128)S(1)}, f32[8,256]{1,0:T(8,128)S(1)}, bf16[512,256]{1,0:T(8,128)(2,1)S(1)}, bf16[80,256]{1,0:T(8,128)(2,1)S(1)}, bf16[80,256]{1,...) custom-call(s32[4,1,4]{2,1,0:T(1,128)S(1)} %copy-done.2, bf16[8,8,4,256]{3,2,1,0:T(4,128)(2,1)S(1)} %copy-done), custom_call_target="tpu_custom_call" | custom-call | bytes 1000000 | tf_op jit(solution)/shard_map/pre/pallas_call | solution.py:561
  3.2 3.1 %collective-permute-start = (bf16[80,256]{1,0:T(8,128)(2,1)S(1)}, bf16[80,256]{1,0:T(8,128)(2,1)S(1)}, u32[]{:S(2)}, u32[]{:S(2)}) collective-permute-start(bf16[80,256]{1,0:T(8,128)(2,1)S(1)} %get-tuple-element.32), channel_id=1, source_target_pairs={{0,8},{8,0},{16,24},{24,16},{1,9},{9,1},{17,25},{25,17},{2,10},{10... | collective-permute-start | bytes 122888 | tf_op jit(solution)/shard_map/ppermute | solution.py:603
  6.3 2.5 %collective-permute-start.1 = (bf16[80,256]{1,0:T(8,128)(2,1)S(1)}, bf16[80,256]{1,0:T(8,128)(2,1)S(1)}, u32[]{:S(2)}, u32[]{:S(2)}) collective-permute-start(bf16[80,256]{1,0:T(8,128)(2,1)S(1)} %get-tuple-element.33), channel_id=1, source_target_pairs={{0,24},{8,16},{16,8},{24,0},{1,25},{9,17},{17,9},{25,1},{2,26},{10... | collective-permute-start | bytes 122888 | tf_op jit(solution)/shard_map/ppermute | solution.py:604
  8.7 0.1 collective-permute-start.2
  8.8 0.0 copy-start.1
  8.9 0.9 %copy-done.1 = bf16[2,32,864]{2,1,0:T(8,128)(2,1)S(1)} copy-done((bf16[2,32,864]{2,1,0:T(8,128)(2,1)S(1)}, bf16[2,32,864]{2,1,0:T(8,128)(2,1)}, u32[]{:S(2)}) %copy-start.1) | copy-done | bytes 110616
  9.7 1.4 %band0.1 = (bf16[3,1024,256]{2,1,0:T(8,128)(2,1)S(1)}, bf16[1,32,864]{2,1,0:T(8,128)(2,1)S(1)}) custom-call(bf16[2,32,864]{2,1,0:T(8,128)(2,1)S(1)} %copy-done.1), custom_call_target="tpu_custom_call" | custom-call | bytes 8000000 | tf_op jit(solution)/shard_map/band0/pallas_call | solution.py:561
  11.1 2.2 %collective-permute-done.2.rest_1_ = bf16[16,256]{1,0:T(8,128)(2,1)S(1)} collective-permute-done((bf16[16,256]{1,0:T(8,128)(2,1)S(1)}, bf16[16,256]{1,0:T(8,128)(2,1)S(1)}, u32[]{:S(2)}, u32[]{:S(2)}) %collective-permute-start.2) | collective-permute-done | bytes 8224 | tf_op jit(solution)/shard_map/ppermute | solution.py:608
  13.3 0.0 collective-permute-done.first_ref
  13.3 0.0 collective-permute-done.1.second_ref
  13.3 0.2 line.1
  13.5 0.1 collective-permute-start.3
  13.5 1.2 %collective-permute-done.3.other_ref.core_ref = bf16[112,256]{1,0:T(8,128)(2,1)S(1)} collective-permute-done((bf16[112,256]{1,0:T(8,128)(2,1)S(1)}, bf16[112,256]{1,0:T(8,128)(2,1)S(1)}, u32[]{:S(2)}, u32[]{:S(2)}) %collective-permute-start.3) | collective-permute-done | bytes 57376 | tf_op jit(solution)/shard_map/ppermute | solution.py:626
  14.8 0.2 chip.1
  15.0 1.6 %collective-permute-start.5 = (bf16[144,256]{1,0:T(8,128)(2,1)S(1)}, bf16[144,256]{1,0:T(8,128)(2,1)S(1)}, u32[]{:S(2)}, u32[]{:S(2)}) collective-permute-start(bf16[144,256]{1,0:T(8,128)(2,1)S(1)} %get-tuple-element.38), channel_id=1, source_target_pairs={{0,4},{4,0},{1,5},{5,1},{2,6},{6,2},{3,7},{7,3},{8,12},{12,8},{9,1... | collective-permute-start | bytes 221192 | tf_op jit(solution)/shard_map/ppermute | solution.py:644
  16.5 1.0 %collective-permute-start.4 = (bf16[112,256]{1,0:T(8,128)(2,1)S(1)}, bf16[112,256]{1,0:T(8,128)(2,1)S(1)}, u32[]{:S(2)}, u32[]{:S(2)}) collective-permute-start(bf16[112,256]{1,0:T(8,128)(2,1)S(1)} %get-tuple-element.37.own_ref), channel_id=1, source_target_pairs={{0,3},{1,2},{2,1},{3,0},{4,7},{5,6},{6,5},{7,4},{8,11},{9,10},{10,... | collective-permute-start | bytes 172040 | tf_op jit(solution)/shard_map/ppermute | solution.py:640
  17.5 0.7 %collective-permute-start.6 = (bf16[48,256]{1,0:T(8,128)(2,1)S(1)}, bf16[48,256]{1,0:T(8,128)(2,1)S(1)}, u32[]{:S(2)}, u32[]{:S(2)}) collective-permute-start(bf16[48,256]{1,0:T(8,128)(2,1)S(1)} %get-tuple-element.39), channel_id=1, source_target_pairs={{0,7},{1,6},{2,5},{3,4},{4,3},{5,2},{6,1},{7,0},{8,15},{9,14},{10,... | collective-permute-start | bytes 73736 | tf_op jit(solution)/shard_map/ppermute | solution.py:648
  18.3 0.7 %pad_maximum_fusion.rest_0_ = f32[6,32]{1,0:T(8,128)S(1)} fusion(f32[2,32]{1,0:T(2,128)} %param.12, f32[2,32]{1,0:T(2,128)} %param.10, f32[2,32]{1,0:T(2,128)} %param.9), kind=kLoop, calls=%fused_computation | loop fusion | flops 384 | bytes 1536 | tf_op jit(solution)/shard_map/concatenate | solution.py:610
  19.0 1.4 %band1.1 = (bf16[3,1024,256]{2,1,0:T(8,128)(2,1)S(1)}, f32[8,256]{1,0:T(8,128)S(1)}) custom-call(bf16[1,32,864]{2,1,0:T(8,128)(2,1)S(1)} %get-tuple-element.30._.weight_ref, f32[6,32]{1,0:T(8,128)S(1)} %pad_maximum_fusion.rest_0_), custom_call_target="tpu_custom_call" | custom-call | bytes 8000000 | tf_op jit(solution)/shard_map/band1/pallas_call | solution.py:561
  20.4 1.3 %collective-permute-done.6.rest_1_ = bf16[48,256]{1,0:T(8,128)(2,1)S(1)} collective-permute-done((bf16[48,256]{1,0:T(8,128)(2,1)S(1)}, bf16[48,256]{1,0:T(8,128)(2,1)S(1)}, u32[]{:S(2)}, u32[]{:S(2)}) %collective-permute-start.6) | collective-permute-done | bytes 24608 | tf_op jit(solution)/shard_map/ppermute | solution.py:648
  21.7 0.0 collective-permute-done.4.zface_ref
  21.7 0.0 collective-permute-done.5.rest_0_
  21.7 3.0 %first.1 = (f32[800,256]{1,0:T(8,128)S(1)}, f32[32,128]{1,0:T(8,128)S(1)}, f32[1152,128]{1,0:T(8,128)S(1)}) custom-call(bf16[768,256]{1,0:T(8,128)(2,1)S(1)} %get-tuple-element.35.ext_ref, bf16[112,256]{1,0:T(8,128)(2,1)S(1)} %get-tuple-element.37.own_ref, bf16[112,256]{1,0:T(8,128)(2,1)S(1)} %collective-permute-done.3.other_ref.core_ref, ...), custom_call_target="tpu_custom_call" | custom-call | flops 2000000000 | bytes 4000000 | tf_op jit(solution)/shard_map/first/pallas_call | solution.py:561
  24.7 9.3 %all_to_all.11 = f32[32,1,128]{2,1,0:T(1,128)S(1)} all-to-all(f32[32,1,128]{2,1,0:T(1,128)S(1)} %bitcast.5), channel_id=1, replica_groups=mesh['gx'=4,'gy'=2,'gz'=4] {'gx','gy','gz'}, dimensions={0} | all-to-all | bytes 32768 | tf_op jit(solution)/shard_map/all_to_all | solution.py:668
  34.0 0.0 copy-start.3
  34.0 1.8 %second.1 = (bf16[256,256]{1,0:T(8,128)(2,1)S(1)}, bf16[64,1024]{1,0:T(8,128)(2,1)S(1)}, bf16[32,1024]{1,0:T(8,128)(2,1)S(1)}, bf16[32,1024]{1,0:T(8,128)(2,1)S(1)}) custom-call(f32[32,128]{1,0:T(8,128)S(1)} %bitcast.4, f32[800,256]{1,0:T(8,128)S(1)} %get-tuple-element.44.mid_ref, f32[1152,128]{1,0:T(8,128)S(1)} %get-tuple-element.45.msk_ref, ...), custom_call_target="tpu_custom_call" | custom-call | flops 1000000000 | bytes 4000000 | tf_op jit(solution)/shard_map/second/pallas_call | solution.py:561
  35.8 0.7 %collective-permute-start.7 = (bf16[32,1024]{1,0:T(8,128)(2,1)S(1)}, bf16[32,1024]{1,0:T(8,128)(2,1)S(1)}, u32[]{:S(2)}, u32[]{:S(2)}) collective-permute-start(bf16[32,1024]{1,0:T(8,128)(2,1)S(1)} %get-tuple-element.50), channel_id=1, source_target_pairs={{0,16},{8,24},{16,0},{24,8},{1,17},{9,25},{17,1},{25,9},{2,18},{10... | collective-permute-start | bytes 196616 | tf_op jit(solution)/shard_map/ppermute | solution.py:687
  36.5 2.3 %collective-permute-start.9 = (bf16[32,1024]{1,0:T(8,128)(2,1)S(1)}, bf16[32,1024]{1,0:T(8,128)(2,1)S(1)}, u32[]{:S(2)}, u32[]{:S(2)}) collective-permute-start(bf16[32,1024]{1,0:T(8,128)(2,1)S(1)} %get-tuple-element.53), channel_id=1, source_target_pairs={{0,16},{8,24},{16,0},{24,8},{1,17},{9,25},{17,1},{25,9},{2,18},{10... | collective-permute-start | bytes 196616 | tf_op jit(solution)/shard_map/ppermute | solution.py:687
  38.8 4.6 %collective-permute-done.7.refs_2_ = bf16[32,1024]{1,0:T(8,128)(2,1)S(1)} collective-permute-done((bf16[32,1024]{1,0:T(8,128)(2,1)S(1)}, bf16[32,1024]{1,0:T(8,128)(2,1)S(1)}, u32[]{:S(2)}, u32[]{:S(2)}) %collective-permute-start.7) | collective-permute-done | bytes 65568 | tf_op jit(solution)/shard_map/ppermute | solution.py:687
  43.4 0.0 collective-permute-start.8
  43.4 2.0 %collective-permute-start.10 = (bf16[32,1024]{1,0:T(8,128)(2,1)S(1)}, bf16[32,1024]{1,0:T(8,128)(2,1)S(1)}, u32[]{:S(2)}, u32[]{:S(2)}) collective-permute-start(bf16[32,1024]{1,0:T(8,128)(2,1)S(1)} %collective-permute-done.7.refs_2_), channel_id=1, source_target_pairs={{0,8},{8,0},{16,24},{24,16},{1,9},{9,1},{17,25},{25,17},{2,10},{10... | collective-permute-start | bytes 196616 | tf_op jit(solution)/shard_map/ppermute | solution.py:687
  45.4 0.0 collective-permute-done.9.refs_3_
  45.4 0.0 collective-permute-start.11
  45.5 0.0 copy-done.3
  45.5 1.9 %turn.1.weight_ref = bf16[1024,768]{1,0:T(8,128)(2,1)S(1)} custom-call(bf16[3,256,1024]{2,1,0:T(8,128)(2,1)S(1)} %copy-done.3), custom_call_target="tpu_custom_call" | custom-call | flops 1610612736 | bytes 6000000 | tf_op jit(solution)/shard_map/turn/pallas_call | solution.py:561
  47.4 3.4 %collective-permute-done.10.refs_4_ = bf16[32,1024]{1,0:T(8,128)(2,1)S(1)} collective-permute-done((bf16[32,1024]{1,0:T(8,128)(2,1)S(1)}, bf16[32,1024]{1,0:T(8,128)(2,1)S(1)}, u32[]{:S(2)}, u32[]{:S(2)}) %collective-permute-start.10) | collective-permute-done | bytes 65568 | tf_op jit(solution)/shard_map/ppermute | solution.py:687
  50.8 0.7 %collective-permute-done.11.refs_5_ = bf16[32,1024]{1,0:T(8,128)(2,1)S(1)} collective-permute-done((bf16[32,1024]{1,0:T(8,128)(2,1)S(1)}, bf16[32,1024]{1,0:T(8,128)(2,1)S(1)}, u32[]{:S(2)}, u32[]{:S(2)}) %collective-permute-start.11) | collective-permute-done | bytes 65568 | tf_op jit(solution)/shard_map/ppermute | solution.py:687
  51.5 0.0 collective-permute-done.8.refs_1_
  51.5 1.3 %attend.1 = (bf16[64,256]{1,0:T(8,128)(2,1)S(1)}, bf16[64,256]{1,0:T(8,128)(2,1)S(1)}, bf16[64,256]{1,0:T(8,128)(2,1)S(1)}, bf16[64,256]{1,0:T(8,128)(2,1)S(1)}) custom-call(f32[8,256]{1,0:T(8,128)S(1)} %get-tuple-element.48.keys_ref, bf16[1024,768]{1,0:T(8,128)(2,1)S(1)} %turn.1.weight_ref, bf16[64,1024]{1,0:T(8,128)(2,1)S(1)} %get-tuple-element.51.refs_0_, ...), custom_call_target="tpu_custom_call" | custom-call | flops 1000000000 | bytes 3000000 | tf_op jit(solution)/shard_map/attend/pallas_call | solution.py:561
  52.9 0.1 collective-permute-start.12
  53.0 1.7 %collective-permute-start.13 = (bf16[64,256]{1,0:T(8,128)(2,1)S(1)}, bf16[64,256]{1,0:T(8,128)(2,1)S(1)}, u32[]{:S(2)}, u32[]{:S(2)}) collective-permute-start(bf16[64,256]{1,0:T(8,128)(2,1)S(1)} %get-tuple-element.55), channel_id=1, source_target_pairs={{0,16},{8,24},{16,0},{24,8},{1,17},{9,25},{17,1},{25,9},{2,18},{10... | collective-permute-start | bytes 98312 | tf_op jit(solution)/shard_map/ppermute | solution.py:695
  54.7 2.6 %collective-permute-start.14 = (bf16[64,256]{1,0:T(8,128)(2,1)S(1)}, bf16[64,256]{1,0:T(8,128)(2,1)S(1)}, u32[]{:S(2)}, u32[]{:S(2)}) collective-permute-start(bf16[64,256]{1,0:T(8,128)(2,1)S(1)} %get-tuple-element.56), channel_id=1, source_target_pairs={{0,8},{8,0},{16,24},{24,16},{1,9},{9,1},{17,25},{25,17},{2,10},{10... | collective-permute-start | bytes 98312 | tf_op jit(solution)/shard_map/ppermute | solution.py:695
  57.4 0.7 %fine.1 = bf16[8,8,4,256]{3,2,1,0:T(4,128)(2,1)} custom-call(bf16[256,256]{1,0:T(8,128)(2,1)S(1)} %get-tuple-element.47.field_ref), custom_call_target="tpu_custom_call" | custom-call | bytes 4000000 | tf_op jit(solution)/shard_map/fine/pallas_call | solution.py:561
  58.0 0.6 %collective-permute-done.12.refs_0_ = bf16[64,256]{1,0:T(8,128)(2,1)S(1)} collective-permute-done((bf16[64,256]{1,0:T(8,128)(2,1)S(1)}, bf16[64,256]{1,0:T(8,128)(2,1)S(1)}, u32[]{:S(2)}, u32[]{:S(2)}) %collective-permute-start.12) | collective-permute-done | bytes 32800 | tf_op jit(solution)/shard_map/ppermute | solution.py:695
  58.7 0.0 collective-permute-done.13.refs_1_
  58.7 0.6 collective-permute-done.14.refs_2_
  59.2 0.7 %place.1 = bf16[1,64,1024]{2,1,0:T(8,128)(2,1)} custom-call(f32[8,256]{1,0:T(8,128)S(1)} %get-tuple-element.40.rest_2_.keep_ref, bf16[64,256]{1,0:T(8,128)(2,1)S(1)} %collective-permute-done.12.refs_0_, bf16[64,256]{1,0:T(8,128)(2,1)S(1)} %collective-permute-done.13.refs_1_, bf16[64,256]{1,0:T(8,128)(2,1)S(1)} %collective-permute-done.14.refs_2_, ...), custom_call_target="tpu_custom_call" | custom-call | bytes 300000 | tf_op jit(solution)/shard_map/place/pallas_call | solution.py:561
Async XLA Ops:
  0.6 0.9 %copy-start = (bf16[8,8,4,256]{3,2,1,0:T(4,128)(2,1)S(1)}, bf16[8,8,4,256]{3,2,1,0:T(4,128)(2,1)}, u32[]{:S(2)}) copy-start(bf16[8,8,4,256]{3,2,1,0:T(4,128)(2,1)} %feat_ref.1) | copy-start | bytes 393220
  1.5 0.7 %copy-start.2 = (s32[4,1,4]{2,1,0:T(1,128)S(1)}, s32[4,1,4]{2,1,0:T(1,128)}, u32[]{:S(2)}) copy-start(s32[4,1,4]{2,1,0:T(1,128)} %occ_ref.1) | copy-start | bytes 196
  3.2 10.1 %collective-permute-start = (bf16[80,256]{1,0:T(8,128)(2,1)S(1)}, bf16[80,256]{1,0:T(8,128)(2,1)S(1)}, u32[]{:S(2)}, u32[]{:S(2)}) collective-permute-start(bf16[80,256]{1,0:T(8,128)(2,1)S(1)} %get-tuple-element.32), channel_id=1, source_target_pairs={{0,8},{8,0},{16,24},{24,16},{1,9},{9,1},{17,25},{25,17},{2,10},{10... | collective-permute-start | bytes 122888 | tf_op jit(solution)/shard_map/ppermute | solution.py:603
  6.3 7.0 %collective-permute-start.1 = (bf16[80,256]{1,0:T(8,128)(2,1)S(1)}, bf16[80,256]{1,0:T(8,128)(2,1)S(1)}, u32[]{:S(2)}, u32[]{:S(2)}) collective-permute-start(bf16[80,256]{1,0:T(8,128)(2,1)S(1)} %get-tuple-element.33), channel_id=1, source_target_pairs={{0,24},{8,16},{16,8},{24,0},{1,25},{9,17},{17,9},{25,1},{2,26},{10... | collective-permute-start | bytes 122888 | tf_op jit(solution)/shard_map/ppermute | solution.py:604
  8.7 4.5 %collective-permute-start.2 = (bf16[16,256]{1,0:T(8,128)(2,1)S(1)}, bf16[16,256]{1,0:T(8,128)(2,1)S(1)}, u32[]{:S(2)}, u32[]{:S(2)}) collective-permute-start(bf16[16,256]{1,0:T(8,128)(2,1)S(1)} %get-tuple-element.34.rest_0_), channel_id=1, source_target_pairs={{0,16},{8,24},{16,0},{24,8},{1,17},{9,25},{17,1},{25,9},{2,18},{10... | collective-permute-start | bytes 24584 | tf_op jit(solution)/shard_map/ppermute | solution.py:608
  8.8 0.9 %copy-start.1 = (bf16[2,32,864]{2,1,0:T(8,128)(2,1)S(1)}, bf16[2,32,864]{2,1,0:T(8,128)(2,1)}, u32[]{:S(2)}) copy-start(bf16[2,32,864]{2,1,0:T(8,128)(2,1)} %weight_ref.2) | copy-start | bytes 331780
  13.5 1.3 %collective-permute-start.3 = (bf16[112,256]{1,0:T(8,128)(2,1)S(1)}, bf16[112,256]{1,0:T(8,128)(2,1)S(1)}, u32[]{:S(2)}, u32[]{:S(2)}) collective-permute-start(bf16[112,256]{1,0:T(8,128)(2,1)S(1)} %get-tuple-element.36.own_ref), channel_id=1, source_target_pairs={{0,1},{1,0},{2,3},{3,2},{4,5},{5,4},{6,7},{7,6},{8,9},{9,8},{10,11... | collective-permute-start | bytes 172040 | tf_op jit(solution)/shard_map/ppermute | solution.py:626
  15.0 6.7 %collective-permute-start.5 = (bf16[144,256]{1,0:T(8,128)(2,1)S(1)}, bf16[144,256]{1,0:T(8,128)(2,1)S(1)}, u32[]{:S(2)}, u32[]{:S(2)}) collective-permute-start(bf16[144,256]{1,0:T(8,128)(2,1)S(1)} %get-tuple-element.38), channel_id=1, source_target_pairs={{0,4},{4,0},{1,5},{5,1},{2,6},{6,2},{3,7},{7,3},{8,12},{12,8},{9,1... | collective-permute-start | bytes 221192 | tf_op jit(solution)/shard_map/ppermute | solution.py:644
  16.5 5.2 %collective-permute-start.4 = (bf16[112,256]{1,0:T(8,128)(2,1)S(1)}, bf16[112,256]{1,0:T(8,128)(2,1)S(1)}, u32[]{:S(2)}, u32[]{:S(2)}) collective-permute-start(bf16[112,256]{1,0:T(8,128)(2,1)S(1)} %get-tuple-element.37.own_ref), channel_id=1, source_target_pairs={{0,3},{1,2},{2,1},{3,0},{4,7},{5,6},{6,5},{7,4},{8,11},{9,10},{10,... | collective-permute-start | bytes 172040 | tf_op jit(solution)/shard_map/ppermute | solution.py:640
  17.5 4.2 %collective-permute-start.6 = (bf16[48,256]{1,0:T(8,128)(2,1)S(1)}, bf16[48,256]{1,0:T(8,128)(2,1)S(1)}, u32[]{:S(2)}, u32[]{:S(2)}) collective-permute-start(bf16[48,256]{1,0:T(8,128)(2,1)S(1)} %get-tuple-element.39), channel_id=1, source_target_pairs={{0,7},{1,6},{2,5},{3,4},{4,3},{5,2},{6,1},{7,0},{8,15},{9,14},{10,... | collective-permute-start | bytes 73736 | tf_op jit(solution)/shard_map/ppermute | solution.py:648
  34.0 11.5 %copy-start.3 = (bf16[3,256,1024]{2,1,0:T(8,128)(2,1)S(1)}, bf16[3,256,1024]{2,1,0:T(8,128)(2,1)}, u32[]{:S(2)}) copy-start(bf16[3,256,1024]{2,1,0:T(8,128)(2,1)} %weight_ref.3) | copy-start | bytes 4718596
  35.8 7.6 %collective-permute-start.7 = (bf16[32,1024]{1,0:T(8,128)(2,1)S(1)}, bf16[32,1024]{1,0:T(8,128)(2,1)S(1)}, u32[]{:S(2)}, u32[]{:S(2)}) collective-permute-start(bf16[32,1024]{1,0:T(8,128)(2,1)S(1)} %get-tuple-element.50), channel_id=1, source_target_pairs={{0,16},{8,24},{16,0},{24,8},{1,17},{9,25},{17,1},{25,9},{2,18},{10... | collective-permute-start | bytes 196616 | tf_op jit(solution)/shard_map/ppermute | solution.py:687
  36.5 9.0 %collective-permute-start.9 = (bf16[32,1024]{1,0:T(8,128)(2,1)S(1)}, bf16[32,1024]{1,0:T(8,128)(2,1)S(1)}, u32[]{:S(2)}, u32[]{:S(2)}) collective-permute-start(bf16[32,1024]{1,0:T(8,128)(2,1)S(1)} %get-tuple-element.53), channel_id=1, source_target_pairs={{0,16},{8,24},{16,0},{24,8},{1,17},{9,25},{17,1},{25,9},{2,18},{10... | collective-permute-start | bytes 196616 | tf_op jit(solution)/shard_map/ppermute | solution.py:687
  43.4 8.1 %collective-permute-start.8 = (bf16[64,1024]{1,0:T(8,128)(2,1)S(1)}, bf16[64,1024]{1,0:T(8,128)(2,1)S(1)}, u32[]{:S(2)}, u32[]{:S(2)}) collective-permute-start(bf16[64,1024]{1,0:T(8,128)(2,1)S(1)} %get-tuple-element.51.refs_0_), channel_id=1, source_target_pairs={{0,8},{8,0},{16,24},{24,16},{1,9},{9,1},{17,25},{25,17},{2,10},{10... | collective-permute-start | bytes 393224 | tf_op jit(solution)/shard_map/ppermute | solution.py:687
  43.4 7.4 %collective-permute-start.10 = (bf16[32,1024]{1,0:T(8,128)(2,1)S(1)}, bf16[32,1024]{1,0:T(8,128)(2,1)S(1)}, u32[]{:S(2)}, u32[]{:S(2)}) collective-permute-start(bf16[32,1024]{1,0:T(8,128)(2,1)S(1)} %collective-permute-done.7.refs_2_), channel_id=1, source_target_pairs={{0,8},{8,0},{16,24},{24,16},{1,9},{9,1},{17,25},{25,17},{2,10},{10... | collective-permute-start | bytes 196616 | tf_op jit(solution)/shard_map/ppermute | solution.py:687
  45.4 6.1 %collective-permute-start.11 = (bf16[32,1024]{1,0:T(8,128)(2,1)S(1)}, bf16[32,1024]{1,0:T(8,128)(2,1)S(1)}, u32[]{:S(2)}, u32[]{:S(2)}) collective-permute-start(bf16[32,1024]{1,0:T(8,128)(2,1)S(1)} %collective-permute-done.9.refs_3_), channel_id=1, source_target_pairs={{0,8},{8,0},{16,24},{24,16},{1,9},{9,1},{17,25},{25,17},{2,10},{10... | collective-permute-start | bytes 196616 | tf_op jit(solution)/shard_map/ppermute | solution.py:687
  52.9 5.8 %collective-permute-start.12 = (bf16[64,256]{1,0:T(8,128)(2,1)S(1)}, bf16[64,256]{1,0:T(8,128)(2,1)S(1)}, u32[]{:S(2)}, u32[]{:S(2)}) collective-permute-start(bf16[64,256]{1,0:T(8,128)(2,1)S(1)} %get-tuple-element.54), channel_id=1, source_target_pairs={{0,24},{8,16},{16,8},{24,0},{1,25},{9,17},{17,9},{25,1},{2,26},{10... | collective-permute-start | bytes 98312 | tf_op jit(solution)/shard_map/ppermute | solution.py:695
  53.0 5.7 %collective-permute-start.13 = (bf16[64,256]{1,0:T(8,128)(2,1)S(1)}, bf16[64,256]{1,0:T(8,128)(2,1)S(1)}, u32[]{:S(2)}, u32[]{:S(2)}) collective-permute-start(bf16[64,256]{1,0:T(8,128)(2,1)S(1)} %get-tuple-element.55), channel_id=1, source_target_pairs={{0,16},{8,24},{16,0},{24,8},{1,17},{9,25},{17,1},{25,9},{2,18},{10... | collective-permute-start | bytes 98312 | tf_op jit(solution)/shard_map/ppermute | solution.py:695
  54.7 4.5 %collective-permute-start.14 = (bf16[64,256]{1,0:T(8,128)(2,1)S(1)}, bf16[64,256]{1,0:T(8,128)(2,1)S(1)}, u32[]{:S(2)}, u32[]{:S(2)}) collective-permute-start(bf16[64,256]{1,0:T(8,128)(2,1)S(1)} %get-tuple-element.56), channel_id=1, source_target_pairs={{0,8},{8,0},{16,24},{24,16},{1,9},{9,1},{17,25},{25,17},{2,10},{10... | collective-permute-start | bytes 98312 | tf_op jit(solution)/shard_map/ppermute | solution.py:695

commit v13 on v9

--- a/solution.py
+++ b/solution.py
@@ -680,8 +680,13 @@
     blocks = {0: parts}
     for k in sorted(range(1, nx), key=lambda k: (bin(k).count("1"), -k)):
         low = k & -k
-        source = [tokens] if k == 1 else blocks[k ^ low]
-        blocks[k] = [lax.ppermute(v, "gx", swaps[low]) for v in source]
+        if k == 1:
+            blocks[k] = [lax.ppermute(tokens, "gx", swaps[k])]
+        else:
+            blocks[k] = [
+                lax.ppermute(blocks[k ^ low][0], "gx", swaps[low]),
+                lax.ppermute(parts[1], "gx", swaps[k]),
+            ]
     blocks = [tokens] + [v for k in range(1, nx) for v in blocks[k]]
     outs = call(
         functools.partial(attend_kernel, nx), "attend", (VM,) * (2 + len(blocks)),

time: 57.8 us -> 58.1 us (level)
  starting transfers between devices: 17.8 us -> 18.5 us
    ppermute x5, starting transfers between devices: 4.28 us -> 5.05 us  [the longest x2 2.35 us: body(): lax.ppermute(parts[1], 'gx', swaps[k])]
  transfers between devices with their start and end apart: 15 -> 15, of which waited for: 9 -> 8; matrix products, arithmetic and copies ran while one was open for 1% -> 1% of each run, Pallas kernels for 9% -> 9%
where the time goes in v13:
time: 58.1 us; the launch traced here: 57.9 us
  starting transfers between devices  18.5 us (32%)
  Pallas kernels  13.5 us (23%)
  waiting for transfers between devices  12.7 us (22%)
  blocking collectives  9.3 us (16%)
  local copies, waits for them, and re-layouts  2.48 us (4%)
  other arithmetic  0.72 us (1%)
  between operations  0.72 us (1%)
    pallas_call x11, Pallas kernels, call(): pl.pallas_call(kernel, out_shape=out, in_specs=list(specs), out_specs=jax...  13.5 us
    all_to_all x1, blocking collectives, body(): stats = lax.all_to_all(mine, ALL, 0, 0, tiled=True)  9.3 us
    ppermute x2, waiting for transfers between devices, body(): lax.ppermute(blocks[k ^ low][0], 'gx', swaps[low])  6.3 us
    ppermute x3, starting transfers between devices, body(): lax.ppermute(v, 'gx', swaps[nx - 1 - i])  4.45 us
    ppermute x1, starting transfers between devices, body(): lax.ppermute(first, 'gx', list(pairing(nx, False, False).items()))  3.09 us
    unnamed x8, local copies, waits for them, and re-layouts  2.48 us
    ppermute x1, starting transfers between devices, body(): lax.ppermute(second, 'gx', list(pairing(nx, True, narrow).items()))  2.47 us
    ppermute x2, starting transfers between devices, body(): lax.ppermute(parts[1], 'gx', swaps[k])  2.35 us
  transfers between devices with their start and end apart: 15, of which 8 were waited for; matrix products, arithmetic and copies ran while one was open for 1% of the time, Pallas kernels for 9%

profile of v13, /device:TPU:0, one launch (start us, length us, event | category | flops | bytes accessed | tf_op | source)
XLA Modules:
  0.0 57.9 jit_solution(7284896553141016512)
XLA Ops:
  0.6 0.0 copy-start
  0.6 0.9 %copy-done = bf16[8,8,4,256]{3,2,1,0:T(4,128)(2,1)S(1)} copy-done((bf16[8,8,4,256]{3,2,1,0:T(4,128)(2,1)S(1)}, bf16[8,8,4,256]{3,2,1,0:T(4,128)(2,1)}, u32[]{:S(2)}) %copy-start) | copy-done | bytes 131096
  1.5 0.0 copy-start.2
  1.5 0.7 %copy-done.2 = s32[4,1,4]{2,1,0:T(1,128)S(1)} copy-done((s32[4,1,4]{2,1,0:T(1,128)S(1)}, s32[4,1,4]{2,1,0:T(1,128)}, u32[]{:S(2)}) %copy-start.2) | copy-done | bytes 88
  2.2 0.9 %pre.1 = (f32[8,256]{1,0:T(8,128)S(1)}, f32[8,256]{1,0:T(8,128)S(1)}, bf16[512,256]{1,0:T(8,128)(2,1)S(1)}, bf16[80,256]{1,0:T(8,128)(2,1)S(1)}, bf16[80,256]{1,...) custom-call(s32[4,1,4]{2,1,0:T(1,128)S(1)} %copy-done.2, bf16[8,8,4,256]{3,2,1,0:T(4,128)(2,1)S(1)} %copy-done), custom_call_target="tpu_custom_call" | custom-call | bytes 1000000 | tf_op jit(solution)/shard_map/pre/pallas_call | solution.py:561
  3.2 3.1 %collective-permute-start = (bf16[80,256]{1,0:T(8,128)(2,1)S(1)}, bf16[80,256]{1,0:T(8,128)(2,1)S(1)}, u32[]{:S(2)}, u32[]{:S(2)}) collective-permute-start(bf16[80,256]{1,0:T(8,128)(2,1)S(1)} %get-tuple-element.30), channel_id=1, source_target_pairs={{0,8},{8,0},{16,24},{24,16},{1,9},{9,1},{17,25},{25,17},{2,10},{10... | collective-permute-start | bytes 122888 | tf_op jit(solution)/shard_map/ppermute | solution.py:603
  6.3 2.5 %collective-permute-start.1 = (bf16[80,256]{1,0:T(8,128)(2,1)S(1)}, bf16[80,256]{1,0:T(8,128)(2,1)S(1)}, u32[]{:S(2)}, u32[]{:S(2)}) collective-permute-start(bf16[80,256]{1,0:T(8,128)(2,1)S(1)} %get-tuple-element.31), channel_id=1, source_target_pairs={{0,24},{8,16},{16,8},{24,0},{1,25},{9,17},{17,9},{25,1},{2,26},{10... | collective-permute-start | bytes 122888 | tf_op jit(solution)/shard_map/ppermute | solution.py:604
  8.7 0.1 collective-permute-start.2
  8.8 0.0 copy-start.1
  8.9 0.9 %copy-done.1 = bf16[2,32,864]{2,1,0:T(8,128)(2,1)S(1)} copy-done((bf16[2,32,864]{2,1,0:T(8,128)(2,1)S(1)}, bf16[2,32,864]{2,1,0:T(8,128)(2,1)}, u32[]{:S(2)}) %copy-start.1) | copy-done | bytes 110616
  9.7 1.4 %band0.1 = (bf16[3,1024,256]{2,1,0:T(8,128)(2,1)S(1)}, bf16[1,32,864]{2,1,0:T(8,128)(2,1)S(1)}) custom-call(bf16[2,32,864]{2,1,0:T(8,128)(2,1)S(1)} %copy-done.1), custom_call_target="tpu_custom_call" | custom-call | bytes 8000000 | tf_op jit(solution)/shard_map/band0/pallas_call | solution.py:561
  11.1 2.2 %collective-permute-done.2.rest_1_ = bf16[16,256]{1,0:T(8,128)(2,1)S(1)} collective-permute-done((bf16[16,256]{1,0:T(8,128)(2,1)S(1)}, bf16[16,256]{1,0:T(8,128)(2,1)S(1)}, u32[]{:S(2)}, u32[]{:S(2)}) %collective-permute-start.2) | collective-permute-done | bytes 8224 | tf_op jit(solution)/shard_map/ppermute | solution.py:608
  13.3 0.0 collective-permute-done.first_ref
  13.3 0.0 collective-permute-done.1.second_ref
  13.3 0.2 line.1
  13.5 0.1 collective-permute-start.3
  13.5 1.2 %collective-permute-done.3.other_ref.core_ref = bf16[112,256]{1,0:T(8,128)(2,1)S(1)} collective-permute-done((bf16[112,256]{1,0:T(8,128)(2,1)S(1)}, bf16[112,256]{1,0:T(8,128)(2,1)S(1)}, u32[]{:S(2)}, u32[]{:S(2)}) %collective-permute-start.3) | collective-permute-done | bytes 57376 | tf_op jit(solution)/shard_map/ppermute | solution.py:626
  14.8 0.2 chip.1
  15.0 1.6 %collective-permute-start.5 = (bf16[144,256]{1,0:T(8,128)(2,1)S(1)}, bf16[144,256]{1,0:T(8,128)(2,1)S(1)}, u32[]{:S(2)}, u32[]{:S(2)}) collective-permute-start(bf16[144,256]{1,0:T(8,128)(2,1)S(1)} %get-tuple-element.36), channel_id=1, source_target_pairs={{0,4},{4,0},{1,5},{5,1},{2,6},{6,2},{3,7},{7,3},{8,12},{12,8},{9,1... | collective-permute-start | bytes 221192 | tf_op jit(solution)/shard_map/ppermute | solution.py:644
  16.5 1.0 %collective-permute-start.4 = (bf16[112,256]{1,0:T(8,128)(2,1)S(1)}, bf16[112,256]{1,0:T(8,128)(2,1)S(1)}, u32[]{:S(2)}, u32[]{:S(2)}) collective-permute-start(bf16[112,256]{1,0:T(8,128)(2,1)S(1)} %get-tuple-element.35.own_ref), channel_id=1, source_target_pairs={{0,3},{1,2},{2,1},{3,0},{4,7},{5,6},{6,5},{7,4},{8,11},{9,10},{10,... | collective-permute-start | bytes 172040 | tf_op jit(solution)/shard_map/ppermute | solution.py:640
  17.5 0.7 %collective-permute-start.6 = (bf16[48,256]{1,0:T(8,128)(2,1)S(1)}, bf16[48,256]{1,0:T(8,128)(2,1)S(1)}, u32[]{:S(2)}, u32[]{:S(2)}) collective-permute-start(bf16[48,256]{1,0:T(8,128)(2,1)S(1)} %get-tuple-element.37), channel_id=1, source_target_pairs={{0,7},{1,6},{2,5},{3,4},{4,3},{5,2},{6,1},{7,0},{8,15},{9,14},{10,... | collective-permute-start | bytes 73736 | tf_op jit(solution)/shard_map/ppermute | solution.py:648
  18.3 0.7 %pad_maximum_fusion.rest_0_ = f32[6,32]{1,0:T(8,128)S(1)} fusion(f32[2,32]{1,0:T(2,128)} %param.12, f32[2,32]{1,0:T(2,128)} %param.10, f32[2,32]{1,0:T(2,128)} %param.9), kind=kLoop, calls=%fused_computation | loop fusion | flops 384 | bytes 1536 | tf_op jit(solution)/shard_map/concatenate | solution.py:610
  19.0 1.4 %band1.1 = (bf16[3,1024,256]{2,1,0:T(8,128)(2,1)S(1)}, f32[8,256]{1,0:T(8,128)S(1)}) custom-call(bf16[1,32,864]{2,1,0:T(8,128)(2,1)S(1)} %get-tuple-element.28._.weight_ref, f32[6,32]{1,0:T(8,128)S(1)} %pad_maximum_fusion.rest_0_), custom_call_target="tpu_custom_call" | custom-call | bytes 8000000 | tf_op jit(solution)/shard_map/band1/pallas_call | solution.py:561
  20.4 1.3 %collective-permute-done.6.rest_1_ = bf16[48,256]{1,0:T(8,128)(2,1)S(1)} collective-permute-done((bf16[48,256]{1,0:T(8,128)(2,1)S(1)}, bf16[48,256]{1,0:T(8,128)(2,1)S(1)}, u32[]{:S(2)}, u32[]{:S(2)}) %collective-permute-start.6) | collective-permute-done | bytes 24608 | tf_op jit(solution)/shard_map/ppermute | solution.py:648
  21.7 0.0 collective-permute-done.4.zface_ref
  21.7 0.0 collective-permute-done.5.rest_0_
  21.7 3.0 %first.1 = (f32[800,256]{1,0:T(8,128)S(1)}, f32[32,128]{1,0:T(8,128)S(1)}, f32[1152,128]{1,0:T(8,128)S(1)}) custom-call(bf16[768,256]{1,0:T(8,128)(2,1)S(1)} %get-tuple-element.33.ext_ref, bf16[112,256]{1,0:T(8,128)(2,1)S(1)} %get-tuple-element.35.own_ref, bf16[112,256]{1,0:T(8,128)(2,1)S(1)} %collective-permute-done.3.other_ref.core_ref, ...), custom_call_target="tpu_custom_call" | custom-call | flops 2000000000 | bytes 4000000 | tf_op jit(solution)/shard_map/first/pallas_call | solution.py:561
  24.7 9.3 %all_to_all.11 = f32[32,1,128]{2,1,0:T(1,128)S(1)} all-to-all(f32[32,1,128]{2,1,0:T(1,128)S(1)} %bitcast.5), channel_id=1, replica_groups=mesh['gx'=4,'gy'=2,'gz'=4] {'gx','gy','gz'}, dimensions={0} | all-to-all | bytes 32768 | tf_op jit(solution)/shard_map/all_to_all | solution.py:668
  34.0 0.0 copy-start.3
  34.0 1.8 %second.1 = (bf16[256,256]{1,0:T(8,128)(2,1)S(1)}, bf16[64,1024]{1,0:T(8,128)(2,1)S(1)}, bf16[32,1024]{1,0:T(8,128)(2,1)S(1)}, bf16[32,1024]{1,0:T(8,128)(2,1)S(1)}) custom-call(f32[32,128]{1,0:T(8,128)S(1)} %bitcast.4, f32[800,256]{1,0:T(8,128)S(1)} %get-tuple-element.42.mid_ref, f32[1152,128]{1,0:T(8,128)S(1)} %get-tuple-element.43.msk_ref, ...), custom_call_target="tpu_custom_call" | custom-call | flops 1000000000 | bytes 4000000 | tf_op jit(solution)/shard_map/second/pallas_call | solution.py:561
  35.8 0.7 %collective-permute-start.8 = (bf16[32,1024]{1,0:T(8,128)(2,1)S(1)}, bf16[32,1024]{1,0:T(8,128)(2,1)S(1)}, u32[]{:S(2)}, u32[]{:S(2)}) collective-permute-start(bf16[32,1024]{1,0:T(8,128)(2,1)S(1)} %get-tuple-element.48), channel_id=1, source_target_pairs={{0,16},{8,24},{16,0},{24,8},{1,17},{9,25},{17,1},{25,9},{2,18},{10... | collective-permute-start | bytes 196616 | tf_op jit(solution)/shard_map/ppermute | solution.py:687
  36.5 2.3 %collective-permute-start.11 = (bf16[32,1024]{1,0:T(8,128)(2,1)S(1)}, bf16[32,1024]{1,0:T(8,128)(2,1)S(1)}, u32[]{:S(2)}, u32[]{:S(2)}) collective-permute-start(bf16[32,1024]{1,0:T(8,128)(2,1)S(1)} %get-tuple-element.49), channel_id=1, source_target_pairs={{0,24},{8,16},{16,8},{24,0},{1,25},{9,17},{17,9},{25,1},{2,26},{10... | collective-permute-start | bytes 196616 | tf_op jit(solution)/shard_map/ppermute | solution.py:688
  38.8 0.0 collective-permute-start.9
  38.8 2.0 %collective-permute-start.7 = (bf16[64,1024]{1,0:T(8,128)(2,1)S(1)}, bf16[64,1024]{1,0:T(8,128)(2,1)S(1)}, u32[]{:S(2)}, u32[]{:S(2)}) collective-permute-start(bf16[64,1024]{1,0:T(8,128)(2,1)S(1)} %get-tuple-element.47.refs_0_), channel_id=1, source_target_pairs={{0,8},{8,0},{16,24},{24,16},{1,9},{9,1},{17,25},{25,17},{2,10},{10... | collective-permute-start | bytes 393224 | tf_op jit(solution)/shard_map/ppermute | solution.py:684
  40.8 4.4 %collective-permute-done.8.refs_2_ = bf16[32,1024]{1,0:T(8,128)(2,1)S(1)} collective-permute-done((bf16[32,1024]{1,0:T(8,128)(2,1)S(1)}, bf16[32,1024]{1,0:T(8,128)(2,1)S(1)}, u32[]{:S(2)}, u32[]{:S(2)}) %collective-permute-start.8) | collective-permute-done | bytes 65568 | tf_op jit(solution)/shard_map/ppermute | solution.py:687
  45.2 0.0 collective-permute-start.10
  45.2 0.0 copy-done.3
  45.2 1.9 %turn.1.weight_ref = bf16[1024,768]{1,0:T(8,128)(2,1)S(1)} custom-call(bf16[3,256,1024]{2,1,0:T(8,128)(2,1)S(1)} %copy-done.3), custom_call_target="tpu_custom_call" | custom-call | flops 1610612736 | bytes 6000000 | tf_op jit(solution)/shard_map/turn/pallas_call | solution.py:561
  47.2 0.0 collective-permute-done.11.refs_5_
  47.2 0.4 collective-permute-done.9.refs_3_
  47.6 1.9 %collective-permute-done.10.refs_4_ = bf16[32,1024]{1,0:T(8,128)(2,1)S(1)} collective-permute-done((bf16[32,1024]{1,0:T(8,128)(2,1)S(1)}, bf16[32,1024]{1,0:T(8,128)(2,1)S(1)}, u32[]{:S(2)}, u32[]{:S(2)}) %collective-permute-start.10) | collective-permute-done | bytes 65568 | tf_op jit(solution)/shard_map/ppermute | solution.py:687
  49.5 0.0 collective-permute-done.7.refs_1_
  49.5 1.3 %attend.1 = (bf16[64,256]{1,0:T(8,128)(2,1)S(1)}, bf16[64,256]{1,0:T(8,128)(2,1)S(1)}, bf16[64,256]{1,0:T(8,128)(2,1)S(1)}, bf16[64,256]{1,0:T(8,128)(2,1)S(1)}) custom-call(f32[8,256]{1,0:T(8,128)S(1)} %get-tuple-element.46.keys_ref, bf16[1024,768]{1,0:T(8,128)(2,1)S(1)} %turn.1.weight_ref, bf16[64,1024]{1,0:T(8,128)(2,1)S(1)} %get-tuple-element.47.refs_0_, ...), custom_call_target="tpu_custom_call" | custom-call | flops 1000000000 | bytes 3000000 | tf_op jit(solution)/shard_map/attend/pallas_call | solution.py:561
  50.9 0.3 collective-permute-start.12
  51.2 1.2 %collective-permute-start.13 = (bf16[64,256]{1,0:T(8,128)(2,1)S(1)}, bf16[64,256]{1,0:T(8,128)(2,1)S(1)}, u32[]{:S(2)}, u32[]{:S(2)}) collective-permute-start(bf16[64,256]{1,0:T(8,128)(2,1)S(1)} %get-tuple-element.51), channel_id=1, source_target_pairs={{0,16},{8,24},{16,0},{24,8},{1,17},{9,25},{17,1},{25,9},{2,18},{10... | collective-permute-start | bytes 98312 | tf_op jit(solution)/shard_map/ppermute | solution.py:697
  52.4 2.9 %collective-permute-start.14 = (bf16[64,256]{1,0:T(8,128)(2,1)S(1)}, bf16[64,256]{1,0:T(8,128)(2,1)S(1)}, u32[]{:S(2)}, u32[]{:S(2)}) collective-permute-start(bf16[64,256]{1,0:T(8,128)(2,1)S(1)} %get-tuple-element.52), channel_id=1, source_target_pairs={{0,8},{8,0},{16,24},{24,16},{1,9},{9,1},{17,25},{25,17},{2,10},{10... | collective-permute-start | bytes 98312 | tf_op jit(solution)/shard_map/ppermute | solution.py:697
  55.3 0.7 %fine.1 = bf16[8,8,4,256]{3,2,1,0:T(4,128)(2,1)} custom-call(bf16[256,256]{1,0:T(8,128)(2,1)S(1)} %get-tuple-element.45.field_ref), custom_call_target="tpu_custom_call" | custom-call | bytes 4000000 | tf_op jit(solution)/shard_map/fine/pallas_call | solution.py:561
  56.0 0.6 %collective-permute-done.12.refs_0_ = bf16[64,256]{1,0:T(8,128)(2,1)S(1)} collective-permute-done((bf16[64,256]{1,0:T(8,128)(2,1)S(1)}, bf16[64,256]{1,0:T(8,128)(2,1)S(1)}, u32[]{:S(2)}, u32[]{:S(2)}) %collective-permute-start.12) | collective-permute-done | bytes 32800 | tf_op jit(solution)/shard_map/ppermute | solution.py:697
  56.6 0.0 collective-permute-done.13.refs_1_
  56.6 0.6 collective-permute-done.14.refs_2_
  57.2 0.7 %place.1 = bf16[1,64,1024]{2,1,0:T(8,128)(2,1)} custom-call(f32[8,256]{1,0:T(8,128)S(1)} %get-tuple-element.38.rest_2_.keep_ref, bf16[64,256]{1,0:T(8,128)(2,1)S(1)} %collective-permute-done.12.refs_0_, bf16[64,256]{1,0:T(8,128)(2,1)S(1)} %collective-permute-done.13.refs_1_, bf16[64,256]{1,0:T(8,128)(2,1)S(1)} %collective-permute-done.14.refs_2_, ...), custom_call_target="tpu_custom_call" | custom-call | bytes 300000 | tf_op jit(solution)/shard_map/place/pallas_call | solution.py:561
Async XLA Ops:
  0.6 0.9 %copy-start = (bf16[8,8,4,256]{3,2,1,0:T(4,128)(2,1)S(1)}, bf16[8,8,4,256]{3,2,1,0:T(4,128)(2,1)}, u32[]{:S(2)}) copy-start(bf16[8,8,4,256]{3,2,1,0:T(4,128)(2,1)} %feat_ref.1) | copy-start | bytes 393220
  1.5 0.7 %copy-start.2 = (s32[4,1,4]{2,1,0:T(1,128)S(1)}, s32[4,1,4]{2,1,0:T(1,128)}, u32[]{:S(2)}) copy-start(s32[4,1,4]{2,1,0:T(1,128)} %occ_ref.1) | copy-start | bytes 196
  3.2 10.1 %collective-permute-start = (bf16[80,256]{1,0:T(8,128)(2,1)S(1)}, bf16[80,256]{1,0:T(8,128)(2,1)S(1)}, u32[]{:S(2)}, u32[]{:S(2)}) collective-permute-start(bf16[80,256]{1,0:T(8,128)(2,1)S(1)} %get-tuple-element.30), channel_id=1, source_target_pairs={{0,8},{8,0},{16,24},{24,16},{1,9},{9,1},{17,25},{25,17},{2,10},{10... | collective-permute-start | bytes 122888 | tf_op jit(solution)/shard_map/ppermute | solution.py:603
  6.3 7.0 %collective-permute-start.1 = (bf16[80,256]{1,0:T(8,128)(2,1)S(1)}, bf16[80,256]{1,0:T(8,128)(2,1)S(1)}, u32[]{:S(2)}, u32[]{:S(2)}) collective-permute-start(bf16[80,256]{1,0:T(8,128)(2,1)S(1)} %get-tuple-element.31), channel_id=1, source_target_pairs={{0,24},{8,16},{16,8},{24,0},{1,25},{9,17},{17,9},{25,1},{2,26},{10... | collective-permute-start | bytes 122888 | tf_op jit(solution)/shard_map/ppermute | solution.py:604
  8.7 4.5 %collective-permute-start.2 = (bf16[16,256]{1,0:T(8,128)(2,1)S(1)}, bf16[16,256]{1,0:T(8,128)(2,1)S(1)}, u32[]{:S(2)}, u32[]{:S(2)}) collective-permute-start(bf16[16,256]{1,0:T(8,128)(2,1)S(1)} %get-tuple-element.32.rest_0_), channel_id=1, source_target_pairs={{0,16},{8,24},{16,0},{24,8},{1,17},{9,25},{17,1},{25,9},{2,18},{10... | collective-permute-start | bytes 24584 | tf_op jit(solution)/shard_map/ppermute | solution.py:608
  8.8 0.9 %copy-start.1 = (bf16[2,32,864]{2,1,0:T(8,128)(2,1)S(1)}, bf16[2,32,864]{2,1,0:T(8,128)(2,1)}, u32[]{:S(2)}) copy-start(bf16[2,32,864]{2,1,0:T(8,128)(2,1)} %weight_ref.2) | copy-start | bytes 331780
  13.5 1.3 %collective-permute-start.3 = (bf16[112,256]{1,0:T(8,128)(2,1)S(1)}, bf16[112,256]{1,0:T(8,128)(2,1)S(1)}, u32[]{:S(2)}, u32[]{:S(2)}) collective-permute-start(bf16[112,256]{1,0:T(8,128)(2,1)S(1)} %get-tuple-element.34.own_ref), channel_id=1, source_target_pairs={{0,1},{1,0},{2,3},{3,2},{4,5},{5,4},{6,7},{7,6},{8,9},{9,8},{10,11... | collective-permute-start | bytes 172040 | tf_op jit(solution)/shard_map/ppermute | solution.py:626
  15.0 6.7 %collective-permute-start.5 = (bf16[144,256]{1,0:T(8,128)(2,1)S(1)}, bf16[144,256]{1,0:T(8,128)(2,1)S(1)}, u32[]{:S(2)}, u32[]{:S(2)}) collective-permute-start(bf16[144,256]{1,0:T(8,128)(2,1)S(1)} %get-tuple-element.36), channel_id=1, source_target_pairs={{0,4},{4,0},{1,5},{5,1},{2,6},{6,2},{3,7},{7,3},{8,12},{12,8},{9,1... | collective-permute-start | bytes 221192 | tf_op jit(solution)/shard_map/ppermute | solution.py:644
  16.5 5.2 %collective-permute-start.4 = (bf16[112,256]{1,0:T(8,128)(2,1)S(1)}, bf16[112,256]{1,0:T(8,128)(2,1)S(1)}, u32[]{:S(2)}, u32[]{:S(2)}) collective-permute-start(bf16[112,256]{1,0:T(8,128)(2,1)S(1)} %get-tuple-element.35.own_ref), channel_id=1, source_target_pairs={{0,3},{1,2},{2,1},{3,0},{4,7},{5,6},{6,5},{7,4},{8,11},{9,10},{10,... | collective-permute-start | bytes 172040 | tf_op jit(solution)/shard_map/ppermute | solution.py:640
  17.5 4.2 %collective-permute-start.6 = (bf16[48,256]{1,0:T(8,128)(2,1)S(1)}, bf16[48,256]{1,0:T(8,128)(2,1)S(1)}, u32[]{:S(2)}, u32[]{:S(2)}) collective-permute-start(bf16[48,256]{1,0:T(8,128)(2,1)S(1)} %get-tuple-element.37), channel_id=1, source_target_pairs={{0,7},{1,6},{2,5},{3,4},{4,3},{5,2},{6,1},{7,0},{8,15},{9,14},{10,... | collective-permute-start | bytes 73736 | tf_op jit(solution)/shard_map/ppermute | solution.py:648
  34.0 11.2 %copy-start.3 = (bf16[3,256,1024]{2,1,0:T(8,128)(2,1)S(1)}, bf16[3,256,1024]{2,1,0:T(8,128)(2,1)}, u32[]{:S(2)}) copy-start(bf16[3,256,1024]{2,1,0:T(8,128)(2,1)} %weight_ref.3) | copy-start | bytes 4718596
  35.8 9.4 %collective-permute-start.8 = (bf16[32,1024]{1,0:T(8,128)(2,1)S(1)}, bf16[32,1024]{1,0:T(8,128)(2,1)S(1)}, u32[]{:S(2)}, u32[]{:S(2)}) collective-permute-start(bf16[32,1024]{1,0:T(8,128)(2,1)S(1)} %get-tuple-element.48), channel_id=1, source_target_pairs={{0,16},{8,24},{16,0},{24,8},{1,17},{9,25},{17,1},{25,9},{2,18},{10... | collective-permute-start | bytes 196616 | tf_op jit(solution)/shard_map/ppermute | solution.py:687
  36.5 10.7 %collective-permute-start.11 = (bf16[32,1024]{1,0:T(8,128)(2,1)S(1)}, bf16[32,1024]{1,0:T(8,128)(2,1)S(1)}, u32[]{:S(2)}, u32[]{:S(2)}) collective-permute-start(bf16[32,1024]{1,0:T(8,128)(2,1)S(1)} %get-tuple-element.49), channel_id=1, source_target_pairs={{0,24},{8,16},{16,8},{24,0},{1,25},{9,17},{17,9},{25,1},{2,26},{10... | collective-permute-start | bytes 196616 | tf_op jit(solution)/shard_map/ppermute | solution.py:688
  38.8 8.8 %collective-permute-start.9 = (bf16[32,1024]{1,0:T(8,128)(2,1)S(1)}, bf16[32,1024]{1,0:T(8,128)(2,1)S(1)}, u32[]{:S(2)}, u32[]{:S(2)}) collective-permute-start(bf16[32,1024]{1,0:T(8,128)(2,1)S(1)} %get-tuple-element.49), channel_id=1, source_target_pairs={{0,16},{8,24},{16,0},{24,8},{1,17},{9,25},{17,1},{25,9},{2,18},{10... | collective-permute-start | bytes 196616 | tf_op jit(solution)/shard_map/ppermute | solution.py:688
  38.8 10.7 %collective-permute-start.7 = (bf16[64,1024]{1,0:T(8,128)(2,1)S(1)}, bf16[64,1024]{1,0:T(8,128)(2,1)S(1)}, u32[]{:S(2)}, u32[]{:S(2)}) collective-permute-start(bf16[64,1024]{1,0:T(8,128)(2,1)S(1)} %get-tuple-element.47.refs_0_), channel_id=1, source_target_pairs={{0,8},{8,0},{16,24},{24,16},{1,9},{9,1},{17,25},{25,17},{2,10},{10... | collective-permute-start | bytes 393224 | tf_op jit(solution)/shard_map/ppermute | solution.py:684
  45.2 4.3 %collective-permute-start.10 = (bf16[32,1024]{1,0:T(8,128)(2,1)S(1)}, bf16[32,1024]{1,0:T(8,128)(2,1)S(1)}, u32[]{:S(2)}, u32[]{:S(2)}) collective-permute-start(bf16[32,1024]{1,0:T(8,128)(2,1)S(1)} %collective-permute-done.8.refs_2_), channel_id=1, source_target_pairs={{0,8},{8,0},{16,24},{24,16},{1,9},{9,1},{17,25},{25,17},{2,10},{10... | collective-permute-start | bytes 196616 | tf_op jit(solution)/shard_map/ppermute | solution.py:687
  50.9 5.8 %collective-permute-start.12 = (bf16[64,256]{1,0:T(8,128)(2,1)S(1)}, bf16[64,256]{1,0:T(8,128)(2,1)S(1)}, u32[]{:S(2)}, u32[]{:S(2)}) collective-permute-start(bf16[64,256]{1,0:T(8,128)(2,1)S(1)} %get-tuple-element.50), channel_id=1, source_target_pairs={{0,24},{8,16},{16,8},{24,0},{1,25},{9,17},{17,9},{25,1},{2,26},{10... | collective-permute-start | bytes 98312 | tf_op jit(solution)/shard_map/ppermute | solution.py:697
  51.2 5.5 %collective-permute-start.13 = (bf16[64,256]{1,0:T(8,128)(2,1)S(1)}, bf16[64,256]{1,0:T(8,128)(2,1)S(1)}, u32[]{:S(2)}, u32[]{:S(2)}) collective-permute-start(bf16[64,256]{1,0:T(8,128)(2,1)S(1)} %get-tuple-element.51), channel_id=1, source_target_pairs={{0,16},{8,24},{16,0},{24,8},{1,17},{9,25},{17,1},{25,9},{2,18},{10... | collective-permute-start | bytes 98312 | tf_op jit(solution)/shard_map/ppermute | solution.py:697
  52.4 4.8 %collective-permute-start.14 = (bf16[64,256]{1,0:T(8,128)(2,1)S(1)}, bf16[64,256]{1,0:T(8,128)(2,1)S(1)}, u32[]{:S(2)}, u32[]{:S(2)}) collective-permute-start(bf16[64,256]{1,0:T(8,128)(2,1)S(1)} %get-tuple-element.52), channel_id=1, source_target_pairs={{0,8},{8,0},{16,24},{24,16},{1,9},{9,1},{17,25},{25,17},{2,10},{10... | collective-permute-start | bytes 98312 | tf_op jit(solution)/shard_map/ppermute | solution.py:697

commit v14 on v9

--- a/solution.py
+++ b/solution.py
@@ -493,8 +493,9 @@
     order = onehot(j == i // 8 * 8 + i % 2 * 4 + i % 8 // 2)
     tokens = jnp.dot(order, tokens, preferred_element_type=F32).astype(BF16)
     tok_ref[...] = tokens
-    low_ref[...] = tokens[0 : n // 2]
-    high_ref[...] = tokens[n // 2 : n]
+    cut = low_ref.shape[0]
+    low_ref[...] = tokens[0:cut]
+    high_ref[...] = tokens[cut:n]
 
 
 def fine_kernel(field_ref, fine_ref):
@@ -668,7 +669,7 @@
     stats = lax.all_to_all(mine, ALL, 0, 0, tiled=True)
     field, tokens, *parts = call(
         functools.partial(second_kernel, sx, sy, sb), "second", (VM,) * 6,
-        [shape(sx * sy * 4, lanes), shape(own, feats)] + [shape(own // 2, feats)] * 2,
+        [shape(sx * sy * 4, lanes), shape(own, feats)] + [shape(own // 4 * 3, feats), shape(own // 4, feats)],
         (stats, mid, there, band1, rows, coded),
         [pltpu.VMEM(((sx + 2) * sy * 4, 4 * lanes), BF16)],
         flops=10**9, nbytes=4 * 10**6,

time: 57.8 us -> 59.2 us (1.024)
  starting transfers between devices: 17.8 us -> 19.1 us
    ppermute x5, starting transfers between devices: 4.28 us -> 5.59 us  [body(): blocks[k] = [lax.ppermute(v, 'gx', swaps[low]) for v in source]]
  transfers between devices with their start and end apart: 15 -> 15, of which waited for: 9 -> 8; matrix products, arithmetic and copies ran while one was open for 1% -> 1% of each run, Pallas kernels for 9% -> 9%
where the time goes in v14:
time: 59.2 us; the launch traced here: 59 us
  starting transfers between devices  19.1 us (32%)
  Pallas kernels  13.5 us (23%)
  waiting for transfers between devices  13.2 us (22%)
  blocking collectives  9.3 us (16%)
  local copies, waits for them, and re-layouts  2.48 us (4%)
  other arithmetic  0.72 us (1%)
  between operations  0.72 us (1%)
    pallas_call x11, Pallas kernels, call(): pl.pallas_call(kernel, out_shape=out, in_specs=list(specs), out_specs=jax...  13.5 us
    all_to_all x1, blocking collectives, body(): stats = lax.all_to_all(mine, ALL, 0, 0, tiled=True)  9.3 us
    ppermute x5, waiting for transfers between devices, body(): blocks[k] = [lax.ppermute(v, 'gx', swaps[low]) for v in source]  6.86 us
    ppermute x5, starting transfers between devices, body(): blocks[k] = [lax.ppermute(v, 'gx', swaps[low]) for v in source]  5.59 us
    ppermute x3, starting transfers between devices, body(): lax.ppermute(v, 'gx', swaps[nx - 1 - i])  4.45 us
    ppermute x1, starting transfers between devices, body(): lax.ppermute(first, 'gx', list(pairing(nx, False, False).items()))  3.09 us
    unnamed x8, local copies, waits for them, and re-layouts  2.48 us
    ppermute x1, starting transfers between devices, body(): lax.ppermute(second, 'gx', list(pairing(nx, True, narrow).items()))  2.47 us
  transfers between devices with their start and end apart: 15, of which 8 were waited for; matrix products, arithmetic and copies ran while one was open for 1% of the time, Pallas kernels for 9%

profile of v14, /device:TPU:0, one launch (start us, length us, event | category | flops | bytes accessed | tf_op | source)
XLA Modules:
  0.0 59.0 jit_solution(12289087143573655442)
XLA Ops:
  0.6 0.0 copy-start
  0.6 0.9 %copy-done = bf16[8,8,4,256]{3,2,1,0:T(4,128)(2,1)S(1)} copy-done((bf16[8,8,4,256]{3,2,1,0:T(4,128)(2,1)S(1)}, bf16[8,8,4,256]{3,2,1,0:T(4,128)(2,1)}, u32[]{:S(2)}) %copy-start) | copy-done | bytes 131096
  1.5 0.0 copy-start.2
  1.5 0.7 %copy-done.2 = s32[4,1,4]{2,1,0:T(1,128)S(1)} copy-done((s32[4,1,4]{2,1,0:T(1,128)S(1)}, s32[4,1,4]{2,1,0:T(1,128)}, u32[]{:S(2)}) %copy-start.2) | copy-done | bytes 88
  2.2 0.9 %pre.1 = (f32[8,256]{1,0:T(8,128)S(1)}, f32[8,256]{1,0:T(8,128)S(1)}, bf16[512,256]{1,0:T(8,128)(2,1)S(1)}, bf16[80,256]{1,0:T(8,128)(2,1)S(1)}, bf16[80,256]{1,...) custom-call(s32[4,1,4]{2,1,0:T(1,128)S(1)} %copy-done.2, bf16[8,8,4,256]{3,2,1,0:T(4,128)(2,1)S(1)} %copy-done), custom_call_target="tpu_custom_call" | custom-call | bytes 1000000 | tf_op jit(solution)/shard_map/pre/pallas_call | solution.py:562
  3.2 3.1 %collective-permute-start = (bf16[80,256]{1,0:T(8,128)(2,1)S(1)}, bf16[80,256]{1,0:T(8,128)(2,1)S(1)}, u32[]{:S(2)}, u32[]{:S(2)}) collective-permute-start(bf16[80,256]{1,0:T(8,128)(2,1)S(1)} %get-tuple-element.30), channel_id=1, source_target_pairs={{0,8},{8,0},{16,24},{24,16},{1,9},{9,1},{17,25},{25,17},{2,10},{10... | collective-permute-start | bytes 122888 | tf_op jit(solution)/shard_map/ppermute | solution.py:604
  6.3 2.5 %collective-permute-start.1 = (bf16[80,256]{1,0:T(8,128)(2,1)S(1)}, bf16[80,256]{1,0:T(8,128)(2,1)S(1)}, u32[]{:S(2)}, u32[]{:S(2)}) collective-permute-start(bf16[80,256]{1,0:T(8,128)(2,1)S(1)} %get-tuple-element.31), channel_id=1, source_target_pairs={{0,24},{8,16},{16,8},{24,0},{1,25},{9,17},{17,9},{25,1},{2,26},{10... | collective-permute-start | bytes 122888 | tf_op jit(solution)/shard_map/ppermute | solution.py:605
  8.7 0.1 collective-permute-start.2
  8.8 0.0 copy-start.1
  8.9 0.9 %copy-done.1 = bf16[2,32,864]{2,1,0:T(8,128)(2,1)S(1)} copy-done((bf16[2,32,864]{2,1,0:T(8,128)(2,1)S(1)}, bf16[2,32,864]{2,1,0:T(8,128)(2,1)}, u32[]{:S(2)}) %copy-start.1) | copy-done | bytes 110616
  9.7 1.4 %band0.1 = (bf16[3,1024,256]{2,1,0:T(8,128)(2,1)S(1)}, bf16[1,32,864]{2,1,0:T(8,128)(2,1)S(1)}) custom-call(bf16[2,32,864]{2,1,0:T(8,128)(2,1)S(1)} %copy-done.1), custom_call_target="tpu_custom_call" | custom-call | bytes 8000000 | tf_op jit(solution)/shard_map/band0/pallas_call | solution.py:562
  11.1 2.2 %collective-permute-done.2.rest_1_ = bf16[16,256]{1,0:T(8,128)(2,1)S(1)} collective-permute-done((bf16[16,256]{1,0:T(8,128)(2,1)S(1)}, bf16[16,256]{1,0:T(8,128)(2,1)S(1)}, u32[]{:S(2)}, u32[]{:S(2)}) %collective-permute-start.2) | collective-permute-done | bytes 8224 | tf_op jit(solution)/shard_map/ppermute | solution.py:609
  13.3 0.0 collective-permute-done.first_ref
  13.3 0.0 collective-permute-done.1.second_ref
  13.3 0.2 line.1
  13.5 0.1 collective-permute-start.3
  13.5 1.2 %collective-permute-done.3.other_ref.core_ref = bf16[112,256]{1,0:T(8,128)(2,1)S(1)} collective-permute-done((bf16[112,256]{1,0:T(8,128)(2,1)S(1)}, bf16[112,256]{1,0:T(8,128)(2,1)S(1)}, u32[]{:S(2)}, u32[]{:S(2)}) %collective-permute-start.3) | collective-permute-done | bytes 57376 | tf_op jit(solution)/shard_map/ppermute | solution.py:627
  14.8 0.2 chip.1
  15.0 1.6 %collective-permute-start.5 = (bf16[144,256]{1,0:T(8,128)(2,1)S(1)}, bf16[144,256]{1,0:T(8,128)(2,1)S(1)}, u32[]{:S(2)}, u32[]{:S(2)}) collective-permute-start(bf16[144,256]{1,0:T(8,128)(2,1)S(1)} %get-tuple-element.36), channel_id=1, source_target_pairs={{0,4},{4,0},{1,5},{5,1},{2,6},{6,2},{3,7},{7,3},{8,12},{12,8},{9,1... | collective-permute-start | bytes 221192 | tf_op jit(solution)/shard_map/ppermute | solution.py:645
  16.5 1.0 %collective-permute-start.4 = (bf16[112,256]{1,0:T(8,128)(2,1)S(1)}, bf16[112,256]{1,0:T(8,128)(2,1)S(1)}, u32[]{:S(2)}, u32[]{:S(2)}) collective-permute-start(bf16[112,256]{1,0:T(8,128)(2,1)S(1)} %get-tuple-element.35.own_ref), channel_id=1, source_target_pairs={{0,3},{1,2},{2,1},{3,0},{4,7},{5,6},{6,5},{7,4},{8,11},{9,10},{10,... | collective-permute-start | bytes 172040 | tf_op jit(solution)/shard_map/ppermute | solution.py:641
  17.5 0.7 %collective-permute-start.6 = (bf16[48,256]{1,0:T(8,128)(2,1)S(1)}, bf16[48,256]{1,0:T(8,128)(2,1)S(1)}, u32[]{:S(2)}, u32[]{:S(2)}) collective-permute-start(bf16[48,256]{1,0:T(8,128)(2,1)S(1)} %get-tuple-element.37), channel_id=1, source_target_pairs={{0,7},{1,6},{2,5},{3,4},{4,3},{5,2},{6,1},{7,0},{8,15},{9,14},{10,... | collective-permute-start | bytes 73736 | tf_op jit(solution)/shard_map/ppermute | solution.py:649
  18.3 0.7 %pad_maximum_fusion.rest_0_ = f32[6,32]{1,0:T(8,128)S(1)} fusion(f32[2,32]{1,0:T(2,128)} %param.12, f32[2,32]{1,0:T(2,128)} %param.10, f32[2,32]{1,0:T(2,128)} %param.9), kind=kLoop, calls=%fused_computation | loop fusion | flops 384 | bytes 1536 | tf_op jit(solution)/shard_map/concatenate | solution.py:611
  19.0 1.4 %band1.1 = (bf16[3,1024,256]{2,1,0:T(8,128)(2,1)S(1)}, f32[8,256]{1,0:T(8,128)S(1)}) custom-call(bf16[1,32,864]{2,1,0:T(8,128)(2,1)S(1)} %get-tuple-element.28._.weight_ref, f32[6,32]{1,0:T(8,128)S(1)} %pad_maximum_fusion.rest_0_), custom_call_target="tpu_custom_call" | custom-call | bytes 8000000 | tf_op jit(solution)/shard_map/band1/pallas_call | solution.py:562
  20.4 1.3 %collective-permute-done.6.rest_1_ = bf16[48,256]{1,0:T(8,128)(2,1)S(1)} collective-permute-done((bf16[48,256]{1,0:T(8,128)(2,1)S(1)}, bf16[48,256]{1,0:T(8,128)(2,1)S(1)}, u32[]{:S(2)}, u32[]{:S(2)}) %collective-permute-start.6) | collective-permute-done | bytes 24608 | tf_op jit(solution)/shard_map/ppermute | solution.py:649
  21.7 0.0 collective-permute-done.4.zface_ref
  21.7 0.0 collective-permute-done.5.rest_0_
  21.7 3.0 %first.1 = (f32[800,256]{1,0:T(8,128)S(1)}, f32[32,128]{1,0:T(8,128)S(1)}, f32[1152,128]{1,0:T(8,128)S(1)}) custom-call(bf16[768,256]{1,0:T(8,128)(2,1)S(1)} %get-tuple-element.33.ext_ref, bf16[112,256]{1,0:T(8,128)(2,1)S(1)} %get-tuple-element.35.own_ref, bf16[112,256]{1,0:T(8,128)(2,1)S(1)} %collective-permute-done.3.other_ref.core_ref, ...), custom_call_target="tpu_custom_call" | custom-call | flops 2000000000 | bytes 4000000 | tf_op jit(solution)/shard_map/first/pallas_call | solution.py:562
  24.7 9.3 %all_to_all.11 = f32[32,1,128]{2,1,0:T(1,128)S(1)} all-to-all(f32[32,1,128]{2,1,0:T(1,128)S(1)} %bitcast.5), channel_id=1, replica_groups=mesh['gx'=4,'gy'=2,'gz'=4] {'gx','gy','gz'}, dimensions={0} | all-to-all | bytes 32768 | tf_op jit(solution)/shard_map/all_to_all | solution.py:669
  34.0 0.0 copy-start.3
  34.0 1.8 %second.1 = (bf16[256,256]{1,0:T(8,128)(2,1)S(1)}, bf16[64,1024]{1,0:T(8,128)(2,1)S(1)}, bf16[48,1024]{1,0:T(8,128)(2,1)S(1)}, bf16[16,1024]{1,0:T(8,128)(2,1)S(1)}) custom-call(f32[32,128]{1,0:T(8,128)S(1)} %bitcast.4, f32[800,256]{1,0:T(8,128)S(1)} %get-tuple-element.42.mid_ref, f32[1152,128]{1,0:T(8,128)S(1)} %get-tuple-element.43.msk_ref, ...), custom_call_target="tpu_custom_call" | custom-call | flops 1000000000 | bytes 4000000 | tf_op jit(solution)/shard_map/second/pallas_call | solution.py:562
  35.8 0.7 %collective-permute-start.8 = (bf16[48,1024]{1,0:T(8,128)(2,1)S(1)}, bf16[48,1024]{1,0:T(8,128)(2,1)S(1)}, u32[]{:S(2)}, u32[]{:S(2)}) collective-permute-start(bf16[48,1024]{1,0:T(8,128)(2,1)S(1)} %get-tuple-element.48), channel_id=1, source_target_pairs={{0,16},{8,24},{16,0},{24,8},{1,17},{9,25},{17,1},{25,9},{2,18},{10... | collective-permute-start | bytes 294920 | tf_op jit(solution)/shard_map/ppermute | solution.py:685
  36.5 2.3 %collective-permute-start.9 = (bf16[16,1024]{1,0:T(8,128)(2,1)S(1)}, bf16[16,1024]{1,0:T(8,128)(2,1)S(1)}, u32[]{:S(2)}, u32[]{:S(2)}) collective-permute-start(bf16[16,1024]{1,0:T(8,128)(2,1)S(1)} %get-tuple-element.49), channel_id=1, source_target_pairs={{0,16},{8,24},{16,0},{24,8},{1,17},{9,25},{17,1},{25,9},{2,18},{10... | collective-permute-start | bytes 98312 | tf_op jit(solution)/shard_map/ppermute | solution.py:685
  38.8 0.6 collective-permute-start.7
  39.4 5.5 %collective-permute-done.9.refs_3_ = bf16[16,1024]{1,0:T(8,128)(2,1)S(1)} collective-permute-done((bf16[16,1024]{1,0:T(8,128)(2,1)S(1)}, bf16[16,1024]{1,0:T(8,128)(2,1)S(1)}, u32[]{:S(2)}, u32[]{:S(2)}) %collective-permute-start.9) | collective-permute-done | bytes 32800 | tf_op jit(solution)/shard_map/ppermute | solution.py:685
  44.8 0.0 collective-permute-start.11
  44.8 0.0 collective-permute-done.8.refs_2_
  44.8 2.0 %collective-permute-start.10 = (bf16[48,1024]{1,0:T(8,128)(2,1)S(1)}, bf16[48,1024]{1,0:T(8,128)(2,1)S(1)}, u32[]{:S(2)}, u32[]{:S(2)}) collective-permute-start(bf16[48,1024]{1,0:T(8,128)(2,1)S(1)} %collective-permute-done.8.refs_2_), channel_id=1, source_target_pairs={{0,8},{8,0},{16,24},{24,16},{1,9},{9,1},{17,25},{25,17},{2,10},{10... | collective-permute-start | bytes 294920 | tf_op jit(solution)/shard_map/ppermute | solution.py:685
  46.8 0.0 copy-done.3
  46.9 1.9 %turn.1.weight_ref = bf16[1024,768]{1,0:T(8,128)(2,1)S(1)} custom-call(bf16[3,256,1024]{2,1,0:T(8,128)(2,1)S(1)} %copy-done.3), custom_call_target="tpu_custom_call" | custom-call | flops 1610612736 | bytes 6000000 | tf_op jit(solution)/shard_map/turn/pallas_call | solution.py:562
  48.8 0.3 collective-permute-done.11.refs_5_
  49.1 0.0 collective-permute-done.7.refs_1_
  49.1 1.1 %collective-permute-done.10.refs_4_ = bf16[48,1024]{1,0:T(8,128)(2,1)S(1)} collective-permute-done((bf16[48,1024]{1,0:T(8,128)(2,1)S(1)}, bf16[48,1024]{1,0:T(8,128)(2,1)S(1)}, u32[]{:S(2)}, u32[]{:S(2)}) %collective-permute-start.10) | collective-permute-done | bytes 98336 | tf_op jit(solution)/shard_map/ppermute | solution.py:685
  50.2 1.3 %attend.1 = (bf16[64,256]{1,0:T(8,128)(2,1)S(1)}, bf16[64,256]{1,0:T(8,128)(2,1)S(1)}, bf16[64,256]{1,0:T(8,128)(2,1)S(1)}, bf16[64,256]{1,0:T(8,128)(2,1)S(1)}) custom-call(f32[8,256]{1,0:T(8,128)S(1)} %get-tuple-element.46.keys_ref, bf16[1024,768]{1,0:T(8,128)(2,1)S(1)} %turn.1.weight_ref, bf16[64,1024]{1,0:T(8,128)(2,1)S(1)} %get-tuple-element.47.refs_0_, ...), custom_call_target="tpu_custom_call" | custom-call | flops 1000000000 | bytes 3000000 | tf_op jit(solution)/shard_map/attend/pallas_call | solution.py:562
  51.5 0.4 collective-permute-start.12
  52.0 2.4 %collective-permute-start.13 = (bf16[64,256]{1,0:T(8,128)(2,1)S(1)}, bf16[64,256]{1,0:T(8,128)(2,1)S(1)}, u32[]{:S(2)}, u32[]{:S(2)}) collective-permute-start(bf16[64,256]{1,0:T(8,128)(2,1)S(1)} %get-tuple-element.51), channel_id=1, source_target_pairs={{0,16},{8,24},{16,0},{24,8},{1,17},{9,25},{17,1},{25,9},{2,18},{10... | collective-permute-start | bytes 98312 | tf_op jit(solution)/shard_map/ppermute | solution.py:693
  54.4 1.6 %collective-permute-start.14 = (bf16[64,256]{1,0:T(8,128)(2,1)S(1)}, bf16[64,256]{1,0:T(8,128)(2,1)S(1)}, u32[]{:S(2)}, u32[]{:S(2)}) collective-permute-start(bf16[64,256]{1,0:T(8,128)(2,1)S(1)} %get-tuple-element.52), channel_id=1, source_target_pairs={{0,8},{8,0},{16,24},{24,16},{1,9},{9,1},{17,25},{25,17},{2,10},{10... | collective-permute-start | bytes 98312 | tf_op jit(solution)/shard_map/ppermute | solution.py:693
  56.0 0.7 %fine.1 = bf16[8,8,4,256]{3,2,1,0:T(4,128)(2,1)} custom-call(bf16[256,256]{1,0:T(8,128)(2,1)S(1)} %get-tuple-element.45.field_ref), custom_call_target="tpu_custom_call" | custom-call | bytes 4000000 | tf_op jit(solution)/shard_map/fine/pallas_call | solution.py:562
  56.7 0.6 %collective-permute-done.12.refs_0_ = bf16[64,256]{1,0:T(8,128)(2,1)S(1)} collective-permute-done((bf16[64,256]{1,0:T(8,128)(2,1)S(1)}, bf16[64,256]{1,0:T(8,128)(2,1)S(1)}, u32[]{:S(2)}, u32[]{:S(2)}) %collective-permute-start.12) | collective-permute-done | bytes 32800 | tf_op jit(solution)/shard_map/ppermute | solution.py:693
  57.3 0.0 collective-permute-done.13.refs_1_
  57.3 1.0 %collective-permute-done.14.refs_2_ = bf16[64,256]{1,0:T(8,128)(2,1)S(1)} collective-permute-done((bf16[64,256]{1,0:T(8,128)(2,1)S(1)}, bf16[64,256]{1,0:T(8,128)(2,1)S(1)}, u32[]{:S(2)}, u32[]{:S(2)}) %collective-permute-start.14) | collective-permute-done | bytes 32800 | tf_op jit(solution)/shard_map/ppermute | solution.py:693
  58.3 0.7 %place.1 = bf16[1,64,1024]{2,1,0:T(8,128)(2,1)} custom-call(f32[8,256]{1,0:T(8,128)S(1)} %get-tuple-element.38.rest_2_.keep_ref, bf16[64,256]{1,0:T(8,128)(2,1)S(1)} %collective-permute-done.12.refs_0_, bf16[64,256]{1,0:T(8,128)(2,1)S(1)} %collective-permute-done.13.refs_1_, bf16[64,256]{1,0:T(8,128)(2,1)S(1)} %collective-permute-done.14.refs_2_, ...), custom_call_target="tpu_custom_call" | custom-call | bytes 300000 | tf_op jit(solution)/shard_map/place/pallas_call | solution.py:562
Async XLA Ops:
  0.6 0.9 %copy-start = (bf16[8,8,4,256]{3,2,1,0:T(4,128)(2,1)S(1)}, bf16[8,8,4,256]{3,2,1,0:T(4,128)(2,1)}, u32[]{:S(2)}) copy-start(bf16[8,8,4,256]{3,2,1,0:T(4,128)(2,1)} %feat_ref.1) | copy-start | bytes 393220
  1.5 0.7 %copy-start.2 = (s32[4,1,4]{2,1,0:T(1,128)S(1)}, s32[4,1,4]{2,1,0:T(1,128)}, u32[]{:S(2)}) copy-start(s32[4,1,4]{2,1,0:T(1,128)} %occ_ref.1) | copy-start | bytes 196
  3.2 10.1 %collective-permute-start = (bf16[80,256]{1,0:T(8,128)(2,1)S(1)}, bf16[80,256]{1,0:T(8,128)(2,1)S(1)}, u32[]{:S(2)}, u32[]{:S(2)}) collective-permute-start(bf16[80,256]{1,0:T(8,128)(2,1)S(1)} %get-tuple-element.30), channel_id=1, source_target_pairs={{0,8},{8,0},{16,24},{24,16},{1,9},{9,1},{17,25},{25,17},{2,10},{10... | collective-permute-start | bytes 122888 | tf_op jit(solution)/shard_map/ppermute | solution.py:604
  6.3 7.0 %collective-permute-start.1 = (bf16[80,256]{1,0:T(8,128)(2,1)S(1)}, bf16[80,256]{1,0:T(8,128)(2,1)S(1)}, u32[]{:S(2)}, u32[]{:S(2)}) collective-permute-start(bf16[80,256]{1,0:T(8,128)(2,1)S(1)} %get-tuple-element.31), channel_id=1, source_target_pairs={{0,24},{8,16},{16,8},{24,0},{1,25},{9,17},{17,9},{25,1},{2,26},{10... | collective-permute-start | bytes 122888 | tf_op jit(solution)/shard_map/ppermute | solution.py:605
  8.7 4.5 %collective-permute-start.2 = (bf16[16,256]{1,0:T(8,128)(2,1)S(1)}, bf16[16,256]{1,0:T(8,128)(2,1)S(1)}, u32[]{:S(2)}, u32[]{:S(2)}) collective-permute-start(bf16[16,256]{1,0:T(8,128)(2,1)S(1)} %get-tuple-element.32.rest_0_), channel_id=1, source_target_pairs={{0,16},{8,24},{16,0},{24,8},{1,17},{9,25},{17,1},{25,9},{2,18},{10... | collective-permute-start | bytes 24584 | tf_op jit(solution)/shard_map/ppermute | solution.py:609
  8.8 0.9 %copy-start.1 = (bf16[2,32,864]{2,1,0:T(8,128)(2,1)S(1)}, bf16[2,32,864]{2,1,0:T(8,128)(2,1)}, u32[]{:S(2)}) copy-start(bf16[2,32,864]{2,1,0:T(8,128)(2,1)} %weight_ref.2) | copy-start | bytes 331780
  13.5 1.3 %collective-permute-start.3 = (bf16[112,256]{1,0:T(8,128)(2,1)S(1)}, bf16[112,256]{1,0:T(8,128)(2,1)S(1)}, u32[]{:S(2)}, u32[]{:S(2)}) collective-permute-start(bf16[112,256]{1,0:T(8,128)(2,1)S(1)} %get-tuple-element.34.own_ref), channel_id=1, source_target_pairs={{0,1},{1,0},{2,3},{3,2},{4,5},{5,4},{6,7},{7,6},{8,9},{9,8},{10,11... | collective-permute-start | bytes 172040 | tf_op jit(solution)/shard_map/ppermute | solution.py:627
  15.0 6.7 %collective-permute-start.5 = (bf16[144,256]{1,0:T(8,128)(2,1)S(1)}, bf16[144,256]{1,0:T(8,128)(2,1)S(1)}, u32[]{:S(2)}, u32[]{:S(2)}) collective-permute-start(bf16[144,256]{1,0:T(8,128)(2,1)S(1)} %get-tuple-element.36), channel_id=1, source_target_pairs={{0,4},{4,0},{1,5},{5,1},{2,6},{6,2},{3,7},{7,3},{8,12},{12,8},{9,1... | collective-permute-start | bytes 221192 | tf_op jit(solution)/shard_map/ppermute | solution.py:645
  16.5 5.2 %collective-permute-start.4 = (bf16[112,256]{1,0:T(8,128)(2,1)S(1)}, bf16[112,256]{1,0:T(8,128)(2,1)S(1)}, u32[]{:S(2)}, u32[]{:S(2)}) collective-permute-start(bf16[112,256]{1,0:T(8,128)(2,1)S(1)} %get-tuple-element.35.own_ref), channel_id=1, source_target_pairs={{0,3},{1,2},{2,1},{3,0},{4,7},{5,6},{6,5},{7,4},{8,11},{9,10},{10,... | collective-permute-start | bytes 172040 | tf_op jit(solution)/shard_map/ppermute | solution.py:641
  17.5 4.2 %collective-permute-start.6 = (bf16[48,256]{1,0:T(8,128)(2,1)S(1)}, bf16[48,256]{1,0:T(8,128)(2,1)S(1)}, u32[]{:S(2)}, u32[]{:S(2)}) collective-permute-start(bf16[48,256]{1,0:T(8,128)(2,1)S(1)} %get-tuple-element.37), channel_id=1, source_target_pairs={{0,7},{1,6},{2,5},{3,4},{4,3},{5,2},{6,1},{7,0},{8,15},{9,14},{10,... | collective-permute-start | bytes 73736 | tf_op jit(solution)/shard_map/ppermute | solution.py:649
  34.0 12.8 %copy-start.3 = (bf16[3,256,1024]{2,1,0:T(8,128)(2,1)S(1)}, bf16[3,256,1024]{2,1,0:T(8,128)(2,1)}, u32[]{:S(2)}) copy-start(bf16[3,256,1024]{2,1,0:T(8,128)(2,1)} %weight_ref.3) | copy-start | bytes 4718596
  35.8 9.0 %collective-permute-start.8 = (bf16[48,1024]{1,0:T(8,128)(2,1)S(1)}, bf16[48,1024]{1,0:T(8,128)(2,1)S(1)}, u32[]{:S(2)}, u32[]{:S(2)}) collective-permute-start(bf16[48,1024]{1,0:T(8,128)(2,1)S(1)} %get-tuple-element.48), channel_id=1, source_target_pairs={{0,16},{8,24},{16,0},{24,8},{1,17},{9,25},{17,1},{25,9},{2,18},{10... | collective-permute-start | bytes 294920 | tf_op jit(solution)/shard_map/ppermute | solution.py:685
  36.5 8.4 %collective-permute-start.9 = (bf16[16,1024]{1,0:T(8,128)(2,1)S(1)}, bf16[16,1024]{1,0:T(8,128)(2,1)S(1)}, u32[]{:S(2)}, u32[]{:S(2)}) collective-permute-start(bf16[16,1024]{1,0:T(8,128)(2,1)S(1)} %get-tuple-element.49), channel_id=1, source_target_pairs={{0,16},{8,24},{16,0},{24,8},{1,17},{9,25},{17,1},{25,9},{2,18},{10... | collective-permute-start | bytes 98312 | tf_op jit(solution)/shard_map/ppermute | solution.py:685
  38.8 10.3 %collective-permute-start.7 = (bf16[64,1024]{1,0:T(8,128)(2,1)S(1)}, bf16[64,1024]{1,0:T(8,128)(2,1)S(1)}, u32[]{:S(2)}, u32[]{:S(2)}) collective-permute-start(bf16[64,1024]{1,0:T(8,128)(2,1)S(1)} %get-tuple-element.47.refs_0_), channel_id=1, source_target_pairs={{0,8},{8,0},{16,24},{24,16},{1,9},{9,1},{17,25},{25,17},{2,10},{10... | collective-permute-start | bytes 393224 | tf_op jit(solution)/shard_map/ppermute | solution.py:685
  44.8 4.3 %collective-permute-start.11 = (bf16[16,1024]{1,0:T(8,128)(2,1)S(1)}, bf16[16,1024]{1,0:T(8,128)(2,1)S(1)}, u32[]{:S(2)}, u32[]{:S(2)}) collective-permute-start(bf16[16,1024]{1,0:T(8,128)(2,1)S(1)} %collective-permute-done.9.refs_3_), channel_id=1, source_target_pairs={{0,8},{8,0},{16,24},{24,16},{1,9},{9,1},{17,25},{25,17},{2,10},{10... | collective-permute-start | bytes 98312 | tf_op jit(solution)/shard_map/ppermute | solution.py:685
  44.8 5.4 %collective-permute-start.10 = (bf16[48,1024]{1,0:T(8,128)(2,1)S(1)}, bf16[48,1024]{1,0:T(8,128)(2,1)S(1)}, u32[]{:S(2)}, u32[]{:S(2)}) collective-permute-start(bf16[48,1024]{1,0:T(8,128)(2,1)S(1)} %collective-permute-done.8.refs_2_), channel_id=1, source_target_pairs={{0,8},{8,0},{16,24},{24,16},{1,9},{9,1},{17,25},{25,17},{2,10},{10... | collective-permute-start | bytes 294920 | tf_op jit(solution)/shard_map/ppermute | solution.py:685
  51.5 5.8 %collective-permute-start.12 = (bf16[64,256]{1,0:T(8,128)(2,1)S(1)}, bf16[64,256]{1,0:T(8,128)(2,1)S(1)}, u32[]{:S(2)}, u32[]{:S(2)}) collective-permute-start(bf16[64,256]{1,0:T(8,128)(2,1)S(1)} %get-tuple-element.50), channel_id=1, source_target_pairs={{0,24},{8,16},{16,8},{24,0},{1,25},{9,17},{17,9},{25,1},{2,26},{10... | collective-permute-start | bytes 98312 | tf_op jit(solution)/shard_map/ppermute | solution.py:693
  52.0 5.3 %collective-permute-start.13 = (bf16[64,256]{1,0:T(8,128)(2,1)S(1)}, bf16[64,256]{1,0:T(8,128)(2,1)S(1)}, u32[]{:S(2)}, u32[]{:S(2)}) collective-permute-start(bf16[64,256]{1,0:T(8,128)(2,1)S(1)} %get-tuple-element.51), channel_id=1, source_target_pairs={{0,16},{8,24},{16,0},{24,8},{1,17},{9,25},{17,1},{25,9},{2,18},{10... | collective-permute-start | bytes 98312 | tf_op jit(solution)/shard_map/ppermute | solution.py:693
  54.4 3.9 %collective-permute-start.14 = (bf16[64,256]{1,0:T(8,128)(2,1)S(1)}, bf16[64,256]{1,0:T(8,128)(2,1)S(1)}, u32[]{:S(2)}, u32[]{:S(2)}) collective-permute-start(bf16[64,256]{1,0:T(8,128)(2,1)S(1)} %get-tuple-element.52), channel_id=1, source_target_pairs={{0,8},{8,0},{16,24},{24,16},{1,9},{9,1},{17,25},{25,17},{2,10},{10... | collective-permute-start | bytes 98312 | tf_op jit(solution)/shard_map/ppermute | solution.py:693

commit v15 on v9

--- a/solution.py
+++ b/solution.py
@@ -523,15 +523,15 @@
         head = iota((seq, width), 1) // HD
         merged = jnp.zeros((seq, width), F32)
         for h in range(width // HD):
-            mine = jnp.where(head == h, q.astype(F32), 0.0).astype(BF16)
+            mine = jnp.where(head == h, q.astype(F32) * float(HD) ** (-0.5), 0.0).astype(BF16)
             scores = lax.dot_general(
                 mine, keys, (((1,), (1,)), ((), ())), preferred_element_type=F32
-            ) * float(HD) ** (-0.5)
+            )
             scores = jnp.where(there, scores, -BIG)
             probs = jnp.exp(scores - jnp.max(scores, axis=1, keepdims=True))
             total = jnp.sum(probs, axis=1, keepdims=True)
             mixed = jnp.dot(probs.astype(BF16), values, preferred_element_type=F32)
-            merged = jnp.where(head == h, mixed / total, merged)
+            merged = jnp.where(head == h, mixed * (1.0 / total), merged)
         merged = merged.astype(BF16)
         for k in range(members):
             out_refs[-1 - k][:, t * width : (t + 1) * width] = merged[k * own : (k + 1) * own]

time: 57.8 us -> 57.8 us (level)
  no operation moved by 1% of the time
where the time goes in v15:
time: 57.8 us; the launch traced here: 57.6 us
  starting transfers between devices  17.8 us (31%)
  Pallas kernels  13.5 us (23%)
  waiting for transfers between devices  13.1 us (23%)
  blocking collectives  9.3 us (16%)
  local copies, waits for them, and re-layouts  2.48 us (4%)
  other arithmetic  0.72 us (1%)
  between operations  0.72 us (1%)
    pallas_call x11, Pallas kernels, call(): pl.pallas_call(kernel, out_shape=out, in_specs=list(specs), out_specs=jax...  13.5 us
    all_to_all x1, blocking collectives, body(): stats = lax.all_to_all(mine, ALL, 0, 0, tiled=True)  9.3 us
    ppermute x5, waiting for transfers between devices, body(): blocks[k] = [lax.ppermute(v, 'gx', swaps[low]) for v in source]  7.17 us
    ppermute x3, starting transfers between devices, body(): lax.ppermute(v, 'gx', swaps[nx - 1 - i])  4.45 us
    ppermute x5, starting transfers between devices, body(): blocks[k] = [lax.ppermute(v, 'gx', swaps[low]) for v in source]  4.28 us
    ppermute x1, starting transfers between devices, body(): lax.ppermute(first, 'gx', list(pairing(nx, False, False).items()))  3.09 us
    unnamed x8, local copies, waits for them, and re-layouts  2.48 us
    ppermute x1, starting transfers between devices, body(): lax.ppermute(second, 'gx', list(pairing(nx, True, narrow).items()))  2.47 us
  transfers between devices with their start and end apart: 15, of which 9 were waited for; matrix products, arithmetic and copies ran while one was open for 1% of the time, Pallas kernels for 9%

profile of v15, /device:TPU:0, one launch (start us, length us, event | category | flops | bytes accessed | tf_op | source)
XLA Modules:
  0.0 57.6 jit_solution(5719526534311328463)
XLA Ops:
  0.6 0.0 copy-start
  0.6 0.9 %copy-done = bf16[8,8,4,256]{3,2,1,0:T(4,128)(2,1)S(1)} copy-done((bf16[8,8,4,256]{3,2,1,0:T(4,128)(2,1)S(1)}, bf16[8,8,4,256]{3,2,1,0:T(4,128)(2,1)}, u32[]{:S(2)}) %copy-start) | copy-done | bytes 131096
  1.5 0.0 copy-start.2
  1.5 0.7 %copy-done.2 = s32[4,1,4]{2,1,0:T(1,128)S(1)} copy-done((s32[4,1,4]{2,1,0:T(1,128)S(1)}, s32[4,1,4]{2,1,0:T(1,128)}, u32[]{:S(2)}) %copy-start.2) | copy-done | bytes 88
  2.2 0.9 %pre.1 = (f32[8,256]{1,0:T(8,128)S(1)}, f32[8,256]{1,0:T(8,128)S(1)}, bf16[512,256]{1,0:T(8,128)(2,1)S(1)}, bf16[80,256]{1,0:T(8,128)(2,1)S(1)}, bf16[80,256]{1,...) custom-call(s32[4,1,4]{2,1,0:T(1,128)S(1)} %copy-done.2, bf16[8,8,4,256]{3,2,1,0:T(4,128)(2,1)S(1)} %copy-done), custom_call_target="tpu_custom_call" | custom-call | bytes 1000000 | tf_op jit(solution)/shard_map/pre/pallas_call | solution.py:561
  3.2 3.1 %collective-permute-start = (bf16[80,256]{1,0:T(8,128)(2,1)S(1)}, bf16[80,256]{1,0:T(8,128)(2,1)S(1)}, u32[]{:S(2)}, u32[]{:S(2)}) collective-permute-start(bf16[80,256]{1,0:T(8,128)(2,1)S(1)} %get-tuple-element.30), channel_id=1, source_target_pairs={{0,8},{8,0},{16,24},{24,16},{1,9},{9,1},{17,25},{25,17},{2,10},{10... | collective-permute-start | bytes 122888 | tf_op jit(solution)/shard_map/ppermute | solution.py:603
  6.3 2.5 %collective-permute-start.1 = (bf16[80,256]{1,0:T(8,128)(2,1)S(1)}, bf16[80,256]{1,0:T(8,128)(2,1)S(1)}, u32[]{:S(2)}, u32[]{:S(2)}) collective-permute-start(bf16[80,256]{1,0:T(8,128)(2,1)S(1)} %get-tuple-element.31), channel_id=1, source_target_pairs={{0,24},{8,16},{16,8},{24,0},{1,25},{9,17},{17,9},{25,1},{2,26},{10... | collective-permute-start | bytes 122888 | tf_op jit(solution)/shard_map/ppermute | solution.py:604
  8.7 0.1 collective-permute-start.2
  8.8 0.0 copy-start.1
  8.9 0.9 %copy-done.1 = bf16[2,32,864]{2,1,0:T(8,128)(2,1)S(1)} copy-done((bf16[2,32,864]{2,1,0:T(8,128)(2,1)S(1)}, bf16[2,32,864]{2,1,0:T(8,128)(2,1)}, u32[]{:S(2)}) %copy-start.1) | copy-done | bytes 110616
  9.7 1.4 %band0.1 = (bf16[3,1024,256]{2,1,0:T(8,128)(2,1)S(1)}, bf16[1,32,864]{2,1,0:T(8,128)(2,1)S(1)}) custom-call(bf16[2,32,864]{2,1,0:T(8,128)(2,1)S(1)} %copy-done.1), custom_call_target="tpu_custom_call" | custom-call | bytes 8000000 | tf_op jit(solution)/shard_map/band0/pallas_call | solution.py:561
  11.1 2.2 %collective-permute-done.2.rest_1_ = bf16[16,256]{1,0:T(8,128)(2,1)S(1)} collective-permute-done((bf16[16,256]{1,0:T(8,128)(2,1)S(1)}, bf16[16,256]{1,0:T(8,128)(2,1)S(1)}, u32[]{:S(2)}, u32[]{:S(2)}) %collective-permute-start.2) | collective-permute-done | bytes 8224 | tf_op jit(solution)/shard_map/ppermute | solution.py:608
  13.3 0.0 collective-permute-done.first_ref
  13.3 0.0 collective-permute-done.1.second_ref
  13.3 0.2 line.1
  13.5 0.1 collective-permute-start.3
  13.5 1.2 %collective-permute-done.3.other_ref.core_ref = bf16[112,256]{1,0:T(8,128)(2,1)S(1)} collective-permute-done((bf16[112,256]{1,0:T(8,128)(2,1)S(1)}, bf16[112,256]{1,0:T(8,128)(2,1)S(1)}, u32[]{:S(2)}, u32[]{:S(2)}) %collective-permute-start.3) | collective-permute-done | bytes 57376 | tf_op jit(solution)/shard_map/ppermute | solution.py:626
  14.8 0.2 chip.1
  15.0 1.6 %collective-permute-start.5 = (bf16[144,256]{1,0:T(8,128)(2,1)S(1)}, bf16[144,256]{1,0:T(8,128)(2,1)S(1)}, u32[]{:S(2)}, u32[]{:S(2)}) collective-permute-start(bf16[144,256]{1,0:T(8,128)(2,1)S(1)} %get-tuple-element.36), channel_id=1, source_target_pairs={{0,4},{4,0},{1,5},{5,1},{2,6},{6,2},{3,7},{7,3},{8,12},{12,8},{9,1... | collective-permute-start | bytes 221192 | tf_op jit(solution)/shard_map/ppermute | solution.py:644
  16.5 1.0 %collective-permute-start.4 = (bf16[112,256]{1,0:T(8,128)(2,1)S(1)}, bf16[112,256]{1,0:T(8,128)(2,1)S(1)}, u32[]{:S(2)}, u32[]{:S(2)}) collective-permute-start(bf16[112,256]{1,0:T(8,128)(2,1)S(1)} %get-tuple-element.35.own_ref), channel_id=1, source_target_pairs={{0,3},{1,2},{2,1},{3,0},{4,7},{5,6},{6,5},{7,4},{8,11},{9,10},{10,... | collective-permute-start | bytes 172040 | tf_op jit(solution)/shard_map/ppermute | solution.py:640
  17.5 0.7 %collective-permute-start.6 = (bf16[48,256]{1,0:T(8,128)(2,1)S(1)}, bf16[48,256]{1,0:T(8,128)(2,1)S(1)}, u32[]{:S(2)}, u32[]{:S(2)}) collective-permute-start(bf16[48,256]{1,0:T(8,128)(2,1)S(1)} %get-tuple-element.37), channel_id=1, source_target_pairs={{0,7},{1,6},{2,5},{3,4},{4,3},{5,2},{6,1},{7,0},{8,15},{9,14},{10,... | collective-permute-start | bytes 73736 | tf_op jit(solution)/shard_map/ppermute | solution.py:648
  18.3 0.7 %pad_maximum_fusion.rest_0_ = f32[6,32]{1,0:T(8,128)S(1)} fusion(f32[2,32]{1,0:T(2,128)} %param.12, f32[2,32]{1,0:T(2,128)} %param.10, f32[2,32]{1,0:T(2,128)} %param.9), kind=kLoop, calls=%fused_computation | loop fusion | flops 384 | bytes 1536 | tf_op jit(solution)/shard_map/concatenate | solution.py:610
  19.0 1.4 %band1.1 = (bf16[3,1024,256]{2,1,0:T(8,128)(2,1)S(1)}, f32[8,256]{1,0:T(8,128)S(1)}) custom-call(bf16[1,32,864]{2,1,0:T(8,128)(2,1)S(1)} %get-tuple-element.28._.weight_ref, f32[6,32]{1,0:T(8,128)S(1)} %pad_maximum_fusion.rest_0_), custom_call_target="tpu_custom_call" | custom-call | bytes 8000000 | tf_op jit(solution)/shard_map/band1/pallas_call | solution.py:561
  20.4 1.3 %collective-permute-done.6.rest_1_ = bf16[48,256]{1,0:T(8,128)(2,1)S(1)} collective-permute-done((bf16[48,256]{1,0:T(8,128)(2,1)S(1)}, bf16[48,256]{1,0:T(8,128)(2,1)S(1)}, u32[]{:S(2)}, u32[]{:S(2)}) %collective-permute-start.6) | collective-permute-done | bytes 24608 | tf_op jit(solution)/shard_map/ppermute | solution.py:648
  21.7 0.0 collective-permute-done.4.zface_ref
  21.7 0.0 collective-permute-done.5.rest_0_
  21.7 3.0 %first.1 = (f32[800,256]{1,0:T(8,128)S(1)}, f32[32,128]{1,0:T(8,128)S(1)}, f32[1152,128]{1,0:T(8,128)S(1)}) custom-call(bf16[768,256]{1,0:T(8,128)(2,1)S(1)} %get-tuple-element.33.ext_ref, bf16[112,256]{1,0:T(8,128)(2,1)S(1)} %get-tuple-element.35.own_ref, bf16[112,256]{1,0:T(8,128)(2,1)S(1)} %collective-permute-done.3.other_ref.core_ref, ...), custom_call_target="tpu_custom_call" | custom-call | flops 2000000000 | bytes 4000000 | tf_op jit(solution)/shard_map/first/pallas_call | solution.py:561
  24.7 9.3 %all_to_all.11 = f32[32,1,128]{2,1,0:T(1,128)S(1)} all-to-all(f32[32,1,128]{2,1,0:T(1,128)S(1)} %bitcast.5), channel_id=1, replica_groups=mesh['gx'=4,'gy'=2,'gz'=4] {'gx','gy','gz'}, dimensions={0} | all-to-all | bytes 32768 | tf_op jit(solution)/shard_map/all_to_all | solution.py:668
  34.0 0.0 copy-start.3
  34.0 1.8 %second.1 = (bf16[256,256]{1,0:T(8,128)(2,1)S(1)}, bf16[64,1024]{1,0:T(8,128)(2,1)S(1)}, bf16[32,1024]{1,0:T(8,128)(2,1)S(1)}, bf16[32,1024]{1,0:T(8,128)(2,1)S(1)}) custom-call(f32[32,128]{1,0:T(8,128)S(1)} %bitcast.4, f32[800,256]{1,0:T(8,128)S(1)} %get-tuple-element.42.mid_ref, f32[1152,128]{1,0:T(8,128)S(1)} %get-tuple-element.43.msk_ref, ...), custom_call_target="tpu_custom_call" | custom-call | flops 1000000000 | bytes 4000000 | tf_op jit(solution)/shard_map/second/pallas_call | solution.py:561
  35.8 0.7 %collective-permute-start.8 = (bf16[32,1024]{1,0:T(8,128)(2,1)S(1)}, bf16[32,1024]{1,0:T(8,128)(2,1)S(1)}, u32[]{:S(2)}, u32[]{:S(2)}) collective-permute-start(bf16[32,1024]{1,0:T(8,128)(2,1)S(1)} %get-tuple-element.48), channel_id=1, source_target_pairs={{0,16},{8,24},{16,0},{24,8},{1,17},{9,25},{17,1},{25,9},{2,18},{10... | collective-permute-start | bytes 196616 | tf_op jit(solution)/shard_map/ppermute | solution.py:684
  36.5 2.3 %collective-permute-start.9 = (bf16[32,1024]{1,0:T(8,128)(2,1)S(1)}, bf16[32,1024]{1,0:T(8,128)(2,1)S(1)}, u32[]{:S(2)}, u32[]{:S(2)}) collective-permute-start(bf16[32,1024]{1,0:T(8,128)(2,1)S(1)} %get-tuple-element.49), channel_id=1, source_target_pairs={{0,16},{8,24},{16,0},{24,8},{1,17},{9,25},{17,1},{25,9},{2,18},{10... | collective-permute-start | bytes 196616 | tf_op jit(solution)/shard_map/ppermute | solution.py:684
  38.8 0.6 collective-permute-start.7
  39.4 4.1 %collective-permute-done.8.refs_2_ = bf16[32,1024]{1,0:T(8,128)(2,1)S(1)} collective-permute-done((bf16[32,1024]{1,0:T(8,128)(2,1)S(1)}, bf16[32,1024]{1,0:T(8,128)(2,1)S(1)}, u32[]{:S(2)}, u32[]{:S(2)}) %collective-permute-start.8) | collective-permute-done | bytes 65568 | tf_op jit(solution)/shard_map/ppermute | solution.py:684
  43.5 0.0 collective-permute-start.10
  43.5 1.3 %collective-permute-done.9.refs_3_ = bf16[32,1024]{1,0:T(8,128)(2,1)S(1)} collective-permute-done((bf16[32,1024]{1,0:T(8,128)(2,1)S(1)}, bf16[32,1024]{1,0:T(8,128)(2,1)S(1)}, u32[]{:S(2)}, u32[]{:S(2)}) %collective-permute-start.9) | collective-permute-done | bytes 65568 | tf_op jit(solution)/shard_map/ppermute | solution.py:684
  44.8 0.7 %collective-permute-start.11 = (bf16[32,1024]{1,0:T(8,128)(2,1)S(1)}, bf16[32,1024]{1,0:T(8,128)(2,1)S(1)}, u32[]{:S(2)}, u32[]{:S(2)}) collective-permute-start(bf16[32,1024]{1,0:T(8,128)(2,1)S(1)} %collective-permute-done.9.refs_3_), channel_id=1, source_target_pairs={{0,8},{8,0},{16,24},{24,16},{1,9},{9,1},{17,25},{25,17},{2,10},{10... | collective-permute-start | bytes 196616 | tf_op jit(solution)/shard_map/ppermute | solution.py:684
  45.5 0.0 copy-done.3
  45.5 1.9 %turn.1.weight_ref = bf16[1024,768]{1,0:T(8,128)(2,1)S(1)} custom-call(bf16[3,256,1024]{2,1,0:T(8,128)(2,1)S(1)} %copy-done.3), custom_call_target="tpu_custom_call" | custom-call | flops 1610612736 | bytes 6000000 | tf_op jit(solution)/shard_map/turn/pallas_call | solution.py:561
  47.5 0.7 %collective-permute-done.10.refs_4_ = bf16[32,1024]{1,0:T(8,128)(2,1)S(1)} collective-permute-done((bf16[32,1024]{1,0:T(8,128)(2,1)S(1)}, bf16[32,1024]{1,0:T(8,128)(2,1)S(1)}, u32[]{:S(2)}, u32[]{:S(2)}) %collective-permute-start.10) | collective-permute-done | bytes 65568 | tf_op jit(solution)/shard_map/ppermute | solution.py:684
  48.2 1.0 %collective-permute-done.11.refs_5_ = bf16[32,1024]{1,0:T(8,128)(2,1)S(1)} collective-permute-done((bf16[32,1024]{1,0:T(8,128)(2,1)S(1)}, bf16[32,1024]{1,0:T(8,128)(2,1)S(1)}, u32[]{:S(2)}, u32[]{:S(2)}) %collective-permute-start.11) | collective-permute-done | bytes 65568 | tf_op jit(solution)/shard_map/ppermute | solution.py:684
  49.2 0.0 collective-permute-done.7.refs_1_
  49.2 1.3 %attend.1 = (bf16[64,256]{1,0:T(8,128)(2,1)S(1)}, bf16[64,256]{1,0:T(8,128)(2,1)S(1)}, bf16[64,256]{1,0:T(8,128)(2,1)S(1)}, bf16[64,256]{1,0:T(8,128)(2,1)S(1)}) custom-call(f32[8,256]{1,0:T(8,128)S(1)} %get-tuple-element.46.keys_ref, bf16[1024,768]{1,0:T(8,128)(2,1)S(1)} %turn.1.weight_ref, bf16[64,1024]{1,0:T(8,128)(2,1)S(1)} %get-tuple-element.47.refs_0_, ...), custom_call_target="tpu_custom_call" | custom-call | flops 1000000000 | bytes 3000000 | tf_op jit(solution)/shard_map/attend/pallas_call | solution.py:561
  50.5 0.6 collective-permute-start.12
  51.1 1.6 %collective-permute-start.13 = (bf16[64,256]{1,0:T(8,128)(2,1)S(1)}, bf16[64,256]{1,0:T(8,128)(2,1)S(1)}, u32[]{:S(2)}, u32[]{:S(2)}) collective-permute-start(bf16[64,256]{1,0:T(8,128)(2,1)S(1)} %get-tuple-element.51), channel_id=1, source_target_pairs={{0,16},{8,24},{16,0},{24,8},{1,17},{9,25},{17,1},{25,9},{2,18},{10... | collective-permute-start | bytes 98312 | tf_op jit(solution)/shard_map/ppermute | solution.py:692
  52.7 2.3 %collective-permute-start.14 = (bf16[64,256]{1,0:T(8,128)(2,1)S(1)}, bf16[64,256]{1,0:T(8,128)(2,1)S(1)}, u32[]{:S(2)}, u32[]{:S(2)}) collective-permute-start(bf16[64,256]{1,0:T(8,128)(2,1)S(1)} %get-tuple-element.52), channel_id=1, source_target_pairs={{0,8},{8,0},{16,24},{24,16},{1,9},{9,1},{17,25},{25,17},{2,10},{10... | collective-permute-start | bytes 98312 | tf_op jit(solution)/shard_map/ppermute | solution.py:692
  55.0 0.7 %fine.1 = bf16[8,8,4,256]{3,2,1,0:T(4,128)(2,1)} custom-call(bf16[256,256]{1,0:T(8,128)(2,1)S(1)} %get-tuple-element.45.field_ref), custom_call_target="tpu_custom_call" | custom-call | bytes 4000000 | tf_op jit(solution)/shard_map/fine/pallas_call | solution.py:561
  55.7 0.6 %collective-permute-done.12.refs_0_ = bf16[64,256]{1,0:T(8,128)(2,1)S(1)} collective-permute-done((bf16[64,256]{1,0:T(8,128)(2,1)S(1)}, bf16[64,256]{1,0:T(8,128)(2,1)S(1)}, u32[]{:S(2)}, u32[]{:S(2)}) %collective-permute-start.12) | collective-permute-done | bytes 32800 | tf_op jit(solution)/shard_map/ppermute | solution.py:692
  56.3 0.0 collective-permute-done.13.refs_1_
  56.3 0.6 collective-permute-done.14.refs_2_
  56.9 0.7 %place.1 = bf16[1,64,1024]{2,1,0:T(8,128)(2,1)} custom-call(f32[8,256]{1,0:T(8,128)S(1)} %get-tuple-element.38.rest_2_.keep_ref, bf16[64,256]{1,0:T(8,128)(2,1)S(1)} %collective-permute-done.12.refs_0_, bf16[64,256]{1,0:T(8,128)(2,1)S(1)} %collective-permute-done.13.refs_1_, bf16[64,256]{1,0:T(8,128)(2,1)S(1)} %collective-permute-done.14.refs_2_, ...), custom_call_target="tpu_custom_call" | custom-call | bytes 300000 | tf_op jit(solution)/shard_map/place/pallas_call | solution.py:561
Async XLA Ops:
  0.6 0.9 %copy-start = (bf16[8,8,4,256]{3,2,1,0:T(4,128)(2,1)S(1)}, bf16[8,8,4,256]{3,2,1,0:T(4,128)(2,1)}, u32[]{:S(2)}) copy-start(bf16[8,8,4,256]{3,2,1,0:T(4,128)(2,1)} %feat_ref.1) | copy-start | bytes 393220
  1.5 0.7 %copy-start.2 = (s32[4,1,4]{2,1,0:T(1,128)S(1)}, s32[4,1,4]{2,1,0:T(1,128)}, u32[]{:S(2)}) copy-start(s32[4,1,4]{2,1,0:T(1,128)} %occ_ref.1) | copy-start | bytes 196
  3.2 10.1 %collective-permute-start = (bf16[80,256]{1,0:T(8,128)(2,1)S(1)}, bf16[80,256]{1,0:T(8,128)(2,1)S(1)}, u32[]{:S(2)}, u32[]{:S(2)}) collective-permute-start(bf16[80,256]{1,0:T(8,128)(2,1)S(1)} %get-tuple-element.30), channel_id=1, source_target_pairs={{0,8},{8,0},{16,24},{24,16},{1,9},{9,1},{17,25},{25,17},{2,10},{10... | collective-permute-start | bytes 122888 | tf_op jit(solution)/shard_map/ppermute | solution.py:603
  6.3 7.0 %collective-permute-start.1 = (bf16[80,256]{1,0:T(8,128)(2,1)S(1)}, bf16[80,256]{1,0:T(8,128)(2,1)S(1)}, u32[]{:S(2)}, u32[]{:S(2)}) collective-permute-start(bf16[80,256]{1,0:T(8,128)(2,1)S(1)} %get-tuple-element.31), channel_id=1, source_target_pairs={{0,24},{8,16},{16,8},{24,0},{1,25},{9,17},{17,9},{25,1},{2,26},{10... | collective-permute-start | bytes 122888 | tf_op jit(solution)/shard_map/ppermute | solution.py:604
  8.7 4.5 %collective-permute-start.2 = (bf16[16,256]{1,0:T(8,128)(2,1)S(1)}, bf16[16,256]{1,0:T(8,128)(2,1)S(1)}, u32[]{:S(2)}, u32[]{:S(2)}) collective-permute-start(bf16[16,256]{1,0:T(8,128)(2,1)S(1)} %get-tuple-element.32.rest_0_), channel_id=1, source_target_pairs={{0,16},{8,24},{16,0},{24,8},{1,17},{9,25},{17,1},{25,9},{2,18},{10... | collective-permute-start | bytes 24584 | tf_op jit(solution)/shard_map/ppermute | solution.py:608
  8.8 0.9 %copy-start.1 = (bf16[2,32,864]{2,1,0:T(8,128)(2,1)S(1)}, bf16[2,32,864]{2,1,0:T(8,128)(2,1)}, u32[]{:S(2)}) copy-start(bf16[2,32,864]{2,1,0:T(8,128)(2,1)} %weight_ref.2) | copy-start | bytes 331780
  13.5 1.3 %collective-permute-start.3 = (bf16[112,256]{1,0:T(8,128)(2,1)S(1)}, bf16[112,256]{1,0:T(8,128)(2,1)S(1)}, u32[]{:S(2)}, u32[]{:S(2)}) collective-permute-start(bf16[112,256]{1,0:T(8,128)(2,1)S(1)} %get-tuple-element.34.own_ref), channel_id=1, source_target_pairs={{0,1},{1,0},{2,3},{3,2},{4,5},{5,4},{6,7},{7,6},{8,9},{9,8},{10,11... | collective-permute-start | bytes 172040 | tf_op jit(solution)/shard_map/ppermute | solution.py:626
  15.0 6.7 %collective-permute-start.5 = (bf16[144,256]{1,0:T(8,128)(2,1)S(1)}, bf16[144,256]{1,0:T(8,128)(2,1)S(1)}, u32[]{:S(2)}, u32[]{:S(2)}) collective-permute-start(bf16[144,256]{1,0:T(8,128)(2,1)S(1)} %get-tuple-element.36), channel_id=1, source_target_pairs={{0,4},{4,0},{1,5},{5,1},{2,6},{6,2},{3,7},{7,3},{8,12},{12,8},{9,1... | collective-permute-start | bytes 221192 | tf_op jit(solution)/shard_map/ppermute | solution.py:644
  16.5 5.2 %collective-permute-start.4 = (bf16[112,256]{1,0:T(8,128)(2,1)S(1)}, bf16[112,256]{1,0:T(8,128)(2,1)S(1)}, u32[]{:S(2)}, u32[]{:S(2)}) collective-permute-start(bf16[112,256]{1,0:T(8,128)(2,1)S(1)} %get-tuple-element.35.own_ref), channel_id=1, source_target_pairs={{0,3},{1,2},{2,1},{3,0},{4,7},{5,6},{6,5},{7,4},{8,11},{9,10},{10,... | collective-permute-start | bytes 172040 | tf_op jit(solution)/shard_map/ppermute | solution.py:640
  17.5 4.2 %collective-permute-start.6 = (bf16[48,256]{1,0:T(8,128)(2,1)S(1)}, bf16[48,256]{1,0:T(8,128)(2,1)S(1)}, u32[]{:S(2)}, u32[]{:S(2)}) collective-permute-start(bf16[48,256]{1,0:T(8,128)(2,1)S(1)} %get-tuple-element.37), channel_id=1, source_target_pairs={{0,7},{1,6},{2,5},{3,4},{4,3},{5,2},{6,1},{7,0},{8,15},{9,14},{10,... | collective-permute-start | bytes 73736 | tf_op jit(solution)/shard_map/ppermute | solution.py:648
  34.0 11.5 %copy-start.3 = (bf16[3,256,1024]{2,1,0:T(8,128)(2,1)S(1)}, bf16[3,256,1024]{2,1,0:T(8,128)(2,1)}, u32[]{:S(2)}) copy-start(bf16[3,256,1024]{2,1,0:T(8,128)(2,1)} %weight_ref.3) | copy-start | bytes 4718596
  35.8 7.7 %collective-permute-start.8 = (bf16[32,1024]{1,0:T(8,128)(2,1)S(1)}, bf16[32,1024]{1,0:T(8,128)(2,1)S(1)}, u32[]{:S(2)}, u32[]{:S(2)}) collective-permute-start(bf16[32,1024]{1,0:T(8,128)(2,1)S(1)} %get-tuple-element.48), channel_id=1, source_target_pairs={{0,16},{8,24},{16,0},{24,8},{1,17},{9,25},{17,1},{25,9},{2,18},{10... | collective-permute-start | bytes 196616 | tf_op jit(solution)/shard_map/ppermute | solution.py:684
  36.5 8.4 %collective-permute-start.9 = (bf16[32,1024]{1,0:T(8,128)(2,1)S(1)}, bf16[32,1024]{1,0:T(8,128)(2,1)S(1)}, u32[]{:S(2)}, u32[]{:S(2)}) collective-permute-start(bf16[32,1024]{1,0:T(8,128)(2,1)S(1)} %get-tuple-element.49), channel_id=1, source_target_pairs={{0,16},{8,24},{16,0},{24,8},{1,17},{9,25},{17,1},{25,9},{2,18},{10... | collective-permute-start | bytes 196616 | tf_op jit(solution)/shard_map/ppermute | solution.py:684
  38.8 10.4 %collective-permute-start.7 = (bf16[64,1024]{1,0:T(8,128)(2,1)S(1)}, bf16[64,1024]{1,0:T(8,128)(2,1)S(1)}, u32[]{:S(2)}, u32[]{:S(2)}) collective-permute-start(bf16[64,1024]{1,0:T(8,128)(2,1)S(1)} %get-tuple-element.47.refs_0_), channel_id=1, source_target_pairs={{0,8},{8,0},{16,24},{24,16},{1,9},{9,1},{17,25},{25,17},{2,10},{10... | collective-permute-start | bytes 393224 | tf_op jit(solution)/shard_map/ppermute | solution.py:684
  43.5 4.7 %collective-permute-start.10 = (bf16[32,1024]{1,0:T(8,128)(2,1)S(1)}, bf16[32,1024]{1,0:T(8,128)(2,1)S(1)}, u32[]{:S(2)}, u32[]{:S(2)}) collective-permute-start(bf16[32,1024]{1,0:T(8,128)(2,1)S(1)} %collective-permute-done.8.refs_2_), channel_id=1, source_target_pairs={{0,8},{8,0},{16,24},{24,16},{1,9},{9,1},{17,25},{25,17},{2,10},{10... | collective-permute-start | bytes 196616 | tf_op jit(solution)/shard_map/ppermute | solution.py:684
  44.8 4.4 %collective-permute-start.11 = (bf16[32,1024]{1,0:T(8,128)(2,1)S(1)}, bf16[32,1024]{1,0:T(8,128)(2,1)S(1)}, u32[]{:S(2)}, u32[]{:S(2)}) collective-permute-start(bf16[32,1024]{1,0:T(8,128)(2,1)S(1)} %collective-permute-done.9.refs_3_), channel_id=1, source_target_pairs={{0,8},{8,0},{16,24},{24,16},{1,9},{9,1},{17,25},{25,17},{2,10},{10... | collective-permute-start | bytes 196616 | tf_op jit(solution)/shard_map/ppermute | solution.py:684
  50.5 5.8 %collective-permute-start.12 = (bf16[64,256]{1,0:T(8,128)(2,1)S(1)}, bf16[64,256]{1,0:T(8,128)(2,1)S(1)}, u32[]{:S(2)}, u32[]{:S(2)}) collective-permute-start(bf16[64,256]{1,0:T(8,128)(2,1)S(1)} %get-tuple-element.50), channel_id=1, source_target_pairs={{0,24},{8,16},{16,8},{24,0},{1,25},{9,17},{17,9},{25,1},{2,26},{10... | collective-permute-start | bytes 98312 | tf_op jit(solution)/shard_map/ppermute | solution.py:692
  51.1 5.2 %collective-permute-start.13 = (bf16[64,256]{1,0:T(8,128)(2,1)S(1)}, bf16[64,256]{1,0:T(8,128)(2,1)S(1)}, u32[]{:S(2)}, u32[]{:S(2)}) collective-permute-start(bf16[64,256]{1,0:T(8,128)(2,1)S(1)} %get-tuple-element.51), channel_id=1, source_target_pairs={{0,16},{8,24},{16,0},{24,8},{1,17},{9,25},{17,1},{25,9},{2,18},{10... | collective-permute-start | bytes 98312 | tf_op jit(solution)/shard_map/ppermute | solution.py:692
  52.7 4.2 %collective-permute-start.14 = (bf16[64,256]{1,0:T(8,128)(2,1)S(1)}, bf16[64,256]{1,0:T(8,128)(2,1)S(1)}, u32[]{:S(2)}, u32[]{:S(2)}) collective-permute-start(bf16[64,256]{1,0:T(8,128)(2,1)S(1)} %get-tuple-element.52), channel_id=1, source_target_pairs={{0,8},{8,0},{16,24},{24,16},{1,9},{9,1},{17,25},{25,17},{2,10},{10... | collective-permute-start | bytes 98312 | tf_op jit(solution)/shard_map/ppermute | solution.py:692
